TPU v7x, 32 devices: a whole 2x2x4 slice. The times are simulated.
32 devices in a mesh: samp: 8 (over z, y), tok: 4 (over x, core).
Axes of the slice: x: 2, y: 2, z: 4, core: 2. Of those that a mesh axis runs over, the one named last changes fastest.
Arguments:
- atom_feats: bfloat16 [32, 5120, 128], P('samp', 'tok'), may hold values from -6 to 6
- atom_counts: int32 [4, 64], P('tok'), may hold values from 1 to 24, 1280 in all within a row
- atom_mask: int32 [5120], replicated, may hold values 0 or 1
- token_single: bfloat16 [256, 768], P('tok'), may hold values from -6 to 6
- pair: bfloat16 [256, 256, 128], P('tok', 'samp'), may hold values from -6 to 6
- pair_gain: float32 [128], replicated, may hold values from 0.5 to 2
- w_bias: bfloat16 [128, 16], replicated
- w_atom_qkv: bfloat16 [128, 384], replicated
- w_atom_out: bfloat16 [128, 128], replicated, may hold values from -0.5 to 0.5
- w_embed: bfloat16 [128, 768], replicated, may hold values from -0.5 to 0.5
- w_qkv: bfloat16 [768, 2304], replicated, may hold values from -0.21875 to 0.21875
- w_out: bfloat16 [768, 768], replicated, may hold values from -0.21875 to 0.21875
- w_gate: bfloat16 [768, 1536], replicated, may hold values from -0.21875 to 0.21875
- w_up: bfloat16 [768, 1536], replicated, may hold values from -0.21875 to 0.21875
- w_down: bfloat16 [1536, 768], replicated, may hold values from -0.15625 to 0.15625
- cotangent: bfloat16 [32, 256, 768], P('samp', 'tok'), may hold values from -6 to 6
Outputs:
- token_out: bfloat16 [32, 256, 768], P('samp', 'tok')
- pair_grad: float32 [256, 256, 128], P('tok', 'samp')
Inputs may be any that keep to these rules, and one draw needn't show every extreme that they name: `atom_counts`: each row sums to 1280.
All inputs are finite; a program needn't handle non-finite values.
Results may differ from a plain program's by a relative error of at most 0.015.
The roundings to bfloat16 on the way count: a program that leaves them out, or rounds other values in their place, can miss the bound.
Values may be sent and summed in bfloat16 or wider, within the bound.
No kernel may reach another device: no remote copies, remote signals or barrier semaphores. Data moves between devices by JAX's collectives and lax.ppermute only.
A program may use at most 192 MiB of HBM per device.

v0:
```python
import functools

import jax
import jax.numpy as jnp
from jax import lax
from jax.experimental import pallas as pl
from jax.experimental.pallas import tpu as pltpu
from jax.sharding import PartitionSpec as P

C_ATOM = 128
ATOM_HEADS = 4
C_TOK = 768
HEADS = 16
ATOM_HD = 32
HD = 48
CZ = 128
HALO = 48
PAIRS = HEADS // 2

epsilon = 1e-05
f32 = jnp.float32
bf16 = jnp.bfloat16

WINDOWS = ((0, 128), (0, 256), (128, 384), (256, 384))


def nn(a, b):
    return lax.dot_general(a, b, (((1,), (0,)), ((), ())), preferred_element_type=f32)


def nt(a, b):
    return lax.dot_general(a, b, (((1,), (1,)), ((), ())), preferred_element_type=f32)


def tn(a, b):
    return lax.dot_general(a, b, (((0,), (0,)), ((), ())), preferred_element_type=f32)


def norm_rows(values):
    center = values - jnp.mean(values, axis=-1, keepdims=True)
    scale_inv = lax.rsqrt(jnp.mean(center * center, axis=-1, keepdims=True) + epsilon)
    return (center * scale_inv, scale_inv)


def iota(shape, dim):
    return lax.broadcasted_iota(jnp.int32, shape, dim)


def split_heads(w_bias):
    row, col = iota((PAIRS, HEADS), 0), iota((PAIRS, HEADS), 1)
    even = (col == 2 * row).astype(f32).astype(bf16)
    odd = (col == 2 * row + 1).astype(f32).astype(bf16)
    return nt(even, w_bias).astype(bf16), nt(odd, w_bias).astype(bf16)


def bias_kernel(pair_ref, gain_ref, w_bias_ref, out_ref, scaled_ref, stage_ref):
    rows, keys = pair_ref.shape[0], pair_ref.shape[1]
    gain = gain_ref[...]

    def norm_step(i, carry):
        block = pair_ref[pl.ds(i * 8, 8)].astype(f32).reshape(8 * keys, CZ)
        hat, unused = norm_rows(block)
        scaled_ref[pl.ds(pl.multiple_of(i * 8 * keys, 8 * keys), 8 * keys), :] = hat * gain
        return carry

    lax.fori_loop(0, rows // 8, norm_step, 0)
    even, odd = split_heads(w_bias_ref[...])
    weights = jnp.concatenate([even, odd], axis=1)
    blank = jnp.zeros((rows, CZ), bf16)
    for j in range(keys):
        block = scaled_ref[pl.ds(j, rows, stride=keys), :].astype(bf16)
        both = jnp.concatenate(
            [jnp.concatenate([block, blank], axis=1), jnp.concatenate([blank, block], axis=1)],
            axis=0,
        )
        stage_ref[pl.ds(j * PAIRS, PAIRS), :] = nt(weights, both)
    out_ref[...] = stage_ref[...].astype(bf16)


def pair_bias(pair, pair_gain, w_bias):
    rows, keys = pair.shape[0], pair.shape[1]
    return pl.pallas_call(
        bias_kernel,
        out_shape=jax.ShapeDtypeStruct((keys * PAIRS, 2 * rows), bf16),
        scratch_shapes=[
            pltpu.VMEM((rows * keys, CZ), f32),
            pltpu.VMEM((keys * PAIRS, 2 * rows), f32),
        ],
        compiler_params=pltpu.CompilerParams(vmem_limit_bytes=16 << 20),
        cost_estimate=pl.CostEstimate(flops=10**7, bytes_accessed=10**7, transcendentals=0),
        name="pair_bias",
    )(pair, pair_gain.reshape(1, CZ), w_bias)


def atom_kernel(
    feats_ref, left_ref, right_ref, flags_ref, counts_ref, single_ref, w_qkv_ref, w_out_ref,
    w_embed_ref, tokens_ref, normed_ref, xn_ref, qkv_ref, keybias_ref, onehot_ref, pooled_ref,
    counts_col_ref,
):
    atoms = feats_ref.shape[1]
    padded = atoms + 2 * HALO
    tok_rows = single_ref.shape[0]

    @pl.when(pl.program_id(0) == 0)
    def prepare():
        eye = iota((128, 128), 0) == iota((128, 128), 1)
        for b in range(flags_ref.shape[0]):
            row = jnp.broadcast_to(flags_ref[b : b + 1, :], (128, 128))
            col = jnp.sum(jnp.where(eye, row, 0.0), axis=1, keepdims=True)
            keybias_ref[b * 128 : (b + 1) * 128, :] = jnp.broadcast_to(
                (col - 1.0) * 1e30, (128, 128)
            )
        counts = jnp.broadcast_to(counts_ref[...].astype(f32), (tok_rows, tok_rows))
        sub, lane = iota((tok_rows, tok_rows), 0), iota((tok_rows, tok_rows), 1)
        start = jnp.sum(jnp.where(lane < sub, counts, 0.0), axis=1, keepdims=True)
        own = jnp.sum(jnp.where(lane == sub, counts, 0.0), axis=1, keepdims=True)
        counts_col_ref[...] = jnp.broadcast_to(own, (tok_rows, 128))
        pos = iota((tok_rows, 128), 1).astype(f32)
        for g in range(atoms // 128):
            at = pos + float(g * 128)
            hit = jnp.where((at >= start) & (at < start + own), 1.0, 0.0).astype(bf16)
            onehot_ref[g] = jnp.concatenate([hit, hit], axis=1)

    xn_ref[0:HALO, :] = norm_rows(left_ref[0].astype(f32))[0].astype(bf16)
    xn_ref[atoms + HALO : padded, :] = norm_rows(right_ref[0].astype(f32))[0].astype(bf16)

    def norm_step(i, carry):
        at = pl.multiple_of(i * 256, 256)
        block = feats_ref[0, pl.ds(at, 256), :].astype(f32)
        xn_ref[pl.ds(HALO + at, 256), :] = norm_rows(block)[0].astype(bf16)
        return carry

    lax.fori_loop(0, atoms // 256, norm_step, 0)

    chunk = padded // 4
    w_qkv = w_qkv_ref[...]

    def qkv_step(i, carry):
        at = pl.multiple_of(i * chunk, 8)
        qkv_ref[pl.ds(at, chunk), :] = nn(xn_ref[pl.ds(at, chunk), :], w_qkv).astype(bf16)
        return carry

    for i in range(4):
        qkv_ref[i * chunk : (i + 1) * chunk, :] = nn(
            xn_ref[i * chunk : (i + 1) * chunk, :], w_qkv
        ).astype(bf16)

    pooled_ref[...] = jnp.zeros_like(pooled_ref)
    lane = iota((32, 128), 1)
    head_of = lane // ATOM_HD
    head_mask = [(head_of == h).astype(f32).astype(bf16) for h in range(ATOM_HEADS)]
    own_atom = (lane % 32) == iota((32, 128), 0)
    factor = ATOM_HD ** (-0.5)

    def group_step(g, carry):
        base = pl.multiple_of(g * 128, 128)
        queries = qkv_ref[pl.ds(base + HALO, 128), 0:C_ATOM]
        mixed = []
        for w in range(4):
            query = queries[32 * w : 32 * w + 32]
            spread = jnp.concatenate([query * head_mask[h] for h in range(ATOM_HEADS)], axis=0)
            keys = qkv_ref[pl.ds(base + 32 * w, 128), C_ATOM : 2 * C_ATOM]
            values = qkv_ref[pl.ds(base + 32 * w, 128), 2 * C_ATOM : 3 * C_ATOM]
            scores = nt(keys, spread) * factor
            keybias = keybias_ref[pl.ds(base + 32 * w, 128), :]
            keybias = jnp.concatenate(
                [keybias[0:48], jnp.where(own_atom, 0.0, keybias[48:80]), keybias[80:128]], axis=0
            )
            scores = scores + keybias
            expo = jnp.exp(scores - jnp.max(scores, axis=0, keepdims=True))
            weights = expo * (1.0 / jnp.sum(expo, axis=0, keepdims=True))
            part = tn(weights.astype(bf16), values)
            mix = part[0:32]
            for h in range(1, ATOM_HEADS):
                mix = jnp.where(head_of == h, part[32 * h : 32 * h + 32], mix)
            mixed.append(mix.astype(bf16))
        mixed = jnp.concatenate(mixed, axis=0)
        feats = feats_ref[0, pl.ds(base, 128), :].astype(f32)
        updated = (feats + nn(mixed, w_out_ref[...])).astype(bf16)
        embedded = jnp.maximum(nn(updated, w_embed_ref[...]), 0.0)
        high = embedded.astype(bf16)
        low = (embedded - high.astype(f32)).astype(bf16)
        pooled_ref[...] += nn(onehot_ref[g], jnp.concatenate([high, low], axis=0))
        return carry

    lax.fori_loop(0, atoms // 128, group_step, 0)
    counts = counts_col_ref[:, 0:1]
    tokens = pooled_ref[...] / counts + single_ref[...].astype(f32)
    tokens_ref[0] = tokens
    normed_ref[0] = norm_rows(tokens)[0].astype(bf16)


def atom_stage(feats, left, right, flags, counts, single, w_qkv, w_out, w_embed):
    batch, atoms, _ = feats.shape
    tok_rows = single.shape[0]
    padded = atoms + 2 * HALO
    by_sample = lambda rows, cols: pl.BlockSpec((1, rows, cols), lambda s: (s, 0, 0))
    whole = lambda a: pl.BlockSpec(a.shape, lambda s: (0,) * a.ndim)
    return pl.pallas_call(
        atom_kernel,
        grid=(batch,),
        in_specs=[
            by_sample(atoms, C_ATOM), by_sample(HALO, C_ATOM), by_sample(HALO, C_ATOM),
            whole(flags), whole(counts), whole(single), whole(w_qkv), whole(w_out), whole(w_embed),
        ],
        out_specs=[by_sample(tok_rows, C_TOK), by_sample(tok_rows, C_TOK)],
        out_shape=[
            jax.ShapeDtypeStruct((batch, tok_rows, C_TOK), f32),
            jax.ShapeDtypeStruct((batch, tok_rows, C_TOK), bf16),
        ],
        scratch_shapes=[
            pltpu.VMEM((padded, C_ATOM), bf16),
            pltpu.VMEM((padded, 3 * C_ATOM), bf16),
            pltpu.VMEM((flags.shape[0] * 128, 128), f32),
            pltpu.VMEM((atoms // 128, tok_rows, 256), bf16),
            pltpu.VMEM((tok_rows, C_TOK), f32),
            pltpu.VMEM((tok_rows, 128), f32),
        ],
        compiler_params=pltpu.CompilerParams(vmem_limit_bytes=24 << 20),
        cost_estimate=pl.CostEstimate(
            flops=6 * 10**9, bytes_accessed=4 * 10**6, transcendentals=3 * 10**6
        ),
        name="atoms",
    )(feats, left, right, flags, counts, single, w_qkv, w_out, w_embed)


def head_masks(rows):
    masks = []
    for pair in range(4):
        low, high = WINDOWS[pair]
        lane = iota((rows, high - low), 1) + low
        first = 2 * pair * HD
        masks.append(
            [(lane >= first + HD * k) & (lane < first + HD * (k + 1)) for k in range(2)]
        )
    return masks


def token_kernel(
    local_ref, all_ref, tokens_ref, bias_ref, cot_ref, w_qkv_hbm, w_out_hbm, w_gate_hbm, w_up_hbm,
    w_down_hbm, resid_ref, hidden_ref, d_bias_ref, w_qkv_ref, w_out_ref, w_gate_ref, w_up_ref,
    w_down_ref, sems, q_ref, kv_ref, biasf_ref, probs_ref, att_ref, d_gate_ref, d_up_ref, hat_ref,
    d_bias_f_ref,
):
    batch, keys_all = all_ref.shape[0], all_ref.shape[1]
    tok_rows = tokens_ref.shape[1]
    rows = batch * tok_rows
    copies = [
        pltpu.make_async_copy(src, dst, sems.at[i])
        for i, (src, dst) in enumerate(
            [
                (w_qkv_hbm, w_qkv_ref), (w_out_hbm, w_out_ref), (w_gate_hbm, w_gate_ref),
                (w_up_hbm, w_up_ref), (w_down_hbm, w_down_ref),
            ]
        )
    ]
    for copy in copies:
        copy.start()
    biasf_ref[...] = bias_ref[...].astype(f32)
    copies[0].wait()

    def q_step(n, carry):
        at = pl.multiple_of(n * 256, 256)
        q_ref[:, pl.ds(at, 256)] = nn(
            local_ref[...].reshape(rows, C_TOK), w_qkv_ref[:, pl.ds(at, 256)]
        ).astype(bf16)
        return carry

    lax.fori_loop(0, C_TOK // 256, q_step, 0)

    def kv_step(i, carry):
        s, n = i // 3, i % 3
        at = pl.multiple_of(n * 512, 512)
        kv_ref[s, :, pl.ds(at, 512)] = nn(
            all_ref[s], w_qkv_ref[:, pl.ds(pl.multiple_of(C_TOK + at, 256), 512)]
        ).astype(bf16)
        return carry

    lax.fori_loop(0, batch * 3, kv_step, 0)

    masks = head_masks(tok_rows)
    factor = HD ** (-0.5)

    def two_heads(block, pair):
        first, second = masks[pair % 4]
        blank = jnp.zeros_like(block)
        return jnp.concatenate([jnp.where(first, block, blank), jnp.where(second, block, blank)], 0)

    def attend_step(s, carry):
        at = pl.multiple_of(s * tok_rows, 64)
        for half in range(2):
            lanes = [jnp.zeros((tok_rows, 128), f32) for _ in range(3)]
            for sub in range(4):
                pair = half * 4 + sub
                low, high = (384 * half + v for v in WINDOWS[sub])
                queries = two_heads(q_ref[pl.ds(at, tok_rows), low:high], pair)
                scores = nt(kv_ref[s, :, low:high], queries) * factor
                scores = scores + biasf_ref[pl.ds(pair, keys_all, stride=PAIRS), :]
                expo = jnp.exp(scores - jnp.max(scores, axis=0, keepdims=True))
                probs = expo * (1.0 / jnp.sum(expo, axis=0, keepdims=True))
                probs_ref[s, pair] = probs
                part = tn(probs.astype(bf16), kv_ref[s, :, C_TOK + low : C_TOK + high])
                first, second = masks[sub]
                mix = jnp.where(first, part[0:tok_rows], 0.0)
                mix = jnp.where(second, part[tok_rows : 2 * tok_rows], mix)
                for t in range((high - low) // 128):
                    tile = WINDOWS[sub][0] // 128 + t
                    lanes[tile] = lanes[tile] + mix[:, 128 * t : 128 * t + 128]
            att_ref[pl.ds(at, tok_rows), 384 * half : 384 * half + 384] = jnp.concatenate(
                lanes, axis=1
            ).astype(bf16)
        return carry

    lax.fori_loop(0, batch, attend_step, 0)

    copies[1].wait()
    resid = tokens_ref[...].reshape(rows, C_TOK) + nn(att_ref[...], w_out_ref[...])
    resid_ref[...] = resid
    hat, rstd = norm_rows(resid)
    hat_ref[...] = hat
    shaped = hat.astype(bf16)
    att_ref[...] = shaped
    copies[2].wait()
    copies[3].wait()
    copies[4].wait()

    def transition_step(n, carry):
        at = pl.multiple_of(n * 256, 256)
        shaped = att_ref[...]
        gate = nn(shaped, w_gate_ref[:, pl.ds(at, 256)])
        up = nn(shaped, w_up_ref[:, pl.ds(at, 256)])
        d_hidden = nt(cot_ref[...].reshape(rows, C_TOK), w_down_ref[pl.ds(at, 256), :])
        sig = 1.0 / (1.0 + jnp.exp(-gate))
        act = gate * sig
        hidden_ref[:, pl.ds(at, 256)] = (act * up).astype(bf16)
        d_gate_ref[:, pl.ds(at, 256)] = (
            d_hidden * up * sig * (1.0 + gate * (1.0 - sig))
        ).astype(bf16)
        d_up_ref[:, pl.ds(at, 256)] = (d_hidden * act).astype(bf16)
        return carry

    lax.fori_loop(0, w_gate_ref.shape[1] // 256, transition_step, 0)
    parts = []
    for n in range(C_TOK // 256):
        parts.append(
            nt(d_gate_ref[...], w_gate_ref[256 * n : 256 * n + 256, :])
            + nt(d_up_ref[...], w_up_ref[256 * n : 256 * n + 256, :])
        )
    d_normed = jnp.concatenate(parts, axis=1)
    hat = hat_ref[...]
    first = jnp.mean(d_normed, axis=-1, keepdims=True)
    second = jnp.mean(d_normed * hat, axis=-1, keepdims=True)
    d_resid = cot_ref[...].reshape(rows, C_TOK).astype(f32) + rstd * (
        d_normed - first - hat * second
    )
    q_ref[...] = nt(d_resid.astype(bf16), w_out_ref[...]).astype(bf16)

    for pair in range(PAIRS):
        half, sub = pair // 4, pair % 4
        low, high = (384 * half + v for v in WINDOWS[sub])

        def back_step(s, total):
            at = pl.multiple_of(s * tok_rows, 64)
            grads = two_heads(q_ref[pl.ds(at, tok_rows), low:high], pair)
            d_probs = nt(kv_ref[s, :, C_TOK + low : C_TOK + high], grads)
            probs = probs_ref[s, pair]
            delta = jnp.sum(probs * d_probs, axis=0, keepdims=True)
            return total + probs * (d_probs - delta)

        total = back_step(0, jnp.zeros((keys_all, 2 * tok_rows), f32))
        for s in range(1, batch):
            total = back_step(s, total)
        d_bias_f_ref[pl.ds(pair, keys_all, stride=PAIRS), :] = total
    d_bias_ref[...] = d_bias_f_ref[...].astype(bf16)


def token_stage(local, every, tokens, bias, cot, w_qkv, w_out, w_gate, w_up, w_down):
    batch, tok_rows, _ = tokens.shape
    keys_all = every.shape[1]
    rows = batch * tok_rows
    hidden = w_gate.shape[1]
    vmem = pl.BlockSpec(memory_space=pltpu.VMEM)
    hbm = pl.BlockSpec(memory_space=pl.ANY)
    return pl.pallas_call(
        token_kernel,
        in_specs=[vmem] * 5 + [hbm] * 5,
        out_specs=[vmem] * 3,
        out_shape=[
            jax.ShapeDtypeStruct((rows, C_TOK), f32),
            jax.ShapeDtypeStruct((rows, hidden), bf16),
            jax.ShapeDtypeStruct((keys_all * PAIRS, 2 * tok_rows), bf16),
        ],
        scratch_shapes=[
            pltpu.VMEM(w_qkv.shape, bf16),
            pltpu.VMEM(w_out.shape, bf16),
            pltpu.VMEM(w_gate.shape, bf16),
            pltpu.VMEM(w_up.shape, bf16),
            pltpu.VMEM(w_down.shape, bf16),
            pltpu.SemaphoreType.DMA((5,)),
            pltpu.VMEM((rows, C_TOK), bf16),
            pltpu.VMEM((batch, keys_all, 2 * C_TOK), bf16),
            pltpu.VMEM((keys_all * PAIRS, 2 * tok_rows), f32),
            pltpu.VMEM((batch, PAIRS, keys_all, 2 * tok_rows), f32),
            pltpu.VMEM((rows, C_TOK), bf16),
            pltpu.VMEM((rows, hidden), bf16),
            pltpu.VMEM((rows, hidden), bf16),
            pltpu.VMEM((rows, C_TOK), f32),
            pltpu.VMEM((keys_all * PAIRS, 2 * tok_rows), f32),
        ],
        compiler_params=pltpu.CompilerParams(vmem_limit_bytes=52 << 20),
        cost_estimate=pl.CostEstimate(
            flops=8 * 10**9, bytes_accessed=2 * 10**7, transcendentals=2 * 10**6
        ),
        name="tokens",
    )(local, every, tokens, bias, cot, w_qkv, w_out, w_gate, w_up, w_down)


def output_kernel(resid_ref, hidden_ref, w_down_ref, out_ref):
    out_ref[...] = (resid_ref[...] + nn(hidden_ref[...], w_down_ref[...])).astype(bf16)


def output_stage(resid, hidden, w_down):
    return pl.pallas_call(
        output_kernel,
        out_shape=jax.ShapeDtypeStruct(resid.shape, bf16),
        compiler_params=pltpu.CompilerParams(vmem_limit_bytes=16 << 20),
        cost_estimate=pl.CostEstimate(
            flops=6 * 10**8, bytes_accessed=5 * 10**6, transcendentals=0
        ),
        name="output",
    )(resid, hidden, w_down)


def grad_kernel(parts_ref, pair_ref, gain_ref, w_bias_ref, out_ref, pairf_ref):
    rows, keys = pair_ref.shape[0], pair_ref.shape[1]
    gain = gain_ref[...]
    for i in range(rows // 8):
        pairf_ref[8 * keys * i : 8 * keys * (i + 1), :] = (
            pair_ref[8 * i : 8 * i + 8].astype(f32).reshape(8 * keys, CZ)
        )
    even, odd = split_heads(w_bias_ref[...])
    weights = jnp.concatenate([even, odd], axis=1).astype(f32)
    weights = jnp.concatenate([weights, weights, weights], axis=0).astype(bf16)
    for j in range(keys):
        total = parts_ref[0, PAIRS * j : PAIRS * (j + 1), :].astype(f32)
        for k in range(1, parts_ref.shape[0]):
            total = total + parts_ref[k, PAIRS * j : PAIRS * (j + 1), :].astype(f32)
        high = total.astype(bf16).astype(f32)
        rest = total - high
        middle = rest.astype(bf16).astype(f32)
        stack = jnp.concatenate([high, middle, rest - middle], axis=0)
        both = nn(stack.T.astype(bf16), weights)
        scaled = (both[0:rows, 0:CZ] + both[rows : 2 * rows, CZ : 2 * CZ]) * gain
        hat, rstd = norm_rows(pairf_ref[pl.ds(j, rows, stride=keys), :])
        first = jnp.mean(scaled, axis=-1, keepdims=True)
        second = jnp.mean(scaled * hat, axis=-1, keepdims=True)
        out_ref[pl.ds(j, rows, stride=keys), :] = rstd * (scaled - first - hat * second)


def pair_back(parts, pair, pair_gain, w_bias):
    rows, keys = pair.shape[0], pair.shape[1]
    out = pl.pallas_call(
        grad_kernel,
        out_shape=jax.ShapeDtypeStruct((rows * keys, CZ), f32),
        scratch_shapes=[pltpu.VMEM((rows * keys, CZ), f32)],
        compiler_params=pltpu.CompilerParams(vmem_limit_bytes=24 << 20),
        cost_estimate=pl.CostEstimate(flops=10**8, bytes_accessed=3 * 10**6, transcendentals=0),
        name="pair_grad",
    )(parts, pair, pair_gain.reshape(1, CZ), w_bias)
    return out.reshape(rows, keys, CZ)


def body(
    atom_feats, atom_counts, atom_mask, token_single, pair, pair_gain, w_bias, w_atom_qkv,
    w_atom_out, w_embed, w_qkv, w_out, w_gate, w_up, w_down, cotangent,
):
    batch, atom_rows, _ = atom_feats.shape
    tok_rows = token_single.shape[0]
    shard, shards = lax.axis_index("tok"), lax.axis_size("tok")
    groups = lax.axis_size("samp")

    steps = [(i, i + 1) for i in range(shards - 1)]
    left = lax.ppermute(atom_feats[:, atom_rows - HALO :], "tok", steps)
    right = lax.ppermute(atom_feats[:, :HALO], "tok", [(j, i) for i, j in steps])

    local_bias = pair_bias(pair, pair_gain, w_bias)
    bias = lax.all_gather(local_bias, "samp", axis=0, tiled=True)

    reach = -(-(atom_rows + 2 * HALO) // 128) * 128
    flags = jnp.pad(atom_mask.astype(f32), (HALO, reach - atom_rows - HALO))
    flags = lax.dynamic_slice(flags, (shard * atom_rows,), (reach,)).reshape(reach // 128, 128)

    tokens, normed = atom_stage(
        atom_feats, left, right, flags, atom_counts, token_single, w_atom_qkv, w_atom_out, w_embed
    )
    every = lax.all_gather(normed, "tok", axis=1, tiled=True)
    resid, hidden, d_bias = token_stage(
        normed, every, tokens, bias, cotangent, w_qkv, w_out, w_gate, w_up, w_down
    )
    parts = d_bias.reshape(groups, -1, 2 * tok_rows)
    parts = lax.all_to_all(parts, "samp", 0, 0)
    token_out = output_stage(resid, hidden, w_down).reshape(batch, tok_rows, C_TOK)
    pair_grad = pair_back(parts, pair, pair_gain, w_bias)
    return (token_out, pair_grad)


def solution(mesh):
    in_specs = (
        P("samp", "tok", None),
        P("tok", None),
        P(),
        P("tok", None),
        P("tok", "samp", None),
        P(), P(), P(), P(), P(), P(), P(), P(), P(), P(),
        P("samp", "tok", None),
    )
    out_specs = (P("samp", "tok", None), P("tok", "samp", None))
    return jax.shard_map(body, mesh=mesh, in_specs=in_specs, out_specs=out_specs, check_vma=False)
```

profile of v0, /device:TPU:0, one launch (start us, length us, event | category | flops | bytes accessed | tf_op | source)
XLA Modules:
  0.0 186.9 jit_solution(8946703395684013475)
XLA Ops:
  7.2 0.0 all-gather.2.cloned.1.call-start
  7.2 0.8 fusion.1
  8.0 1.3 collective-permute-start.1
  9.3 3.0 %collective-permute-start = (bf16[4,48,128]{2,1,0:T(8,128)(2,1)S(1)}, bf16[4,48,128]{2,1,0:T(8,128)(2,1)S(1)}, u32[]{:S(2)}, u32[]{:S(2)}) collective-permute-start(bf16[4,48,128]{2,1,0:T(8,128)(2,1)S(1)} %get-tuple-element.13), channel_id=1, source_target_pairs={{0,1},{1,2},{2,3},{4,5},{5,6},{6,7},{8,9},{9,10},{10,11},{12,13},{... | collective-permute-start | bytes 147464 | tf_op jit(solution)/shard_map/ppermute | solution.py:483
  12.4 0.7 convert_element_type.5
  13.1 0.1 fusion.flags_ref
  13.2 0.0 collective-permute-done.1.right_ref
  13.2 0.0 collective-permute-done.left_ref
  13.2 1.4 copy-done.5
  14.6 0.9 copy-done.8
  15.5 0.9 copy-done.9
  16.4 0.9 copy-done.10
  17.3 0.8 copy-done.11
  18.1 0.7 copy-done.12
  18.7 74.6 %atoms.1 = (f32[4,64,768]{2,1,0:T(8,128)S(1)}, bf16[4,64,768]{2,1,0:T(8,128)(2,1)}) custom-call(bf16[4,1280,128]{2,1,0:T(8,128)(2,1)S(1)} %copy-done.5, bf16[4,48,128]{2,1,0:T(8,128)(2,1)S(1)} %collective-permute-done.left_ref, bf16[4,48,128]{2,1,0:T(8,128)(2,1)S(1)} %collective-permute-done.1.right_ref, f32[11,128]{1,0:T(8,128)S(1)} %fusion.flags_ref, ...), custom_call_target="tpu_custom_call" | custom-call | flops 6000000000 | bytes 4000000 | tf_op jit(solution)/shard_map/atoms/pallas_call | solution.py:199
  93.3 0.9 copy-done.13
  94.2 0.0 all-gather.2.cloned.1.call-update
  94.2 0.1 copy.18.w_bias_ref
  94.4 2.3 %pair_bias.1 = bf16[256,128]{1,0:T(8,128)(2,1)S(1)} custom-call(bf16[64,32,128]{2,1,0:T(8,128)(2,1)S(1)} %copy-done.1, f32[1,128]{1,0:T(1,128)S(1)} %bitcast.7, bf16[128,16]{1,0:T(8,128)(2,1)S(1)} %copy.18.w_bias_ref), custom_call_target="tpu_custom_call" | custom-call | flops 10000000 | bytes 10000000 | tf_op jit(solution)/shard_map/pair_bias/pallas_call | solution.py:82
  96.7 33.0 %all_gather.7.bias_ref = bf16[2048,128]{1,0:T(8,128)(2,1)S(1)} all-gather(bf16[256,128]{1,0:T(8,128)(2,1)S(1)} %pair_bias.1), channel_id=1, replica_groups=mesh['samp'=8,'tok'=4] {'samp'}, dimensions={0}, use_global_device_ids=true | all-gather | bytes 589824 | tf_op jit(solution)/shard_map/all_gather | solution.py:487
  129.7 1.0 copy-done.7
  130.7 25.7 %tokens.1 = (f32[256,768]{1,0:T(8,128)}, bf16[256,1536]{1,0:T(8,128)(2,1)}, bf16[2048,128]{1,0:T(8,128)(2,1)S(1)}) custom-call(bf16[4,64,768]{2,1,0:T(8,128)(2,1)} %get-tuple-element.7.local_ref, bf16[4,256,768]{2,1,0:T(8,128)(2,1)} %all-gather.2.cloned.1.call-done.all_ref, f32[4,64,768]{2,1,0:T(8,128)} %copy-done.13, ...), custom_call_target="tpu_custom_call" | custom-call | flops 8000000000 | bytes 20000000 | tf_op jit(solution)/shard_map/tokens/pallas_call | solution.py:384
  156.5 0.0 copy-start.4
  156.5 0.8 copy-done.4
  157.3 5.8 %all-to-all-start = ((bf16[8,256,128]{2,1,0:T(8,128)(2,1)}), bf16[8,256,128]{2,1,0:T(8,128)(2,1)S(1)}, u32[]{:S(2)}, u32[]{:S(2)}) async-start(bf16[8,256,128]{2,1,0:T(8,128)(2,1)} %bitcast.6), calls=%async_computation | async-start | bytes 1048576 | tf_op jit(solution)/shard_map/all_to_all | solution.py:501
  163.1 0.0 copy-done
  163.1 0.0 copy-start.2
  163.1 1.1 copy-done.2
  164.2 1.1 copy-done.3
  165.4 1.5 output.1
  166.9 6.5 %all-to-all-done.parts_ref = bf16[8,256,128]{2,1,0:T(8,128)(2,1)S(1)} async-done(((bf16[8,256,128]{2,1,0:T(8,128)(2,1)}), bf16[8,256,128]{2,1,0:T(8,128)(2,1)S(1)}, u32[]{:S(2)}, u32[]{:S(2)}) %all-to-all-start) | async-done | bytes 524320 | tf_op jit(solution)/shard_map/all_to_all | solution.py:501
  173.4 6.7 %pair_grad.1 = f32[2048,128]{1,0:T(8,128)} custom-call(bf16[8,256,128]{2,1,0:T(8,128)(2,1)S(1)} %all-to-all-done.parts_ref, bf16[64,32,128]{2,1,0:T(8,128)(2,1)S(1)} %copy-done.1, f32[1,128]{1,0:T(1,128)S(1)} %bitcast.8, bf16[128,16]{1,0:T(8,128)(2,1)S(1)} %copy.18.w_bias_ref), custom_call_target="tpu_custom_call" | custom-call | flops 100000000 | bytes 3000000 | tf_op jit(solution)/shard_map/pair_grad/pallas_call | solution.py:462
  (17 shorter events, 0.0 us)
Async XLA Ops:
  7.2 122.6 %all-gather.2.cloned.1.call-start = ((), (), s32[]{:S(2)}) async-start(), calls=%async_computation.1 | async-start | bytes 1966080 | tf_op jit(solution)/shard_map/all_gather | solution.py:496
  8.0 5.2 %collective-permute-start.1 = (bf16[4,48,128]{2,1,0:T(8,128)(2,1)S(1)}, bf16[4,48,128]{2,1,0:T(8,128)(2,1)S(1)}, u32[]{:S(2)}, u32[]{:S(2)}) collective-permute-start(bf16[4,48,128]{2,1,0:T(8,128)(2,1)S(1)} %get-tuple-element.12), channel_id=1, source_target_pairs={{1,0},{2,1},{3,2},{5,4},{6,5},{7,6},{9,8},{10,9},{11,10},{13,12},{... | collective-permute-start | bytes 147464 | tf_op jit(solution)/shard_map/ppermute | solution.py:484
  9.3 3.9 %collective-permute-start = (bf16[4,48,128]{2,1,0:T(8,128)(2,1)S(1)}, bf16[4,48,128]{2,1,0:T(8,128)(2,1)S(1)}, u32[]{:S(2)}, u32[]{:S(2)}) collective-permute-start(bf16[4,48,128]{2,1,0:T(8,128)(2,1)S(1)} %get-tuple-element.13), channel_id=1, source_target_pairs={{0,1},{1,2},{2,3},{4,5},{5,6},{6,7},{8,9},{9,10},{10,11},{12,13},{... | collective-permute-start | bytes 147464 | tf_op jit(solution)/shard_map/ppermute | solution.py:483
  13.1 81.1 %copy-start.14 = (bf16[128,16]{0,1:T(8,128)(2,1)S(1)}, bf16[128,16]{0,1:T(8,128)(2,1)}, u32[]{:S(2)}) copy-start(bf16[128,16]{0,1:T(8,128)(2,1)} %param.22) | copy-start | bytes 12292
  13.1 81.2 %copy-start.6 = (f32[128]{0:T(128)S(1)}, f32[128]{0:T(128)}, u32[]{:S(2)}) copy-start(f32[128]{0:T(128)} %param.21) | copy-start | bytes 1540
  13.2 81.2 %copy-start.1 = (bf16[64,32,128]{2,1,0:T(8,128)(2,1)S(1)}, bf16[64,32,128]{2,1,0:T(8,128)(2,1)}, u32[]{:S(2)}) copy-start(bf16[64,32,128]{2,1,0:T(8,128)(2,1)} %pair_ref.3) | copy-start | bytes 1572868
  13.2 1.4 copy-start.5
  14.6 0.9 copy-start.8
  15.5 0.9 copy-start.9
  16.4 0.9 copy-start.10
  17.3 0.8 copy-start.11
  18.1 0.7 copy-start.12
  93.3 0.9 copy-start.13
  129.7 1.0 copy-start.7
  130.7 32.4 %copy-start = (bf16[1536,768]{1,0:T(8,128)(2,1)S(1)}, bf16[1536,768]{1,0:T(8,128)(2,1)}, u32[]{:S(2)}) copy-start(bf16[1536,768]{1,0:T(8,128)(2,1)} %w_down_ref.1) | copy-start | bytes 7077892
  156.5 0.8 copy-start.4
  157.3 16.1 %all-to-all-start = ((bf16[8,256,128]{2,1,0:T(8,128)(2,1)}), bf16[8,256,128]{2,1,0:T(8,128)(2,1)S(1)}, u32[]{:S(2)}, u32[]{:S(2)}) async-start(bf16[8,256,128]{2,1,0:T(8,128)(2,1)} %bitcast.6), calls=%async_computation | async-start | bytes 1048576 | tf_op jit(solution)/shard_map/all_to_all | solution.py:501
  163.1 1.1 copy-start.2
  164.2 1.1 copy-start.3
Sparse Core Ops, SparseCore 0:
  94.3 24.4 all-gather.1
where the time goes:
time: 188 us; the launch traced here: 187 us
  Pallas kernels  111 us (59%)
  blocking collectives  33 us (18%)
  between operations  14.1 us (8%)
  local copies, waits for them, and re-layouts  11.5 us (6%)
  starting transfers between devices  10.2 us (5%)
  waiting for transfers between devices  6.54 us (3%)
    pallas_call x1, Pallas kernels, atom_stage(): pl.pallas_call(atom_kernel, grid=(batch,), in_specs=[by_sample(atoms, C_A...  74.6 us
    all_gather x1, blocking collectives, body(): bias = lax.all_gather(local_bias, 'samp', axis=0, tiled=True)  33 us
    pallas_call x1, Pallas kernels, token_stage(): pl.pallas_call(token_kernel, in_specs=[vmem] * 5 + [hbm] * 5, out_specs=[...  25.7 us
    unnamed x31, local copies, waits for them, and re-layouts  10.5 us
    pallas_call x1, Pallas kernels, pair_back(): pl.pallas_call(grad_kernel, out_shape=jax.ShapeDtypeStruct((rows * keys,...  6.68 us
    all_to_all x1, waiting for transfers between devices, body(): parts = lax.all_to_all(parts, 'samp', 0, 0)  6.49 us
    all_to_all x1, starting transfers between devices, body(): parts = lax.all_to_all(parts, 'samp', 0, 0)  5.82 us
  transfers between devices with their start and end apart: 4, of which 1 were waited for; matrix products, arithmetic and copies ran while one was open for 1% of the time, Pallas kernels for 2%

commit v1 on v0

v1 whole, which is shorter than its diff:
```python
import functools

import jax
import jax.numpy as jnp
from jax import lax
from jax.experimental import pallas as pl
from jax.experimental.pallas import tpu as pltpu
from jax.sharding import PartitionSpec as P

C_ATOM = 128
ATOM_HEADS = 4
C_TOK = 768
HEADS = 16
ATOM_HD = 32
HD = 48
CZ = 128
HALO = 48
PAIRS = HEADS // 2
GRANT = 60 << 20
LOG2E = 1.4426950408889634

epsilon = 1e-05
f32 = jnp.float32
bf16 = jnp.bfloat16

WINDOWS = ((0, 128), (0, 256), (128, 384), (256, 384))


def nn(a, b):
    return lax.dot_general(a, b, (((1,), (0,)), ((), ())), preferred_element_type=f32)


def nt(a, b):
    return lax.dot_general(a, b, (((1,), (1,)), ((), ())), preferred_element_type=f32)


def tn(a, b):
    return lax.dot_general(a, b, (((0,), (0,)), ((), ())), preferred_element_type=f32)


def norm_rows(values):
    center = values - jnp.mean(values, axis=-1, keepdims=True)
    scale_inv = lax.rsqrt(jnp.mean(center * center, axis=-1, keepdims=True) + epsilon)
    return (center * scale_inv, scale_inv)


def iota(shape, dim):
    return lax.broadcasted_iota(jnp.int32, shape, dim)


def split_heads(w_bias):
    row, col = iota((PAIRS, HEADS), 0), iota((PAIRS, HEADS), 1)
    even = (col == 2 * row).astype(f32).astype(bf16)
    odd = (col == 2 * row + 1).astype(f32).astype(bf16)
    return nt(even, w_bias).astype(bf16), nt(odd, w_bias).astype(bf16)


def bias_kernel(pair_ref, gain_ref, w_bias_ref, out_ref, scaled_ref, stage_ref):
    rows, keys = pair_ref.shape[0], pair_ref.shape[1]
    gain = gain_ref[...]

    def norm_step(i, carry):
        block = pair_ref[pl.ds(i * 8, 8)].astype(f32).reshape(8 * keys, CZ)
        hat, unused = norm_rows(block)
        scaled_ref[pl.ds(pl.multiple_of(i * 8 * keys, 8 * keys), 8 * keys), :] = hat * gain
        return carry

    lax.fori_loop(0, rows // 8, norm_step, 0)
    even, odd = split_heads(w_bias_ref[...])
    weights = jnp.concatenate([even, odd], axis=1)
    blank = jnp.zeros((rows, CZ), bf16)
    for j in range(keys):
        block = scaled_ref[pl.ds(j, rows, stride=keys), :].astype(bf16)
        both = jnp.concatenate(
            [jnp.concatenate([block, blank], axis=1), jnp.concatenate([blank, block], axis=1)],
            axis=0,
        )
        stage_ref[pl.ds(j * PAIRS, PAIRS), :] = nt(weights, both)
    for k in range(out_ref.shape[0]):
        out_ref[k] = stage_ref[...].astype(bf16)


def pair_bias(pair, pair_gain, w_bias, copies):
    rows, keys = pair.shape[0], pair.shape[1]
    return pl.pallas_call(
        bias_kernel,
        out_shape=jax.ShapeDtypeStruct((copies, keys * PAIRS, 2 * rows), bf16),
        scratch_shapes=[
            pltpu.VMEM((rows * keys, CZ), f32),
            pltpu.VMEM((keys * PAIRS, 2 * rows), f32),
        ],
        compiler_params=pltpu.CompilerParams(vmem_limit_bytes=GRANT),
        cost_estimate=pl.CostEstimate(flops=10**7, bytes_accessed=10**7, transcendentals=0),
        name="pair_bias",
    )(pair, pair_gain.reshape(1, CZ), w_bias)


def atom_kernel(
    feats_ref, left_ref, right_ref, flags_ref, counts_ref, single_ref, w_qkv_ref, w_out_ref,
    w_embed_ref, tokens_ref, normed_ref, xn_ref, qkv_ref, scores_ref, probs_ref, mixed_ref,
    keybias_ref, onehot_ref, pooled_ref, counts_col_ref,
):
    atoms = feats_ref.shape[1]
    padded = atoms + 2 * HALO
    tok_rows = single_ref.shape[0]

    @pl.when(pl.program_id(0) == 0)
    def prepare():
        eye = iota((128, 128), 0) == iota((128, 128), 1)
        for b in range(flags_ref.shape[0]):
            row = jnp.broadcast_to(flags_ref[b : b + 1, :], (128, 128))
            col = jnp.sum(jnp.where(eye, row, 0.0), axis=1, keepdims=True)
            keybias_ref[b * 128 : (b + 1) * 128, :] = jnp.broadcast_to(
                (col - 1.0) * 1e30, (128, 128)
            )
        counts = jnp.broadcast_to(counts_ref[...].astype(f32), (tok_rows, tok_rows))
        sub, lane = iota((tok_rows, tok_rows), 0), iota((tok_rows, tok_rows), 1)
        start = jnp.sum(jnp.where(lane < sub, counts, 0.0), axis=1, keepdims=True)
        own = jnp.sum(jnp.where(lane == sub, counts, 0.0), axis=1, keepdims=True)
        counts_col_ref[...] = jnp.broadcast_to(own, (tok_rows, 128))
        pos = iota((tok_rows, 256), 1).astype(f32)
        for g in range(atoms // 256):
            at = pos + float(g * 256)
            hit = jnp.where((at >= start) & (at < start + own), 1.0, 0.0).astype(bf16)
            onehot_ref[g] = jnp.concatenate([hit, hit], axis=1)
        probs_ref[...] = jnp.zeros_like(probs_ref)

    xn_ref[0:HALO, :] = norm_rows(left_ref[0].astype(f32))[0].astype(bf16)
    xn_ref[atoms + HALO : padded, :] = norm_rows(right_ref[0].astype(f32))[0].astype(bf16)

    def norm_step(i, carry):
        at = pl.multiple_of(i * 256, 256)
        block = feats_ref[0, pl.ds(at, 256), :].astype(f32)
        xn_ref[pl.ds(HALO + at, 256), :] = norm_rows(block)[0].astype(bf16)
        return carry

    lax.fori_loop(0, atoms // 256, norm_step, 0)

    chunk = padded // 4
    w_qkv = w_qkv_ref[...]
    for i in range(4):
        qkv_ref[i * chunk : (i + 1) * chunk, :] = nn(
            xn_ref[i * chunk : (i + 1) * chunk, :], w_qkv
        ).astype(bf16)

    lane = iota((32, 128), 1)
    head_of = lane // ATOM_HD
    head_mask = [(head_of == h).astype(f32).astype(bf16) for h in range(ATOM_HEADS)]
    own_atom = (lane % 32) == iota((32, 128), 0)
    factor = ATOM_HD ** (-0.5) * LOG2E
    pairs = atoms // 64
    per = 4

    def score_step(i, carry):
        for k in range(per):
            pair = i * per + k
            base = pl.multiple_of(pair * 64, 64)
            queries = qkv_ref[pl.ds(base + HALO, 64), 0:C_ATOM]
            spread = jnp.concatenate(
                [
                    queries[32 * w : 32 * w + 32] * head_mask[h]
                    for w in range(2)
                    for h in range(ATOM_HEADS)
                ],
                axis=0,
            )
            scores_ref[pair] = nt(qkv_ref[pl.ds(base, 160), C_ATOM : 2 * C_ATOM], spread)
        return carry

    lax.fori_loop(0, pairs // per, score_step, 0)

    def softmax_step(i, carry):
        for k in range(2):
            pair = i * 2 + k
            base = pl.multiple_of(pair * 64, 64)
            for w in range(2):
                keybias = keybias_ref[pl.ds(base + 32 * w, 128), :]
                keybias = jnp.concatenate(
                    [keybias[0:48], jnp.where(own_atom, 0.0, keybias[48:80]), keybias[80:128]],
                    axis=0,
                )
                scores = scores_ref[pair, 32 * w : 32 * w + 128, 128 * w : 128 * w + 128] + keybias
                expo = jnp.exp2((scores - jnp.max(scores, axis=0, keepdims=True)) * factor)
                weights = expo * (1.0 / jnp.sum(expo, axis=0, keepdims=True))
                probs_ref[pair, 32 * w : 32 * w + 128, 128 * w : 128 * w + 128] = weights.astype(
                    bf16
                )
        return carry

    lax.fori_loop(0, pairs // 2, softmax_step, 0)

    def value_step(i, carry):
        for k in range(per):
            pair = i * per + k
            base = pl.multiple_of(pair * 64, 64)
            part = tn(probs_ref[pair], qkv_ref[pl.ds(base, 160), 2 * C_ATOM : 3 * C_ATOM])
            mixes = []
            for w in range(2):
                mix = part[128 * w : 128 * w + 32]
                for h in range(1, ATOM_HEADS):
                    low = 128 * w + 32 * h
                    mix = jnp.where(head_of == h, part[low : low + 32], mix)
                mixes.append(mix.astype(bf16))
            mixed_ref[pl.ds(base, 64), :] = jnp.concatenate(mixes, axis=0)
        return carry

    lax.fori_loop(0, pairs // per, value_step, 0)

    pooled_ref[...] = jnp.zeros_like(pooled_ref)

    def embed_step(g, carry):
        base = pl.multiple_of(g * 256, 256)
        feats = feats_ref[0, pl.ds(base, 256), :].astype(f32)
        updated = (feats + nn(mixed_ref[pl.ds(base, 256), :], w_out_ref[...])).astype(bf16)
        embedded = jnp.maximum(nn(updated, w_embed_ref[...]), 0.0)
        high = embedded.astype(bf16)
        low = (embedded - high.astype(f32)).astype(bf16)
        pooled_ref[...] += nn(onehot_ref[g], jnp.concatenate([high, low], axis=0))
        return carry

    lax.fori_loop(0, atoms // 256, embed_step, 0)
    counts = counts_col_ref[:, 0:1]
    tokens = pooled_ref[...] / counts + single_ref[...].astype(f32)
    tokens_ref[0] = tokens
    normed_ref[0] = norm_rows(tokens)[0].astype(bf16)


def atom_stage(first, batch, feats, left, right, flags, counts, single, w_qkv, w_out, w_embed):
    atoms = feats.shape[1]
    tok_rows = single.shape[0]
    padded = atoms + 2 * HALO
    pairs = atoms // 64
    of_sample = lambda rows, cols: pl.BlockSpec((1, rows, cols), lambda s: (s + first, 0, 0))
    by_sample = lambda rows, cols: pl.BlockSpec((1, rows, cols), lambda s: (s, 0, 0))
    whole = lambda a: pl.BlockSpec(a.shape, lambda s: (0,) * a.ndim)
    return pl.pallas_call(
        atom_kernel,
        grid=(batch,),
        in_specs=[
            of_sample(atoms, C_ATOM), of_sample(HALO, C_ATOM), of_sample(HALO, C_ATOM),
            whole(flags), whole(counts), whole(single), whole(w_qkv), whole(w_out), whole(w_embed),
        ],
        out_specs=[by_sample(tok_rows, C_TOK), by_sample(tok_rows, C_TOK)],
        out_shape=[
            jax.ShapeDtypeStruct((batch, tok_rows, C_TOK), f32),
            jax.ShapeDtypeStruct((batch, tok_rows, C_TOK), bf16),
        ],
        scratch_shapes=[
            pltpu.VMEM((padded, C_ATOM), bf16),
            pltpu.VMEM((padded, 3 * C_ATOM), bf16),
            pltpu.VMEM((pairs, 160, 256), f32),
            pltpu.VMEM((pairs, 160, 256), bf16),
            pltpu.VMEM((atoms, C_ATOM), bf16),
            pltpu.VMEM((flags.shape[0] * 128, 128), f32),
            pltpu.VMEM((atoms // 256, tok_rows, 512), bf16),
            pltpu.VMEM((tok_rows, C_TOK), f32),
            pltpu.VMEM((tok_rows, 128), f32),
        ],
        compiler_params=pltpu.CompilerParams(vmem_limit_bytes=GRANT),
        cost_estimate=pl.CostEstimate(
            flops=10**10, bytes_accessed=4 * 10**6, transcendentals=3 * 10**6
        ),
        name="atoms",
    )(feats, left, right, flags, counts, single, w_qkv, w_out, w_embed)


def head_masks(rows):
    masks = []
    for pair in range(4):
        low, high = WINDOWS[pair]
        lane = iota((rows, high - low), 1) + low
        first = 2 * pair * HD
        masks.append(
            [(lane >= first + HD * k) & (lane < first + HD * (k + 1)) for k in range(2)]
        )
    return masks


def two_heads(block, masks):
    blank = jnp.zeros_like(block)
    return jnp.concatenate([jnp.where(mask, block, blank) for mask in masks], axis=0)


def attend_kernel(
    *refs, sources,
):
    piece_refs = refs[: len(sources)]
    bias_ref, w_qkv_hbm, att_ref, probs_ref, values_ref = refs[len(sources) : len(sources) + 5]
    w_qkv_ref, sems, all_ref, qk_ref, biasf_ref = refs[len(sources) + 5 :]
    batch, tok_rows = piece_refs[0].shape[0], piece_refs[0].shape[1]
    keys_all = tok_rows * len(sources)
    copies = [
        pltpu.make_async_copy(
            w_qkv_hbm.at[:, pl.ds(C_TOK * i, C_TOK)], w_qkv_ref.at[i], sems.at[i]
        )
        for i in range(3)
    ]
    for copy in copies:
        copy.start()
    here = lax.axis_index("tok")
    count = len(sources)
    for piece, (shift, flip) in zip(piece_refs, sources):
        owner = lax.rem(here + shift, count)
        if flip:
            owner = owner + 1 - 2 * lax.rem(owner, 2)
        at = pl.multiple_of(owner * tok_rows, tok_rows)
        for s in range(batch):
            all_ref[s, pl.ds(at, tok_rows), :] = piece[s]
    biasf_ref[...] = bias_ref[...].astype(f32)
    copies[0].wait()
    own = piece_refs[0][...].reshape(batch * tok_rows, C_TOK)
    queries_ref = att_ref
    for n in range(3):
        queries_ref[:, 256 * n : 256 * n + 256] = nn(
            own, w_qkv_ref[0, :, 256 * n : 256 * n + 256]
        ).astype(bf16)
    copies[1].wait()
    copies[2].wait()

    def project_step(n, carry):
        at = pl.multiple_of(n * 256, 256)
        for s in range(batch):
            qk_ref[s, :, pl.ds(at, 256)] = nn(
                all_ref[s], w_qkv_ref[1, :, pl.ds(at, 256)]
            ).astype(bf16)
            values_ref[s, :, pl.ds(at, 256)] = nn(
                all_ref[s], w_qkv_ref[2, :, pl.ds(at, 256)]
            ).astype(bf16)
        return carry

    lax.fori_loop(0, C_TOK // 256, project_step, 0)
    masks = head_masks(tok_rows)
    factor = HD ** (-0.5)

    def attend_step(s, carry):
        at = pl.multiple_of(s * tok_rows, 64)
        for half in range(2):
            lanes = [jnp.zeros((tok_rows, 128), f32) for _ in range(3)]
            for sub in range(4):
                pair = half * 4 + sub
                low, high = (384 * half + v for v in WINDOWS[sub])
                queries = two_heads(queries_ref[pl.ds(at, tok_rows), low:high], masks[sub])
                scores = nt(qk_ref[s, :, low:high], queries) * factor
                scores = scores + biasf_ref[pl.ds(pair, keys_all, stride=PAIRS), :]
                expo = jnp.exp(scores - jnp.max(scores, axis=0, keepdims=True))
                probs = expo * (1.0 / jnp.sum(expo, axis=0, keepdims=True))
                probs_ref[s, pair] = probs
                part = tn(probs.astype(bf16), values_ref[s, :, low:high])
                first, second = masks[sub]
                mix = jnp.where(first, part[0:tok_rows], 0.0)
                mix = jnp.where(second, part[tok_rows : 2 * tok_rows], mix)
                for t in range((high - low) // 128):
                    tile = WINDOWS[sub][0] // 128 + t
                    lanes[tile] = lanes[tile] + mix[:, 128 * t : 128 * t + 128]
            att_ref[pl.ds(at, tok_rows), 384 * half : 384 * half + 384] = jnp.concatenate(
                lanes, axis=1
            ).astype(bf16)
        return carry

    lax.fori_loop(0, batch, attend_step, 0)


def attend_stage(pieces, sources, bias, w_qkv):
    batch, tok_rows, _ = pieces[0].shape
    keys_all = tok_rows * len(pieces)
    vmem = pl.BlockSpec(memory_space=pltpu.VMEM)
    hbm = pl.BlockSpec(memory_space=pl.ANY)
    return pl.pallas_call(
        functools.partial(attend_kernel, sources=sources),
        in_specs=[vmem] * (len(pieces) + 1) + [hbm],
        out_specs=[vmem] * 3,
        out_shape=[
            jax.ShapeDtypeStruct((batch * tok_rows, C_TOK), bf16),
            jax.ShapeDtypeStruct((batch, PAIRS, keys_all, 2 * tok_rows), f32),
            jax.ShapeDtypeStruct((batch, keys_all, C_TOK), bf16),
        ],
        scratch_shapes=[
            pltpu.VMEM((3, C_TOK, C_TOK), bf16),
            pltpu.SemaphoreType.DMA((3,)),
            pltpu.VMEM((batch, keys_all, C_TOK), bf16),
            pltpu.VMEM((batch, keys_all, C_TOK), bf16),
            pltpu.VMEM((keys_all * PAIRS, 2 * tok_rows), f32),
        ],
        compiler_params=pltpu.CompilerParams(vmem_limit_bytes=GRANT),
        cost_estimate=pl.CostEstimate(
            flops=4 * 10**9, bytes_accessed=10**7, transcendentals=10**6
        ),
        name="attend",
    )(*pieces, bias, w_qkv)


def token_kernel(*refs, halves):
    tokens_refs, att_refs = refs[0:halves], refs[halves : 2 * halves]
    probs_hbm, values_hbm = refs[2 * halves : 3 * halves], refs[3 * halves : 4 * halves]
    cot_ref, w_out_hbm, w_gate_hbm, w_up_hbm, w_down_hbm = refs[4 * halves : 4 * halves + 5]
    resid_ref, hidden_ref, d_bias_ref = refs[4 * halves + 5 : 4 * halves + 8]
    (
        w_out_ref, w_gate_ref, w_up_ref, w_down_ref, probs_ref, values_ref, sems, grads_ref,
        d_gate_ref, d_up_ref, hat_ref, d_bias_f_ref,
    ) = refs[4 * halves + 8 :]
    batch, tok_rows = cot_ref.shape[0], cot_ref.shape[1]
    keys_all = values_ref.shape[1]
    rows = batch * tok_rows
    each = batch // halves
    moves = [
        (w_out_hbm, w_out_ref), (w_gate_hbm, w_gate_ref), (w_up_hbm, w_up_ref),
        (w_down_hbm, w_down_ref),
    ]
    for i in range(halves):
        moves.append((values_hbm[i], values_ref.at[pl.ds(i * each, each)]))
        moves.append((probs_hbm[i], probs_ref.at[pl.ds(i * each, each)]))
    copies = [pltpu.make_async_copy(s, d, sems.at[i]) for i, (s, d) in enumerate(moves)]
    for copy in copies:
        copy.start()
    cot = cot_ref[...].reshape(rows, C_TOK)
    copies[0].wait()
    for i in range(halves):
        part = slice(i * each * tok_rows, (i + 1) * each * tok_rows)
        resid_ref[part, :] = tokens_refs[i][...].reshape(each * tok_rows, C_TOK) + nn(
            att_refs[i][...], w_out_ref[...]
        )
    hat, rstd = norm_rows(resid_ref[...])
    hat_ref[...] = hat
    grads_ref[...] = hat.astype(bf16)
    copies[1].wait()
    copies[2].wait()
    copies[3].wait()

    def transition_step(n, carry):
        at = pl.multiple_of(n * 256, 256)
        shaped = grads_ref[...]
        gate = nn(shaped, w_gate_ref[:, pl.ds(at, 256)])
        up = nn(shaped, w_up_ref[:, pl.ds(at, 256)])
        d_hidden = nt(cot_ref[...].reshape(rows, C_TOK), w_down_ref[pl.ds(at, 256), :])
        sig = 1.0 / (1.0 + jnp.exp(-gate))
        act = gate * sig
        hidden_ref[:, pl.ds(at, 256)] = (act * up).astype(bf16)
        d_gate_ref[:, pl.ds(at, 256)] = (
            d_hidden * up * sig * (1.0 + gate * (1.0 - sig))
        ).astype(bf16)
        d_up_ref[:, pl.ds(at, 256)] = (d_hidden * act).astype(bf16)
        return carry

    lax.fori_loop(0, w_gate_ref.shape[1] // 256, transition_step, 0)
    parts = []
    for n in range(C_TOK // 256):
        parts.append(
            nt(d_gate_ref[...], w_gate_ref[256 * n : 256 * n + 256, :])
            + nt(d_up_ref[...], w_up_ref[256 * n : 256 * n + 256, :])
        )
    d_normed = jnp.concatenate(parts, axis=1)
    hat = hat_ref[...]
    first = jnp.mean(d_normed, axis=-1, keepdims=True)
    second = jnp.mean(d_normed * hat, axis=-1, keepdims=True)
    d_resid = cot.astype(f32) + rstd * (d_normed - first - hat * second)
    grads_ref[...] = nt(d_resid.astype(bf16), w_out_ref[...]).astype(bf16)
    for copy in copies[4:]:
        copy.wait()
    masks = head_masks(tok_rows)
    for pair in range(PAIRS):
        half, sub = pair // 4, pair % 4
        low, high = (384 * half + v for v in WINDOWS[sub])
        total = jnp.zeros((keys_all, 2 * tok_rows), f32)
        for s in range(batch):
            grads = two_heads(
                grads_ref[s * tok_rows : (s + 1) * tok_rows, low:high], masks[sub]
            )
            d_probs = nt(values_ref[s, :, low:high], grads)
            probs = probs_ref[s, pair]
            delta = jnp.sum(probs * d_probs, axis=0, keepdims=True)
            total = total + probs * (d_probs - delta)
        d_bias_f_ref[pl.ds(pair, keys_all, stride=PAIRS), :] = total
    d_bias_ref[...] = d_bias_f_ref[...].astype(bf16)


def token_stage(tokens, att, probs, values, cot, w_out, w_gate, w_up, w_down):
    halves = len(tokens)
    batch, tok_rows, _ = cot.shape
    keys_all = values[0].shape[1]
    rows = batch * tok_rows
    hidden = w_gate.shape[1]
    vmem = pl.BlockSpec(memory_space=pltpu.VMEM)
    hbm = pl.BlockSpec(memory_space=pl.ANY)
    return pl.pallas_call(
        functools.partial(token_kernel, halves=halves),
        in_specs=[vmem] * (2 * halves) + [hbm] * (2 * halves) + [vmem] + [hbm] * 4,
        out_specs=[vmem] * 3,
        out_shape=[
            jax.ShapeDtypeStruct((rows, C_TOK), f32),
            jax.ShapeDtypeStruct((rows, hidden), bf16),
            jax.ShapeDtypeStruct((keys_all * PAIRS, 2 * tok_rows), bf16),
        ],
        scratch_shapes=[
            pltpu.VMEM(w_out.shape, bf16),
            pltpu.VMEM(w_gate.shape, bf16),
            pltpu.VMEM(w_up.shape, bf16),
            pltpu.VMEM(w_down.shape, bf16),
            pltpu.VMEM((batch, PAIRS, keys_all, 2 * tok_rows), f32),
            pltpu.VMEM((batch, keys_all, C_TOK), bf16),
            pltpu.SemaphoreType.DMA((4 + 2 * halves,)),
            pltpu.VMEM((rows, C_TOK), bf16),
            pltpu.VMEM((rows, hidden), bf16),
            pltpu.VMEM((rows, hidden), bf16),
            pltpu.VMEM((rows, C_TOK), f32),
            pltpu.VMEM((keys_all * PAIRS, 2 * tok_rows), f32),
        ],
        compiler_params=pltpu.CompilerParams(vmem_limit_bytes=GRANT),
        cost_estimate=pl.CostEstimate(
            flops=8 * 10**9, bytes_accessed=2 * 10**7, transcendentals=10**6
        ),
        name="tokens",
    )(*tokens, *att, *probs, *values, cot, w_out, w_gate, w_up, w_down)


def output_kernel(resid_ref, hidden_ref, w_down_ref, out_ref):
    out_ref[...] = (resid_ref[...] + nn(hidden_ref[...], w_down_ref[...])).astype(bf16)


def output_stage(resid, hidden, w_down):
    return pl.pallas_call(
        output_kernel,
        out_shape=jax.ShapeDtypeStruct(resid.shape, bf16),
        compiler_params=pltpu.CompilerParams(vmem_limit_bytes=GRANT),
        cost_estimate=pl.CostEstimate(
            flops=6 * 10**8, bytes_accessed=5 * 10**6, transcendentals=0
        ),
        name="output",
    )(resid, hidden, w_down)


def grad_kernel(parts_ref, pair_ref, gain_ref, w_bias_ref, out_ref, pairf_ref):
    rows, keys = pair_ref.shape[0], pair_ref.shape[1]
    gain = gain_ref[...]
    for i in range(rows // 8):
        pairf_ref[8 * keys * i : 8 * keys * (i + 1), :] = (
            pair_ref[8 * i : 8 * i + 8].astype(f32).reshape(8 * keys, CZ)
        )
    even, odd = split_heads(w_bias_ref[...])
    weights = jnp.concatenate([even, odd], axis=1).astype(f32)
    weights = jnp.concatenate([weights, weights, weights], axis=0).astype(bf16)
    for j in range(keys):
        total = parts_ref[0, PAIRS * j : PAIRS * (j + 1), :].astype(f32)
        for k in range(1, parts_ref.shape[0]):
            total = total + parts_ref[k, PAIRS * j : PAIRS * (j + 1), :].astype(f32)
        high = total.astype(bf16).astype(f32)
        rest = total - high
        middle = rest.astype(bf16).astype(f32)
        stack = jnp.concatenate([high, middle, rest - middle], axis=0)
        both = nn(stack.T.astype(bf16), weights)
        scaled = (both[0:rows, 0:CZ] + both[rows : 2 * rows, CZ : 2 * CZ]) * gain
        hat, rstd = norm_rows(pairf_ref[pl.ds(j, rows, stride=keys), :])
        first = jnp.mean(scaled, axis=-1, keepdims=True)
        second = jnp.mean(scaled * hat, axis=-1, keepdims=True)
        out_ref[pl.ds(j, rows, stride=keys), :] = rstd * (scaled - first - hat * second)


def pair_back(parts, pair, pair_gain, w_bias):
    rows, keys = pair.shape[0], pair.shape[1]
    out = pl.pallas_call(
        grad_kernel,
        out_shape=jax.ShapeDtypeStruct((rows * keys, CZ), f32),
        scratch_shapes=[pltpu.VMEM((rows * keys, CZ), f32)],
        compiler_params=pltpu.CompilerParams(vmem_limit_bytes=GRANT),
        cost_estimate=pl.CostEstimate(flops=10**8, bytes_accessed=3 * 10**6, transcendentals=0),
        name="pair_grad",
    )(parts, pair, pair_gain.reshape(1, CZ), w_bias)
    return out.reshape(rows, keys, CZ)


def gather_tokens(normed):
    count = lax.axis_size("tok")
    swap = [(i, i ^ 1) for i in range(count)]
    pieces, sources = [normed], [(0, False)]
    for k in range(1, count // 2):
        steps = [(i, (i + 2 * k) % count) for i in range(count)]
        pieces.append(lax.ppermute(normed, "tok", steps))
        sources.append((count - 2 * k, False))
    for piece, (shift, _) in list(zip(pieces, sources)):
        pieces.append(lax.ppermute(piece, "tok", swap))
        sources.append((shift, True))
    return pieces, tuple(sources)


def body(
    atom_feats, atom_counts, atom_mask, token_single, pair, pair_gain, w_bias, w_atom_qkv,
    w_atom_out, w_embed, w_qkv, w_out, w_gate, w_up, w_down, cotangent,
):
    batch, atom_rows, _ = atom_feats.shape
    tok_rows = token_single.shape[0]
    shard, shards = lax.axis_index("tok"), lax.axis_size("tok")
    groups = lax.axis_size("samp")

    steps = [(i, i + 1) for i in range(shards - 1)]
    left = lax.ppermute(atom_feats[:, atom_rows - HALO :], "tok", steps)
    right = lax.ppermute(atom_feats[:, :HALO], "tok", [(j, i) for i, j in steps])

    local_bias = pair_bias(pair, pair_gain, w_bias, groups)
    bias = lax.all_to_all(local_bias, "samp", 0, 0).reshape(-1, 2 * tok_rows)

    reach = -(-(atom_rows + 2 * HALO) // 128) * 128
    flags = jnp.pad(atom_mask.astype(f32), (HALO, reach - atom_rows - HALO))
    flags = lax.dynamic_slice(flags, (shard * atom_rows,), (reach,)).reshape(reach // 128, 128)
    flags, local_bias = lax.optimization_barrier((flags, local_bias))

    halves = 2
    each = batch // halves
    tokens, att, probs, values = [], [], [], []
    gathered = []
    for i in range(halves):
        tok, normed = atom_stage(
            i * each, each, atom_feats, left, right, flags, atom_counts, token_single, w_atom_qkv,
            w_atom_out, w_embed,
        )
        tokens.append(tok)
        gathered.append(gather_tokens(normed))
    for pieces, sources in gathered:
        for kept, new in zip((att, probs, values), attend_stage(pieces, sources, bias, w_qkv)):
            kept.append(new)
    resid, hidden, d_bias = token_stage(
        tokens, att, probs, values, cotangent, w_out, w_gate, w_up, w_down
    )
    parts = d_bias.reshape(groups, -1, 2 * tok_rows)
    parts = lax.all_to_all(parts, "samp", 0, 0)
    token_out = output_stage(resid, hidden, w_down).reshape(batch, tok_rows, C_TOK)
    pair_grad = pair_back(parts, pair, pair_gain, w_bias)
    return (token_out, pair_grad)


def solution(mesh):
    in_specs = (
        P("samp", "tok", None),
        P("tok", None),
        P(),
        P("tok", None),
        P("tok", "samp", None),
        P(), P(), P(), P(), P(), P(), P(), P(), P(), P(),
        P("samp", "tok", None),
    )
    out_specs = (P("samp", "tok", None), P("tok", "samp", None))
    return jax.shard_map(body, mesh=mesh, in_specs=in_specs, out_specs=out_specs, check_vma=False)
```

time: 188 us -> 137 us (0.73)
  blocking collectives: 33 us -> 0 us
  Pallas kernels: 111 us -> 91.3 us
  between operations: 14.1 us -> 0.79 us
  starting transfers between devices: 10.2 us -> 20.2 us
  waiting for transfers between devices: 6.54 us -> 16.5 us
  local copies, waits for them, and re-layouts: 11.5 us -> 7.24 us
    all_gather x1 -> x0, blocking collectives: 33 us -> none  [body(): bias = lax.all_gather(local_bias, 'samp', axis=0, tiled=True)]
    pallas_call x3 -> x6, Pallas kernels: 103 us -> 79.7 us  [the longest x2 40.4 us: atom_stage(): pl.pallas_call(atom_kernel, grid=(batch,), in_specs=[of_sample(atoms, C_A...]
    all_to_all x0 -> x1, starting transfers between devices: none -> 7.28 us  [body(): bias = lax.all_to_all(local_bias, 'samp', 0, 0).reshape(-1, 2 * tok_rows)]
    ppermute x0 -> x6, waiting for transfers between devices: none -> 5.09 us  [the longest x2 5.08 us: gather_tokens(): pieces.append(lax.ppermute(normed, 'tok', steps))]
    all_to_all x1, waiting for transfers between devices: 6.49 us -> 11.5 us  [body(): parts = lax.all_to_all(parts, 'samp', 0, 0)]
    unnamed x31 -> x25, local copies, waits for them, and re-layouts: 10.5 us -> 5.72 us
    ppermute x0 -> x6, starting transfers between devices: none -> 2.87 us  [the longest x2 2.09 us: gather_tokens(): pieces.append(lax.ppermute(normed, 'tok', steps))]
    pallas_call x1, Pallas kernels: 1.52 us -> 3.68 us  [output_stage(): pl.pallas_call(output_kernel, out_shape=jax.ShapeDtypeStruct(resid.shape,...]
  transfers between devices with their start and end apart: 4 -> 10, of which waited for: 1 -> 2; matrix products, arithmetic and copies ran while one was open for 1% -> 2% of each run, Pallas kernels for 2% -> 44%
where the time goes in v1:
time: 137 us; the launch traced here: 136 us
  Pallas kernels  91.3 us (67%)
  starting transfers between devices  20.2 us (15%)
  waiting for transfers between devices  16.5 us (12%)
  local copies, waits for them, and re-layouts  7.24 us (5%)
    pallas_call x2, Pallas kernels, atom_stage(): pl.pallas_call(atom_kernel, grid=(batch,), in_specs=[of_sample(atoms, C_A...  40.4 us
    pallas_call x2, Pallas kernels, attend_stage(): pl.pallas_call(functools.partial(attend_kernel, sources=sources), in_spec...  21.9 us
    pallas_call x1, Pallas kernels, token_stage(): pl.pallas_call(functools.partial(token_kernel, halves=halves), in_specs=[...  13.1 us
    all_to_all x1, waiting for transfers between devices, body(): parts = lax.all_to_all(parts, 'samp', 0, 0)  11.5 us
    pallas_call x1, Pallas kernels, pair_back(): pl.pallas_call(grad_kernel, out_shape=jax.ShapeDtypeStruct((rows * keys,...  7.89 us
    all_to_all x1, starting transfers between devices, body(): bias = lax.all_to_all(local_bias, 'samp', 0, 0).reshape(-1, 2 * tok_rows)  7.28 us
    unnamed x25, local copies, waits for them, and re-layouts  5.72 us
    all_to_all x1, starting transfers between devices, body(): parts = lax.all_to_all(parts, 'samp', 0, 0)  5.72 us
  transfers between devices with their start and end apart: 10, of which 2 were waited for; matrix products, arithmetic and copies ran while one was open for 2% of the time, Pallas kernels for 44%

profile of v1, /device:TPU:0, one launch (start us, length us, event | category | flops | bytes accessed | tf_op | source)
XLA Modules:
  0.0 136.1 jit_solution(4858800127004864325)
XLA Ops:
  0.6 0.8 fusion.1
  1.5 1.3 collective-permute-start.1
  2.8 3.0 %collective-permute-start = (bf16[4,48,128]{2,1,0:T(8,128)(2,1)S(1)}, bf16[4,48,128]{2,1,0:T(8,128)(2,1)S(1)}, u32[]{:S(2)}, u32[]{:S(2)}) collective-permute-start(bf16[4,48,128]{2,1,0:T(8,128)(2,1)S(1)} %get-tuple-element.31), channel_id=1, source_target_pairs={{0,1},{1,2},{2,3},{4,5},{5,6},{6,7},{8,9},{9,10},{10,11},{12,13},{... | collective-permute-start | bytes 147464 | tf_op jit(solution)/shard_map/ppermute | solution.py:594
  5.8 1.4 %copy.18.w_bias_ref = bf16[128,16]{1,0:T(8,128)(2,1)} copy(bf16[128,16]{0,1:T(8,128)(2,1)} %param.22) | data formatting | bytes 8192 | tf_op args[6]
  7.2 4.2 %pair_bias.1 = bf16[8,256,128]{2,1,0:T(8,128)(2,1)} custom-call(bf16[64,32,128]{2,1,0:T(8,128)(2,1)} %pair_ref.3, f32[1,128]{1,0:T(1,128)} %bitcast.12, bf16[128,16]{1,0:T(8,128)(2,1)} %copy.18.w_bias_ref), custom_call_target="tpu_custom_call" | custom-call | flops 10000000 | bytes 10000000 | tf_op jit(solution)/shard_map/pair_bias/pallas_call | solution.py:85
  11.4 7.3 %all-to-all-start = ((bf16[8,256,128]{2,1,0:T(8,128)(2,1)}), bf16[8,256,128]{2,1,0:T(8,128)(2,1)S(1)}, u32[]{:S(2)}, u32[]{:S(2)}) async-start(bf16[8,256,128]{2,1,0:T(8,128)(2,1)} %pair_bias.1), calls=%async_computation | async-start | bytes 1048576 | tf_op jit(solution)/shard_map/all_to_all | solution.py:598
  18.7 0.7 fusion.flags_ref
  19.4 0.0 collective-permute-done.1.right_ref
  19.4 0.0 collective-permute-done.left_ref
  19.4 0.6 copy-done.10
  20.0 0.6 copy-done.11
  20.7 20.2 %atoms.2 = (f32[2,64,768]{2,1,0:T(8,128)}, bf16[2,64,768]{2,1,0:T(8,128)(2,1)}) custom-call(bf16[4,1280,128]{2,1,0:T(8,128)(2,1)} %feats_ref.3, bf16[4,48,128]{2,1,0:T(8,128)(2,1)} %copy-done.11, bf16[4,48,128]{2,1,0:T(8,128)(2,1)} %copy-done.10, f32[11,128]{1,0:T(8,128)} %fusion.flags_ref, s32[1,64]{1,0:T(1,128)} %counts_ref.3, bf16[64,768]{1,0:T(8,128)(2,1)} %single_ref.3, ...), custom_call_target="tpu_custom_call" | custom-call | flops 10000000000 | bytes 4000000 | tf_op jit(solution)/shard_map/atoms/pallas_call | solution.py:236
  40.9 1.6 %collective-permute-start.2 = (bf16[2,64,768]{2,1,0:T(8,128)(2,1)}, bf16[2,64,768]{2,1,0:T(8,128)(2,1)S(1)}, u32[]{:S(2)}, u32[]{:S(2)}) collective-permute-start(bf16[2,64,768]{2,1,0:T(8,128)(2,1)} %get-tuple-element.19.refs_0_), channel_id=1, source_target_pairs={{0,2},{1,3},{2,0},{3,1},{4,6},{5,7},{6,4},{7,5},{8,10},{9,11},{10,... | collective-permute-start | bytes 589832 | tf_op jit(solution)/shard_map/ppermute | solution.py:576
  42.4 20.2 %atoms.3 = (f32[2,64,768]{2,1,0:T(8,128)}, bf16[2,64,768]{2,1,0:T(8,128)(2,1)}) custom-call(bf16[4,1280,128]{2,1,0:T(8,128)(2,1)} %feats_ref.3, bf16[4,48,128]{2,1,0:T(8,128)(2,1)} %copy-done.11, bf16[4,48,128]{2,1,0:T(8,128)(2,1)} %copy-done.10, f32[11,128]{1,0:T(8,128)} %fusion.flags_ref, s32[1,64]{1,0:T(1,128)} %counts_ref.3, bf16[64,768]{1,0:T(8,128)(2,1)} %single_ref.3, ...), custom_call_target="tpu_custom_call" | custom-call | flops 10000000000 | bytes 4000000 | tf_op jit(solution)/shard_map/atoms/pallas_call | solution.py:236
  62.6 0.5 collective-permute-start.5
  63.2 0.3 collective-permute-start.3
  63.4 0.2 collective-permute-start.4
  63.7 0.3 collective-permute-start.6
  64.0 5.1 %collective-permute-done.5.refs_1_ = bf16[2,64,768]{2,1,0:T(8,128)(2,1)S(1)} collective-permute-done((bf16[2,64,768]{2,1,0:T(8,128)(2,1)}, bf16[2,64,768]{2,1,0:T(8,128)(2,1)S(1)}, u32[]{:S(2)}, u32[]{:S(2)}) %collective-permute-start.5) | collective-permute-done | bytes 196640 | tf_op jit(solution)/shard_map/ppermute | solution.py:576
  69.1 0.6 copy-done.7
  69.8 0.1 copy-done.9
  69.8 0.2 copy-done.1
  70.0 11.0 %attend.2 = (bf16[128,768]{1,0:T(8,128)(2,1)}, f32[2,8,256,128]{3,2,1,0:T(8,128)}, bf16[2,256,768]{2,1,0:T(8,128)(2,1)}) custom-call(bf16[2,64,768]{2,1,0:T(8,128)(2,1)} %get-tuple-element.19.refs_0_, bf16[2,64,768]{2,1,0:T(8,128)(2,1)} %copy-done.5, bf16[2,64,768]{2,1,0:T(8,128)(2,1)} %copy-done.7, bf16[2,64,768]{2,1,0:T(8,128)(2,1)} %copy-done.9, ...), custom_call_target="tpu_custom_call" | custom-call | flops 4000000000 | bytes 10000000 | tf_op jit(solution)/shard_map/attend/pallas_call | solution.py:368
  81.0 0.7 copy-done.6
  81.7 0.7 copy-done.8
  82.4 11.0 %attend.3 = (bf16[128,768]{1,0:T(8,128)(2,1)}, f32[2,8,256,128]{3,2,1,0:T(8,128)}, bf16[2,256,768]{2,1,0:T(8,128)(2,1)}) custom-call(bf16[2,64,768]{2,1,0:T(8,128)(2,1)} %get-tuple-element.21.refs_0_, bf16[2,64,768]{2,1,0:T(8,128)(2,1)} %copy-done.4, bf16[2,64,768]{2,1,0:T(8,128)(2,1)} %copy-done.6, bf16[2,64,768]{2,1,0:T(8,128)(2,1)} %copy-done.8, ...), custom_call_target="tpu_custom_call" | custom-call | flops 4000000000 | bytes 10000000 | tf_op jit(solution)/shard_map/attend/pallas_call | solution.py:368
  93.4 13.1 %tokens.1 = (f32[256,768]{1,0:T(8,128)}, bf16[256,1536]{1,0:T(8,128)(2,1)}, bf16[2048,128]{1,0:T(8,128)(2,1)}) custom-call(f32[2,64,768]{2,1,0:T(8,128)} %get-tuple-element.17.refs_0_, f32[2,64,768]{2,1,0:T(8,128)} %get-tuple-element.18.refs_1_, bf16[128,768]{1,0:T(8,128)(2,1)} %get-tuple-element.20.refs_2_, bf16[128,768]{1,0:T(8,128)(2,1)} %get-tuple-element.22.refs_3_, ...), custom_call_target="tpu_custom_call" | custom-call | flops 8000000000 | bytes 20000000 | tf_op jit(solution)/shard_map/tokens/pallas_call | solution.py:484
  106.5 5.7 %all-to-all-start.1 = ((bf16[8,256,128]{2,1,0:T(8,128)(2,1)}), bf16[8,256,128]{2,1,0:T(8,128)(2,1)S(1)}, u32[]{:S(2)}, u32[]{:S(2)}) async-start(bf16[8,256,128]{2,1,0:T(8,128)(2,1)} %bitcast.10), calls=%async_computation.1 | async-start | bytes 1048576 | tf_op jit(solution)/shard_map/all_to_all | solution.py:623
  112.2 3.7 %output.1 = bf16[256,768]{1,0:T(8,128)(2,1)} custom-call(f32[256,768]{1,0:T(8,128)} %get-tuple-element.27.resid_ref, bf16[256,1536]{1,0:T(8,128)(2,1)} %get-tuple-element.28.hidden_ref, bf16[1536,768]{1,0:T(8,128)(2,1)} %w_down_ref.1), custom_call_target="tpu_custom_call" | custom-call | flops 600000000 | bytes 5000000 | tf_op jit(solution)/shard_map/output/pallas_call | solution.py:520
  115.9 11.5 %all-to-all-done.1.parts_ref = bf16[8,256,128]{2,1,0:T(8,128)(2,1)S(1)} async-done(((bf16[8,256,128]{2,1,0:T(8,128)(2,1)}), bf16[8,256,128]{2,1,0:T(8,128)(2,1)S(1)}, u32[]{:S(2)}, u32[]{:S(2)}) %all-to-all-start.1) | async-done | bytes 524320 | tf_op jit(solution)/shard_map/all_to_all | solution.py:623
  127.4 0.8 copy-done
  128.2 7.9 %pair_grad.1 = f32[2048,128]{1,0:T(8,128)} custom-call(bf16[8,256,128]{2,1,0:T(8,128)(2,1)} %copy-done, bf16[64,32,128]{2,1,0:T(8,128)(2,1)} %pair_ref.3, f32[1,128]{1,0:T(1,128)} %bitcast.13, bf16[128,16]{1,0:T(8,128)(2,1)} %copy.18.w_bias_ref), custom_call_target="tpu_custom_call" | custom-call | flops 100000000 | bytes 3000000 | tf_op jit(solution)/shard_map/pair_grad/pallas_call | solution.py:559
  (24 shorter events, 0.1 us)
Async XLA Ops:
  0.6 18.1 %copy-start.2 = (s32[5120]{0:T(1024)S(1)}, s32[5120]{0:T(1024)}, u32[]{:S(2)}) copy-start(s32[5120]{0:T(1024)} %param.18) | copy-start | bytes 61444
  1.5 17.9 %collective-permute-start.1 = (bf16[4,48,128]{2,1,0:T(8,128)(2,1)S(1)}, bf16[4,48,128]{2,1,0:T(8,128)(2,1)S(1)}, u32[]{:S(2)}, u32[]{:S(2)}) collective-permute-start(bf16[4,48,128]{2,1,0:T(8,128)(2,1)S(1)} %get-tuple-element.30), channel_id=1, source_target_pairs={{1,0},{2,1},{3,2},{5,4},{6,5},{7,6},{9,8},{10,9},{11,10},{13,12},{... | collective-permute-start | bytes 147464 | tf_op jit(solution)/shard_map/ppermute | solution.py:595
  2.8 16.6 %collective-permute-start = (bf16[4,48,128]{2,1,0:T(8,128)(2,1)S(1)}, bf16[4,48,128]{2,1,0:T(8,128)(2,1)S(1)}, u32[]{:S(2)}, u32[]{:S(2)}) collective-permute-start(bf16[4,48,128]{2,1,0:T(8,128)(2,1)S(1)} %get-tuple-element.31), channel_id=1, source_target_pairs={{0,1},{1,2},{2,3},{4,5},{5,6},{6,7},{8,9},{9,10},{10,11},{12,13},{... | collective-permute-start | bytes 147464 | tf_op jit(solution)/shard_map/ppermute | solution.py:594
  11.4 57.7 %all-to-all-start = ((bf16[8,256,128]{2,1,0:T(8,128)(2,1)}), bf16[8,256,128]{2,1,0:T(8,128)(2,1)S(1)}, u32[]{:S(2)}, u32[]{:S(2)}) async-start(bf16[8,256,128]{2,1,0:T(8,128)(2,1)} %pair_bias.1), calls=%async_computation | async-start | bytes 1048576 | tf_op jit(solution)/shard_map/all_to_all | solution.py:598
  19.4 0.6 copy-start.10
  20.0 0.6 copy-start.11
  40.9 22.3 %copy-start.3 = (bf16[2,64,768]{2,1,0:T(8,128)(2,1)S(1)}, bf16[2,64,768]{2,1,0:T(8,128)(2,1)}, u32[]{:S(2)}) copy-start(bf16[2,64,768]{2,1,0:T(8,128)(2,1)} %get-tuple-element.19.refs_0_) | copy-start | bytes 589828
  40.9 22.6 %collective-permute-start.2 = (bf16[2,64,768]{2,1,0:T(8,128)(2,1)}, bf16[2,64,768]{2,1,0:T(8,128)(2,1)S(1)}, u32[]{:S(2)}, u32[]{:S(2)}) collective-permute-start(bf16[2,64,768]{2,1,0:T(8,128)(2,1)} %get-tuple-element.19.refs_0_), channel_id=1, source_target_pairs={{0,2},{1,3},{2,0},{3,1},{4,6},{5,7},{6,4},{7,5},{8,10},{9,11},{10,... | collective-permute-start | bytes 589832 | tf_op jit(solution)/shard_map/ppermute | solution.py:576
  62.6 6.4 %collective-permute-start.5 = (bf16[2,64,768]{2,1,0:T(8,128)(2,1)}, bf16[2,64,768]{2,1,0:T(8,128)(2,1)S(1)}, u32[]{:S(2)}, u32[]{:S(2)}) collective-permute-start(bf16[2,64,768]{2,1,0:T(8,128)(2,1)} %get-tuple-element.21.refs_0_), channel_id=1, source_target_pairs={{0,2},{1,3},{2,0},{3,1},{4,6},{5,7},{6,4},{7,5},{8,10},{9,11},{10,... | collective-permute-start | bytes 589832 | tf_op jit(solution)/shard_map/ppermute | solution.py:576
  63.2 5.9 %collective-permute-start.3 = (bf16[2,64,768]{2,1,0:T(8,128)(2,1)S(1)}, bf16[2,64,768]{2,1,0:T(8,128)(2,1)S(1)}, u32[]{:S(2)}, u32[]{:S(2)}) collective-permute-start(bf16[2,64,768]{2,1,0:T(8,128)(2,1)S(1)} %copy-done.3), channel_id=1, source_target_pairs={{0,1},{1,0},{2,3},{3,2},{4,5},{5,4},{6,7},{7,6},{8,9},{9,8},{10,11... | collective-permute-start | bytes 589832 | tf_op jit(solution)/shard_map/ppermute | solution.py:579
  63.4 5.7 %copy-start.5 = (bf16[2,64,768]{2,1,0:T(8,128)(2,1)}, bf16[2,64,768]{2,1,0:T(8,128)(2,1)S(1)}, u32[]{:S(2)}) copy-start(bf16[2,64,768]{2,1,0:T(8,128)(2,1)S(1)} %collective-permute-done.2.refs_1_) | copy-start | bytes 589828
  63.4 5.6 %collective-permute-start.4 = (bf16[2,64,768]{2,1,0:T(8,128)(2,1)S(1)}, bf16[2,64,768]{2,1,0:T(8,128)(2,1)S(1)}, u32[]{:S(2)}, u32[]{:S(2)}) collective-permute-start(bf16[2,64,768]{2,1,0:T(8,128)(2,1)S(1)} %collective-permute-done.2.refs_1_), channel_id=1, source_target_pairs={{0,1},{1,0},{2,3},{3,2},{4,5},{5,4},{6,7},{7,6},{8,9},{9,8},{10,11... | collective-permute-start | bytes 589832 | tf_op jit(solution)/shard_map/ppermute | solution.py:579
  63.7 17.3 %collective-permute-start.6 = (bf16[2,64,768]{2,1,0:T(8,128)(2,1)}, bf16[2,64,768]{2,1,0:T(8,128)(2,1)S(1)}, u32[]{:S(2)}, u32[]{:S(2)}) collective-permute-start(bf16[2,64,768]{2,1,0:T(8,128)(2,1)} %get-tuple-element.21.refs_0_), channel_id=1, source_target_pairs={{0,1},{1,0},{2,3},{3,2},{4,5},{5,4},{6,7},{7,6},{8,9},{9,8},{10,11... | collective-permute-start | bytes 589832 | tf_op jit(solution)/shard_map/ppermute | solution.py:579
  69.0 12.0 %copy-start.4 = (bf16[2,64,768]{2,1,0:T(8,128)(2,1)}, bf16[2,64,768]{2,1,0:T(8,128)(2,1)S(1)}, u32[]{:S(2)}) copy-start(bf16[2,64,768]{2,1,0:T(8,128)(2,1)S(1)} %collective-permute-done.5.refs_1_) | copy-start | bytes 589828
  69.0 12.0 %collective-permute-start.7 = (bf16[2,64,768]{2,1,0:T(8,128)(2,1)S(1)}, bf16[2,64,768]{2,1,0:T(8,128)(2,1)S(1)}, u32[]{:S(2)}, u32[]{:S(2)}) collective-permute-start(bf16[2,64,768]{2,1,0:T(8,128)(2,1)S(1)} %collective-permute-done.5.refs_1_), channel_id=1, source_target_pairs={{0,1},{1,0},{2,3},{3,2},{4,5},{5,4},{6,7},{7,6},{8,9},{9,8},{10,11... | collective-permute-start | bytes 589832 | tf_op jit(solution)/shard_map/ppermute | solution.py:579
  69.0 0.7 copy-start.7
  69.1 0.8 copy-start.9
  69.1 0.9 copy-start.1
  81.0 0.7 copy-start.6
  81.7 0.7 copy-start.8
  106.5 20.9 %all-to-all-start.1 = ((bf16[8,256,128]{2,1,0:T(8,128)(2,1)}), bf16[8,256,128]{2,1,0:T(8,128)(2,1)S(1)}, u32[]{:S(2)}, u32[]{:S(2)}) async-start(bf16[8,256,128]{2,1,0:T(8,128)(2,1)} %bitcast.10), calls=%async_computation.1 | async-start | bytes 1048576 | tf_op jit(solution)/shard_map/all_to_all | solution.py:623
  127.4 0.8 copy-start

commit v2 on v1

--- a/solution.py
+++ b/solution.py
@@ -48,11 +48,13 @@
     return lax.broadcasted_iota(jnp.int32, shape, dim)
 
 
-def split_heads(w_bias):
+def pick_heads(parity):
     row, col = iota((PAIRS, HEADS), 0), iota((PAIRS, HEADS), 1)
-    even = (col == 2 * row).astype(f32).astype(bf16)
-    odd = (col == 2 * row + 1).astype(f32).astype(bf16)
-    return nt(even, w_bias).astype(bf16), nt(odd, w_bias).astype(bf16)
+    return (col == 2 * row + parity).astype(f32).astype(bf16)
+
+
+def split_heads(w_bias_t):
+    return [nn(pick_heads(parity), w_bias_t) for parity in range(2)]
 
 
 def bias_kernel(pair_ref, gain_ref, w_bias_ref, out_ref, scaled_ref, stage_ref):
@@ -66,8 +68,7 @@
         return carry
 
     lax.fori_loop(0, rows // 8, norm_step, 0)
-    even, odd = split_heads(w_bias_ref[...])
-    weights = jnp.concatenate([even, odd], axis=1)
+    weights = jnp.concatenate(split_heads(w_bias_ref[...]), axis=1).astype(bf16)
     blank = jnp.zeros((rows, CZ), bf16)
     for j in range(keys):
         block = scaled_ref[pl.ds(j, rows, stride=keys), :].astype(bf16)
@@ -76,15 +77,14 @@
             axis=0,
         )
         stage_ref[pl.ds(j * PAIRS, PAIRS), :] = nt(weights, both)
-    for k in range(out_ref.shape[0]):
-        out_ref[k] = stage_ref[...].astype(bf16)
-
-
-def pair_bias(pair, pair_gain, w_bias, copies):
+    out_ref[...] = stage_ref[...].astype(bf16)
+
+
+def pair_bias(pair, pair_gain, w_bias_t):
     rows, keys = pair.shape[0], pair.shape[1]
     return pl.pallas_call(
         bias_kernel,
-        out_shape=jax.ShapeDtypeStruct((copies, keys * PAIRS, 2 * rows), bf16),
+        out_shape=jax.ShapeDtypeStruct((keys * PAIRS, 2 * rows), bf16),
         scratch_shapes=[
             pltpu.VMEM((rows * keys, CZ), f32),
             pltpu.VMEM((keys * PAIRS, 2 * rows), f32),
@@ -92,13 +92,13 @@
         compiler_params=pltpu.CompilerParams(vmem_limit_bytes=GRANT),
         cost_estimate=pl.CostEstimate(flops=10**7, bytes_accessed=10**7, transcendentals=0),
         name="pair_bias",
-    )(pair, pair_gain.reshape(1, CZ), w_bias)
+    )(pair, pair_gain.reshape(1, CZ), w_bias_t)
 
 
 def atom_kernel(
     feats_ref, left_ref, right_ref, flags_ref, counts_ref, single_ref, w_qkv_ref, w_out_ref,
-    w_embed_ref, tokens_ref, normed_ref, xn_ref, qkv_ref, scores_ref, probs_ref, mixed_ref,
-    keybias_ref, onehot_ref, pooled_ref, counts_col_ref,
+    w_embed_ref, tokens_ref, normed_ref, xn_ref, qkv_ref, scores_a, scores_b, probs_a, probs_b,
+    mixed_ref, updated_ref, split_ref, keybias_ref, onehot_ref, counts_col_ref,
 ):
     atoms = feats_ref.shape[1]
     padded = atoms + 2 * HALO
@@ -123,19 +123,15 @@
             at = pos + float(g * 256)
             hit = jnp.where((at >= start) & (at < start + own), 1.0, 0.0).astype(bf16)
             onehot_ref[g] = jnp.concatenate([hit, hit], axis=1)
-        probs_ref[...] = jnp.zeros_like(probs_ref)
+        probs_a[...] = jnp.zeros_like(probs_a)
+        probs_b[...] = jnp.zeros_like(probs_b)
 
     xn_ref[0:HALO, :] = norm_rows(left_ref[0].astype(f32))[0].astype(bf16)
     xn_ref[atoms + HALO : padded, :] = norm_rows(right_ref[0].astype(f32))[0].astype(bf16)
 
-    def norm_step(i, carry):
-        at = pl.multiple_of(i * 256, 256)
-        block = feats_ref[0, pl.ds(at, 256), :].astype(f32)
-        xn_ref[pl.ds(HALO + at, 256), :] = norm_rows(block)[0].astype(bf16)
-        return carry
-
-    lax.fori_loop(0, atoms // 256, norm_step, 0)
-
+    for i in range(atoms // 256):
+        block = feats_ref[0, 256 * i : 256 * i + 256, :].astype(f32)
+        xn_ref[HALO + 256 * i : HALO + 256 * i + 256, :] = norm_rows(block)[0].astype(bf16)
     chunk = padded // 4
     w_qkv = w_qkv_ref[...]
     for i in range(4):
@@ -143,18 +139,15 @@
             xn_ref[i * chunk : (i + 1) * chunk, :], w_qkv
         ).astype(bf16)
 
-    lane = iota((32, 128), 1)
-    head_of = lane // ATOM_HD
+    head_of = iota((32, 128), 1) // ATOM_HD
     head_mask = [(head_of == h).astype(f32).astype(bf16) for h in range(ATOM_HEADS)]
-    own_atom = (lane % 32) == iota((32, 128), 0)
+    own_atom = (iota((32, 128), 1) % 32) == iota((32, 128), 0)
     factor = ATOM_HD ** (-0.5) * LOG2E
-    pairs = atoms // 64
-    per = 4
-
-    def score_step(i, carry):
-        for k in range(per):
-            pair = i * per + k
-            base = pl.multiple_of(pair * 64, 64)
+    groups = atoms // 128
+
+    def score_step(group, to_ref):
+        for k in range(2):
+            base = pl.multiple_of(group * 128 + 64 * k, 64)
             queries = qkv_ref[pl.ds(base + HALO, 64), 0:C_ATOM]
             spread = jnp.concatenate(
                 [
@@ -164,36 +157,26 @@
                 ],
                 axis=0,
             )
-            scores_ref[pair] = nt(qkv_ref[pl.ds(base, 160), C_ATOM : 2 * C_ATOM], spread)
-        return carry
-
-    lax.fori_loop(0, pairs // per, score_step, 0)
-
-    def softmax_step(i, carry):
+            to_ref[k] = nt(qkv_ref[pl.ds(base, 160), C_ATOM : 2 * C_ATOM], spread)
+
+    def softmax_step(group, from_ref, to_ref):
         for k in range(2):
-            pair = i * 2 + k
-            base = pl.multiple_of(pair * 64, 64)
+            base = pl.multiple_of(group * 128 + 64 * k, 64)
             for w in range(2):
                 keybias = keybias_ref[pl.ds(base + 32 * w, 128), :]
                 keybias = jnp.concatenate(
                     [keybias[0:48], jnp.where(own_atom, 0.0, keybias[48:80]), keybias[80:128]],
                     axis=0,
                 )
-                scores = scores_ref[pair, 32 * w : 32 * w + 128, 128 * w : 128 * w + 128] + keybias
+                scores = from_ref[k, 32 * w : 32 * w + 128, 128 * w : 128 * w + 128] + keybias
                 expo = jnp.exp2((scores - jnp.max(scores, axis=0, keepdims=True)) * factor)
                 weights = expo * (1.0 / jnp.sum(expo, axis=0, keepdims=True))
-                probs_ref[pair, 32 * w : 32 * w + 128, 128 * w : 128 * w + 128] = weights.astype(
-                    bf16
-                )
-        return carry
-
-    lax.fori_loop(0, pairs // 2, softmax_step, 0)
-
-    def value_step(i, carry):
-        for k in range(per):
-            pair = i * per + k
-            base = pl.multiple_of(pair * 64, 64)
-            part = tn(probs_ref[pair], qkv_ref[pl.ds(base, 160), 2 * C_ATOM : 3 * C_ATOM])
+                to_ref[k, 32 * w : 32 * w + 128, 128 * w : 128 * w + 128] = weights.astype(bf16)
+
+    def value_step(group, from_ref):
+        for k in range(2):
+            base = pl.multiple_of(group * 128 + 64 * k, 64)
+            part = tn(from_ref[k], qkv_ref[pl.ds(base, 160), 2 * C_ATOM : 3 * C_ATOM])
             mixes = []
             for w in range(2):
                 mix = part[128 * w : 128 * w + 32]
@@ -202,25 +185,37 @@
                     mix = jnp.where(head_of == h, part[low : low + 32], mix)
                 mixes.append(mix.astype(bf16))
             mixed_ref[pl.ds(base, 64), :] = jnp.concatenate(mixes, axis=0)
+
+    score_step(0, scores_a)
+
+    def window_step(i, carry):
+        even, odd = 2 * i, 2 * i + 1
+        score_step(odd, scores_b)
+        softmax_step(even, scores_a, probs_a)
+        value_step(jnp.maximum(even - 1, 0), probs_b)
+        score_step(jnp.minimum(odd + 1, groups - 1), scores_a)
+        softmax_step(odd, scores_b, probs_b)
+        value_step(even, probs_a)
         return carry
 
-    lax.fori_loop(0, pairs // per, value_step, 0)
-
-    pooled_ref[...] = jnp.zeros_like(pooled_ref)
-
-    def embed_step(g, carry):
-        base = pl.multiple_of(g * 256, 256)
-        feats = feats_ref[0, pl.ds(base, 256), :].astype(f32)
-        updated = (feats + nn(mixed_ref[pl.ds(base, 256), :], w_out_ref[...])).astype(bf16)
-        embedded = jnp.maximum(nn(updated, w_embed_ref[...]), 0.0)
+    lax.fori_loop(0, groups // 2, window_step, 0)
+    value_step(groups - 1, probs_b)
+
+    w_out = w_out_ref[...]
+    for g in range(atoms // 256):
+        part = slice(256 * g, 256 * g + 256)
+        feats = feats_ref[0, part, :].astype(f32)
+        updated_ref[part, :] = (feats + nn(mixed_ref[part, :], w_out)).astype(bf16)
+    pooled = jnp.zeros((tok_rows, C_TOK), f32)
+    for g in range(atoms // 256):
+        embedded = jnp.maximum(
+            nn(updated_ref[256 * g : 256 * g + 256, :], w_embed_ref[...]), 0.0
+        )
         high = embedded.astype(bf16)
-        low = (embedded - high.astype(f32)).astype(bf16)
-        pooled_ref[...] += nn(onehot_ref[g], jnp.concatenate([high, low], axis=0))
-        return carry
-
-    lax.fori_loop(0, atoms // 256, embed_step, 0)
-    counts = counts_col_ref[:, 0:1]
-    tokens = pooled_ref[...] / counts + single_ref[...].astype(f32)
+        split_ref[g, 0:256, :] = high
+        split_ref[g, 256:512, :] = (embedded - high.astype(f32)).astype(bf16)
+        pooled = pooled + nn(onehot_ref[g], split_ref[g])
+    tokens = pooled / counts_col_ref[:, 0:1] + single_ref[...].astype(f32)
     tokens_ref[0] = tokens
     normed_ref[0] = norm_rows(tokens)[0].astype(bf16)
 
@@ -229,7 +224,6 @@
     atoms = feats.shape[1]
     tok_rows = single.shape[0]
     padded = atoms + 2 * HALO
-    pairs = atoms // 64
     of_sample = lambda rows, cols: pl.BlockSpec((1, rows, cols), lambda s: (s + first, 0, 0))
     by_sample = lambda rows, cols: pl.BlockSpec((1, rows, cols), lambda s: (s, 0, 0))
     whole = lambda a: pl.BlockSpec(a.shape, lambda s: (0,) * a.ndim)
@@ -248,12 +242,15 @@
         scratch_shapes=[
             pltpu.VMEM((padded, C_ATOM), bf16),
             pltpu.VMEM((padded, 3 * C_ATOM), bf16),
-            pltpu.VMEM((pairs, 160, 256), f32),
-            pltpu.VMEM((pairs, 160, 256), bf16),
+            pltpu.VMEM((2, 160, 256), f32),
+            pltpu.VMEM((2, 160, 256), f32),
+            pltpu.VMEM((2, 160, 256), bf16),
+            pltpu.VMEM((2, 160, 256), bf16),
             pltpu.VMEM((atoms, C_ATOM), bf16),
+            pltpu.VMEM((atoms, C_ATOM), bf16),
+            pltpu.VMEM((atoms // 256, 512, C_TOK), bf16),
             pltpu.VMEM((flags.shape[0] * 128, 128), f32),
             pltpu.VMEM((atoms // 256, tok_rows, 512), bf16),
-            pltpu.VMEM((tok_rows, C_TOK), f32),
             pltpu.VMEM((tok_rows, 128), f32),
         ],
         compiler_params=pltpu.CompilerParams(vmem_limit_bytes=GRANT),
@@ -282,13 +279,13 @@
 
 
 def attend_kernel(
-    *refs, sources,
+    *refs, count, groups,
 ):
-    piece_refs = refs[: len(sources)]
-    bias_ref, w_qkv_hbm, att_ref, probs_ref, values_ref = refs[len(sources) : len(sources) + 5]
-    w_qkv_ref, sems, all_ref, qk_ref, biasf_ref = refs[len(sources) + 5 :]
+    piece_refs, bias_refs = refs[:count], refs[count : count + groups]
+    w_qkv_hbm, att_ref, probs_ref, values_ref = refs[count + groups : count + groups + 4]
+    w_qkv_ref, sems, all_ref, qk_ref, biasf_ref = refs[count + groups + 4 :]
     batch, tok_rows = piece_refs[0].shape[0], piece_refs[0].shape[1]
-    keys_all = tok_rows * len(sources)
+    keys_all = tok_rows * count
     copies = [
         pltpu.make_async_copy(
             w_qkv_hbm.at[:, pl.ds(C_TOK * i, C_TOK)], w_qkv_ref.at[i], sems.at[i]
@@ -298,15 +295,14 @@
     for copy in copies:
         copy.start()
     here = lax.axis_index("tok")
-    count = len(sources)
-    for piece, (shift, flip) in zip(piece_refs, sources):
-        owner = lax.rem(here + shift, count)
-        if flip:
-            owner = owner + 1 - 2 * lax.rem(owner, 2)
-        at = pl.multiple_of(owner * tok_rows, tok_rows)
+    for k, piece in enumerate(piece_refs):
+        at = pl.multiple_of((here ^ k) * tok_rows, tok_rows)
         for s in range(batch):
             all_ref[s, pl.ds(at, tok_rows), :] = piece[s]
-    biasf_ref[...] = bias_ref[...].astype(f32)
+    here = lax.axis_index("samp")
+    for k, piece in enumerate(bias_refs):
+        size = piece.shape[0]
+        biasf_ref[pl.ds(pl.multiple_of((here ^ k) * size, size), size), :] = piece[...].astype(f32)
     copies[0].wait()
     own = piece_refs[0][...].reshape(batch * tok_rows, C_TOK)
     queries_ref = att_ref
@@ -360,14 +356,14 @@
     lax.fori_loop(0, batch, attend_step, 0)
 
 
-def attend_stage(pieces, sources, bias, w_qkv):
+def attend_stage(pieces, bias, w_qkv):
     batch, tok_rows, _ = pieces[0].shape
     keys_all = tok_rows * len(pieces)
     vmem = pl.BlockSpec(memory_space=pltpu.VMEM)
     hbm = pl.BlockSpec(memory_space=pl.ANY)
     return pl.pallas_call(
-        functools.partial(attend_kernel, sources=sources),
-        in_specs=[vmem] * (len(pieces) + 1) + [hbm],
+        functools.partial(attend_kernel, count=len(pieces), groups=len(bias)),
+        in_specs=[vmem] * (len(pieces) + len(bias)) + [hbm],
         out_specs=[vmem] * 3,
         out_shape=[
             jax.ShapeDtypeStruct((batch * tok_rows, C_TOK), bf16),
@@ -386,18 +382,19 @@
             flops=4 * 10**9, bytes_accessed=10**7, transcendentals=10**6
         ),
         name="attend",
-    )(*pieces, bias, w_qkv)
-
-
-def token_kernel(*refs, halves):
+    )(*pieces, *bias, w_qkv)
+
+
+def token_kernel(*refs, halves, groups):
     tokens_refs, att_refs = refs[0:halves], refs[halves : 2 * halves]
     probs_hbm, values_hbm = refs[2 * halves : 3 * halves], refs[3 * halves : 4 * halves]
     cot_ref, w_out_hbm, w_gate_hbm, w_up_hbm, w_down_hbm = refs[4 * halves : 4 * halves + 5]
-    resid_ref, hidden_ref, d_bias_ref = refs[4 * halves + 5 : 4 * halves + 8]
+    resid_ref, hidden_ref = refs[4 * halves + 5 : 4 * halves + 7]
+    block_refs = refs[4 * halves + 7 : 4 * halves + 7 + groups]
     (
         w_out_ref, w_gate_ref, w_up_ref, w_down_ref, probs_ref, values_ref, sems, grads_ref,
         d_gate_ref, d_up_ref, hat_ref, d_bias_f_ref,
-    ) = refs[4 * halves + 8 :]
+    ) = refs[4 * halves + 7 + groups :]
     batch, tok_rows = cot_ref.shape[0], cot_ref.shape[1]
     keys_all = values_ref.shape[1]
     rows = batch * tok_rows
@@ -470,10 +467,14 @@
             delta = jnp.sum(probs * d_probs, axis=0, keepdims=True)
             total = total + probs * (d_probs - delta)
         d_bias_f_ref[pl.ds(pair, keys_all, stride=PAIRS), :] = total
-    d_bias_ref[...] = d_bias_f_ref[...].astype(bf16)
-
-
-def token_stage(tokens, att, probs, values, cot, w_out, w_gate, w_up, w_down):
+    here = lax.axis_index("samp")
+    for k, block in enumerate(block_refs):
+        size = block.shape[0]
+        at = pl.multiple_of((here ^ k) * size, size)
+        block[...] = d_bias_f_ref[pl.ds(at, size), :].astype(bf16)
+
+
+def token_stage(groups, tokens, att, probs, values, cot, w_out, w_gate, w_up, w_down):
     halves = len(tokens)
     batch, tok_rows, _ = cot.shape
     keys_all = values[0].shape[1]
@@ -482,14 +483,14 @@
     vmem = pl.BlockSpec(memory_space=pltpu.VMEM)
     hbm = pl.BlockSpec(memory_space=pl.ANY)
     return pl.pallas_call(
-        functools.partial(token_kernel, halves=halves),
+        functools.partial(token_kernel, halves=halves, groups=groups),
         in_specs=[vmem] * (2 * halves) + [hbm] * (2 * halves) + [vmem] + [hbm] * 4,
-        out_specs=[vmem] * 3,
+        out_specs=[vmem] * (2 + groups),
         out_shape=[
             jax.ShapeDtypeStruct((rows, C_TOK), f32),
             jax.ShapeDtypeStruct((rows, hidden), bf16),
-            jax.ShapeDtypeStruct((keys_all * PAIRS, 2 * tok_rows), bf16),
-        ],
+        ]
+        + [jax.ShapeDtypeStruct((keys_all * PAIRS // groups, 2 * tok_rows), bf16)] * groups,
         scratch_shapes=[
             pltpu.VMEM(w_out.shape, bf16),
             pltpu.VMEM(w_gate.shape, bf16),
@@ -512,73 +513,94 @@
     )(*tokens, *att, *probs, *values, cot, w_out, w_gate, w_up, w_down)
 
 
-def output_kernel(resid_ref, hidden_ref, w_down_ref, out_ref):
+def output_kernel(
+    resid_ref, hidden_ref, w_down_ref, pair_ref, out_ref, hat_ref, rstd_ref, pairf_ref
+):
     out_ref[...] = (resid_ref[...] + nn(hidden_ref[...], w_down_ref[...])).astype(bf16)
-
-
-def output_stage(resid, hidden, w_down):
-    return pl.pallas_call(
-        output_kernel,
-        out_shape=jax.ShapeDtypeStruct(resid.shape, bf16),
-        compiler_params=pltpu.CompilerParams(vmem_limit_bytes=GRANT),
-        cost_estimate=pl.CostEstimate(
-            flops=6 * 10**8, bytes_accessed=5 * 10**6, transcendentals=0
-        ),
-        name="output",
-    )(resid, hidden, w_down)
-
-
-def grad_kernel(parts_ref, pair_ref, gain_ref, w_bias_ref, out_ref, pairf_ref):
     rows, keys = pair_ref.shape[0], pair_ref.shape[1]
-    gain = gain_ref[...]
     for i in range(rows // 8):
         pairf_ref[8 * keys * i : 8 * keys * (i + 1), :] = (
             pair_ref[8 * i : 8 * i + 8].astype(f32).reshape(8 * keys, CZ)
         )
-    even, odd = split_heads(w_bias_ref[...])
-    weights = jnp.concatenate([even, odd], axis=1).astype(f32)
-    weights = jnp.concatenate([weights, weights, weights], axis=0).astype(bf16)
-    for j in range(keys):
-        total = parts_ref[0, PAIRS * j : PAIRS * (j + 1), :].astype(f32)
-        for k in range(1, parts_ref.shape[0]):
-            total = total + parts_ref[k, PAIRS * j : PAIRS * (j + 1), :].astype(f32)
-        high = total.astype(bf16).astype(f32)
-        rest = total - high
-        middle = rest.astype(bf16).astype(f32)
-        stack = jnp.concatenate([high, middle, rest - middle], axis=0)
-        both = nn(stack.T.astype(bf16), weights)
-        scaled = (both[0:rows, 0:CZ] + both[rows : 2 * rows, CZ : 2 * CZ]) * gain
+
+    def norm_step(j, carry):
         hat, rstd = norm_rows(pairf_ref[pl.ds(j, rows, stride=keys), :])
-        first = jnp.mean(scaled, axis=-1, keepdims=True)
-        second = jnp.mean(scaled * hat, axis=-1, keepdims=True)
-        out_ref[pl.ds(j, rows, stride=keys), :] = rstd * (scaled - first - hat * second)
-
-
-def pair_back(parts, pair, pair_gain, w_bias):
+        at = pl.multiple_of(j * rows, rows)
+        hat_ref[pl.ds(at, rows), :] = hat
+        rstd_ref[pl.ds(at, rows), :] = jnp.broadcast_to(rstd, (rows, CZ))
+        return carry
+
+    lax.fori_loop(0, keys, norm_step, 0, unroll=4)
+
+
+def output_stage(resid, hidden, w_down, pair):
     rows, keys = pair.shape[0], pair.shape[1]
-    out = pl.pallas_call(
-        grad_kernel,
-        out_shape=jax.ShapeDtypeStruct((rows * keys, CZ), f32),
+    return pl.pallas_call(
+        output_kernel,
+        out_shape=[jax.ShapeDtypeStruct(resid.shape, bf16)]
+        + [jax.ShapeDtypeStruct((rows * keys, CZ), f32)] * 2,
         scratch_shapes=[pltpu.VMEM((rows * keys, CZ), f32)],
         compiler_params=pltpu.CompilerParams(vmem_limit_bytes=GRANT),
-        cost_estimate=pl.CostEstimate(flops=10**8, bytes_accessed=3 * 10**6, transcendentals=0),
+        cost_estimate=pl.CostEstimate(
+            flops=10**9, bytes_accessed=8 * 10**6, transcendentals=0
+        ),
+        name="output",
+    )(resid, hidden, w_down, pair)
+
+
+def grad_kernel(*refs, groups):
+    part_refs = refs[:groups]
+    hat_ref, rstd_ref, gain_ref, w_bias_ref, out_ref, total_ref = refs[groups:]
+    keys = part_refs[0].shape[0] // PAIRS
+    rows = hat_ref.shape[0] // keys
+    total = part_refs[0][...].astype(f32)
+    for part in part_refs[1:]:
+        total = total + part[...].astype(f32)
+    total_ref[...] = total
+    weights = jnp.concatenate(split_heads(w_bias_ref[...]), axis=0) * gain_ref[...]
+    weights = weights - jnp.mean(weights, axis=-1, keepdims=True)
+    weights = jnp.concatenate([weights[0:PAIRS], weights[PAIRS:HEADS]], axis=1)
+    w_high = weights.astype(bf16).astype(f32)
+    w_middle = (weights - w_high).astype(bf16).astype(f32)
+    w_low = weights - w_high - w_middle
+    weights = jnp.concatenate([w_high, w_middle, w_low, w_high, w_middle, w_high], axis=0)
+    weights = weights.astype(bf16)
+    for j in range(keys):
+        total = total_ref[PAIRS * j : PAIRS * (j + 1), :]
+        high = total.astype(bf16).astype(f32)
+        middle = (total - high).astype(bf16).astype(f32)
+        low = total - high - middle
+        stack = jnp.concatenate([high, high, high, middle, middle, low], axis=0)
+        both = nn(stack.T.astype(bf16), weights)
+        scaled = both[0:rows, 0:CZ] + both[rows : 2 * rows, CZ : 2 * CZ]
+        hat = hat_ref[rows * j : rows * (j + 1), :]
+        second = jnp.mean(scaled * hat, axis=-1, keepdims=True)
+        out_ref[pl.ds(j, rows, stride=keys), :] = rstd_ref[rows * j : rows * (j + 1), :] * (
+            scaled - hat * second
+        )
+
+
+def pair_back(parts, hat, rstd, pair_gain, w_bias_t):
+    keys = parts[0].shape[0] // PAIRS
+    rows = hat.shape[0] // keys
+    out = pl.pallas_call(
+        functools.partial(grad_kernel, groups=len(parts)),
+        out_shape=jax.ShapeDtypeStruct((rows * keys, CZ), f32),
+        scratch_shapes=[pltpu.VMEM((keys * PAIRS, 2 * rows), f32)],
+        compiler_params=pltpu.CompilerParams(vmem_limit_bytes=GRANT),
+        cost_estimate=pl.CostEstimate(flops=10**8, bytes_accessed=4 * 10**6, transcendentals=0),
         name="pair_grad",
-    )(parts, pair, pair_gain.reshape(1, CZ), w_bias)
+    )(*parts, hat, rstd, pair_gain.reshape(1, CZ), w_bias_t)
     return out.reshape(rows, keys, CZ)
 
 
-def gather_tokens(normed):
-    count = lax.axis_size("tok")
-    swap = [(i, i ^ 1) for i in range(count)]
-    pieces, sources = [normed], [(0, False)]
-    for k in range(1, count // 2):
-        steps = [(i, (i + 2 * k) % count) for i in range(count)]
-        pieces.append(lax.ppermute(normed, "tok", steps))
-        sources.append((count - 2 * k, False))
-    for piece, (shift, _) in list(zip(pieces, sources)):
-        pieces.append(lax.ppermute(piece, "tok", swap))
-        sources.append((shift, True))
-    return pieces, tuple(sources)
+def swap(values, axis, k):
+    return lax.ppermute(values, axis, [(i, i ^ k) for i in range(lax.axis_size(axis))])
+
+
+def gather(values, axis):
+    far = range(lax.axis_size(axis) - 1, 0, -1)
+    return [values] + [swap(values, axis, k) for k in far][::-1]
 
 
 def body(
@@ -594,13 +616,13 @@
     left = lax.ppermute(atom_feats[:, atom_rows - HALO :], "tok", steps)
     right = lax.ppermute(atom_feats[:, :HALO], "tok", [(j, i) for i, j in steps])
 
-    local_bias = pair_bias(pair, pair_gain, w_bias, groups)
-    bias = lax.all_to_all(local_bias, "samp", 0, 0).reshape(-1, 2 * tok_rows)
+    w_bias_t = w_bias.T
+    bias = gather(pair_bias(pair, pair_gain, w_bias_t), "samp")
 
     reach = -(-(atom_rows + 2 * HALO) // 128) * 128
     flags = jnp.pad(atom_mask.astype(f32), (HALO, reach - atom_rows - HALO))
     flags = lax.dynamic_slice(flags, (shard * atom_rows,), (reach,)).reshape(reach // 128, 128)
-    flags, local_bias = lax.optimization_barrier((flags, local_bias))
+    flags, bias[0] = lax.optimization_barrier((flags, bias[0]))
 
     halves = 2
     each = batch // halves
@@ -612,17 +634,18 @@
             w_atom_out, w_embed,
         )
         tokens.append(tok)
-        gathered.append(gather_tokens(normed))
-    for pieces, sources in gathered:
-        for kept, new in zip((att, probs, values), attend_stage(pieces, sources, bias, w_qkv)):
+        gathered.append(gather(normed, "tok"))
+    for pieces in gathered:
+        for kept, new in zip((att, probs, values), attend_stage(pieces, bias, w_qkv)):
             kept.append(new)
-    resid, hidden, d_bias = token_stage(
-        tokens, att, probs, values, cotangent, w_out, w_gate, w_up, w_down
+    resid, hidden, *blocks = token_stage(
+        groups, tokens, att, probs, values, cotangent, w_out, w_gate, w_up, w_down
     )
-    parts = d_bias.reshape(groups, -1, 2 * tok_rows)
-    parts = lax.all_to_all(parts, "samp", 0, 0)
-    token_out = output_stage(resid, hidden, w_down).reshape(batch, tok_rows, C_TOK)
-    pair_grad = pair_back(parts, pair, pair_gain, w_bias)
+    far = range(groups - 1, 0, -1)
+    parts = [blocks[0]] + [swap(blocks[k], "samp", k) for k in far]
+    token_out, hat, rstd = output_stage(resid, hidden, w_down, pair)
+    pair_grad = pair_back(parts, hat, rstd, pair_gain, w_bias_t)
+    token_out = token_out.reshape(batch, tok_rows, C_TOK)
     return (token_out, pair_grad)
 
 

time: 137 us -> 119 us (0.87)
  waiting for transfers between devices: 16.5 us -> 0.06 us
  starting transfers between devices: 20.2 us -> 36.2 us
  Pallas kernels: 91.3 us -> 75.4 us
  local copies, waits for them, and re-layouts: 7.24 us -> 4.96 us
    ppermute x6 -> x20, starting transfers between devices: 2.87 us -> 31.9 us  [swap(): lax.ppermute(values, axis, [(i, i ^ k) for i in range(lax.axis_size(axis))])]
    pallas_call x2, Pallas kernels: 40.4 us -> 25.8 us  [atom_stage(): pl.pallas_call(atom_kernel, grid=(batch,), in_specs=[of_sample(atoms, C_A...]
    all_to_all x2 -> x0, starting transfers between devices: 13 us -> none  [the longest x1 7.28 us: body(): bias = lax.all_to_all(local_bias, 'samp', 0, 0).reshape(-1, 2 * tok_rows)]
    all_to_all x2 -> x0, waiting for transfers between devices: 11.5 us -> none  [the longest x1 11.5 us: body(): parts = lax.all_to_all(parts, 'samp', 0, 0)]
    ppermute x6 -> x20, waiting for transfers between devices: 5.09 us -> 0.05 us  [swap(): lax.ppermute(values, axis, [(i, i ^ k) for i in range(lax.axis_size(axis))])]
    unnamed x25 -> x46, local copies, waits for them, and re-layouts: 5.72 us -> 3.46 us
  transfers between devices with their start and end apart: 10 -> 22, of which waited for: 2 -> 0; matrix products, arithmetic and copies ran while one was open for 2% -> 2% of each run, Pallas kernels for 44% -> 36%
where the time goes in v2:
time: 119 us; the launch traced here: 118 us
  Pallas kernels  75.4 us (63%)
  starting transfers between devices  36.2 us (30%)
  local copies, waits for them, and re-layouts  4.96 us (4%)
    ppermute x20, starting transfers between devices, swap(): lax.ppermute(values, axis, [(i, i ^ k) for i in range(lax.axis_size(axis))])  31.9 us
    pallas_call x2, Pallas kernels, atom_stage(): pl.pallas_call(atom_kernel, grid=(batch,), in_specs=[of_sample(atoms, C_A...  25.8 us
    pallas_call x2, Pallas kernels, attend_stage(): pl.pallas_call(functools.partial(attend_kernel, count=len(pieces), groups...  21.8 us
    pallas_call x1, Pallas kernels, token_stage(): pl.pallas_call(functools.partial(token_kernel, halves=halves, groups=grou...  13.2 us
    pallas_call x1, Pallas kernels, output_stage(): pl.pallas_call(output_kernel, out_shape=[jax.ShapeDtypeStruct(resid.shape...  6.4 us
    pallas_call x1, Pallas kernels, pair_back(): pl.pallas_call(functools.partial(grad_kernel, groups=len(parts)), out_sha...  4.16 us
    pallas_call x1, Pallas kernels, pair_bias(): pl.pallas_call(bias_kernel, out_shape=jax.ShapeDtypeStruct((keys * PAIRS,...  4.01 us
    unnamed x46, local copies, waits for them, and re-layouts  3.46 us
  transfers between devices with their start and end apart: 22, of which 0 were waited for; matrix products, arithmetic and copies ran while one was open for 2% of the time, Pallas kernels for 36%

profile of v2, /device:TPU:0, one launch (start us, length us, event | category | flops | bytes accessed | tf_op | source)
XLA Modules:
  0.0 118.2 jit_solution(13703896858111607241)
XLA Ops:
  0.6 4.0 %pair_bias.1.refs_4_ = bf16[256,128]{1,0:T(8,128)(2,1)} custom-call(bf16[64,32,128]{2,1,0:T(8,128)(2,1)} %pair_ref.3, f32[1,128]{1,0:T(1,128)} %bitcast.9, bf16[16,128]{1,0:T(8,128)(2,1)} %bitcast.7), custom_call_target="tpu_custom_call" | custom-call | flops 10000000 | bytes 10000000 | tf_op jit(solution)/shard_map/pair_bias/pallas_call | solution.py:85
  4.6 6.0 %collective-permute-start.11 = (bf16[256,128]{1,0:T(8,128)(2,1)}, bf16[256,128]{1,0:T(8,128)(2,1)S(1)}, u32[]{:S(2)}, u32[]{:S(2)}) collective-permute-start(bf16[256,128]{1,0:T(8,128)(2,1)} %pair_bias.1.refs_4_), channel_id=1, source_target_pairs={{0,28},{4,24},{8,20},{12,16},{16,12},{20,8},{24,4},{28,0},{1,29},{... | collective-permute-start | bytes 196616 | tf_op jit(solution)/shard_map/ppermute | solution.py:598
  10.9 0.7 collective-permute-start.9
  11.6 0.8 fusion.1
  12.4 1.3 %collective-permute-start.1 = (bf16[4,48,128]{2,1,0:T(8,128)(2,1)S(1)}, bf16[4,48,128]{2,1,0:T(8,128)(2,1)S(1)}, u32[]{:S(2)}, u32[]{:S(2)}) collective-permute-start(bf16[4,48,128]{2,1,0:T(8,128)(2,1)S(1)} %get-tuple-element.52), channel_id=1, source_target_pairs={{1,0},{2,1},{3,2},{5,4},{6,5},{7,6},{9,8},{10,9},{11,10},{13,12},{... | collective-permute-start | bytes 147464 | tf_op jit(solution)/shard_map/ppermute | solution.py:617
  13.7 3.0 %collective-permute-start = (bf16[4,48,128]{2,1,0:T(8,128)(2,1)S(1)}, bf16[4,48,128]{2,1,0:T(8,128)(2,1)S(1)}, u32[]{:S(2)}, u32[]{:S(2)}) collective-permute-start(bf16[4,48,128]{2,1,0:T(8,128)(2,1)S(1)} %get-tuple-element.53), channel_id=1, source_target_pairs={{0,1},{1,2},{2,3},{4,5},{5,6},{6,7},{8,9},{9,10},{10,11},{12,13},{... | collective-permute-start | bytes 147464 | tf_op jit(solution)/shard_map/ppermute | solution.py:616
  16.8 0.7 convert_element_type.5
  17.5 0.7 fusion.flags_ref
  18.2 2.0 %collective-permute-start.8 = (bf16[256,128]{1,0:T(8,128)(2,1)}, bf16[256,128]{1,0:T(8,128)(2,1)S(1)}, u32[]{:S(2)}, u32[]{:S(2)}) collective-permute-start(bf16[256,128]{1,0:T(8,128)(2,1)} %pair_bias.1.refs_4_), channel_id=1, source_target_pairs={{0,16},{4,20},{8,24},{12,28},{16,0},{20,4},{24,8},{28,12},{1,17},{... | collective-permute-start | bytes 196616 | tf_op jit(solution)/shard_map/ppermute | solution.py:598
  20.2 2.4 %collective-permute-start.7 = (bf16[256,128]{1,0:T(8,128)(2,1)}, bf16[256,128]{1,0:T(8,128)(2,1)S(1)}, u32[]{:S(2)}, u32[]{:S(2)}) collective-permute-start(bf16[256,128]{1,0:T(8,128)(2,1)} %pair_bias.1.refs_4_), channel_id=1, source_target_pairs={{0,12},{4,8},{8,4},{12,0},{16,28},{20,24},{24,20},{28,16},{1,13},{... | collective-permute-start | bytes 196616 | tf_op jit(solution)/shard_map/ppermute | solution.py:598
  22.6 12.9 %atoms.2 = (f32[2,64,768]{2,1,0:T(8,128)}, bf16[2,64,768]{2,1,0:T(8,128)(2,1)}) custom-call(bf16[4,1280,128]{2,1,0:T(8,128)(2,1)} %feats_ref.3, bf16[4,48,128]{2,1,0:T(8,128)(2,1)} %copy-done.22, bf16[4,48,128]{2,1,0:T(8,128)(2,1)} %copy-done.21, f32[11,128]{1,0:T(8,128)} %fusion.flags_ref, s32[1,64]{1,0:T(1,128)} %counts_ref.3, bf16[64,768]{1,0:T(8,128)(2,1)} %single_ref.3, ...), custom_call_target="tpu_custom_call" | custom-call | flops 10000000000 | bytes 4000000 | tf_op jit(solution)/shard_map/atoms/pallas_call | solution.py:230
  35.6 0.8 collective-permute-start.6
  37.0 2.8 %collective-permute-start.3 = (bf16[2,64,768]{2,1,0:T(8,128)(2,1)}, bf16[2,64,768]{2,1,0:T(8,128)(2,1)S(1)}, u32[]{:S(2)}, u32[]{:S(2)}) collective-permute-start(bf16[2,64,768]{2,1,0:T(8,128)(2,1)} %get-tuple-element.30.refs_0_), channel_id=1, source_target_pairs={{0,2},{1,3},{2,0},{3,1},{4,6},{5,7},{6,4},{7,5},{8,10},{9,11},{10,... | collective-permute-start | bytes 589832 | tf_op jit(solution)/shard_map/ppermute | solution.py:598
  40.0 12.9 %atoms.3 = (f32[2,64,768]{2,1,0:T(8,128)}, bf16[2,64,768]{2,1,0:T(8,128)(2,1)}) custom-call(bf16[4,1280,128]{2,1,0:T(8,128)(2,1)} %feats_ref.3, bf16[4,48,128]{2,1,0:T(8,128)(2,1)} %copy-done.22, bf16[4,48,128]{2,1,0:T(8,128)(2,1)} %copy-done.21, f32[11,128]{1,0:T(8,128)} %fusion.flags_ref, s32[1,64]{1,0:T(1,128)} %counts_ref.3, bf16[64,768]{1,0:T(8,128)(2,1)} %single_ref.3, ...), custom_call_target="tpu_custom_call" | custom-call | flops 10000000000 | bytes 4000000 | tf_op jit(solution)/shard_map/atoms/pallas_call | solution.py:230
  52.9 1.4 %collective-permute-start.14 = (bf16[2,64,768]{2,1,0:T(8,128)(2,1)}, bf16[2,64,768]{2,1,0:T(8,128)(2,1)S(1)}, u32[]{:S(2)}, u32[]{:S(2)}) collective-permute-start(bf16[2,64,768]{2,1,0:T(8,128)(2,1)} %get-tuple-element.33.refs_0_), channel_id=1, source_target_pairs={{0,3},{1,2},{2,1},{3,0},{4,7},{5,6},{6,5},{7,4},{8,11},{9,10},{10,... | collective-permute-start | bytes 589832 | tf_op jit(solution)/shard_map/ppermute | solution.py:598
  54.3 0.7 collective-permute-start.13
  55.1 0.6 copy-done.8
  55.8 0.7 copy-done.12
  56.5 10.9 %attend.2 = (bf16[128,768]{1,0:T(8,128)(2,1)}, f32[2,8,256,128]{3,2,1,0:T(8,128)}, bf16[2,256,768]{2,1,0:T(8,128)(2,1)}) custom-call(bf16[2,64,768]{2,1,0:T(8,128)(2,1)} %get-tuple-element.30.refs_0_, bf16[2,64,768]{2,1,0:T(8,128)(2,1)} %copy-done.12, bf16[2,64,768]{2,1,0:T(8,128)(2,1)} %copy-done.10, bf16[2,64,768]{2,1,0:T(8,128)(2,1)} %copy-done.8, ...), custom_call_target="tpu_custom_call" | custom-call | flops 4000000000 | bytes 10000000 | tf_op jit(solution)/shard_map/attend/pallas_call | solution.py:364
  67.4 0.6 copy-done.9
  68.1 0.7 copy-done.13
  68.8 11.0 %attend.3 = (bf16[128,768]{1,0:T(8,128)(2,1)}, f32[2,8,256,128]{3,2,1,0:T(8,128)}, bf16[2,256,768]{2,1,0:T(8,128)(2,1)}) custom-call(bf16[2,64,768]{2,1,0:T(8,128)(2,1)} %get-tuple-element.33.refs_0_, bf16[2,64,768]{2,1,0:T(8,128)(2,1)} %copy-done.13, bf16[2,64,768]{2,1,0:T(8,128)(2,1)} %copy-done.11, bf16[2,64,768]{2,1,0:T(8,128)(2,1)} %copy-done.9, ...), custom_call_target="tpu_custom_call" | custom-call | flops 4000000000 | bytes 10000000 | tf_op jit(solution)/shard_map/attend/pallas_call | solution.py:364
  79.8 13.2 %tokens.1 = (f32[256,768]{1,0:T(8,128)}, bf16[256,1536]{1,0:T(8,128)(2,1)}, bf16[256,128]{1,0:T(8,128)(2,1)}, bf16[256,128]{1,0:T(8,128)(2,1)}, bf16[256,128]{1,...) custom-call(f32[2,64,768]{2,1,0:T(8,128)} %get-tuple-element.28.refs, ...), custom_call_target="tpu_custom_call" | custom-call | flops 8000000000 | bytes 20000000 | tf_op jit(solution)/shard_map/tokens/pallas_call | solution.py:485
  92.9 3.2 %collective-permute-start.15 = (bf16[256,128]{1,0:T(8,128)(2,1)}, bf16[256,128]{1,0:T(8,128)(2,1)S(1)}, u32[]{:S(2)}, u32[]{:S(2)}) collective-permute-start(bf16[256,128]{1,0:T(8,128)(2,1)} %get-tuple-element.43), channel_id=1, source_target_pairs={{0,28},{4,24},{8,20},{12,16},{16,12},{20,8},{24,4},{28,0},{1,29},{... | collective-permute-start | bytes 196616 | tf_op jit(solution)/shard_map/ppermute | solution.py:598
  96.2 1.1 collective-permute-start.16
  97.6 3.0 %collective-permute-start.18 = (bf16[256,128]{1,0:T(8,128)(2,1)}, bf16[256,128]{1,0:T(8,128)(2,1)S(1)}, u32[]{:S(2)}, u32[]{:S(2)}) collective-permute-start(bf16[256,128]{1,0:T(8,128)(2,1)} %get-tuple-element.46), channel_id=1, source_target_pairs={{0,16},{4,20},{8,24},{12,28},{16,0},{20,4},{24,8},{28,12},{1,17},{... | collective-permute-start | bytes 196616 | tf_op jit(solution)/shard_map/ppermute | solution.py:598
  100.6 0.8 collective-permute-start.19
  101.5 3.3 %collective-permute-start.20 = (bf16[256,128]{1,0:T(8,128)(2,1)}, bf16[256,128]{1,0:T(8,128)(2,1)S(1)}, u32[]{:S(2)}, u32[]{:S(2)}) collective-permute-start(bf16[256,128]{1,0:T(8,128)(2,1)} %get-tuple-element.48), channel_id=1, source_target_pairs={{0,8},{4,12},{8,0},{12,4},{16,24},{20,28},{24,16},{28,20},{1,9},{5... | collective-permute-start | bytes 196616 | tf_op jit(solution)/shard_map/ppermute | solution.py:598
  104.7 2.2 %collective-permute-start.21 = (bf16[256,128]{1,0:T(8,128)(2,1)}, bf16[256,128]{1,0:T(8,128)(2,1)S(1)}, u32[]{:S(2)}, u32[]{:S(2)}) collective-permute-start(bf16[256,128]{1,0:T(8,128)(2,1)} %get-tuple-element.49), channel_id=1, source_target_pairs={{0,4},{4,0},{8,12},{12,8},{16,20},{20,16},{24,28},{28,24},{1,5},{5... | collective-permute-start | bytes 196616 | tf_op jit(solution)/shard_map/ppermute | solution.py:598
  106.9 6.4 %output.1 = (bf16[256,768]{1,0:T(8,128)(2,1)}, f32[2048,128]{1,0:T(8,128)}, f32[2048,128]{1,0:T(8,128)}) custom-call(f32[256,768]{1,0:T(8,128)} %get-tuple-element.39.resid_ref, bf16[256,1536]{1,0:T(8,128)(2,1)} %get-tuple-element.40.hidden_ref, bf16[1536,768]{1,0:T(8,128)(2,1)} %w_down_ref.1, bf16[64,32,128]{2,1,0:T(8,128)(2,1)} %pair_ref.3), custom_call_target="tpu_custom_call" | custom-call | flops 1000000000 | bytes 8000000 | tf_op jit(solution)/shard_map/output/pallas_call | solution.py:538
  113.4 0.5 copy-done.2
  114.1 4.2 %pair_grad.1 = f32[2048,128]{1,0:T(8,128)} custom-call(bf16[256,128]{1,0:T(8,128)(2,1)} %get-tuple-element.42.refs_0_, bf16[256,128]{1,0:T(8,128)(2,1)} %copy-done, bf16[256,128]{1,0:T(8,128)(2,1)} %copy-done.1, bf16[256,128]{1,0:T(8,128)(2,1)} %copy-done.2, bf16[256,128]{1,0:T(8,128)(2,1)} %copy-done.3, bf16[256,128]{1,0:T(8,128)(2,1)} %copy-done.4, ...), custom_call_target="tpu_custom_call" | custom-call | flops 100000000 | bytes 4000000 | tf_op jit(solution)/shard_map/pair_grad/pallas_call | solution.py:586
  (69 shorter events, 1.8 us)
Async XLA Ops:
  4.6 30.9 %collective-permute-start.11 = (bf16[256,128]{1,0:T(8,128)(2,1)}, bf16[256,128]{1,0:T(8,128)(2,1)S(1)}, u32[]{:S(2)}, u32[]{:S(2)}) collective-permute-start(bf16[256,128]{1,0:T(8,128)(2,1)} %pair_bias.1.refs_4_), channel_id=1, source_target_pairs={{0,28},{4,24},{8,20},{12,16},{16,12},{20,8},{24,4},{28,0},{1,29},{... | collective-permute-start | bytes 196616 | tf_op jit(solution)/shard_map/ppermute | solution.py:598
  10.6 25.7 %collective-permute-start.10 = (bf16[256,128]{1,0:T(8,128)(2,1)}, bf16[256,128]{1,0:T(8,128)(2,1)S(1)}, u32[]{:S(2)}, u32[]{:S(2)}) collective-permute-start(bf16[256,128]{1,0:T(8,128)(2,1)} %pair_bias.1.refs_4_), channel_id=1, source_target_pairs={{0,24},{4,28},{8,16},{12,20},{16,8},{20,12},{24,0},{28,4},{1,25},{... | collective-permute-start | bytes 196616 | tf_op jit(solution)/shard_map/ppermute | solution.py:598
  10.9 25.8 %collective-permute-start.9 = (bf16[256,128]{1,0:T(8,128)(2,1)}, bf16[256,128]{1,0:T(8,128)(2,1)S(1)}, u32[]{:S(2)}, u32[]{:S(2)}) collective-permute-start(bf16[256,128]{1,0:T(8,128)(2,1)} %pair_bias.1.refs_4_), channel_id=1, source_target_pairs={{0,20},{4,16},{8,28},{12,24},{16,4},{20,0},{24,12},{28,8},{1,21},{... | collective-permute-start | bytes 196616 | tf_op jit(solution)/shard_map/ppermute | solution.py:598
  12.4 5.7 %collective-permute-start.1 = (bf16[4,48,128]{2,1,0:T(8,128)(2,1)S(1)}, bf16[4,48,128]{2,1,0:T(8,128)(2,1)S(1)}, u32[]{:S(2)}, u32[]{:S(2)}) collective-permute-start(bf16[4,48,128]{2,1,0:T(8,128)(2,1)S(1)} %get-tuple-element.52), channel_id=1, source_target_pairs={{1,0},{2,1},{3,2},{5,4},{6,5},{7,6},{9,8},{10,9},{11,10},{13,12},{... | collective-permute-start | bytes 147464 | tf_op jit(solution)/shard_map/ppermute | solution.py:617
  13.7 6.4 %collective-permute-start = (bf16[4,48,128]{2,1,0:T(8,128)(2,1)S(1)}, bf16[4,48,128]{2,1,0:T(8,128)(2,1)S(1)}, u32[]{:S(2)}, u32[]{:S(2)}) collective-permute-start(bf16[4,48,128]{2,1,0:T(8,128)(2,1)S(1)} %get-tuple-element.53), channel_id=1, source_target_pairs={{0,1},{1,2},{2,3},{4,5},{5,6},{6,7},{8,9},{9,10},{10,11},{12,13},{... | collective-permute-start | bytes 147464 | tf_op jit(solution)/shard_map/ppermute | solution.py:616
  18.2 17.4 %copy-start.7 = (bf16[256,128]{1,0:T(8,128)(2,1)S(1)}, bf16[256,128]{1,0:T(8,128)(2,1)}, u32[]{:S(2)}) copy-start(bf16[256,128]{1,0:T(8,128)(2,1)} %pair_bias.1.refs_4_) | copy-start | bytes 196612
  18.2 4.4 %copy-start.21 = (bf16[4,48,128]{2,1,0:T(8,128)(2,1)}, bf16[4,48,128]{2,1,0:T(8,128)(2,1)S(1)}, u32[]{:S(2)}) copy-start(bf16[4,48,128]{2,1,0:T(8,128)(2,1)S(1)} %collective-permute-done.1.right_ref) | copy-start | bytes 147460
  18.2 18.8 %collective-permute-start.8 = (bf16[256,128]{1,0:T(8,128)(2,1)}, bf16[256,128]{1,0:T(8,128)(2,1)S(1)}, u32[]{:S(2)}, u32[]{:S(2)}) collective-permute-start(bf16[256,128]{1,0:T(8,128)(2,1)} %pair_bias.1.refs_4_), channel_id=1, source_target_pairs={{0,16},{4,20},{8,24},{12,28},{16,0},{20,4},{24,8},{28,12},{1,17},{... | collective-permute-start | bytes 196616 | tf_op jit(solution)/shard_map/ppermute | solution.py:598
  20.2 2.5 %copy-start.22 = (bf16[4,48,128]{2,1,0:T(8,128)(2,1)}, bf16[4,48,128]{2,1,0:T(8,128)(2,1)S(1)}, u32[]{:S(2)}) copy-start(bf16[4,48,128]{2,1,0:T(8,128)(2,1)S(1)} %collective-permute-done.left_ref) | copy-start | bytes 147460
  20.2 19.7 %collective-permute-start.7 = (bf16[256,128]{1,0:T(8,128)(2,1)}, bf16[256,128]{1,0:T(8,128)(2,1)S(1)}, u32[]{:S(2)}, u32[]{:S(2)}) collective-permute-start(bf16[256,128]{1,0:T(8,128)(2,1)} %pair_bias.1.refs_4_), channel_id=1, source_target_pairs={{0,12},{4,8},{8,4},{12,0},{16,28},{20,24},{24,20},{28,16},{1,13},{... | collective-permute-start | bytes 196616 | tf_op jit(solution)/shard_map/ppermute | solution.py:598
  35.5 17.3 %copy-start.14 = (bf16[256,128]{1,0:T(8,128)(2,1)}, bf16[256,128]{1,0:T(8,128)(2,1)S(1)}, u32[]{:S(2)}) copy-start(bf16[256,128]{1,0:T(8,128)(2,1)S(1)} %collective-permute-done.11.refs_11_) | copy-start | bytes 196612
  35.6 17.4 %collective-permute-start.6 = (bf16[256,128]{1,0:T(8,128)(2,1)S(1)}, bf16[256,128]{1,0:T(8,128)(2,1)S(1)}, u32[]{:S(2)}, u32[]{:S(2)}) collective-permute-start(bf16[256,128]{1,0:T(8,128)(2,1)S(1)} %copy-done.7), channel_id=1, source_target_pairs={{0,8},{4,12},{8,0},{12,4},{16,24},{20,28},{24,16},{28,20},{1,9},{5... | collective-permute-start | bytes 196616 | tf_op jit(solution)/shard_map/ppermute | solution.py:598
  36.3 16.6 %copy-start.15 = (bf16[256,128]{1,0:T(8,128)(2,1)}, bf16[256,128]{1,0:T(8,128)(2,1)S(1)}, u32[]{:S(2)}) copy-start(bf16[256,128]{1,0:T(8,128)(2,1)S(1)} %collective-permute-done.10.refs_10_) | copy-start | bytes 196612
  36.3 18.0 %collective-permute-start.5 = (bf16[256,128]{1,0:T(8,128)(2,1)S(1)}, bf16[256,128]{1,0:T(8,128)(2,1)S(1)}, u32[]{:S(2)}, u32[]{:S(2)}) collective-permute-start(bf16[256,128]{1,0:T(8,128)(2,1)S(1)} %copy-done.7), channel_id=1, source_target_pairs={{0,4},{4,0},{8,12},{12,8},{16,20},{20,16},{24,28},{28,24},{1,5},{5... | collective-permute-start | bytes 196616 | tf_op jit(solution)/shard_map/ppermute | solution.py:598
  36.7 16.2 %copy-start.16 = (bf16[256,128]{1,0:T(8,128)(2,1)}, bf16[256,128]{1,0:T(8,128)(2,1)S(1)}, u32[]{:S(2)}) copy-start(bf16[256,128]{1,0:T(8,128)(2,1)S(1)} %collective-permute-done.9.refs_9_) | copy-start | bytes 196612
  36.7 18.3 %collective-permute-start.4 = (bf16[2,64,768]{2,1,0:T(8,128)(2,1)}, bf16[2,64,768]{2,1,0:T(8,128)(2,1)S(1)}, u32[]{:S(2)}, u32[]{:S(2)}) collective-permute-start(bf16[2,64,768]{2,1,0:T(8,128)(2,1)} %get-tuple-element.30.refs_0_), channel_id=1, source_target_pairs={{0,3},{1,2},{2,1},{3,0},{4,7},{5,6},{6,5},{7,4},{8,11},{9,10},{10,... | collective-permute-start | bytes 589832 | tf_op jit(solution)/shard_map/ppermute | solution.py:598
  37.0 15.9 %copy-start.17 = (bf16[256,128]{1,0:T(8,128)(2,1)}, bf16[256,128]{1,0:T(8,128)(2,1)S(1)}, u32[]{:S(2)}) copy-start(bf16[256,128]{1,0:T(8,128)(2,1)S(1)} %collective-permute-done.8.refs_8_) | copy-start | bytes 196612
  37.0 18.0 %collective-permute-start.3 = (bf16[2,64,768]{2,1,0:T(8,128)(2,1)}, bf16[2,64,768]{2,1,0:T(8,128)(2,1)S(1)}, u32[]{:S(2)}, u32[]{:S(2)}) collective-permute-start(bf16[2,64,768]{2,1,0:T(8,128)(2,1)} %get-tuple-element.30.refs_0_), channel_id=1, source_target_pairs={{0,2},{1,3},{2,0},{3,1},{4,6},{5,7},{6,4},{7,5},{8,10},{9,11},{10,... | collective-permute-start | bytes 589832 | tf_op jit(solution)/shard_map/ppermute | solution.py:598
  39.9 13.1 %copy-start.18 = (bf16[256,128]{1,0:T(8,128)(2,1)}, bf16[256,128]{1,0:T(8,128)(2,1)S(1)}, u32[]{:S(2)}) copy-start(bf16[256,128]{1,0:T(8,128)(2,1)S(1)} %collective-permute-done.7.refs_7_) | copy-start | bytes 196612
  39.9 15.2 %collective-permute-start.2 = (bf16[2,64,768]{2,1,0:T(8,128)(2,1)}, bf16[2,64,768]{2,1,0:T(8,128)(2,1)S(1)}, u32[]{:S(2)}, u32[]{:S(2)}) collective-permute-start(bf16[2,64,768]{2,1,0:T(8,128)(2,1)} %get-tuple-element.30.refs_0_), channel_id=1, source_target_pairs={{0,1},{1,0},{2,3},{3,2},{4,5},{5,4},{6,7},{7,6},{8,9},{9,8},{10,11... | collective-permute-start | bytes 589832 | tf_op jit(solution)/shard_map/ppermute | solution.py:598
  52.9 14.4 %collective-permute-start.14 = (bf16[2,64,768]{2,1,0:T(8,128)(2,1)}, bf16[2,64,768]{2,1,0:T(8,128)(2,1)S(1)}, u32[]{:S(2)}, u32[]{:S(2)}) collective-permute-start(bf16[2,64,768]{2,1,0:T(8,128)(2,1)} %get-tuple-element.33.refs_0_), channel_id=1, source_target_pairs={{0,3},{1,2},{2,1},{3,0},{4,7},{5,6},{6,5},{7,4},{8,11},{9,10},{10,... | collective-permute-start | bytes 589832 | tf_op jit(solution)/shard_map/ppermute | solution.py:598
  54.3 13.1 %collective-permute-start.13 = (bf16[2,64,768]{2,1,0:T(8,128)(2,1)}, bf16[2,64,768]{2,1,0:T(8,128)(2,1)S(1)}, u32[]{:S(2)}, u32[]{:S(2)}) collective-permute-start(bf16[2,64,768]{2,1,0:T(8,128)(2,1)} %get-tuple-element.33.refs_0_), channel_id=1, source_target_pairs={{0,2},{1,3},{2,0},{3,1},{4,6},{5,7},{6,4},{7,5},{8,10},{9,11},{10,... | collective-permute-start | bytes 589832 | tf_op jit(solution)/shard_map/ppermute | solution.py:598
  55.0 12.3 %collective-permute-start.12 = (bf16[2,64,768]{2,1,0:T(8,128)(2,1)}, bf16[2,64,768]{2,1,0:T(8,128)(2,1)S(1)}, u32[]{:S(2)}, u32[]{:S(2)}) collective-permute-start(bf16[2,64,768]{2,1,0:T(8,128)(2,1)} %get-tuple-element.33.refs_0_), channel_id=1, source_target_pairs={{0,1},{1,0},{2,3},{3,2},{4,5},{5,4},{6,7},{7,6},{8,9},{9,8},{10,11... | collective-permute-start | bytes 589832 | tf_op jit(solution)/shard_map/ppermute | solution.py:598
  92.9 8.5 %collective-permute-start.15 = (bf16[256,128]{1,0:T(8,128)(2,1)}, bf16[256,128]{1,0:T(8,128)(2,1)S(1)}, u32[]{:S(2)}, u32[]{:S(2)}) collective-permute-start(bf16[256,128]{1,0:T(8,128)(2,1)} %get-tuple-element.43), channel_id=1, source_target_pairs={{0,28},{4,24},{8,20},{12,16},{16,12},{20,8},{24,4},{28,0},{1,29},{... | collective-permute-start | bytes 196616 | tf_op jit(solution)/shard_map/ppermute | solution.py:598
  96.2 8.6 %collective-permute-start.16 = (bf16[256,128]{1,0:T(8,128)(2,1)}, bf16[256,128]{1,0:T(8,128)(2,1)S(1)}, u32[]{:S(2)}, u32[]{:S(2)}) collective-permute-start(bf16[256,128]{1,0:T(8,128)(2,1)} %get-tuple-element.44), channel_id=1, source_target_pairs={{0,24},{4,28},{8,16},{12,20},{16,8},{20,12},{24,0},{28,4},{1,25},{... | collective-permute-start | bytes 196616 | tf_op jit(solution)/shard_map/ppermute | solution.py:598
  97.2 16.1 %collective-permute-start.17 = (bf16[256,128]{1,0:T(8,128)(2,1)}, bf16[256,128]{1,0:T(8,128)(2,1)S(1)}, u32[]{:S(2)}, u32[]{:S(2)}) collective-permute-start(bf16[256,128]{1,0:T(8,128)(2,1)} %get-tuple-element.45), channel_id=1, source_target_pairs={{0,20},{4,16},{8,28},{12,24},{16,4},{20,0},{24,12},{28,8},{1,21},{... | collective-permute-start | bytes 196616 | tf_op jit(solution)/shard_map/ppermute | solution.py:598
  97.6 15.8 %collective-permute-start.18 = (bf16[256,128]{1,0:T(8,128)(2,1)}, bf16[256,128]{1,0:T(8,128)(2,1)S(1)}, u32[]{:S(2)}, u32[]{:S(2)}) collective-permute-start(bf16[256,128]{1,0:T(8,128)(2,1)} %get-tuple-element.46), channel_id=1, source_target_pairs={{0,16},{4,20},{8,24},{12,28},{16,0},{20,4},{24,8},{28,12},{1,17},{... | collective-permute-start | bytes 196616 | tf_op jit(solution)/shard_map/ppermute | solution.py:598
  100.6 12.7 %collective-permute-start.19 = (bf16[256,128]{1,0:T(8,128)(2,1)}, bf16[256,128]{1,0:T(8,128)(2,1)S(1)}, u32[]{:S(2)}, u32[]{:S(2)}) collective-permute-start(bf16[256,128]{1,0:T(8,128)(2,1)} %get-tuple-element.47), channel_id=1, source_target_pairs={{0,12},{4,8},{8,4},{12,0},{16,28},{20,24},{24,20},{28,16},{1,13},{... | collective-permute-start | bytes 196616 | tf_op jit(solution)/shard_map/ppermute | solution.py:598
  101.5 11.9 %copy-start = (bf16[256,128]{1,0:T(8,128)(2,1)}, bf16[256,128]{1,0:T(8,128)(2,1)S(1)}, u32[]{:S(2)}) copy-start(bf16[256,128]{1,0:T(8,128)(2,1)S(1)} %collective-permute-done.15.refs_1_) | copy-start | bytes 196612
  101.5 11.9 %collective-permute-start.20 = (bf16[256,128]{1,0:T(8,128)(2,1)}, bf16[256,128]{1,0:T(8,128)(2,1)S(1)}, u32[]{:S(2)}, u32[]{:S(2)}) collective-permute-start(bf16[256,128]{1,0:T(8,128)(2,1)} %get-tuple-element.48), channel_id=1, source_target_pairs={{0,8},{4,12},{8,0},{12,4},{16,24},{20,28},{24,16},{28,20},{1,9},{5... | collective-permute-start | bytes 196616 | tf_op jit(solution)/shard_map/ppermute | solution.py:598
  104.7 8.6 %copy-start.1 = (bf16[256,128]{1,0:T(8,128)(2,1)}, bf16[256,128]{1,0:T(8,128)(2,1)S(1)}, u32[]{:S(2)}) copy-start(bf16[256,128]{1,0:T(8,128)(2,1)S(1)} %collective-permute-done.16.refs_2_) | copy-start | bytes 196612
  104.7 8.7 %collective-permute-start.21 = (bf16[256,128]{1,0:T(8,128)(2,1)}, bf16[256,128]{1,0:T(8,128)(2,1)S(1)}, u32[]{:S(2)}, u32[]{:S(2)}) collective-permute-start(bf16[256,128]{1,0:T(8,128)(2,1)} %get-tuple-element.49), channel_id=1, source_target_pairs={{0,4},{4,0},{8,12},{12,8},{16,20},{20,16},{24,28},{28,24},{1,5},{5... | collective-permute-start | bytes 196616 | tf_op jit(solution)/shard_map/ppermute | solution.py:598
  (13 other events, 10.2 us)

commit v3 on v2

--- a/solution.py
+++ b/solution.py
@@ -67,7 +67,7 @@
         scaled_ref[pl.ds(pl.multiple_of(i * 8 * keys, 8 * keys), 8 * keys), :] = hat * gain
         return carry
 
-    lax.fori_loop(0, rows // 8, norm_step, 0)
+    lax.fori_loop(0, rows // 8, norm_step, 0, unroll=True)
     weights = jnp.concatenate(split_heads(w_bias_ref[...]), axis=1).astype(bf16)
     blank = jnp.zeros((rows, CZ), bf16)
     for j in range(keys):
@@ -77,14 +77,15 @@
             axis=0,
         )
         stage_ref[pl.ds(j * PAIRS, PAIRS), :] = nt(weights, both)
-    out_ref[...] = stage_ref[...].astype(bf16)
-
-
-def pair_bias(pair, pair_gain, w_bias_t):
+    for k in range(out_ref.shape[0]):
+        out_ref[k] = stage_ref[...].astype(bf16)
+
+
+def pair_bias(pair, pair_gain, w_bias_t, copies):
     rows, keys = pair.shape[0], pair.shape[1]
     return pl.pallas_call(
         bias_kernel,
-        out_shape=jax.ShapeDtypeStruct((keys * PAIRS, 2 * rows), bf16),
+        out_shape=jax.ShapeDtypeStruct((copies, keys * PAIRS, 2 * rows), bf16),
         scratch_shapes=[
             pltpu.VMEM((rows * keys, CZ), f32),
             pltpu.VMEM((keys * PAIRS, 2 * rows), f32),
@@ -278,82 +279,96 @@
     return jnp.concatenate([jnp.where(mask, block, blank) for mask in masks], axis=0)
 
 
-def attend_kernel(
-    *refs, count, groups,
-):
-    piece_refs, bias_refs = refs[:count], refs[count : count + groups]
-    w_qkv_hbm, att_ref, probs_ref, values_ref = refs[count + groups : count + groups + 4]
-    w_qkv_ref, sems, all_ref, qk_ref, biasf_ref = refs[count + groups + 4 :]
+def project(piece_refs, w_qkv_ref, copies, all_ref, queries_ref, keys_ref, values_ref):
     batch, tok_rows = piece_refs[0].shape[0], piece_refs[0].shape[1]
-    keys_all = tok_rows * count
-    copies = [
-        pltpu.make_async_copy(
-            w_qkv_hbm.at[:, pl.ds(C_TOK * i, C_TOK)], w_qkv_ref.at[i], sems.at[i]
-        )
-        for i in range(3)
-    ]
-    for copy in copies:
-        copy.start()
     here = lax.axis_index("tok")
     for k, piece in enumerate(piece_refs):
         at = pl.multiple_of((here ^ k) * tok_rows, tok_rows)
         for s in range(batch):
             all_ref[s, pl.ds(at, tok_rows), :] = piece[s]
-    here = lax.axis_index("samp")
-    for k, piece in enumerate(bias_refs):
-        size = piece.shape[0]
-        biasf_ref[pl.ds(pl.multiple_of((here ^ k) * size, size), size), :] = piece[...].astype(f32)
+    own = piece_refs[0][...].reshape(batch * tok_rows, C_TOK)
     copies[0].wait()
-    own = piece_refs[0][...].reshape(batch * tok_rows, C_TOK)
-    queries_ref = att_ref
-    for n in range(3):
-        queries_ref[:, 256 * n : 256 * n + 256] = nn(
-            own, w_qkv_ref[0, :, 256 * n : 256 * n + 256]
-        ).astype(bf16)
-    copies[1].wait()
-    copies[2].wait()
-
-    def project_step(n, carry):
-        at = pl.multiple_of(n * 256, 256)
-        for s in range(batch):
-            qk_ref[s, :, pl.ds(at, 256)] = nn(
-                all_ref[s], w_qkv_ref[1, :, pl.ds(at, 256)]
-            ).astype(bf16)
-            values_ref[s, :, pl.ds(at, 256)] = nn(
-                all_ref[s], w_qkv_ref[2, :, pl.ds(at, 256)]
-            ).astype(bf16)
-        return carry
-
-    lax.fori_loop(0, C_TOK // 256, project_step, 0)
+    for n in range(0, C_TOK, 256):
+        queries_ref[:, n : n + 256] = nn(own, w_qkv_ref[0, :, n : n + 256]).astype(bf16)
+    for which, to_ref in ((1, keys_ref), (2, values_ref)):
+        copies[which].wait()
+        for n in range(0, C_TOK, 256):
+            for s in range(batch):
+                to_ref[s, :, n : n + 256] = nn(
+                    all_ref[s], w_qkv_ref[which, :, n : n + 256]
+                ).astype(bf16)
+
+
+def windows(pair):
+    low, high = WINDOWS[pair % 4]
+    return 384 * (pair // 4) + low, 384 * (pair // 4) + high
+
+
+def attend(bias_ref, queries_ref, keys_ref, values_ref, probs_ref, att_ref):
+    batch, keys_all = keys_ref.shape[0], keys_ref.shape[1]
+    tok_rows = queries_ref.shape[0] // batch
     masks = head_masks(tok_rows)
     factor = HD ** (-0.5)
 
-    def attend_step(s, carry):
+    def sample_step(s, carry):
         at = pl.multiple_of(s * tok_rows, 64)
-        for half in range(2):
-            lanes = [jnp.zeros((tok_rows, 128), f32) for _ in range(3)]
-            for sub in range(4):
-                pair = half * 4 + sub
-                low, high = (384 * half + v for v in WINDOWS[sub])
-                queries = two_heads(queries_ref[pl.ds(at, tok_rows), low:high], masks[sub])
-                scores = nt(qk_ref[s, :, low:high], queries) * factor
-                scores = scores + biasf_ref[pl.ds(pair, keys_all, stride=PAIRS), :]
-                expo = jnp.exp(scores - jnp.max(scores, axis=0, keepdims=True))
-                probs = expo * (1.0 / jnp.sum(expo, axis=0, keepdims=True))
-                probs_ref[s, pair] = probs
-                part = tn(probs.astype(bf16), values_ref[s, :, low:high])
-                first, second = masks[sub]
-                mix = jnp.where(first, part[0:tok_rows], 0.0)
-                mix = jnp.where(second, part[tok_rows : 2 * tok_rows], mix)
-                for t in range((high - low) // 128):
-                    tile = WINDOWS[sub][0] // 128 + t
-                    lanes[tile] = lanes[tile] + mix[:, 128 * t : 128 * t + 128]
-            att_ref[pl.ds(at, tok_rows), 384 * half : 384 * half + 384] = jnp.concatenate(
-                lanes, axis=1
-            ).astype(bf16)
+        for pair in range(PAIRS):
+            low, high = windows(pair)
+            queries = two_heads(queries_ref[pl.ds(at, tok_rows), low:high], masks[pair % 4])
+            probs_ref[s, pair] = nt(keys_ref[s, :, low:high], queries)
+        for pair in range(PAIRS):
+            scores = probs_ref[s, pair] * factor
+            scores = scores + bias_ref[pl.ds(pair, keys_all, stride=PAIRS), :]
+            expo = jnp.exp(scores - jnp.max(scores, axis=0, keepdims=True))
+            probs_ref[s, pair] = expo * (1.0 / jnp.sum(expo, axis=0, keepdims=True))
+        lanes = [jnp.zeros((tok_rows, 128), f32) for _ in range(C_TOK // 128)]
+        for pair in range(PAIRS):
+            low, high = windows(pair)
+            part = tn(probs_ref[s, pair].astype(bf16), values_ref[s, :, low:high])
+            first, second = masks[pair % 4]
+            mix = jnp.where(first, part[0:tok_rows], 0.0)
+            mix = jnp.where(second, part[tok_rows : 2 * tok_rows], mix)
+            for t in range((high - low) // 128):
+                lanes[low // 128 + t] = lanes[low // 128 + t] + mix[:, 128 * t : 128 * t + 128]
+        for t in range(C_TOK // 128):
+            att_ref[pl.ds(at, tok_rows), 128 * t : 128 * t + 128] = lanes[t].astype(bf16)
         return carry
 
-    lax.fori_loop(0, batch, attend_step, 0)
+    lax.fori_loop(0, batch, sample_step, 0)
+
+
+def start_all(moves, sems):
+    copies = [pltpu.make_async_copy(src, dst, sems.at[i]) for i, (src, dst) in enumerate(moves)]
+    for copy in copies:
+        copy.start()
+    return copies
+
+
+def qkv_moves(w_qkv_hbm, w_qkv_ref):
+    return [
+        (w_qkv_hbm.at[:, pl.ds(C_TOK * i, C_TOK)], w_qkv_ref.at[i]) for i in range(3)
+    ]
+
+
+def attend_kernel(*refs, count):
+    piece_refs = refs[:count]
+    (
+        bias_ref, w_qkv_hbm, att_ref, probs_ref, values_ref, w_qkv_ref, sems, all_ref, queries_ref,
+        keys_ref, biasf_ref,
+    ) = refs[count:]
+    copies = start_all(qkv_moves(w_qkv_hbm, w_qkv_ref), sems)
+    biasf_ref[...] = bias_ref[...].astype(f32)
+    project(piece_refs, w_qkv_ref, copies, all_ref, queries_ref, keys_ref, values_ref)
+    attend(biasf_ref, queries_ref, keys_ref, values_ref, probs_ref, att_ref)
+
+
+def attend_scratch(batch, tok_rows, keys_all):
+    return [
+        pltpu.VMEM((batch, keys_all, C_TOK), bf16),
+        pltpu.VMEM((batch * tok_rows, C_TOK), bf16),
+        pltpu.VMEM((batch, keys_all, C_TOK), bf16),
+        pltpu.VMEM((keys_all * PAIRS, 2 * tok_rows), f32),
+    ]
 
 
 def attend_stage(pieces, bias, w_qkv):
@@ -362,8 +377,8 @@
     vmem = pl.BlockSpec(memory_space=pltpu.VMEM)
     hbm = pl.BlockSpec(memory_space=pl.ANY)
     return pl.pallas_call(
-        functools.partial(attend_kernel, count=len(pieces), groups=len(bias)),
-        in_specs=[vmem] * (len(pieces) + len(bias)) + [hbm],
+        functools.partial(attend_kernel, count=len(pieces)),
+        in_specs=[vmem] * (len(pieces) + 1) + [hbm],
         out_specs=[vmem] * 3,
         out_shape=[
             jax.ShapeDtypeStruct((batch * tok_rows, C_TOK), bf16),
@@ -373,144 +388,148 @@
         scratch_shapes=[
             pltpu.VMEM((3, C_TOK, C_TOK), bf16),
             pltpu.SemaphoreType.DMA((3,)),
-            pltpu.VMEM((batch, keys_all, C_TOK), bf16),
-            pltpu.VMEM((batch, keys_all, C_TOK), bf16),
-            pltpu.VMEM((keys_all * PAIRS, 2 * tok_rows), f32),
-        ],
+        ]
+        + attend_scratch(batch, tok_rows, keys_all),
         compiler_params=pltpu.CompilerParams(vmem_limit_bytes=GRANT),
         cost_estimate=pl.CostEstimate(
             flops=4 * 10**9, bytes_accessed=10**7, transcendentals=10**6
         ),
         name="attend",
-    )(*pieces, *bias, w_qkv)
-
-
-def token_kernel(*refs, halves, groups):
-    tokens_refs, att_refs = refs[0:halves], refs[halves : 2 * halves]
-    probs_hbm, values_hbm = refs[2 * halves : 3 * halves], refs[3 * halves : 4 * halves]
-    cot_ref, w_out_hbm, w_gate_hbm, w_up_hbm, w_down_hbm = refs[4 * halves : 4 * halves + 5]
-    resid_ref, hidden_ref = refs[4 * halves + 5 : 4 * halves + 7]
-    block_refs = refs[4 * halves + 7 : 4 * halves + 7 + groups]
+    )(*pieces, bias, w_qkv)
+
+
+def token_kernel(*refs, count):
+    piece_refs = refs[:count]
     (
-        w_out_ref, w_gate_ref, w_up_ref, w_down_ref, probs_ref, values_ref, sems, grads_ref,
-        d_gate_ref, d_up_ref, hat_ref, d_bias_f_ref,
-    ) = refs[4 * halves + 7 + groups :]
+        bias_ref, tokens_a_ref, tokens_b_ref, att_a_ref, cot_ref, probs_a_hbm, values_a_hbm,
+        w_qkv_hbm, w_out_hbm, w_gate_hbm, w_up_hbm, w_down_hbm,
+        resid_ref, hidden_ref, d_bias_ref,
+        w_qkv_ref, w_out_ref, w_gate_ref, w_up_ref, w_down_ref, probs_ref, values_ref, sems,
+        all_ref, queries_ref, keys_ref, biasf_ref, grads_ref, d_gate_ref, d_up_ref, hat_ref,
+    ) = refs[count:]
     batch, tok_rows = cot_ref.shape[0], cot_ref.shape[1]
     keys_all = values_ref.shape[1]
     rows = batch * tok_rows
-    each = batch // halves
-    moves = [
-        (w_out_hbm, w_out_ref), (w_gate_hbm, w_gate_ref), (w_up_hbm, w_up_ref),
-        (w_down_hbm, w_down_ref),
-    ]
-    for i in range(halves):
-        moves.append((values_hbm[i], values_ref.at[pl.ds(i * each, each)]))
-        moves.append((probs_hbm[i], probs_ref.at[pl.ds(i * each, each)]))
-    copies = [pltpu.make_async_copy(s, d, sems.at[i]) for i, (s, d) in enumerate(moves)]
-    for copy in copies:
-        copy.start()
-    cot = cot_ref[...].reshape(rows, C_TOK)
-    copies[0].wait()
-    for i in range(halves):
-        part = slice(i * each * tok_rows, (i + 1) * each * tok_rows)
-        resid_ref[part, :] = tokens_refs[i][...].reshape(each * tok_rows, C_TOK) + nn(
-            att_refs[i][...], w_out_ref[...]
-        )
+    ahead = values_a_hbm.shape[0]
+    lead = ahead * tok_rows
+    copies = start_all(
+        qkv_moves(w_qkv_hbm, w_qkv_ref)
+        + [
+            (w_out_hbm, w_out_ref), (w_down_hbm, w_down_ref), (w_gate_hbm, w_gate_ref),
+            (w_up_hbm, w_up_ref), (values_a_hbm, values_ref.at[pl.ds(0, ahead)]),
+            (probs_a_hbm, probs_ref.at[pl.ds(0, ahead)]),
+        ],
+        sems,
+    )
+    biasf_ref[...] = bias_ref[...].astype(f32)
+    own_values = values_ref.at[pl.ds(ahead, batch - ahead)]
+    own_probs = probs_ref.at[pl.ds(ahead, batch - ahead)]
+    project(piece_refs, w_qkv_ref, copies, all_ref, queries_ref, keys_ref, own_values)
+    attend(biasf_ref, queries_ref, keys_ref, own_values, own_probs, queries_ref)
+
+    copies[3].wait()
+    resid_ref[0:lead, :] = tokens_a_ref[...].reshape(lead, C_TOK) + nn(
+        att_a_ref[...], w_out_ref[...]
+    )
+    resid_ref[lead:rows, :] = tokens_b_ref[...].reshape(rows - lead, C_TOK) + nn(
+        queries_ref[...], w_out_ref[...]
+    )
     hat, rstd = norm_rows(resid_ref[...])
     hat_ref[...] = hat
     grads_ref[...] = hat.astype(bf16)
-    copies[1].wait()
-    copies[2].wait()
-    copies[3].wait()
-
-    def transition_step(n, carry):
-        at = pl.multiple_of(n * 256, 256)
+    for copy in copies[4:7]:
+        copy.wait()
+
+    for n in range(0, w_gate_ref.shape[1], 256):
         shaped = grads_ref[...]
-        gate = nn(shaped, w_gate_ref[:, pl.ds(at, 256)])
-        up = nn(shaped, w_up_ref[:, pl.ds(at, 256)])
-        d_hidden = nt(cot_ref[...].reshape(rows, C_TOK), w_down_ref[pl.ds(at, 256), :])
+        gate = nn(shaped, w_gate_ref[:, n : n + 256])
+        up = nn(shaped, w_up_ref[:, n : n + 256])
+        d_hidden = nt(cot_ref[...].reshape(rows, C_TOK), w_down_ref[n : n + 256, :])
         sig = 1.0 / (1.0 + jnp.exp(-gate))
         act = gate * sig
-        hidden_ref[:, pl.ds(at, 256)] = (act * up).astype(bf16)
-        d_gate_ref[:, pl.ds(at, 256)] = (
+        hidden_ref[:, n : n + 256] = (act * up).astype(bf16)
+        d_gate_ref[:, n : n + 256] = (
             d_hidden * up * sig * (1.0 + gate * (1.0 - sig))
         ).astype(bf16)
-        d_up_ref[:, pl.ds(at, 256)] = (d_hidden * act).astype(bf16)
-        return carry
-
-    lax.fori_loop(0, w_gate_ref.shape[1] // 256, transition_step, 0)
+        d_up_ref[:, n : n + 256] = (d_hidden * act).astype(bf16)
+
     parts = []
-    for n in range(C_TOK // 256):
+    for n in range(0, C_TOK, 256):
         parts.append(
-            nt(d_gate_ref[...], w_gate_ref[256 * n : 256 * n + 256, :])
-            + nt(d_up_ref[...], w_up_ref[256 * n : 256 * n + 256, :])
+            nt(d_gate_ref[...], w_gate_ref[n : n + 256, :])
+            + nt(d_up_ref[...], w_up_ref[n : n + 256, :])
         )
     d_normed = jnp.concatenate(parts, axis=1)
     hat = hat_ref[...]
     first = jnp.mean(d_normed, axis=-1, keepdims=True)
     second = jnp.mean(d_normed * hat, axis=-1, keepdims=True)
-    d_resid = cot.astype(f32) + rstd * (d_normed - first - hat * second)
+    d_resid = cot_ref[...].reshape(rows, C_TOK).astype(f32) + rstd * (
+        d_normed - first - hat * second
+    )
     grads_ref[...] = nt(d_resid.astype(bf16), w_out_ref[...]).astype(bf16)
-    for copy in copies[4:]:
+    for copy in copies[7:]:
         copy.wait()
     masks = head_masks(tok_rows)
     for pair in range(PAIRS):
-        half, sub = pair // 4, pair % 4
-        low, high = (384 * half + v for v in WINDOWS[sub])
+        low, high = windows(pair)
         total = jnp.zeros((keys_all, 2 * tok_rows), f32)
         for s in range(batch):
             grads = two_heads(
-                grads_ref[s * tok_rows : (s + 1) * tok_rows, low:high], masks[sub]
+                grads_ref[s * tok_rows : (s + 1) * tok_rows, low:high], masks[pair % 4]
             )
             d_probs = nt(values_ref[s, :, low:high], grads)
             probs = probs_ref[s, pair]
             delta = jnp.sum(probs * d_probs, axis=0, keepdims=True)
             total = total + probs * (d_probs - delta)
-        d_bias_f_ref[pl.ds(pair, keys_all, stride=PAIRS), :] = total
-    here = lax.axis_index("samp")
-    for k, block in enumerate(block_refs):
-        size = block.shape[0]
-        at = pl.multiple_of((here ^ k) * size, size)
-        block[...] = d_bias_f_ref[pl.ds(at, size), :].astype(bf16)
-
-
-def token_stage(groups, tokens, att, probs, values, cot, w_out, w_gate, w_up, w_down):
-    halves = len(tokens)
+        biasf_ref[pl.ds(pair, keys_all, stride=PAIRS), :] = total
+    d_bias_ref[...] = biasf_ref[...].astype(bf16)
+
+
+def token_stage(
+    pieces, bias, tokens_a, tokens_b, att_a, cot, probs_a, values_a, w_qkv, w_out, w_gate, w_up,
+    w_down,
+):
     batch, tok_rows, _ = cot.shape
-    keys_all = values[0].shape[1]
+    keys_all = tok_rows * len(pieces)
     rows = batch * tok_rows
     hidden = w_gate.shape[1]
     vmem = pl.BlockSpec(memory_space=pltpu.VMEM)
     hbm = pl.BlockSpec(memory_space=pl.ANY)
     return pl.pallas_call(
-        functools.partial(token_kernel, halves=halves, groups=groups),
-        in_specs=[vmem] * (2 * halves) + [hbm] * (2 * halves) + [vmem] + [hbm] * 4,
-        out_specs=[vmem] * (2 + groups),
+        functools.partial(token_kernel, count=len(pieces)),
+        in_specs=[vmem] * (len(pieces) + 5) + [hbm] * 7,
+        out_specs=[vmem] * 3,
         out_shape=[
             jax.ShapeDtypeStruct((rows, C_TOK), f32),
             jax.ShapeDtypeStruct((rows, hidden), bf16),
-        ]
-        + [jax.ShapeDtypeStruct((keys_all * PAIRS // groups, 2 * tok_rows), bf16)] * groups,
+            jax.ShapeDtypeStruct((keys_all * PAIRS, 2 * tok_rows), bf16),
+        ],
         scratch_shapes=[
+            pltpu.VMEM((3, C_TOK, C_TOK), bf16),
             pltpu.VMEM(w_out.shape, bf16),
             pltpu.VMEM(w_gate.shape, bf16),
             pltpu.VMEM(w_up.shape, bf16),
             pltpu.VMEM(w_down.shape, bf16),
             pltpu.VMEM((batch, PAIRS, keys_all, 2 * tok_rows), f32),
             pltpu.VMEM((batch, keys_all, C_TOK), bf16),
-            pltpu.SemaphoreType.DMA((4 + 2 * halves,)),
+            pltpu.SemaphoreType.DMA((9,)),
+        ]
+        + attend_scratch(pieces[0].shape[0], tok_rows, keys_all)
+        + [
             pltpu.VMEM((rows, C_TOK), bf16),
             pltpu.VMEM((rows, hidden), bf16),
             pltpu.VMEM((rows, hidden), bf16),
             pltpu.VMEM((rows, C_TOK), f32),
-            pltpu.VMEM((keys_all * PAIRS, 2 * tok_rows), f32),
         ],
         compiler_params=pltpu.CompilerParams(vmem_limit_bytes=GRANT),
         cost_estimate=pl.CostEstimate(
-            flops=8 * 10**9, bytes_accessed=2 * 10**7, transcendentals=10**6
+            flops=10**10, bytes_accessed=2 * 10**7, transcendentals=10**6
         ),
         name="tokens",
-    )(*tokens, *att, *probs, *values, cot, w_out, w_gate, w_up, w_down)
+    )(
+        *pieces, bias, tokens_a, tokens_b, att_a, cot, probs_a, values_a, w_qkv, w_out, w_gate,
+        w_up, w_down,
+    )
 
 
 def output_kernel(
@@ -548,14 +567,12 @@
     )(resid, hidden, w_down, pair)
 
 
-def grad_kernel(*refs, groups):
-    part_refs = refs[:groups]
-    hat_ref, rstd_ref, gain_ref, w_bias_ref, out_ref, total_ref = refs[groups:]
-    keys = part_refs[0].shape[0] // PAIRS
+def grad_kernel(parts_ref, hat_ref, rstd_ref, gain_ref, w_bias_ref, out_ref, total_ref):
+    keys = parts_ref.shape[1] // PAIRS
     rows = hat_ref.shape[0] // keys
-    total = part_refs[0][...].astype(f32)
-    for part in part_refs[1:]:
-        total = total + part[...].astype(f32)
+    total = parts_ref[0].astype(f32)
+    for k in range(1, parts_ref.shape[0]):
+        total = total + parts_ref[k].astype(f32)
     total_ref[...] = total
     weights = jnp.concatenate(split_heads(w_bias_ref[...]), axis=0) * gain_ref[...]
     weights = weights - jnp.mean(weights, axis=-1, keepdims=True)
@@ -581,16 +598,16 @@
 
 
 def pair_back(parts, hat, rstd, pair_gain, w_bias_t):
-    keys = parts[0].shape[0] // PAIRS
+    keys = parts.shape[1] // PAIRS
     rows = hat.shape[0] // keys
     out = pl.pallas_call(
-        functools.partial(grad_kernel, groups=len(parts)),
+        grad_kernel,
         out_shape=jax.ShapeDtypeStruct((rows * keys, CZ), f32),
         scratch_shapes=[pltpu.VMEM((keys * PAIRS, 2 * rows), f32)],
         compiler_params=pltpu.CompilerParams(vmem_limit_bytes=GRANT),
         cost_estimate=pl.CostEstimate(flops=10**8, bytes_accessed=4 * 10**6, transcendentals=0),
         name="pair_grad",
-    )(*parts, hat, rstd, pair_gain.reshape(1, CZ), w_bias_t)
+    )(parts, hat, rstd, pair_gain.reshape(1, CZ), w_bias_t)
     return out.reshape(rows, keys, CZ)
 
 
@@ -617,32 +634,29 @@
     right = lax.ppermute(atom_feats[:, :HALO], "tok", [(j, i) for i, j in steps])
 
     w_bias_t = w_bias.T
-    bias = gather(pair_bias(pair, pair_gain, w_bias_t), "samp")
+    local_bias = pair_bias(pair, pair_gain, w_bias_t, groups)
+    bias = lax.all_to_all(local_bias, "samp", 0, 0).reshape(-1, 2 * tok_rows)
 
     reach = -(-(atom_rows + 2 * HALO) // 128) * 128
     flags = jnp.pad(atom_mask.astype(f32), (HALO, reach - atom_rows - HALO))
     flags = lax.dynamic_slice(flags, (shard * atom_rows,), (reach,)).reshape(reach // 128, 128)
-    flags, bias[0] = lax.optimization_barrier((flags, bias[0]))
-
-    halves = 2
-    each = batch // halves
-    tokens, att, probs, values = [], [], [], []
-    gathered = []
-    for i in range(halves):
+    flags, local_bias = lax.optimization_barrier((flags, local_bias))
+
+    ahead = batch // 2
+    tokens, gathered = [], []
+    for first, size in ((0, ahead), (ahead, batch - ahead)):
         tok, normed = atom_stage(
-            i * each, each, atom_feats, left, right, flags, atom_counts, token_single, w_atom_qkv,
+            first, size, atom_feats, left, right, flags, atom_counts, token_single, w_atom_qkv,
             w_atom_out, w_embed,
         )
         tokens.append(tok)
         gathered.append(gather(normed, "tok"))
-    for pieces in gathered:
-        for kept, new in zip((att, probs, values), attend_stage(pieces, bias, w_qkv)):
-            kept.append(new)
-    resid, hidden, *blocks = token_stage(
-        groups, tokens, att, probs, values, cotangent, w_out, w_gate, w_up, w_down
+    att_a, probs_a, values_a = attend_stage(gathered[0], bias, w_qkv)
+    resid, hidden, d_bias = token_stage(
+        gathered[1], bias, *tokens, att_a, cotangent, probs_a, values_a, w_qkv, w_out, w_gate,
+        w_up, w_down,
     )
-    far = range(groups - 1, 0, -1)
-    parts = [blocks[0]] + [swap(blocks[k], "samp", k) for k in far]
+    parts = lax.all_to_all(d_bias.reshape(groups, -1, 2 * tok_rows), "samp", 0, 0)
     token_out, hat, rstd = output_stage(resid, hidden, w_down, pair)
     pair_grad = pair_back(parts, hat, rstd, pair_gain, w_bias_t)
     token_out = token_out.reshape(batch, tok_rows, C_TOK)

time: 119 us -> 100 us (0.84)
  starting transfers between devices: 36.2 us -> 21.9 us
  Pallas kernels: 75.4 us -> 62.1 us
  waiting for transfers between devices: 0.06 us -> 8.83 us
    ppermute x20 -> x6, starting transfers between devices: 31.9 us -> 4.56 us  [swap(): lax.ppermute(values, axis, [(i, i ^ k) for i in range(lax.axis_size(axis))])]
    pallas_call x5 -> x4, Pallas kernels: 43.1 us -> 29.9 us  [the longest x1 14.8 us: token_stage(): pl.pallas_call(functools.partial(token_kernel, count=len(pieces)), in_spe...]
    all_to_all x0 -> x2, starting transfers between devices: none -> 13 us  [the longest x1 7.28 us: body(): bias = lax.all_to_all(local_bias, 'samp', 0, 0).reshape(-1, 2 * tok_rows)]
    all_to_all x0 -> x2, waiting for transfers between devices: none -> 8.3 us  [the longest x1 8.3 us: body(): lax.all_to_all(d_bias.reshape(groups, -1, 2 * tok_rows), 'samp', 0, 0)]
    unnamed x46 -> x20, local copies, waits for them, and re-layouts: 3.46 us -> 3.67 us
  transfers between devices with their start and end apart: 22 -> 10, of which waited for: 0 -> 2; matrix products, arithmetic and copies ran while one was open for 2% -> 1% of each run, Pallas kernels for 36% -> 43%
where the time goes in v3:
time: 100 us; the launch traced here: 99.5 us
  Pallas kernels  62.1 us (62%)
  starting transfers between devices  21.9 us (22%)
  waiting for transfers between devices  8.83 us (9%)
  local copies, waits for them, and re-layouts  5.18 us (5%)
    pallas_call x2, Pallas kernels, atom_stage(): pl.pallas_call(atom_kernel, grid=(batch,), in_specs=[of_sample(atoms, C_A...  25.8 us
    pallas_call x1, Pallas kernels, token_stage(): pl.pallas_call(functools.partial(token_kernel, count=len(pieces)), in_spe...  14.8 us
    all_to_all x1, waiting for transfers between devices, body(): lax.all_to_all(d_bias.reshape(groups, -1, 2 * tok_rows), 'samp', 0, 0)  8.3 us
    pallas_call x1, Pallas kernels, attend_stage(): pl.pallas_call(functools.partial(attend_kernel, count=len(pieces)), in_sp...  7.99 us
    all_to_all x1, starting transfers between devices, body(): bias = lax.all_to_all(local_bias, 'samp', 0, 0).reshape(-1, 2 * tok_rows)  7.28 us
    pallas_call x1, Pallas kernels, output_stage(): pl.pallas_call(output_kernel, out_shape=[jax.ShapeDtypeStruct(resid.shape...  6.35 us
    all_to_all x1, starting transfers between devices, body(): lax.all_to_all(d_bias.reshape(groups, -1, 2 * tok_rows), 'samp', 0, 0)  5.74 us
    ppermute x6, starting transfers between devices, swap(): lax.ppermute(values, axis, [(i, i ^ k) for i in range(lax.axis_size(axis))])  4.56 us
  transfers between devices with their start and end apart: 10, of which 2 were waited for; matrix products, arithmetic and copies ran while one was open for 1% of the time, Pallas kernels for 43%

profile of v3, /device:TPU:0, one launch (start us, length us, event | category | flops | bytes accessed | tf_op | source)
XLA Modules:
  0.0 99.5 jit_solution(12233347045351900366)
XLA Ops:
  0.6 0.8 fusion.1
  1.5 1.3 %collective-permute-start.1 = (bf16[4,48,128]{2,1,0:T(8,128)(2,1)S(1)}, bf16[4,48,128]{2,1,0:T(8,128)(2,1)S(1)}, u32[]{:S(2)}, u32[]{:S(2)}) collective-permute-start(bf16[4,48,128]{2,1,0:T(8,128)(2,1)S(1)} %get-tuple-element.30), channel_id=1, source_target_pairs={{1,0},{2,1},{3,2},{5,4},{6,5},{7,6},{9,8},{10,9},{11,10},{13,12},{... | collective-permute-start | bytes 147464 | tf_op jit(solution)/shard_map/ppermute | solution.py:634
  2.8 3.0 %collective-permute-start = (bf16[4,48,128]{2,1,0:T(8,128)(2,1)S(1)}, bf16[4,48,128]{2,1,0:T(8,128)(2,1)S(1)}, u32[]{:S(2)}, u32[]{:S(2)}) collective-permute-start(bf16[4,48,128]{2,1,0:T(8,128)(2,1)S(1)} %get-tuple-element.31), channel_id=1, source_target_pairs={{0,1},{1,2},{2,3},{4,5},{5,6},{6,7},{8,9},{9,10},{10,11},{12,13},{... | collective-permute-start | bytes 147464 | tf_op jit(solution)/shard_map/ppermute | solution.py:633
  5.8 3.0 %pair_bias.1 = bf16[8,256,128]{2,1,0:T(8,128)(2,1)} custom-call(bf16[64,32,128]{2,1,0:T(8,128)(2,1)} %pair_ref.3, f32[1,128]{1,0:T(1,128)} %bitcast.14, bf16[16,128]{1,0:T(8,128)(2,1)} %bitcast.12), custom_call_target="tpu_custom_call" | custom-call | flops 10000000 | bytes 10000000 | tf_op jit(solution)/shard_map/pair_bias/pallas_call | solution.py:86
  8.8 7.3 %all-to-all-start = ((bf16[8,256,128]{2,1,0:T(8,128)(2,1)}), bf16[8,256,128]{2,1,0:T(8,128)(2,1)S(1)}, u32[]{:S(2)}, u32[]{:S(2)}) async-start(bf16[8,256,128]{2,1,0:T(8,128)(2,1)} %pair_bias.1), calls=%async_computation | async-start | bytes 1048576 | tf_op jit(solution)/shard_map/all_to_all | solution.py:638
  16.1 0.7 convert_element_type.5
  16.8 0.7 fusion.flags_ref
  17.5 0.0 collective-permute-done.left_ref
  17.5 0.6 copy-done.8
  18.1 0.6 copy-done.9
  18.7 12.9 %atoms.3 = (f32[2,64,768]{2,1,0:T(8,128)}, bf16[2,64,768]{2,1,0:T(8,128)(2,1)}) custom-call(bf16[4,1280,128]{2,1,0:T(8,128)(2,1)} %feats_ref.3, bf16[4,48,128]{2,1,0:T(8,128)(2,1)} %copy-done.9, bf16[4,48,128]{2,1,0:T(8,128)(2,1)} %copy-done.8, f32[11,128]{1,0:T(8,128)} %fusion.flags_ref, s32[1,64]{1,0:T(1,128)} %counts_ref.3, bf16[64,768]{1,0:T(8,128)(2,1)} %single_ref.3, ...), custom_call_target="tpu_custom_call" | custom-call | flops 10000000000 | bytes 4000000 | tf_op jit(solution)/shard_map/atoms/pallas_call | solution.py:231
  31.6 0.2 collective-permute-start.7
  31.8 2.2 %collective-permute-start.6 = (bf16[2,64,768]{2,1,0:T(8,128)(2,1)}, bf16[2,64,768]{2,1,0:T(8,128)(2,1)S(1)}, u32[]{:S(2)}, u32[]{:S(2)}) collective-permute-start(bf16[2,64,768]{2,1,0:T(8,128)(2,1)} %get-tuple-element.20.refs_0_), channel_id=1, source_target_pairs={{0,2},{1,3},{2,0},{3,1},{4,6},{5,7},{6,4},{7,5},{8,10},{9,11},{10,... | collective-permute-start | bytes 589832 | tf_op jit(solution)/shard_map/ppermute | solution.py:615
  34.1 12.9 %atoms.2 = (f32[2,64,768]{2,1,0:T(8,128)}, bf16[2,64,768]{2,1,0:T(8,128)(2,1)}) custom-call(bf16[4,1280,128]{2,1,0:T(8,128)(2,1)} %feats_ref.3, bf16[4,48,128]{2,1,0:T(8,128)(2,1)} %copy-done.9, bf16[4,48,128]{2,1,0:T(8,128)(2,1)} %copy-done.8, f32[11,128]{1,0:T(8,128)} %fusion.flags_ref, s32[1,64]{1,0:T(1,128)} %counts_ref.3, bf16[64,768]{1,0:T(8,128)(2,1)} %single_ref.3, ...), custom_call_target="tpu_custom_call" | custom-call | flops 10000000000 | bytes 4000000 | tf_op jit(solution)/shard_map/atoms/pallas_call | solution.py:231
  47.0 0.5 collective-permute-start.4
  47.5 1.6 %collective-permute-start.3 = (bf16[2,64,768]{2,1,0:T(8,128)(2,1)}, bf16[2,64,768]{2,1,0:T(8,128)(2,1)S(1)}, u32[]{:S(2)}, u32[]{:S(2)}) collective-permute-start(bf16[2,64,768]{2,1,0:T(8,128)(2,1)} %get-tuple-element.17.refs_0_), channel_id=1, source_target_pairs={{0,2},{1,3},{2,0},{3,1},{4,6},{5,7},{6,4},{7,5},{8,10},{9,11},{10,... | collective-permute-start | bytes 589832 | tf_op jit(solution)/shard_map/ppermute | solution.py:615
  49.1 0.0 collective-permute-done.6.refs_2_
  49.2 0.6 copy-done.4
  49.8 0.1 copy-done.5
  49.9 0.1 copy-done.7
  49.9 0.2 copy-done.1
  50.1 8.0 %attend.1 = (bf16[128,768]{1,0:T(8,128)(2,1)}, f32[2,8,256,128]{3,2,1,0:T(8,128)}, bf16[2,256,768]{2,1,0:T(8,128)(2,1)}) custom-call(bf16[2,64,768]{2,1,0:T(8,128)(2,1)} %get-tuple-element.20.refs_0_, bf16[2,64,768]{2,1,0:T(8,128)(2,1)} %copy-done.7, bf16[2,64,768]{2,1,0:T(8,128)(2,1)} %copy-done.5, bf16[2,64,768]{2,1,0:T(8,128)(2,1)} %copy-done.4, ...), custom_call_target="tpu_custom_call" | custom-call | flops 4000000000 | bytes 10000000 | tf_op jit(solution)/shard_map/attend/pallas_call | solution.py:379
  58.1 0.5 collective-permute-done.3.refs_2_
  58.6 0.2 copy-done.2
  58.8 0.5 copy-done.3
  59.3 0.1 copy-done.6
  59.3 14.8 %tokens.1 = (f32[256,768]{1,0:T(8,128)}, bf16[256,1536]{1,0:T(8,128)(2,1)}, bf16[2048,128]{1,0:T(8,128)(2,1)}) custom-call(bf16[2,64,768]{2,1,0:T(8,128)(2,1)} %get-tuple-element.17.refs_0_, bf16[2,64,768]{2,1,0:T(8,128)(2,1)} %copy-done.6, bf16[2,64,768]{2,1,0:T(8,128)(2,1)} %copy-done.3, bf16[2,64,768]{2,1,0:T(8,128)(2,1)} %copy-done.2, ...), custom_call_target="tpu_custom_call" | custom-call | flops 10000000000 | bytes 20000000 | tf_op jit(solution)/shard_map/tokens/pallas_call | solution.py:498
  74.2 5.7 %all-to-all-start.1 = ((bf16[8,256,128]{2,1,0:T(8,128)(2,1)}), bf16[8,256,128]{2,1,0:T(8,128)(2,1)S(1)}, u32[]{:S(2)}, u32[]{:S(2)}) async-start(bf16[8,256,128]{2,1,0:T(8,128)(2,1)} %bitcast.11), calls=%async_computation.1 | async-start | bytes 1048576 | tf_op jit(solution)/shard_map/all_to_all | solution.py:659
  79.9 6.4 %output.1 = (bf16[256,768]{1,0:T(8,128)(2,1)}, f32[2048,128]{1,0:T(8,128)}, f32[2048,128]{1,0:T(8,128)}) custom-call(f32[256,768]{1,0:T(8,128)} %get-tuple-element.24.resid_ref, bf16[256,1536]{1,0:T(8,128)(2,1)} %get-tuple-element.25.hidden_ref, bf16[1536,768]{1,0:T(8,128)(2,1)} %w_down_ref.1, bf16[64,32,128]{2,1,0:T(8,128)(2,1)} %pair_ref.3), custom_call_target="tpu_custom_call" | custom-call | flops 1000000000 | bytes 8000000 | tf_op jit(solution)/shard_map/output/pallas_call | solution.py:557
  86.3 8.3 %all-to-all-done.1.parts_ref = bf16[8,256,128]{2,1,0:T(8,128)(2,1)S(1)} async-done(((bf16[8,256,128]{2,1,0:T(8,128)(2,1)}), bf16[8,256,128]{2,1,0:T(8,128)(2,1)S(1)}, u32[]{:S(2)}, u32[]{:S(2)}) %all-to-all-start.1) | async-done | bytes 524320 | tf_op jit(solution)/shard_map/all_to_all | solution.py:659
  94.6 0.8 copy-done
  95.4 4.1 %pair_grad.1 = f32[2048,128]{1,0:T(8,128)} custom-call(bf16[8,256,128]{2,1,0:T(8,128)(2,1)} %copy-done, f32[2048,128]{1,0:T(8,128)} %get-tuple-element.28.hat_ref, f32[2048,128]{1,0:T(8,128)} %get-tuple-element.29.rstd_ref, f32[1,128]{1,0:T(1,128)} %bitcast.15, bf16[16,128]{1,0:T(8,128)(2,1)} %bitcast.13), custom_call_target="tpu_custom_call" | custom-call | flops 100000000 | bytes 4000000 | tf_op jit(solution)/shard_map/pair_grad/pallas_call | solution.py:603
  (18 shorter events, 0.0 us)
Async XLA Ops:
  1.5 16.0 %collective-permute-start.1 = (bf16[4,48,128]{2,1,0:T(8,128)(2,1)S(1)}, bf16[4,48,128]{2,1,0:T(8,128)(2,1)S(1)}, u32[]{:S(2)}, u32[]{:S(2)}) collective-permute-start(bf16[4,48,128]{2,1,0:T(8,128)(2,1)S(1)} %get-tuple-element.30), channel_id=1, source_target_pairs={{1,0},{2,1},{3,2},{5,4},{6,5},{7,6},{9,8},{10,9},{11,10},{13,12},{... | collective-permute-start | bytes 147464 | tf_op jit(solution)/shard_map/ppermute | solution.py:634
  2.8 14.7 %collective-permute-start = (bf16[4,48,128]{2,1,0:T(8,128)(2,1)S(1)}, bf16[4,48,128]{2,1,0:T(8,128)(2,1)S(1)}, u32[]{:S(2)}, u32[]{:S(2)}) collective-permute-start(bf16[4,48,128]{2,1,0:T(8,128)(2,1)S(1)} %get-tuple-element.31), channel_id=1, source_target_pairs={{0,1},{1,2},{2,3},{4,5},{5,6},{6,7},{8,9},{9,10},{10,11},{12,13},{... | collective-permute-start | bytes 147464 | tf_op jit(solution)/shard_map/ppermute | solution.py:633
  8.8 40.4 %all-to-all-start = ((bf16[8,256,128]{2,1,0:T(8,128)(2,1)}), bf16[8,256,128]{2,1,0:T(8,128)(2,1)S(1)}, u32[]{:S(2)}, u32[]{:S(2)}) async-start(bf16[8,256,128]{2,1,0:T(8,128)(2,1)} %pair_bias.1), calls=%async_computation | async-start | bytes 1048576 | tf_op jit(solution)/shard_map/all_to_all | solution.py:638
  17.5 0.6 copy-start.8
  18.1 0.6 copy-start.9
  31.6 17.5 %collective-permute-start.7 = (bf16[2,64,768]{2,1,0:T(8,128)(2,1)}, bf16[2,64,768]{2,1,0:T(8,128)(2,1)S(1)}, u32[]{:S(2)}, u32[]{:S(2)}) collective-permute-start(bf16[2,64,768]{2,1,0:T(8,128)(2,1)} %get-tuple-element.20.refs_0_), channel_id=1, source_target_pairs={{0,3},{1,2},{2,1},{3,0},{4,7},{5,6},{6,5},{7,4},{8,11},{9,10},{10,... | collective-permute-start | bytes 589832 | tf_op jit(solution)/shard_map/ppermute | solution.py:615
  31.8 17.3 %collective-permute-start.6 = (bf16[2,64,768]{2,1,0:T(8,128)(2,1)}, bf16[2,64,768]{2,1,0:T(8,128)(2,1)S(1)}, u32[]{:S(2)}, u32[]{:S(2)}) collective-permute-start(bf16[2,64,768]{2,1,0:T(8,128)(2,1)} %get-tuple-element.20.refs_0_), channel_id=1, source_target_pairs={{0,2},{1,3},{2,0},{3,1},{4,6},{5,7},{6,4},{7,5},{8,10},{9,11},{10,... | collective-permute-start | bytes 589832 | tf_op jit(solution)/shard_map/ppermute | solution.py:615
  34.0 15.1 %collective-permute-start.5 = (bf16[2,64,768]{2,1,0:T(8,128)(2,1)}, bf16[2,64,768]{2,1,0:T(8,128)(2,1)S(1)}, u32[]{:S(2)}, u32[]{:S(2)}) collective-permute-start(bf16[2,64,768]{2,1,0:T(8,128)(2,1)} %get-tuple-element.20.refs_0_), channel_id=1, source_target_pairs={{0,1},{1,0},{2,3},{3,2},{4,5},{5,4},{6,7},{7,6},{8,9},{9,8},{10,11... | collective-permute-start | bytes 589832 | tf_op jit(solution)/shard_map/ppermute | solution.py:615
  47.0 11.1 %collective-permute-start.4 = (bf16[2,64,768]{2,1,0:T(8,128)(2,1)}, bf16[2,64,768]{2,1,0:T(8,128)(2,1)S(1)}, u32[]{:S(2)}, u32[]{:S(2)}) collective-permute-start(bf16[2,64,768]{2,1,0:T(8,128)(2,1)} %get-tuple-element.17.refs_0_), channel_id=1, source_target_pairs={{0,3},{1,2},{2,1},{3,0},{4,7},{5,6},{6,5},{7,4},{8,11},{9,10},{10,... | collective-permute-start | bytes 589832 | tf_op jit(solution)/shard_map/ppermute | solution.py:615
  47.5 11.1 %collective-permute-start.3 = (bf16[2,64,768]{2,1,0:T(8,128)(2,1)}, bf16[2,64,768]{2,1,0:T(8,128)(2,1)S(1)}, u32[]{:S(2)}, u32[]{:S(2)}) collective-permute-start(bf16[2,64,768]{2,1,0:T(8,128)(2,1)} %get-tuple-element.17.refs_0_), channel_id=1, source_target_pairs={{0,2},{1,3},{2,0},{3,1},{4,6},{5,7},{6,4},{7,5},{8,10},{9,11},{10,... | collective-permute-start | bytes 589832 | tf_op jit(solution)/shard_map/ppermute | solution.py:615
  49.1 0.7 copy-start.4
  49.1 9.5 %collective-permute-start.2 = (bf16[2,64,768]{2,1,0:T(8,128)(2,1)}, bf16[2,64,768]{2,1,0:T(8,128)(2,1)S(1)}, u32[]{:S(2)}, u32[]{:S(2)}) collective-permute-start(bf16[2,64,768]{2,1,0:T(8,128)(2,1)} %get-tuple-element.17.refs_0_), channel_id=1, source_target_pairs={{0,1},{1,0},{2,3},{3,2},{4,5},{5,4},{6,7},{7,6},{8,9},{9,8},{10,11... | collective-permute-start | bytes 589832 | tf_op jit(solution)/shard_map/ppermute | solution.py:615
  49.1 0.7 copy-start.5
  49.1 0.8 copy-start.7
  49.2 0.9 copy-start.1
  58.1 0.7 copy-start.2
  58.6 0.7 copy-start.3
  58.6 0.7 copy-start.6
  74.2 20.4 %all-to-all-start.1 = ((bf16[8,256,128]{2,1,0:T(8,128)(2,1)}), bf16[8,256,128]{2,1,0:T(8,128)(2,1)S(1)}, u32[]{:S(2)}, u32[]{:S(2)}) async-start(bf16[8,256,128]{2,1,0:T(8,128)(2,1)} %bitcast.11), calls=%async_computation.1 | async-start | bytes 1048576 | tf_op jit(solution)/shard_map/all_to_all | solution.py:659
  94.6 0.8 copy-start

commit v4 on v3

--- a/solution.py
+++ b/solution.py
@@ -16,7 +16,6 @@
 CZ = 128
 HALO = 48
 PAIRS = HEADS // 2
-GRANT = 60 << 20
 LOG2E = 1.4426950408889634
 
 epsilon = 1e-05
@@ -76,7 +75,7 @@
             [jnp.concatenate([block, blank], axis=1), jnp.concatenate([blank, block], axis=1)],
             axis=0,
         )
-        stage_ref[pl.ds(j * PAIRS, PAIRS), :] = nt(weights, both)
+        stage_ref[pl.ds(j, PAIRS, stride=keys), :] = nt(weights, both)
     for k in range(out_ref.shape[0]):
         out_ref[k] = stage_ref[...].astype(bf16)
 
@@ -90,14 +89,14 @@
             pltpu.VMEM((rows * keys, CZ), f32),
             pltpu.VMEM((keys * PAIRS, 2 * rows), f32),
         ],
-        compiler_params=pltpu.CompilerParams(vmem_limit_bytes=GRANT),
+        compiler_params=pltpu.CompilerParams(vmem_limit_bytes=60 << 20),
         cost_estimate=pl.CostEstimate(flops=10**7, bytes_accessed=10**7, transcendentals=0),
         name="pair_bias",
     )(pair, pair_gain.reshape(1, CZ), w_bias_t)
 
 
 def atom_kernel(
-    feats_ref, left_ref, right_ref, flags_ref, counts_ref, single_ref, w_qkv_ref, w_out_ref,
+    feats_ref, left_ref, right_ref, mask_ref, counts_ref, single_ref, w_qkv_ref, w_out_ref,
     w_embed_ref, tokens_ref, normed_ref, xn_ref, qkv_ref, scores_a, scores_b, probs_a, probs_b,
     mixed_ref, updated_ref, split_ref, keybias_ref, onehot_ref, counts_col_ref,
 ):
@@ -108,12 +107,20 @@
     @pl.when(pl.program_id(0) == 0)
     def prepare():
         eye = iota((128, 128), 0) == iota((128, 128), 1)
-        for b in range(flags_ref.shape[0]):
-            row = jnp.broadcast_to(flags_ref[b : b + 1, :], (128, 128))
+        blocks = atoms // 128
+        for b in range(-1, blocks + 1):
+            at = lax.axis_index("tok") * blocks + b
+            inside = jnp.where((at >= 0) & (at < mask_ref.shape[0]), 1, 0)
+            row = mask_ref[pl.ds(jnp.clip(at, 0, mask_ref.shape[0] - 1), 1), :] * inside
+            row = jnp.broadcast_to(row.astype(f32), (128, 128))
             col = jnp.sum(jnp.where(eye, row, 0.0), axis=1, keepdims=True)
-            keybias_ref[b * 128 : (b + 1) * 128, :] = jnp.broadcast_to(
-                (col - 1.0) * 1e30, (128, 128)
-            )
+            col = jnp.broadcast_to((col - 1.0) * 1e30, (128, 128))
+            if b < 0:
+                keybias_ref[0:HALO, :] = col[128 - HALO : 128]
+            elif b < blocks:
+                keybias_ref[HALO + 128 * b : HALO + 128 * b + 128, :] = col
+            else:
+                keybias_ref[HALO + atoms : padded, :] = col[0:HALO]
         counts = jnp.broadcast_to(counts_ref[...].astype(f32), (tok_rows, tok_rows))
         sub, lane = iota((tok_rows, tok_rows), 0), iota((tok_rows, tok_rows), 1)
         start = jnp.sum(jnp.where(lane < sub, counts, 0.0), axis=1, keepdims=True)
@@ -124,8 +131,6 @@
             at = pos + float(g * 256)
             hit = jnp.where((at >= start) & (at < start + own), 1.0, 0.0).astype(bf16)
             onehot_ref[g] = jnp.concatenate([hit, hit], axis=1)
-        probs_a[...] = jnp.zeros_like(probs_a)
-        probs_b[...] = jnp.zeros_like(probs_b)
 
     xn_ref[0:HALO, :] = norm_rows(left_ref[0].astype(f32))[0].astype(bf16)
     xn_ref[atoms + HALO : padded, :] = norm_rows(right_ref[0].astype(f32))[0].astype(bf16)
@@ -172,18 +177,18 @@
                 scores = from_ref[k, 32 * w : 32 * w + 128, 128 * w : 128 * w + 128] + keybias
                 expo = jnp.exp2((scores - jnp.max(scores, axis=0, keepdims=True)) * factor)
                 weights = expo * (1.0 / jnp.sum(expo, axis=0, keepdims=True))
-                to_ref[k, 32 * w : 32 * w + 128, 128 * w : 128 * w + 128] = weights.astype(bf16)
+                to_ref[2 * k + w] = weights.astype(bf16)
 
     def value_step(group, from_ref):
         for k in range(2):
             base = pl.multiple_of(group * 128 + 64 * k, 64)
-            part = tn(from_ref[k], qkv_ref[pl.ds(base, 160), 2 * C_ATOM : 3 * C_ATOM])
             mixes = []
             for w in range(2):
-                mix = part[128 * w : 128 * w + 32]
+                values = qkv_ref[pl.ds(base + 32 * w, 128), 2 * C_ATOM : 3 * C_ATOM]
+                part = tn(from_ref[2 * k + w], values)
+                mix = part[0:32]
                 for h in range(1, ATOM_HEADS):
-                    low = 128 * w + 32 * h
-                    mix = jnp.where(head_of == h, part[low : low + 32], mix)
+                    mix = jnp.where(head_of == h, part[32 * h : 32 * h + 32], mix)
                 mixes.append(mix.astype(bf16))
             mixed_ref[pl.ds(base, 64), :] = jnp.concatenate(mixes, axis=0)
 
@@ -221,7 +226,7 @@
     normed_ref[0] = norm_rows(tokens)[0].astype(bf16)
 
 
-def atom_stage(first, batch, feats, left, right, flags, counts, single, w_qkv, w_out, w_embed):
+def atom_stage(first, batch, feats, left, right, mask, counts, single, w_qkv, w_out, w_embed):
     atoms = feats.shape[1]
     tok_rows = single.shape[0]
     padded = atoms + 2 * HALO
@@ -233,7 +238,7 @@
         grid=(batch,),
         in_specs=[
             of_sample(atoms, C_ATOM), of_sample(HALO, C_ATOM), of_sample(HALO, C_ATOM),
-            whole(flags), whole(counts), whole(single), whole(w_qkv), whole(w_out), whole(w_embed),
+            whole(mask), whole(counts), whole(single), whole(w_qkv), whole(w_out), whole(w_embed),
         ],
         out_specs=[by_sample(tok_rows, C_TOK), by_sample(tok_rows, C_TOK)],
         out_shape=[
@@ -245,21 +250,21 @@
             pltpu.VMEM((padded, 3 * C_ATOM), bf16),
             pltpu.VMEM((2, 160, 256), f32),
             pltpu.VMEM((2, 160, 256), f32),
-            pltpu.VMEM((2, 160, 256), bf16),
-            pltpu.VMEM((2, 160, 256), bf16),
+            pltpu.VMEM((4, 128, 128), bf16),
+            pltpu.VMEM((4, 128, 128), bf16),
             pltpu.VMEM((atoms, C_ATOM), bf16),
             pltpu.VMEM((atoms, C_ATOM), bf16),
             pltpu.VMEM((atoms // 256, 512, C_TOK), bf16),
-            pltpu.VMEM((flags.shape[0] * 128, 128), f32),
+            pltpu.VMEM((padded, 128), f32),
             pltpu.VMEM((atoms // 256, tok_rows, 512), bf16),
             pltpu.VMEM((tok_rows, 128), f32),
         ],
-        compiler_params=pltpu.CompilerParams(vmem_limit_bytes=GRANT),
+        compiler_params=pltpu.CompilerParams(vmem_limit_bytes=60 << 20),
         cost_estimate=pl.CostEstimate(
             flops=10**10, bytes_accessed=4 * 10**6, transcendentals=3 * 10**6
         ),
         name="atoms",
-    )(feats, left, right, flags, counts, single, w_qkv, w_out, w_embed)
+    )(feats, left, right, mask, counts, single, w_qkv, w_out, w_embed)
 
 
 def head_masks(rows):
@@ -318,7 +323,8 @@
             probs_ref[s, pair] = nt(keys_ref[s, :, low:high], queries)
         for pair in range(PAIRS):
             scores = probs_ref[s, pair] * factor
-            scores = scores + bias_ref[pl.ds(pair, keys_all, stride=PAIRS), :]
+            bias = [bias_ref[k, pair].astype(f32) for k in range(bias_ref.shape[0])]
+            scores = scores + jnp.concatenate(bias, axis=0)
             expo = jnp.exp(scores - jnp.max(scores, axis=0, keepdims=True))
             probs_ref[s, pair] = expo * (1.0 / jnp.sum(expo, axis=0, keepdims=True))
         lanes = [jnp.zeros((tok_rows, 128), f32) for _ in range(C_TOK // 128)]
@@ -354,12 +360,11 @@
     piece_refs = refs[:count]
     (
         bias_ref, w_qkv_hbm, att_ref, probs_ref, values_ref, w_qkv_ref, sems, all_ref, queries_ref,
-        keys_ref, biasf_ref,
+        keys_ref,
     ) = refs[count:]
     copies = start_all(qkv_moves(w_qkv_hbm, w_qkv_ref), sems)
-    biasf_ref[...] = bias_ref[...].astype(f32)
     project(piece_refs, w_qkv_ref, copies, all_ref, queries_ref, keys_ref, values_ref)
-    attend(biasf_ref, queries_ref, keys_ref, values_ref, probs_ref, att_ref)
+    attend(bias_ref, queries_ref, keys_ref, values_ref, probs_ref, att_ref)
 
 
 def attend_scratch(batch, tok_rows, keys_all):
@@ -367,7 +372,6 @@
         pltpu.VMEM((batch, keys_all, C_TOK), bf16),
         pltpu.VMEM((batch * tok_rows, C_TOK), bf16),
         pltpu.VMEM((batch, keys_all, C_TOK), bf16),
-        pltpu.VMEM((keys_all * PAIRS, 2 * tok_rows), f32),
     ]
 
 
@@ -390,7 +394,7 @@
             pltpu.SemaphoreType.DMA((3,)),
         ]
         + attend_scratch(batch, tok_rows, keys_all),
-        compiler_params=pltpu.CompilerParams(vmem_limit_bytes=GRANT),
+        compiler_params=pltpu.CompilerParams(vmem_limit_bytes=32 << 20),
         cost_estimate=pl.CostEstimate(
             flops=4 * 10**9, bytes_accessed=10**7, transcendentals=10**6
         ),
@@ -405,7 +409,7 @@
         w_qkv_hbm, w_out_hbm, w_gate_hbm, w_up_hbm, w_down_hbm,
         resid_ref, hidden_ref, d_bias_ref,
         w_qkv_ref, w_out_ref, w_gate_ref, w_up_ref, w_down_ref, probs_ref, values_ref, sems,
-        all_ref, queries_ref, keys_ref, biasf_ref, grads_ref, d_gate_ref, d_up_ref, hat_ref,
+        all_ref, queries_ref, keys_ref, grads_ref, d_gate_ref, d_up_ref, hat_ref,
     ) = refs[count:]
     batch, tok_rows = cot_ref.shape[0], cot_ref.shape[1]
     keys_all = values_ref.shape[1]
@@ -421,11 +425,10 @@
         ],
         sems,
     )
-    biasf_ref[...] = bias_ref[...].astype(f32)
     own_values = values_ref.at[pl.ds(ahead, batch - ahead)]
     own_probs = probs_ref.at[pl.ds(ahead, batch - ahead)]
     project(piece_refs, w_qkv_ref, copies, all_ref, queries_ref, keys_ref, own_values)
-    attend(biasf_ref, queries_ref, keys_ref, own_values, own_probs, queries_ref)
+    attend(bias_ref, queries_ref, keys_ref, own_values, own_probs, queries_ref)
 
     copies[3].wait()
     resid_ref[0:lead, :] = tokens_a_ref[...].reshape(lead, C_TOK) + nn(
@@ -481,8 +484,9 @@
             probs = probs_ref[s, pair]
             delta = jnp.sum(probs * d_probs, axis=0, keepdims=True)
             total = total + probs * (d_probs - delta)
-        biasf_ref[pl.ds(pair, keys_all, stride=PAIRS), :] = total
-    d_bias_ref[...] = biasf_ref[...].astype(bf16)
+        size = d_bias_ref.shape[2]
+        for k in range(d_bias_ref.shape[0]):
+            d_bias_ref[k, pair] = total[size * k : size * (k + 1)].astype(bf16)
 
 
 def token_stage(
@@ -502,7 +506,7 @@
         out_shape=[
             jax.ShapeDtypeStruct((rows, C_TOK), f32),
             jax.ShapeDtypeStruct((rows, hidden), bf16),
-            jax.ShapeDtypeStruct((keys_all * PAIRS, 2 * tok_rows), bf16),
+            jax.ShapeDtypeStruct(bias.shape, bf16),
         ],
         scratch_shapes=[
             pltpu.VMEM((3, C_TOK, C_TOK), bf16),
@@ -521,7 +525,7 @@
             pltpu.VMEM((rows, hidden), bf16),
             pltpu.VMEM((rows, C_TOK), f32),
         ],
-        compiler_params=pltpu.CompilerParams(vmem_limit_bytes=GRANT),
+        compiler_params=pltpu.CompilerParams(vmem_limit_bytes=44 << 20),
         cost_estimate=pl.CostEstimate(
             flops=10**10, bytes_accessed=2 * 10**7, transcendentals=10**6
         ),
@@ -559,7 +563,7 @@
         out_shape=[jax.ShapeDtypeStruct(resid.shape, bf16)]
         + [jax.ShapeDtypeStruct((rows * keys, CZ), f32)] * 2,
         scratch_shapes=[pltpu.VMEM((rows * keys, CZ), f32)],
-        compiler_params=pltpu.CompilerParams(vmem_limit_bytes=GRANT),
+        compiler_params=pltpu.CompilerParams(vmem_limit_bytes=24 << 20),
         cost_estimate=pl.CostEstimate(
             flops=10**9, bytes_accessed=8 * 10**6, transcendentals=0
         ),
@@ -568,12 +572,13 @@
 
 
 def grad_kernel(parts_ref, hat_ref, rstd_ref, gain_ref, w_bias_ref, out_ref, total_ref):
-    keys = parts_ref.shape[1] // PAIRS
+    keys = parts_ref.shape[2]
     rows = hat_ref.shape[0] // keys
-    total = parts_ref[0].astype(f32)
-    for k in range(1, parts_ref.shape[0]):
-        total = total + parts_ref[k].astype(f32)
-    total_ref[...] = total
+    for pair in range(PAIRS):
+        total = parts_ref[0, pair].astype(f32)
+        for k in range(1, parts_ref.shape[0]):
+            total = total + parts_ref[k, pair].astype(f32)
+        total_ref[pair * keys : (pair + 1) * keys, :] = total
     weights = jnp.concatenate(split_heads(w_bias_ref[...]), axis=0) * gain_ref[...]
     weights = weights - jnp.mean(weights, axis=-1, keepdims=True)
     weights = jnp.concatenate([weights[0:PAIRS], weights[PAIRS:HEADS]], axis=1)
@@ -583,7 +588,7 @@
     weights = jnp.concatenate([w_high, w_middle, w_low, w_high, w_middle, w_high], axis=0)
     weights = weights.astype(bf16)
     for j in range(keys):
-        total = total_ref[PAIRS * j : PAIRS * (j + 1), :]
+        total = total_ref[pl.ds(j, PAIRS, stride=keys), :]
         high = total.astype(bf16).astype(f32)
         middle = (total - high).astype(bf16).astype(f32)
         low = total - high - middle
@@ -598,13 +603,13 @@
 
 
 def pair_back(parts, hat, rstd, pair_gain, w_bias_t):
-    keys = parts.shape[1] // PAIRS
+    keys = parts.shape[2]
     rows = hat.shape[0] // keys
     out = pl.pallas_call(
         grad_kernel,
         out_shape=jax.ShapeDtypeStruct((rows * keys, CZ), f32),
         scratch_shapes=[pltpu.VMEM((keys * PAIRS, 2 * rows), f32)],
-        compiler_params=pltpu.CompilerParams(vmem_limit_bytes=GRANT),
+        compiler_params=pltpu.CompilerParams(vmem_limit_bytes=16 << 20),
         cost_estimate=pl.CostEstimate(flops=10**8, bytes_accessed=4 * 10**6, transcendentals=0),
         name="pair_grad",
     )(parts, hat, rstd, pair_gain.reshape(1, CZ), w_bias_t)
@@ -626,7 +631,7 @@
 ):
     batch, atom_rows, _ = atom_feats.shape
     tok_rows = token_single.shape[0]
-    shard, shards = lax.axis_index("tok"), lax.axis_size("tok")
+    shards = lax.axis_size("tok")
     groups = lax.axis_size("samp")
 
     steps = [(i, i + 1) for i in range(shards - 1)]
@@ -635,18 +640,16 @@
 
     w_bias_t = w_bias.T
     local_bias = pair_bias(pair, pair_gain, w_bias_t, groups)
-    bias = lax.all_to_all(local_bias, "samp", 0, 0).reshape(-1, 2 * tok_rows)
-
-    reach = -(-(atom_rows + 2 * HALO) // 128) * 128
-    flags = jnp.pad(atom_mask.astype(f32), (HALO, reach - atom_rows - HALO))
-    flags = lax.dynamic_slice(flags, (shard * atom_rows,), (reach,)).reshape(reach // 128, 128)
-    flags, local_bias = lax.optimization_barrier((flags, local_bias))
+    bias = lax.all_to_all(local_bias, "samp", 0, 0).reshape(groups, PAIRS, -1, 2 * tok_rows)
+
+    mask = atom_mask.reshape(-1, 128)
+    mask, local_bias = lax.optimization_barrier((mask, local_bias))
 
     ahead = batch // 2
     tokens, gathered = [], []
     for first, size in ((0, ahead), (ahead, batch - ahead)):
         tok, normed = atom_stage(
-            first, size, atom_feats, left, right, flags, atom_counts, token_single, w_atom_qkv,
+            first, size, atom_feats, left, right, mask, atom_counts, token_single, w_atom_qkv,
             w_atom_out, w_embed,
         )
         tokens.append(tok)
@@ -656,7 +659,7 @@
         gathered[1], bias, *tokens, att_a, cotangent, probs_a, values_a, w_qkv, w_out, w_gate,
         w_up, w_down,
     )
-    parts = lax.all_to_all(d_bias.reshape(groups, -1, 2 * tok_rows), "samp", 0, 0)
+    parts = lax.all_to_all(d_bias, "samp", 0, 0)
     token_out, hat, rstd = output_stage(resid, hidden, w_down, pair)
     pair_grad = pair_back(parts, hat, rstd, pair_gain, w_bias_t)
     token_out = token_out.reshape(batch, tok_rows, C_TOK)

time: 100 us -> 100 us (level)
  Pallas kernels: 62.1 us -> 48.9 us
  local copies, waits for them, and re-layouts: 5.18 us -> 18.1 us
    unnamed x20 -> x56, local copies, waits for them, and re-layouts: 3.67 us -> 17.3 us
    pallas_call x1, Pallas kernels: 7.99 us -> 4.01 us  [attend_stage(): pl.pallas_call(functools.partial(attend_kernel, count=len(pieces)), in_sp...]
    pallas_call x1, Pallas kernels: 6.35 us -> 3.39 us  [output_stage(): pl.pallas_call(output_kernel, out_shape=[jax.ShapeDtypeStruct(resid.shape...]
    pallas_call x1, Pallas kernels: 14.8 us -> 11.9 us  [token_stage(): pl.pallas_call(functools.partial(token_kernel, count=len(pieces)), in_spe...]
    ppermute x6, waiting for transfers between devices: 0.52 us -> 2.75 us  [swap(): lax.ppermute(values, axis, [(i, i ^ k) for i in range(lax.axis_size(axis))])]
    pallas_call x2, Pallas kernels: 25.8 us -> 24.1 us  [atom_stage(): pl.pallas_call(atom_kernel, grid=(batch,), in_specs=[of_sample(atoms, C_A...]
    all_to_all x2, waiting for transfers between devices: 8.3 us -> 6.54 us  [the longest x1 6.54 us: body(): parts = lax.all_to_all(d_bias, 'samp', 0, 0)]
    pallas_call x1, Pallas kernels: 4.1 us -> 2.5 us  [pair_back(): pl.pallas_call(grad_kernel, out_shape=jax.ShapeDtypeStruct((rows * keys,...]
  transfers between devices with their start and end apart: 10 -> 10, of which waited for: 2 -> 2; matrix products, arithmetic and copies ran while one was open for 1% -> 0% of each run, Pallas kernels for 43% -> 35%
where the time goes in v4:
time: 100 us; the launch traced here: 99.3 us
  Pallas kernels  48.9 us (49%)
  starting transfers between devices  22.1 us (22%)
  local copies, waits for them, and re-layouts  18.1 us (18%)
  waiting for transfers between devices  9.29 us (9%)
    pallas_call x2, Pallas kernels, atom_stage(): pl.pallas_call(atom_kernel, grid=(batch,), in_specs=[of_sample(atoms, C_A...  24.1 us
    unnamed x56, local copies, waits for them, and re-layouts  17.3 us
    pallas_call x1, Pallas kernels, token_stage(): pl.pallas_call(functools.partial(token_kernel, count=len(pieces)), in_spe...  11.9 us
    all_to_all x1, starting transfers between devices, body(): lax.all_to_all(local_bias, 'samp', 0, 0)  7.28 us
    all_to_all x1, waiting for transfers between devices, body(): parts = lax.all_to_all(d_bias, 'samp', 0, 0)  6.54 us
    all_to_all x1, starting transfers between devices, body(): parts = lax.all_to_all(d_bias, 'samp', 0, 0)  5.84 us
    ppermute x6, starting transfers between devices, swap(): lax.ppermute(values, axis, [(i, i ^ k) for i in range(lax.axis_size(axis))])  4.64 us
    pallas_call x1, Pallas kernels, attend_stage(): pl.pallas_call(functools.partial(attend_kernel, count=len(pieces)), in_sp...  4.01 us
  transfers between devices with their start and end apart: 10, of which 2 were waited for; matrix products, arithmetic and copies ran while one was open for 0% of the time, Pallas kernels for 35%

profile of v4, /device:TPU:0, one launch (start us, length us, event | category | flops | bytes accessed | tf_op | source)
XLA Modules:
  0.0 99.3 jit_solution(5690556938620017175)
XLA Ops:
  0.6 0.8 fusion
  1.5 1.3 %collective-permute-start.1 = (bf16[4,48,128]{2,1,0:T(8,128)(2,1)S(1)}, bf16[4,48,128]{2,1,0:T(8,128)(2,1)S(1)}, u32[]{:S(2)}, u32[]{:S(2)}) collective-permute-start(bf16[4,48,128]{2,1,0:T(8,128)(2,1)S(1)} %get-tuple-element.30), channel_id=1, source_target_pairs={{1,0},{2,1},{3,2},{5,4},{6,5},{7,6},{9,8},{10,9},{11,10},{13,12},{... | collective-permute-start | bytes 147464 | tf_op jit(solution)/shard_map/ppermute | solution.py:639
  2.8 3.0 %collective-permute-start = (bf16[4,48,128]{2,1,0:T(8,128)(2,1)S(1)}, bf16[4,48,128]{2,1,0:T(8,128)(2,1)S(1)}, u32[]{:S(2)}, u32[]{:S(2)}) collective-permute-start(bf16[4,48,128]{2,1,0:T(8,128)(2,1)S(1)} %get-tuple-element.31), channel_id=1, source_target_pairs={{0,1},{1,2},{2,3},{4,5},{5,6},{6,7},{8,9},{9,10},{10,11},{12,13},{... | collective-permute-start | bytes 147464 | tf_op jit(solution)/shard_map/ppermute | solution.py:638
  5.8 3.1 %pair_bias.1 = bf16[8,256,128]{2,1,0:T(8,128)(2,1)} custom-call(bf16[64,32,128]{2,1,0:T(8,128)(2,1)} %pair_ref.3, f32[1,128]{1,0:T(1,128)} %bitcast.10, bf16[16,128]{1,0:T(8,128)(2,1)} %bitcast.8), custom_call_target="tpu_custom_call" | custom-call | flops 10000000 | bytes 10000000 | tf_op jit(solution)/shard_map/pair_bias/pallas_call | solution.py:85
  8.9 7.3 %all-to-all-start = ((bf16[8,256,128]{2,1,0:T(8,128)(2,1)}), bf16[8,256,128]{2,1,0:T(8,128)(2,1)S(1)}, u32[]{:S(2)}, u32[]{:S(2)}) async-start(bf16[8,256,128]{2,1,0:T(8,128)(2,1)} %pair_bias.1), calls=%async_computation | async-start | bytes 1048576 | tf_op jit(solution)/shard_map/all_to_all | solution.py:643
  17.4 12.0 %atoms.3 = (f32[2,64,768]{2,1,0:T(8,128)}, bf16[2,64,768]{2,1,0:T(8,128)(2,1)}) custom-call(bf16[4,1280,128]{2,1,0:T(8,128)(2,1)} %feats_ref.3, bf16[4,48,128]{2,1,0:T(8,128)(2,1)} %copy-done.27, bf16[4,48,128]{2,1,0:T(8,128)(2,1)} %copy-done.26, s32[40,128]{1,0:T(8,128)} %bitcast.14, s32[1,64]{1,0:T(1,128)} %counts_ref.3, bf16[64,768]{1,0:T(8,128)(2,1)} %single_ref.3, ...), custom_call_target="tpu_custom_call" | custom-call | flops 10000000000 | bytes 4000000 | tf_op jit(solution)/shard_map/atoms/pallas_call | solution.py:236
  29.7 2.3 %collective-permute-start.6 = (bf16[2,64,768]{2,1,0:T(8,128)(2,1)}, bf16[2,64,768]{2,1,0:T(8,128)(2,1)S(1)}, u32[]{:S(2)}, u32[]{:S(2)}) collective-permute-start(bf16[2,64,768]{2,1,0:T(8,128)(2,1)} %get-tuple-element.20.refs_0_), channel_id=1, source_target_pairs={{0,2},{1,3},{2,0},{3,1},{4,6},{5,7},{6,4},{7,5},{8,10},{9,11},{10,... | collective-permute-start | bytes 589832 | tf_op jit(solution)/shard_map/ppermute | solution.py:620
  31.9 12.0 %atoms.2 = (f32[2,64,768]{2,1,0:T(8,128)}, bf16[2,64,768]{2,1,0:T(8,128)(2,1)}) custom-call(bf16[4,1280,128]{2,1,0:T(8,128)(2,1)} %feats_ref.3, bf16[4,48,128]{2,1,0:T(8,128)(2,1)} %copy-done.27, bf16[4,48,128]{2,1,0:T(8,128)(2,1)} %copy-done.26, s32[40,128]{1,0:T(8,128)} %bitcast.15, s32[1,64]{1,0:T(1,128)} %counts_ref.3, bf16[64,768]{1,0:T(8,128)(2,1)} %single_ref.3, ...), custom_call_target="tpu_custom_call" | custom-call | flops 10000000000 | bytes 4000000 | tf_op jit(solution)/shard_map/atoms/pallas_call | solution.py:236
  44.5 1.6 %collective-permute-start.3 = (bf16[2,64,768]{2,1,0:T(8,128)(2,1)}, bf16[2,64,768]{2,1,0:T(8,128)(2,1)S(1)}, u32[]{:S(2)}, u32[]{:S(2)}) collective-permute-start(bf16[2,64,768]{2,1,0:T(8,128)(2,1)} %get-tuple-element.17.refs_0_), channel_id=1, source_target_pairs={{0,2},{1,3},{2,0},{3,1},{4,6},{5,7},{6,4},{7,5},{8,10},{9,11},{10,... | collective-permute-start | bytes 589832 | tf_op jit(solution)/shard_map/ppermute | solution.py:620
  46.1 2.0 %copy-done.13 = bf16[768,2304]{1,0:T(8,128)(2,1)S(1)} copy-done((bf16[768,2304]{1,0:T(8,128)(2,1)S(1)}, bf16[768,2304]{1,0:T(8,128)(2,1)}, u32[]{:S(2)}) %copy-start.13) | copy-done | bytes 3538968
  48.2 4.0 %attend.1 = (bf16[128,768]{1,0:T(8,128)(2,1)S(1)}, f32[2,8,256,128]{3,2,1,0:T(8,128)S(1)}, bf16[2,256,768]{2,1,0:T(8,128)(2,1)S(1)}) custom-call(bf16[2,64,768]{2,1,0:T(8,128)(2,1)S(1)} %copy-done.19, bf16[2,64,768]{2,1,0:T(8,128)(2,1)S(1)} %collective-permute-done.5.refs_1_, bf16[2,64,768]{2,1,0:T(8,128)(2,1)S(1)} %collective-permute-done.6.refs_2_, ...), custom_call_target="tpu_custom_call" | custom-call | flops 4000000000 | bytes 10000000 | tf_op jit(solution)/shard_map/attend/pallas_call | solution.py:383
  52.2 0.7 copy-done.17
  52.9 2.7 %collective-permute-done.3.refs_2_ = bf16[2,64,768]{2,1,0:T(8,128)(2,1)S(1)} collective-permute-done((bf16[2,64,768]{2,1,0:T(8,128)(2,1)}, bf16[2,64,768]{2,1,0:T(8,128)(2,1)S(1)}, u32[]{:S(2)}, u32[]{:S(2)}) %collective-permute-start.3) | collective-permute-done | bytes 196640 | tf_op jit(solution)/shard_map/ppermute | solution.py:620
  55.6 0.7 copy-done.20
  56.3 0.7 copy-done.22
  57.0 0.9 copy-done.18
  57.9 0.9 copy-done.21
  58.9 0.9 copy-done.23
  59.8 11.9 %tokens.1 = (f32[256,768]{1,0:T(8,128)S(1)}, bf16[256,1536]{1,0:T(8,128)(2,1)S(1)}, bf16[8,8,32,128]{3,2,1,0:T(8,128)(2,1)S(1)}) custom-call(bf16[2,64,768]{2,1,0:T(8,128)(2,1)S(1)} %copy-done.16, bf16[2,64,768]{2,1,0:T(8,128)(2,1)S(1)} %copy-done.23, bf16[2,64,768]{2,1,0:T(8,128)(2,1)S(1)} %copy-done.21, bf16[2,64,768]{2,1,0:T(8,128)(2,1)S(1)} %copy-done.18, ...), custom_call_target="tpu_custom_call" | custom-call | flops 10000000000 | bytes 20000000 | tf_op jit(solution)/shard_map/tokens/pallas_call | solution.py:502
  71.7 0.9 copy-done.6
  72.6 0.9 copy-done.8
  73.5 0.8 copy-done.10
  74.3 5.8 %all-to-all-start.1 = ((bf16[8,8,32,128]{3,2,1,0:T(8,128)(2,1)}), bf16[8,8,32,128]{3,2,1,0:T(8,128)(2,1)S(1)}, u32[]{:S(2)}, u32[]{:S(2)}) async-start(bf16[8,8,32,128]{3,2,1,0:T(8,128)(2,1)} %copy-done.10), calls=%async_computation.1 | async-start | bytes 1048576 | tf_op jit(solution)/shard_map/all_to_all | solution.py:662
  80.2 1.1 %copy-done.7 = f32[256,768]{1,0:T(8,128)S(1)} copy-done((f32[256,768]{1,0:T(8,128)S(1)}, f32[256,768]{1,0:T(8,128)}, u32[]{:S(2)}) %copy-start.7) | copy-done | bytes 786456
  81.3 1.1 %copy-done.9 = bf16[256,1536]{1,0:T(8,128)(2,1)S(1)} copy-done((bf16[256,1536]{1,0:T(8,128)(2,1)S(1)}, bf16[256,1536]{1,0:T(8,128)(2,1)}, u32[]{:S(2)}) %copy-start.9) | copy-done | bytes 786456
  82.4 3.4 %output.1 = (bf16[256,768]{1,0:T(8,128)(2,1)}, f32[2048,128]{1,0:T(8,128)S(1)}, f32[2048,128]{1,0:T(8,128)S(1)}) custom-call(f32[256,768]{1,0:T(8,128)S(1)} %copy-done.7, bf16[256,1536]{1,0:T(8,128)(2,1)S(1)} %copy-done.9, bf16[1536,768]{1,0:T(8,128)(2,1)S(1)} %copy-done, bf16[64,32,128]{2,1,0:T(8,128)(2,1)S(1)} %copy-done.1), custom_call_target="tpu_custom_call" | custom-call | flops 1000000000 | bytes 8000000 | tf_op jit(solution)/shard_map/output/pallas_call | solution.py:561
  85.8 1.0 copy-done.2
  86.8 1.0 %copy-done.4 = f32[2048,128]{1,0:T(8,128)} copy-done((f32[2048,128]{1,0:T(8,128)}, f32[2048,128]{1,0:T(8,128)S(1)}, u32[]{:S(2)}) %copy-start.4) | copy-done | bytes 1048600
  87.8 6.5 %all-to-all-done.1.parts_ref = bf16[8,8,32,128]{3,2,1,0:T(8,128)(2,1)S(1)} async-done(((bf16[8,8,32,128]{3,2,1,0:T(8,128)(2,1)}), bf16[8,8,32,128]{3,2,1,0:T(8,128)(2,1)S(1)}, u32[]{:S(2)}, u32[]{:S(2)}) %all-to-all-start.1) | async-done | bytes 524320 | tf_op jit(solution)/shard_map/all_to_all | solution.py:662
  94.3 1.2 %copy-done.3 = f32[2048,128]{1,0:T(8,128)S(1)} copy-done((f32[2048,128]{1,0:T(8,128)S(1)}, f32[2048,128]{1,0:T(8,128)}, u32[]{:S(2)}) %copy-start.3) | copy-done | bytes 1048600
  95.5 1.2 %copy-done.5 = f32[2048,128]{1,0:T(8,128)S(1)} copy-done((f32[2048,128]{1,0:T(8,128)S(1)}, f32[2048,128]{1,0:T(8,128)}, u32[]{:S(2)}) %copy-start.5) | copy-done | bytes 1048600
  96.8 2.5 %pair_grad.1 = f32[2048,128]{1,0:T(8,128)} custom-call(bf16[8,8,32,128]{3,2,1,0:T(8,128)(2,1)S(1)} %all-to-all-done.1.parts_ref, f32[2048,128]{1,0:T(8,128)S(1)} %copy-done.3, f32[2048,128]{1,0:T(8,128)S(1)} %copy-done.5, f32[1,128]{1,0:T(1,128)S(1)} %bitcast.11, bf16[16,128]{1,0:T(8,128)(2,1)S(1)} %bitcast.9), custom_call_target="tpu_custom_call" | custom-call | flops 100000000 | bytes 4000000 | tf_op jit(solution)/shard_map/pair_grad/pallas_call | solution.py:608
  (52 shorter events, 2.1 us)
Async XLA Ops:
  1.5 14.7 %collective-permute-start.1 = (bf16[4,48,128]{2,1,0:T(8,128)(2,1)S(1)}, bf16[4,48,128]{2,1,0:T(8,128)(2,1)S(1)}, u32[]{:S(2)}, u32[]{:S(2)}) collective-permute-start(bf16[4,48,128]{2,1,0:T(8,128)(2,1)S(1)} %get-tuple-element.30), channel_id=1, source_target_pairs={{1,0},{2,1},{3,2},{5,4},{6,5},{7,6},{9,8},{10,9},{11,10},{13,12},{... | collective-permute-start | bytes 147464 | tf_op jit(solution)/shard_map/ppermute | solution.py:639
  2.8 13.4 %collective-permute-start = (bf16[4,48,128]{2,1,0:T(8,128)(2,1)S(1)}, bf16[4,48,128]{2,1,0:T(8,128)(2,1)S(1)}, u32[]{:S(2)}, u32[]{:S(2)}) collective-permute-start(bf16[4,48,128]{2,1,0:T(8,128)(2,1)S(1)} %get-tuple-element.31), channel_id=1, source_target_pairs={{0,1},{1,2},{2,3},{4,5},{5,6},{6,7},{8,9},{9,10},{10,11},{12,13},{... | collective-permute-start | bytes 147464 | tf_op jit(solution)/shard_map/ppermute | solution.py:638
  8.9 37.3 %all-to-all-start = ((bf16[8,256,128]{2,1,0:T(8,128)(2,1)}), bf16[8,256,128]{2,1,0:T(8,128)(2,1)S(1)}, u32[]{:S(2)}, u32[]{:S(2)}) async-start(bf16[8,256,128]{2,1,0:T(8,128)(2,1)} %pair_bias.1), calls=%async_computation | async-start | bytes 1048576 | tf_op jit(solution)/shard_map/all_to_all | solution.py:643
  29.4 16.7 %copy-start.19 = (bf16[2,64,768]{2,1,0:T(8,128)(2,1)S(1)}, bf16[2,64,768]{2,1,0:T(8,128)(2,1)}, u32[]{:S(2)}) copy-start(bf16[2,64,768]{2,1,0:T(8,128)(2,1)} %get-tuple-element.20.refs_0_) | copy-start | bytes 589828
  29.4 16.7 %collective-permute-start.7 = (bf16[2,64,768]{2,1,0:T(8,128)(2,1)}, bf16[2,64,768]{2,1,0:T(8,128)(2,1)S(1)}, u32[]{:S(2)}, u32[]{:S(2)}) collective-permute-start(bf16[2,64,768]{2,1,0:T(8,128)(2,1)} %get-tuple-element.20.refs_0_), channel_id=1, source_target_pairs={{0,3},{1,2},{2,1},{3,0},{4,7},{5,6},{6,5},{7,4},{8,11},{9,10},{10,... | collective-permute-start | bytes 589832 | tf_op jit(solution)/shard_map/ppermute | solution.py:620
  29.7 16.4 %collective-permute-start.6 = (bf16[2,64,768]{2,1,0:T(8,128)(2,1)}, bf16[2,64,768]{2,1,0:T(8,128)(2,1)S(1)}, u32[]{:S(2)}, u32[]{:S(2)}) collective-permute-start(bf16[2,64,768]{2,1,0:T(8,128)(2,1)} %get-tuple-element.20.refs_0_), channel_id=1, source_target_pairs={{0,2},{1,3},{2,0},{3,1},{4,6},{5,7},{6,4},{7,5},{8,10},{9,11},{10,... | collective-permute-start | bytes 589832 | tf_op jit(solution)/shard_map/ppermute | solution.py:620
  31.9 14.2 %collective-permute-start.5 = (bf16[2,64,768]{2,1,0:T(8,128)(2,1)}, bf16[2,64,768]{2,1,0:T(8,128)(2,1)S(1)}, u32[]{:S(2)}, u32[]{:S(2)}) collective-permute-start(bf16[2,64,768]{2,1,0:T(8,128)(2,1)} %get-tuple-element.20.refs_0_), channel_id=1, source_target_pairs={{0,1},{1,0},{2,3},{3,2},{4,5},{5,4},{6,7},{7,6},{8,9},{9,8},{10,11... | collective-permute-start | bytes 589832 | tf_op jit(solution)/shard_map/ppermute | solution.py:620
  44.0 8.2 %collective-permute-start.4 = (bf16[2,64,768]{2,1,0:T(8,128)(2,1)}, bf16[2,64,768]{2,1,0:T(8,128)(2,1)S(1)}, u32[]{:S(2)}, u32[]{:S(2)}) collective-permute-start(bf16[2,64,768]{2,1,0:T(8,128)(2,1)} %get-tuple-element.17.refs_0_), channel_id=1, source_target_pairs={{0,3},{1,2},{2,1},{3,0},{4,7},{5,6},{6,5},{7,4},{8,11},{9,10},{10,... | collective-permute-start | bytes 589832 | tf_op jit(solution)/shard_map/ppermute | solution.py:620
  44.5 11.1 %collective-permute-start.3 = (bf16[2,64,768]{2,1,0:T(8,128)(2,1)}, bf16[2,64,768]{2,1,0:T(8,128)(2,1)S(1)}, u32[]{:S(2)}, u32[]{:S(2)}) collective-permute-start(bf16[2,64,768]{2,1,0:T(8,128)(2,1)} %get-tuple-element.17.refs_0_), channel_id=1, source_target_pairs={{0,2},{1,3},{2,0},{3,1},{4,6},{5,7},{6,4},{7,5},{8,10},{9,11},{10,... | collective-permute-start | bytes 589832 | tf_op jit(solution)/shard_map/ppermute | solution.py:620
  46.1 10.2 %collective-permute-start.2 = (bf16[2,64,768]{2,1,0:T(8,128)(2,1)}, bf16[2,64,768]{2,1,0:T(8,128)(2,1)S(1)}, u32[]{:S(2)}, u32[]{:S(2)}) collective-permute-start(bf16[2,64,768]{2,1,0:T(8,128)(2,1)} %get-tuple-element.17.refs_0_), channel_id=1, source_target_pairs={{0,1},{1,0},{2,3},{3,2},{4,5},{5,4},{6,7},{7,6},{8,9},{9,8},{10,11... | collective-permute-start | bytes 589832 | tf_op jit(solution)/shard_map/ppermute | solution.py:620
  46.1 2.0 %copy-start.13 = (bf16[768,2304]{1,0:T(8,128)(2,1)S(1)}, bf16[768,2304]{1,0:T(8,128)(2,1)}, u32[]{:S(2)}) copy-start(bf16[768,2304]{1,0:T(8,128)(2,1)} %refs_11_.1) | copy-start | bytes 10616836
  48.1 8.8 %copy-start.14 = (bf16[768,768]{1,0:T(8,128)(2,1)S(1)}, bf16[768,768]{1,0:T(8,128)(2,1)}, u32[]{:S(2)}) copy-start(bf16[768,768]{1,0:T(8,128)(2,1)} %refs_12_.1) | copy-start | bytes 3538948
  48.1 8.8 %copy-start.15 = (bf16[4,64,768]{2,1,0:T(8,128)(2,1)S(1)}, bf16[4,64,768]{2,1,0:T(8,128)(2,1)}, u32[]{:S(2)}) copy-start(bf16[4,64,768]{2,1,0:T(8,128)(2,1)} %refs_8_.1) | copy-start | bytes 1179652
  48.1 8.8 %copy-start.16 = (bf16[2,64,768]{2,1,0:T(8,128)(2,1)S(1)}, bf16[2,64,768]{2,1,0:T(8,128)(2,1)}, u32[]{:S(2)}) copy-start(bf16[2,64,768]{2,1,0:T(8,128)(2,1)} %get-tuple-element.17.refs_0_) | copy-start | bytes 589828
  48.1 8.8 %copy-start.24 = (f32[2,64,768]{2,1,0:T(8,128)S(1)}, f32[2,64,768]{2,1,0:T(8,128)}, u32[]{:S(2)}) copy-start(f32[2,64,768]{2,1,0:T(8,128)} %get-tuple-element.18.refs_5_) | copy-start | bytes 1179652
  48.1 8.8 %copy-start.25 = (f32[2,64,768]{2,1,0:T(8,128)S(1)}, f32[2,64,768]{2,1,0:T(8,128)}, u32[]{:S(2)}) copy-start(f32[2,64,768]{2,1,0:T(8,128)} %get-tuple-element.19.refs_6_) | copy-start | bytes 1179652
  57.0 0.9 copy-start.18
  57.9 0.9 copy-start.21
  58.8 0.9 copy-start.23
  59.8 20.3 %copy-start = (bf16[1536,768]{1,0:T(8,128)(2,1)S(1)}, bf16[1536,768]{1,0:T(8,128)(2,1)}, u32[]{:S(2)}) copy-start(bf16[1536,768]{1,0:T(8,128)(2,1)} %w_down_ref.1) | copy-start | bytes 7077892
  59.8 20.4 %copy-start.1 = (bf16[64,32,128]{2,1,0:T(8,128)(2,1)S(1)}, bf16[64,32,128]{2,1,0:T(8,128)(2,1)}, u32[]{:S(2)}) copy-start(bf16[64,32,128]{2,1,0:T(8,128)(2,1)} %pair_ref.3) | copy-start | bytes 1572868
  71.7 0.9 copy-start.6
  72.6 0.9 copy-start.8
  74.3 20.0 %copy-start.11 = (bf16[128,16]{0,1:T(8,128)(2,1)S(1)}, bf16[128,16]{0,1:T(8,128)(2,1)}, u32[]{:S(2)}) copy-start(bf16[128,16]{0,1:T(8,128)(2,1)} %param.22) | copy-start | bytes 12292
  74.3 20.0 %all-to-all-start.1 = ((bf16[8,8,32,128]{3,2,1,0:T(8,128)(2,1)}), bf16[8,8,32,128]{3,2,1,0:T(8,128)(2,1)S(1)}, u32[]{:S(2)}, u32[]{:S(2)}) async-start(bf16[8,8,32,128]{3,2,1,0:T(8,128)(2,1)} %copy-done.10), calls=%async_computation.1 | async-start | bytes 1048576 | tf_op jit(solution)/shard_map/all_to_all | solution.py:662
  80.1 14.2 %copy-start.12 = (f32[128]{0:T(128)S(1)}, f32[128]{0:T(128)}, u32[]{:S(2)}) copy-start(f32[128]{0:T(128)} %param.21) | copy-start | bytes 1540
  80.1 1.1 %copy-start.7 = (f32[256,768]{1,0:T(8,128)S(1)}, f32[256,768]{1,0:T(8,128)}, u32[]{:S(2)}) copy-start(f32[256,768]{1,0:T(8,128)} %copy-done.6) | copy-start | bytes 2359300
  81.3 1.1 %copy-start.9 = (bf16[256,1536]{1,0:T(8,128)(2,1)S(1)}, bf16[256,1536]{1,0:T(8,128)(2,1)}, u32[]{:S(2)}) copy-start(bf16[256,1536]{1,0:T(8,128)(2,1)} %copy-done.8) | copy-start | bytes 2359300
  85.8 1.0 copy-start.2
  86.8 1.0 %copy-start.4 = (f32[2048,128]{1,0:T(8,128)}, f32[2048,128]{1,0:T(8,128)S(1)}, u32[]{:S(2)}) copy-start(f32[2048,128]{1,0:T(8,128)S(1)} %get-tuple-element.29.rstd_ref) | copy-start | bytes 3145732
  94.3 1.2 %copy-start.3 = (f32[2048,128]{1,0:T(8,128)S(1)}, f32[2048,128]{1,0:T(8,128)}, u32[]{:S(2)}) copy-start(f32[2048,128]{1,0:T(8,128)} %copy-done.2) | copy-start | bytes 3145732
  95.5 1.2 %copy-start.5 = (f32[2048,128]{1,0:T(8,128)S(1)}, f32[2048,128]{1,0:T(8,128)}, u32[]{:S(2)}) copy-start(f32[2048,128]{1,0:T(8,128)} %copy-done.4) | copy-start | bytes 3145732
  (6 other events, 4.1 us)

commit v5 on v4

--- a/solution.py
+++ b/solution.py
@@ -16,6 +16,7 @@
 CZ = 128
 HALO = 48
 PAIRS = HEADS // 2
+GRANT = 64 << 20
 LOG2E = 1.4426950408889634
 
 epsilon = 1e-05
@@ -89,7 +90,7 @@
             pltpu.VMEM((rows * keys, CZ), f32),
             pltpu.VMEM((keys * PAIRS, 2 * rows), f32),
         ],
-        compiler_params=pltpu.CompilerParams(vmem_limit_bytes=60 << 20),
+        compiler_params=pltpu.CompilerParams(vmem_limit_bytes=GRANT),
         cost_estimate=pl.CostEstimate(flops=10**7, bytes_accessed=10**7, transcendentals=0),
         name="pair_bias",
     )(pair, pair_gain.reshape(1, CZ), w_bias_t)
@@ -97,61 +98,59 @@
 
 def atom_kernel(
     feats_ref, left_ref, right_ref, mask_ref, counts_ref, single_ref, w_qkv_ref, w_out_ref,
-    w_embed_ref, tokens_ref, normed_ref, xn_ref, qkv_ref, scores_a, scores_b, probs_a, probs_b,
-    mixed_ref, updated_ref, split_ref, keybias_ref, onehot_ref, counts_col_ref,
+    w_embed_ref, tokens_ref, normed_ref, padded_ref, qkv_a, qkv_b, scores_a, scores_b, probs_a,
+    probs_b, mixed_ref, split_ref, keybias_ref, onehot_ref, pooled_ref,
 ):
-    atoms = feats_ref.shape[1]
+    batch, atoms = feats_ref.shape[0], feats_ref.shape[1]
     padded = atoms + 2 * HALO
     tok_rows = single_ref.shape[0]
-
-    @pl.when(pl.program_id(0) == 0)
-    def prepare():
-        eye = iota((128, 128), 0) == iota((128, 128), 1)
-        blocks = atoms // 128
-        for b in range(-1, blocks + 1):
-            at = lax.axis_index("tok") * blocks + b
-            inside = jnp.where((at >= 0) & (at < mask_ref.shape[0]), 1, 0)
-            row = mask_ref[pl.ds(jnp.clip(at, 0, mask_ref.shape[0] - 1), 1), :] * inside
-            row = jnp.broadcast_to(row.astype(f32), (128, 128))
-            col = jnp.sum(jnp.where(eye, row, 0.0), axis=1, keepdims=True)
-            col = jnp.broadcast_to((col - 1.0) * 1e30, (128, 128))
-            if b < 0:
-                keybias_ref[0:HALO, :] = col[128 - HALO : 128]
-            elif b < blocks:
-                keybias_ref[HALO + 128 * b : HALO + 128 * b + 128, :] = col
-            else:
-                keybias_ref[HALO + atoms : padded, :] = col[0:HALO]
-        counts = jnp.broadcast_to(counts_ref[...].astype(f32), (tok_rows, tok_rows))
-        sub, lane = iota((tok_rows, tok_rows), 0), iota((tok_rows, tok_rows), 1)
-        start = jnp.sum(jnp.where(lane < sub, counts, 0.0), axis=1, keepdims=True)
-        own = jnp.sum(jnp.where(lane == sub, counts, 0.0), axis=1, keepdims=True)
-        counts_col_ref[...] = jnp.broadcast_to(own, (tok_rows, 128))
-        pos = iota((tok_rows, 256), 1).astype(f32)
-        for g in range(atoms // 256):
-            at = pos + float(g * 256)
-            hit = jnp.where((at >= start) & (at < start + own), 1.0, 0.0).astype(bf16)
-            onehot_ref[g] = jnp.concatenate([hit, hit], axis=1)
-
-    xn_ref[0:HALO, :] = norm_rows(left_ref[0].astype(f32))[0].astype(bf16)
-    xn_ref[atoms + HALO : padded, :] = norm_rows(right_ref[0].astype(f32))[0].astype(bf16)
-
-    for i in range(atoms // 256):
-        block = feats_ref[0, 256 * i : 256 * i + 256, :].astype(f32)
-        xn_ref[HALO + 256 * i : HALO + 256 * i + 256, :] = norm_rows(block)[0].astype(bf16)
-    chunk = padded // 4
-    w_qkv = w_qkv_ref[...]
-    for i in range(4):
-        qkv_ref[i * chunk : (i + 1) * chunk, :] = nn(
-            xn_ref[i * chunk : (i + 1) * chunk, :], w_qkv
-        ).astype(bf16)
+    blocks = atoms // 128
+    chunks = atoms // 256
+    qkv_refs = (qkv_a, qkv_b)
+
+    eye = iota((128, 128), 0) == iota((128, 128), 1)
+    for b in range(-1, blocks + 1):
+        at = lax.axis_index("tok") * blocks + b
+        inside = jnp.where((at >= 0) & (at < mask_ref.shape[0]), 1, 0)
+        row = mask_ref[pl.ds(jnp.clip(at, 0, mask_ref.shape[0] - 1), 1), :] * inside
+        row = jnp.broadcast_to(row.astype(f32), (128, 128))
+        col = jnp.sum(jnp.where(eye, row, 0.0), axis=1, keepdims=True)
+        col = jnp.broadcast_to((col - 1.0) * 1e30, (128, 128))
+        if b < 0:
+            keybias_ref[0:HALO, :] = col[128 - HALO : 128]
+        elif b < blocks:
+            keybias_ref[HALO + 128 * b : HALO + 128 * b + 128, :] = col
+        else:
+            keybias_ref[HALO + atoms : padded, :] = col[0:HALO]
+    counts = jnp.broadcast_to(counts_ref[...].astype(f32), (tok_rows, tok_rows))
+    sub, lane = iota((tok_rows, tok_rows), 0), iota((tok_rows, tok_rows), 1)
+    start = jnp.sum(jnp.where(lane < sub, counts, 0.0), axis=1, keepdims=True)
+    own = jnp.sum(jnp.where(lane == sub, counts, 0.0), axis=1, keepdims=True)
+    pos = iota((tok_rows, 256), 1).astype(f32)
+    for g in range(chunks):
+        at = pos + float(g * 256)
+        hit = jnp.where((at >= start) & (at < start + own), 1.0, 0.0).astype(bf16)
+        onehot_ref[g] = jnp.concatenate([hit, hit], axis=1)
+    pooled_ref[...] = jnp.zeros_like(pooled_ref)
+    for s in range(batch):
+        padded_ref[s, 0:HALO, :] = left_ref[s]
+        padded_ref[s, HALO : HALO + atoms, :] = feats_ref[s]
+        padded_ref[s, HALO + atoms : padded, :] = right_ref[s]
 
     head_of = iota((32, 128), 1) // ATOM_HD
     head_mask = [(head_of == h).astype(f32).astype(bf16) for h in range(ATOM_HEADS)]
     own_atom = (iota((32, 128), 1) % 32) == iota((32, 128), 0)
     factor = ATOM_HD ** (-0.5) * LOG2E
-    groups = atoms // 128
-
-    def score_step(group, to_ref):
+    stride = padded // chunks // 16 * 16
+    span = padded - stride * (chunks - 1)
+
+    def qkv_step(s, i):
+        at = pl.multiple_of(i * stride, 16)
+        normed, unused = norm_rows(padded_ref[s, pl.ds(at, span), :].astype(f32))
+        qkv_refs[s % 2][pl.ds(at, span), :] = nn(normed.astype(bf16), w_qkv_ref[...]).astype(bf16)
+
+    def score_step(s, group, to_ref):
+        qkv_ref = qkv_refs[s % 2]
         for k in range(2):
             base = pl.multiple_of(group * 128 + 64 * k, 64)
             queries = qkv_ref[pl.ds(base + HALO, 64), 0:C_ATOM]
@@ -179,7 +178,8 @@
                 weights = expo * (1.0 / jnp.sum(expo, axis=0, keepdims=True))
                 to_ref[2 * k + w] = weights.astype(bf16)
 
-    def value_step(group, from_ref):
+    def value_step(s, group, from_ref):
+        qkv_ref = qkv_refs[s % 2]
         for k in range(2):
             base = pl.multiple_of(group * 128 + 64 * k, 64)
             mixes = []
@@ -190,76 +190,85 @@
                 for h in range(1, ATOM_HEADS):
                     mix = jnp.where(head_of == h, part[32 * h : 32 * h + 32], mix)
                 mixes.append(mix.astype(bf16))
-            mixed_ref[pl.ds(base, 64), :] = jnp.concatenate(mixes, axis=0)
-
-    score_step(0, scores_a)
-
-    def window_step(i, carry):
-        even, odd = 2 * i, 2 * i + 1
-        score_step(odd, scores_b)
-        softmax_step(even, scores_a, probs_a)
-        value_step(jnp.maximum(even - 1, 0), probs_b)
-        score_step(jnp.minimum(odd + 1, groups - 1), scores_a)
-        softmax_step(odd, scores_b, probs_b)
-        value_step(even, probs_a)
-        return carry
-
-    lax.fori_loop(0, groups // 2, window_step, 0)
-    value_step(groups - 1, probs_b)
-
-    w_out = w_out_ref[...]
-    for g in range(atoms // 256):
-        part = slice(256 * g, 256 * g + 256)
-        feats = feats_ref[0, part, :].astype(f32)
-        updated_ref[part, :] = (feats + nn(mixed_ref[part, :], w_out)).astype(bf16)
-    pooled = jnp.zeros((tok_rows, C_TOK), f32)
-    for g in range(atoms // 256):
-        embedded = jnp.maximum(
-            nn(updated_ref[256 * g : 256 * g + 256, :], w_embed_ref[...]), 0.0
-        )
+            mixed_ref[s, pl.ds(base, 64), :] = jnp.concatenate(mixes, axis=0)
+
+    def embed_step(s, g):
+        base = pl.multiple_of(g * 256, 256)
+        feats = feats_ref[s, pl.ds(base, 256), :].astype(f32)
+        updated = (feats + nn(mixed_ref[s, pl.ds(base, 256), :], w_out_ref[...])).astype(bf16)
+        embedded = jnp.maximum(nn(updated, w_embed_ref[...]), 0.0)
         high = embedded.astype(bf16)
-        split_ref[g, 0:256, :] = high
-        split_ref[g, 256:512, :] = (embedded - high.astype(f32)).astype(bf16)
-        pooled = pooled + nn(onehot_ref[g], split_ref[g])
-    tokens = pooled / counts_col_ref[:, 0:1] + single_ref[...].astype(f32)
-    tokens_ref[0] = tokens
-    normed_ref[0] = norm_rows(tokens)[0].astype(bf16)
-
-
-def atom_stage(first, batch, feats, left, right, mask, counts, single, w_qkv, w_out, w_embed):
+        split_ref[0:256, :] = high
+        split_ref[256:512, :] = (embedded - high.astype(f32)).astype(bf16)
+        pooled_ref[s] += nn(onehot_ref[g], split_ref[...])
+
+    for i in range(chunks):
+        qkv_step(0, i)
+    for s in range(batch):
+        score_step(s, 0, scores_a)
+
+        def window_step(i, carry, s=s, lagging=True):
+            even, odd = 2 * i, 2 * i + 1
+            if lagging:
+                embed_step(s, i - 2)
+            if s + 1 < batch:
+                qkv_step(s + 1, i)
+            score_step(s, odd, scores_b)
+            softmax_step(even, scores_a, probs_a)
+            value_step(s, jnp.maximum(even - 1, 0), probs_b)
+            score_step(s, jnp.minimum(odd + 1, 2 * chunks - 1), scores_a)
+            softmax_step(odd, scores_b, probs_b)
+            value_step(s, even, probs_a)
+            return carry
+
+        for i in range(2):
+            if s > 0:
+                embed_step(s - 1, chunks - 2 + i)
+            window_step(i, 0, lagging=False)
+        lax.fori_loop(2, chunks, window_step, 0)
+        value_step(s, 2 * chunks - 1, probs_b)
+    for i in range(2):
+        embed_step(batch - 1, chunks - 2 + i)
+    for s in range(batch):
+        tokens = pooled_ref[s] / own + single_ref[...].astype(f32)
+        tokens_ref[s] = tokens
+        normed_ref[s] = norm_rows(tokens)[0].astype(bf16)
+
+
+def atom_stage(part, batch, feats, left, right, mask, counts, single, w_qkv, w_out, w_embed):
     atoms = feats.shape[1]
     tok_rows = single.shape[0]
     padded = atoms + 2 * HALO
-    of_sample = lambda rows, cols: pl.BlockSpec((1, rows, cols), lambda s: (s + first, 0, 0))
-    by_sample = lambda rows, cols: pl.BlockSpec((1, rows, cols), lambda s: (s, 0, 0))
-    whole = lambda a: pl.BlockSpec(a.shape, lambda s: (0,) * a.ndim)
+    of_part = lambda rows, cols: pl.BlockSpec((batch, rows, cols), lambda i: (part, 0, 0))
+    whole = lambda a: pl.BlockSpec(a.shape, lambda i: (0,) * a.ndim)
+    every = pl.BlockSpec((batch, tok_rows, C_TOK), lambda i: (0, 0, 0))
     return pl.pallas_call(
         atom_kernel,
-        grid=(batch,),
+        grid=(1,),
         in_specs=[
-            of_sample(atoms, C_ATOM), of_sample(HALO, C_ATOM), of_sample(HALO, C_ATOM),
+            of_part(atoms, C_ATOM), of_part(HALO, C_ATOM), of_part(HALO, C_ATOM),
             whole(mask), whole(counts), whole(single), whole(w_qkv), whole(w_out), whole(w_embed),
         ],
-        out_specs=[by_sample(tok_rows, C_TOK), by_sample(tok_rows, C_TOK)],
+        out_specs=[every, every],
         out_shape=[
             jax.ShapeDtypeStruct((batch, tok_rows, C_TOK), f32),
             jax.ShapeDtypeStruct((batch, tok_rows, C_TOK), bf16),
         ],
         scratch_shapes=[
-            pltpu.VMEM((padded, C_ATOM), bf16),
+            pltpu.VMEM((batch, padded, C_ATOM), bf16),
+            pltpu.VMEM((padded, 3 * C_ATOM), bf16),
             pltpu.VMEM((padded, 3 * C_ATOM), bf16),
             pltpu.VMEM((2, 160, 256), f32),
             pltpu.VMEM((2, 160, 256), f32),
             pltpu.VMEM((4, 128, 128), bf16),
             pltpu.VMEM((4, 128, 128), bf16),
-            pltpu.VMEM((atoms, C_ATOM), bf16),
-            pltpu.VMEM((atoms, C_ATOM), bf16),
-            pltpu.VMEM((atoms // 256, 512, C_TOK), bf16),
+            pltpu.VMEM((batch, atoms, C_ATOM), bf16),
+            pltpu.VMEM((512, C_TOK), bf16),
             pltpu.VMEM((padded, 128), f32),
             pltpu.VMEM((atoms // 256, tok_rows, 512), bf16),
-            pltpu.VMEM((tok_rows, 128), f32),
-        ],
-        compiler_params=pltpu.CompilerParams(vmem_limit_bytes=60 << 20),
+            pltpu.VMEM((batch, tok_rows, C_TOK), f32),
+        ],
+        compiler_params=pltpu.CompilerParams(vmem_limit_bytes=GRANT),
         cost_estimate=pl.CostEstimate(
             flops=10**10, bytes_accessed=4 * 10**6, transcendentals=3 * 10**6
         ),
@@ -394,7 +403,7 @@
             pltpu.SemaphoreType.DMA((3,)),
         ]
         + attend_scratch(batch, tok_rows, keys_all),
-        compiler_params=pltpu.CompilerParams(vmem_limit_bytes=32 << 20),
+        compiler_params=pltpu.CompilerParams(vmem_limit_bytes=GRANT),
         cost_estimate=pl.CostEstimate(
             flops=4 * 10**9, bytes_accessed=10**7, transcendentals=10**6
         ),
@@ -525,7 +534,7 @@
             pltpu.VMEM((rows, hidden), bf16),
             pltpu.VMEM((rows, C_TOK), f32),
         ],
-        compiler_params=pltpu.CompilerParams(vmem_limit_bytes=44 << 20),
+        compiler_params=pltpu.CompilerParams(vmem_limit_bytes=GRANT),
         cost_estimate=pl.CostEstimate(
             flops=10**10, bytes_accessed=2 * 10**7, transcendentals=10**6
         ),
@@ -563,7 +572,7 @@
         out_shape=[jax.ShapeDtypeStruct(resid.shape, bf16)]
         + [jax.ShapeDtypeStruct((rows * keys, CZ), f32)] * 2,
         scratch_shapes=[pltpu.VMEM((rows * keys, CZ), f32)],
-        compiler_params=pltpu.CompilerParams(vmem_limit_bytes=24 << 20),
+        compiler_params=pltpu.CompilerParams(vmem_limit_bytes=GRANT),
         cost_estimate=pl.CostEstimate(
             flops=10**9, bytes_accessed=8 * 10**6, transcendentals=0
         ),
@@ -609,7 +618,7 @@
         grad_kernel,
         out_shape=jax.ShapeDtypeStruct((rows * keys, CZ), f32),
         scratch_shapes=[pltpu.VMEM((keys * PAIRS, 2 * rows), f32)],
-        compiler_params=pltpu.CompilerParams(vmem_limit_bytes=16 << 20),
+        compiler_params=pltpu.CompilerParams(vmem_limit_bytes=GRANT),
         cost_estimate=pl.CostEstimate(flops=10**8, bytes_accessed=4 * 10**6, transcendentals=0),
         name="pair_grad",
     )(parts, hat, rstd, pair_gain.reshape(1, CZ), w_bias_t)
@@ -645,11 +654,11 @@
     mask = atom_mask.reshape(-1, 128)
     mask, local_bias = lax.optimization_barrier((mask, local_bias))
 
-    ahead = batch // 2
+    each = batch // 2
     tokens, gathered = [], []
-    for first, size in ((0, ahead), (ahead, batch - ahead)):
+    for part in range(2):
         tok, normed = atom_stage(
-            first, size, atom_feats, left, right, mask, atom_counts, token_single, w_atom_qkv,
+            part, each, atom_feats, left, right, mask, atom_counts, token_single, w_atom_qkv,
             w_atom_out, w_embed,
         )
         tokens.append(tok)

time: 100 us -> 94.5 us (0.945)
  local copies, waits for them, and re-layouts: 18.1 us -> 1.47 us
  Pallas kernels: 48.9 us -> 59.7 us
    unnamed x56 -> x0, local copies, waits for them, and re-layouts: 17.3 us -> none
    pallas_call x1, Pallas kernels: 4.01 us -> 7.78 us  [attend_stage(): pl.pallas_call(functools.partial(attend_kernel, count=len(pieces)), in_sp...]
    pallas_call x1, Pallas kernels: 3.39 us -> 6.41 us  [output_stage(): pl.pallas_call(output_kernel, out_shape=[jax.ShapeDtypeStruct(resid.shape...]
    pallas_call x1, Pallas kernels: 11.9 us -> 14.1 us  [token_stage(): pl.pallas_call(functools.partial(token_kernel, count=len(pieces)), in_spe...]
    pallas_call x1, Pallas kernels: 2.5 us -> 4.13 us  [pair_back(): pl.pallas_call(grad_kernel, out_shape=jax.ShapeDtypeStruct((rows * keys,...]
    all_to_all x1, waiting for transfers between devices: 6.54 us -> 8.13 us  [body(): parts = lax.all_to_all(d_bias, 'samp', 0, 0)]
  transfers between devices with their start and end apart: 10 -> 10, of which waited for: 2 -> 2; matrix products, arithmetic and copies ran while one was open for 0% -> 0% of each run, Pallas kernels for 35% -> 44%
where the time goes in v5:
time: 94.5 us; the launch traced here: 94 us
  Pallas kernels  59.7 us (63%)
  starting transfers between devices  22.2 us (23%)
  waiting for transfers between devices  9.9 us (10%)
  local copies, waits for them, and re-layouts  1.47 us (2%)
    pallas_call x2, Pallas kernels, atom_stage(): pl.pallas_call(atom_kernel, grid=(1,), in_specs=[of_part(atoms, C_ATOM),...  24.2 us
    pallas_call x1, Pallas kernels, token_stage(): pl.pallas_call(functools.partial(token_kernel, count=len(pieces)), in_spe...  14.1 us
    all_to_all x1, waiting for transfers between devices, body(): parts = lax.all_to_all(d_bias, 'samp', 0, 0)  8.13 us
    pallas_call x1, Pallas kernels, attend_stage(): pl.pallas_call(functools.partial(attend_kernel, count=len(pieces)), in_sp...  7.78 us
    all_to_all x1, starting transfers between devices, body(): lax.all_to_all(local_bias, 'samp', 0, 0)  7.28 us
    pallas_call x1, Pallas kernels, output_stage(): pl.pallas_call(output_kernel, out_shape=[jax.ShapeDtypeStruct(resid.shape...  6.41 us
    all_to_all x1, starting transfers between devices, body(): parts = lax.all_to_all(d_bias, 'samp', 0, 0)  6.01 us
    pallas_call x1, Pallas kernels, pair_back(): pl.pallas_call(grad_kernel, out_shape=jax.ShapeDtypeStruct((rows * keys,...  4.13 us
  transfers between devices with their start and end apart: 10, of which 2 were waited for; matrix products, arithmetic and copies ran while one was open for 0% of the time, Pallas kernels for 44%

profile of v5, /device:TPU:0, one launch (start us, length us, event | category | flops | bytes accessed | tf_op | source)
XLA Modules:
  0.0 94.0 jit_solution(712444042317849441)
XLA Ops:
  0.6 1.5 %fusion = (bf16[4,48,128]{2,1,0:T(8,128)(2,1)}, bf16[4,48,128]{2,1,0:T(8,128)(2,1)}) fusion(bf16[4,1280,128]{2,1,0:T(8,128)(2,1)} %feats_ref.3), kind=kLoop, calls=%fused_computation | loop fusion | bytes 196608 | tf_op jit(solution)/shard_map/slice | solution.py:648
  2.1 1.3 %collective-permute-start.1 = (bf16[4,48,128]{2,1,0:T(8,128)(2,1)}, bf16[4,48,128]{2,1,0:T(8,128)(2,1)}, u32[]{:S(2)}, u32[]{:S(2)}) collective-permute-start(bf16[4,48,128]{2,1,0:T(8,128)(2,1)} %get-tuple-element.30), channel_id=1, source_target_pairs={{1,0},{2,1},{3,2},{5,4},{6,5},{7,6},{9,8},{10,9},{11,10},{13,12},{... | collective-permute-start | bytes 147464 | tf_op jit(solution)/shard_map/ppermute | solution.py:648
  3.4 3.6 %collective-permute-start = (bf16[4,48,128]{2,1,0:T(8,128)(2,1)}, bf16[4,48,128]{2,1,0:T(8,128)(2,1)}, u32[]{:S(2)}, u32[]{:S(2)}) collective-permute-start(bf16[4,48,128]{2,1,0:T(8,128)(2,1)} %get-tuple-element.31), channel_id=1, source_target_pairs={{0,1},{1,2},{2,3},{4,5},{5,6},{6,7},{8,9},{9,10},{10,11},{12,13},{... | collective-permute-start | bytes 147464 | tf_op jit(solution)/shard_map/ppermute | solution.py:647
  7.0 3.1 %pair_bias.1 = bf16[8,256,128]{2,1,0:T(8,128)(2,1)} custom-call(bf16[64,32,128]{2,1,0:T(8,128)(2,1)} %pair_ref.3, f32[1,128]{1,0:T(1,128)} %bitcast.9, bf16[16,128]{1,0:T(8,128)(2,1)} %bitcast.7), custom_call_target="tpu_custom_call" | custom-call | flops 10000000 | bytes 10000000 | tf_op jit(solution)/shard_map/pair_bias/pallas_call | solution.py:86
  10.1 7.3 %all-to-all-start = ((bf16[8,256,128]{2,1,0:T(8,128)(2,1)}), bf16[8,256,128]{2,1,0:T(8,128)(2,1)}, u32[]{:S(2)}, u32[]{:S(2)}) async-start(bf16[8,256,128]{2,1,0:T(8,128)(2,1)} %pair_bias.1), calls=%async_computation | async-start | bytes 1048576 | tf_op jit(solution)/shard_map/all_to_all | solution.py:652
  17.4 0.0 collective-permute-done.1.right_ref
  17.4 0.0 collective-permute-done.left_ref
  17.4 12.0 %atoms.3 = (f32[2,64,768]{2,1,0:T(8,128)}, bf16[2,64,768]{2,1,0:T(8,128)(2,1)}) custom-call(bf16[4,1280,128]{2,1,0:T(8,128)(2,1)} %feats_ref.3, bf16[4,48,128]{2,1,0:T(8,128)(2,1)} %collective-permute-done.left_ref, bf16[4,48,128]{2,1,0:T(8,128)(2,1)} %collective-permute-done.1.right_ref, s32[40,128]{1,0:T(8,128)} %bitcast.12, s32[1,64]{1,0:T(1,128)} %counts_ref.3, ...), custom_call_target="tpu_custom_call" | custom-call | flops 10000000000 | bytes 4000000 | tf_op jit(solution)/shard_map/atoms/pallas_call | solution.py:245
  29.4 0.2 collective-permute-start.7
  29.6 1.6 %collective-permute-start.6 = (bf16[2,64,768]{2,1,0:T(8,128)(2,1)}, bf16[2,64,768]{2,1,0:T(8,128)(2,1)}, u32[]{:S(2)}, u32[]{:S(2)}) collective-permute-start(bf16[2,64,768]{2,1,0:T(8,128)(2,1)} %get-tuple-element.20.refs_0_), channel_id=1, source_target_pairs={{0,2},{1,3},{2,0},{3,1},{4,6},{5,7},{6,4},{7,5},{8,10},{9,11},{10,... | collective-permute-start | bytes 589832 | tf_op jit(solution)/shard_map/ppermute | solution.py:629
  31.3 0.0 collective-permute-start.5
  31.3 12.2 %atoms.2 = (f32[2,64,768]{2,1,0:T(8,128)}, bf16[2,64,768]{2,1,0:T(8,128)(2,1)}) custom-call(bf16[4,1280,128]{2,1,0:T(8,128)(2,1)} %feats_ref.3, bf16[4,48,128]{2,1,0:T(8,128)(2,1)} %collective-permute-done.left_ref, bf16[4,48,128]{2,1,0:T(8,128)(2,1)} %collective-permute-done.1.right_ref, s32[40,128]{1,0:T(8,128)} %bitcast.13, s32[1,64]{1,0:T(1,128)} %counts_ref.3, ...), custom_call_target="tpu_custom_call" | custom-call | flops 10000000000 | bytes 4000000 | tf_op jit(solution)/shard_map/atoms/pallas_call | solution.py:245
  43.5 1.1 %collective-permute-start.4 = (bf16[2,64,768]{2,1,0:T(8,128)(2,1)}, bf16[2,64,768]{2,1,0:T(8,128)(2,1)}, u32[]{:S(2)}, u32[]{:S(2)}) collective-permute-start(bf16[2,64,768]{2,1,0:T(8,128)(2,1)} %get-tuple-element.17.refs_0_), channel_id=1, source_target_pairs={{0,3},{1,2},{2,1},{3,0},{4,7},{5,6},{6,5},{7,4},{8,11},{9,10},{10,... | collective-permute-start | bytes 589832 | tf_op jit(solution)/shard_map/ppermute | solution.py:629
  44.6 1.0 %collective-permute-start.3 = (bf16[2,64,768]{2,1,0:T(8,128)(2,1)}, bf16[2,64,768]{2,1,0:T(8,128)(2,1)}, u32[]{:S(2)}, u32[]{:S(2)}) collective-permute-start(bf16[2,64,768]{2,1,0:T(8,128)(2,1)} %get-tuple-element.17.refs_0_), channel_id=1, source_target_pairs={{0,2},{1,3},{2,0},{3,1},{4,6},{5,7},{6,4},{7,5},{8,10},{9,11},{10,... | collective-permute-start | bytes 589832 | tf_op jit(solution)/shard_map/ppermute | solution.py:629
  45.6 0.0 collective-permute-done.7.refs_3_
  45.6 0.0 collective-permute-start.2
  45.6 0.0 collective-permute-done.6.refs_2_
  45.6 0.0 collective-permute-done.5.refs_1_
  45.6 0.0 all-to-all-done
  45.6 7.8 %attend.1 = (bf16[128,768]{1,0:T(8,128)(2,1)}, f32[2,8,256,128]{3,2,1,0:T(8,128)}, bf16[2,256,768]{2,1,0:T(8,128)(2,1)}) custom-call(bf16[2,64,768]{2,1,0:T(8,128)(2,1)} %get-tuple-element.20.refs_0_, bf16[2,64,768]{2,1,0:T(8,128)(2,1)} %collective-permute-done.5.refs_1_, bf16[2,64,768]{2,1,0:T(8,128)(2,1)} %collective-permute-done.6.refs_2_, ...), custom_call_target="tpu_custom_call" | custom-call | flops 4000000000 | bytes 10000000 | tf_op jit(solution)/shard_map/attend/pallas_call | solution.py:392
  53.4 0.0 collective-permute-done.4.refs_3_
  53.4 1.7 %collective-permute-done.3.refs_2_ = bf16[2,64,768]{2,1,0:T(8,128)(2,1)} collective-permute-done((bf16[2,64,768]{2,1,0:T(8,128)(2,1)}, bf16[2,64,768]{2,1,0:T(8,128)(2,1)}, u32[]{:S(2)}, u32[]{:S(2)}) %collective-permute-start.3) | collective-permute-done | bytes 196640 | tf_op jit(solution)/shard_map/ppermute | solution.py:629
  55.2 0.0 collective-permute-done.2.refs_1_
  55.2 14.1 %tokens.1 = (f32[256,768]{1,0:T(8,128)}, bf16[256,1536]{1,0:T(8,128)(2,1)}, bf16[8,8,32,128]{3,2,1,0:T(8,128)(2,1)}) custom-call(bf16[2,64,768]{2,1,0:T(8,128)(2,1)} %get-tuple-element.17.refs_0_, bf16[2,64,768]{2,1,0:T(8,128)(2,1)} %collective-permute-done.2.refs_1_, bf16[2,64,768]{2,1,0:T(8,128)(2,1)} %collective-permute-done.3.refs_2_, ...), custom_call_target="tpu_custom_call" | custom-call | flops 10000000000 | bytes 20000000 | tf_op jit(solution)/shard_map/tokens/pallas_call | solution.py:511
  69.3 6.0 %all-to-all-start.1 = ((bf16[8,8,32,128]{3,2,1,0:T(8,128)(2,1)}), bf16[8,8,32,128]{3,2,1,0:T(8,128)(2,1)}, u32[]{:S(2)}, u32[]{:S(2)}) async-start(bf16[8,8,32,128]{3,2,1,0:T(8,128)(2,1)} %get-tuple-element.27), calls=%async_computation.1 | async-start | bytes 1048576 | tf_op jit(solution)/shard_map/all_to_all | solution.py:671
  75.3 6.4 %output.1 = (bf16[256,768]{1,0:T(8,128)(2,1)}, f32[2048,128]{1,0:T(8,128)}, f32[2048,128]{1,0:T(8,128)}) custom-call(f32[256,768]{1,0:T(8,128)} %get-tuple-element.24.resid_ref, bf16[256,1536]{1,0:T(8,128)(2,1)} %get-tuple-element.25.hidden_ref, bf16[1536,768]{1,0:T(8,128)(2,1)} %w_down_ref.1, bf16[64,32,128]{2,1,0:T(8,128)(2,1)} %pair_ref.3), custom_call_target="tpu_custom_call" | custom-call | flops 1000000000 | bytes 8000000 | tf_op jit(solution)/shard_map/output/pallas_call | solution.py:570
  81.7 8.1 %all-to-all-done.1.parts_ref = bf16[8,8,32,128]{3,2,1,0:T(8,128)(2,1)} async-done(((bf16[8,8,32,128]{3,2,1,0:T(8,128)(2,1)}), bf16[8,8,32,128]{3,2,1,0:T(8,128)(2,1)}, u32[]{:S(2)}, u32[]{:S(2)}) %all-to-all-start.1) | async-done | bytes 524320 | tf_op jit(solution)/shard_map/all_to_all | solution.py:671
  89.9 4.1 %pair_grad.1 = f32[2048,128]{1,0:T(8,128)} custom-call(bf16[8,8,32,128]{3,2,1,0:T(8,128)(2,1)} %all-to-all-done.1.parts_ref, f32[2048,128]{1,0:T(8,128)} %get-tuple-element.28.hat_ref, f32[2048,128]{1,0:T(8,128)} %get-tuple-element.29.rstd_ref, f32[1,128]{1,0:T(1,128)} %bitcast.10, bf16[16,128]{1,0:T(8,128)(2,1)} %bitcast.8), custom_call_target="tpu_custom_call" | custom-call | flops 100000000 | bytes 4000000 | tf_op jit(solution)/shard_map/pair_grad/pallas_call | solution.py:617
Async XLA Ops:
  2.1 15.3 %collective-permute-start.1 = (bf16[4,48,128]{2,1,0:T(8,128)(2,1)}, bf16[4,48,128]{2,1,0:T(8,128)(2,1)}, u32[]{:S(2)}, u32[]{:S(2)}) collective-permute-start(bf16[4,48,128]{2,1,0:T(8,128)(2,1)} %get-tuple-element.30), channel_id=1, source_target_pairs={{1,0},{2,1},{3,2},{5,4},{6,5},{7,6},{9,8},{10,9},{11,10},{13,12},{... | collective-permute-start | bytes 147464 | tf_op jit(solution)/shard_map/ppermute | solution.py:648
  3.4 14.0 %collective-permute-start = (bf16[4,48,128]{2,1,0:T(8,128)(2,1)}, bf16[4,48,128]{2,1,0:T(8,128)(2,1)}, u32[]{:S(2)}, u32[]{:S(2)}) collective-permute-start(bf16[4,48,128]{2,1,0:T(8,128)(2,1)} %get-tuple-element.31), channel_id=1, source_target_pairs={{0,1},{1,2},{2,3},{4,5},{5,6},{6,7},{8,9},{9,10},{10,11},{12,13},{... | collective-permute-start | bytes 147464 | tf_op jit(solution)/shard_map/ppermute | solution.py:647
  10.1 35.5 %all-to-all-start = ((bf16[8,256,128]{2,1,0:T(8,128)(2,1)}), bf16[8,256,128]{2,1,0:T(8,128)(2,1)}, u32[]{:S(2)}, u32[]{:S(2)}) async-start(bf16[8,256,128]{2,1,0:T(8,128)(2,1)} %pair_bias.1), calls=%async_computation | async-start | bytes 1048576 | tf_op jit(solution)/shard_map/all_to_all | solution.py:652
  29.4 16.2 %collective-permute-start.7 = (bf16[2,64,768]{2,1,0:T(8,128)(2,1)}, bf16[2,64,768]{2,1,0:T(8,128)(2,1)}, u32[]{:S(2)}, u32[]{:S(2)}) collective-permute-start(bf16[2,64,768]{2,1,0:T(8,128)(2,1)} %get-tuple-element.20.refs_0_), channel_id=1, source_target_pairs={{0,3},{1,2},{2,1},{3,0},{4,7},{5,6},{6,5},{7,4},{8,11},{9,10},{10,... | collective-permute-start | bytes 589832 | tf_op jit(solution)/shard_map/ppermute | solution.py:629
  29.6 16.0 %collective-permute-start.6 = (bf16[2,64,768]{2,1,0:T(8,128)(2,1)}, bf16[2,64,768]{2,1,0:T(8,128)(2,1)}, u32[]{:S(2)}, u32[]{:S(2)}) collective-permute-start(bf16[2,64,768]{2,1,0:T(8,128)(2,1)} %get-tuple-element.20.refs_0_), channel_id=1, source_target_pairs={{0,2},{1,3},{2,0},{3,1},{4,6},{5,7},{6,4},{7,5},{8,10},{9,11},{10,... | collective-permute-start | bytes 589832 | tf_op jit(solution)/shard_map/ppermute | solution.py:629
  31.3 14.4 %collective-permute-start.5 = (bf16[2,64,768]{2,1,0:T(8,128)(2,1)}, bf16[2,64,768]{2,1,0:T(8,128)(2,1)}, u32[]{:S(2)}, u32[]{:S(2)}) collective-permute-start(bf16[2,64,768]{2,1,0:T(8,128)(2,1)} %get-tuple-element.20.refs_0_), channel_id=1, source_target_pairs={{0,1},{1,0},{2,3},{3,2},{4,5},{5,4},{6,7},{7,6},{8,9},{9,8},{10,11... | collective-permute-start | bytes 589832 | tf_op jit(solution)/shard_map/ppermute | solution.py:629
  43.5 10.0 %collective-permute-start.4 = (bf16[2,64,768]{2,1,0:T(8,128)(2,1)}, bf16[2,64,768]{2,1,0:T(8,128)(2,1)}, u32[]{:S(2)}, u32[]{:S(2)}) collective-permute-start(bf16[2,64,768]{2,1,0:T(8,128)(2,1)} %get-tuple-element.17.refs_0_), channel_id=1, source_target_pairs={{0,3},{1,2},{2,1},{3,0},{4,7},{5,6},{6,5},{7,4},{8,11},{9,10},{10,... | collective-permute-start | bytes 589832 | tf_op jit(solution)/shard_map/ppermute | solution.py:629
  44.6 10.6 %collective-permute-start.3 = (bf16[2,64,768]{2,1,0:T(8,128)(2,1)}, bf16[2,64,768]{2,1,0:T(8,128)(2,1)}, u32[]{:S(2)}, u32[]{:S(2)}) collective-permute-start(bf16[2,64,768]{2,1,0:T(8,128)(2,1)} %get-tuple-element.17.refs_0_), channel_id=1, source_target_pairs={{0,2},{1,3},{2,0},{3,1},{4,6},{5,7},{6,4},{7,5},{8,10},{9,11},{10,... | collective-permute-start | bytes 589832 | tf_op jit(solution)/shard_map/ppermute | solution.py:629
  45.6 9.6 %collective-permute-start.2 = (bf16[2,64,768]{2,1,0:T(8,128)(2,1)}, bf16[2,64,768]{2,1,0:T(8,128)(2,1)}, u32[]{:S(2)}, u32[]{:S(2)}) collective-permute-start(bf16[2,64,768]{2,1,0:T(8,128)(2,1)} %get-tuple-element.17.refs_0_), channel_id=1, source_target_pairs={{0,1},{1,0},{2,3},{3,2},{4,5},{5,4},{6,7},{7,6},{8,9},{9,8},{10,11... | collective-permute-start | bytes 589832 | tf_op jit(solution)/shard_map/ppermute | solution.py:629
  69.3 20.6 %all-to-all-start.1 = ((bf16[8,8,32,128]{3,2,1,0:T(8,128)(2,1)}), bf16[8,8,32,128]{3,2,1,0:T(8,128)(2,1)}, u32[]{:S(2)}, u32[]{:S(2)}) async-start(bf16[8,8,32,128]{3,2,1,0:T(8,128)(2,1)} %get-tuple-element.27), calls=%async_computation.1 | async-start | bytes 1048576 | tf_op jit(solution)/shard_map/all_to_all | solution.py:671

commit v6 on v5

--- a/solution.py
+++ b/solution.py
@@ -36,6 +36,13 @@
 
 def tn(a, b):
     return lax.dot_general(a, b, (((0,), (0,)), ((), ())), preferred_element_type=f32)
+
+
+def start_all(moves, sems):
+    copies = [pltpu.make_async_copy(src, dst, sems.at[i]) for i, (src, dst) in enumerate(moves)]
+    for copy in copies:
+        copy.start()
+    return copies
 
 
 def norm_rows(values):
@@ -97,12 +104,22 @@
 
 
 def atom_kernel(
-    feats_ref, left_ref, right_ref, mask_ref, counts_ref, single_ref, w_qkv_ref, w_out_ref,
-    w_embed_ref, tokens_ref, normed_ref, padded_ref, qkv_a, qkv_b, scores_a, scores_b, probs_a,
-    probs_b, mixed_ref, split_ref, keybias_ref, onehot_ref, pooled_ref,
+    feats_hbm, left_hbm, right_hbm, mask_hbm, counts_hbm, single_hbm, w_qkv_hbm, w_out_hbm,
+    w_embed_hbm, tokens_ref, normed_ref, mask_ref, counts_ref, single_ref, w_qkv_ref, w_out_ref,
+    w_embed_ref, sems, padded_ref, qkv_a, qkv_b, scores_a, scores_b, probs_a, probs_b, mixed_ref,
+    split_ref, keybias_ref, onehot_ref, pooled_ref, *, first,
 ):
-    batch, atoms = feats_ref.shape[0], feats_ref.shape[1]
+    batch, atoms = tokens_ref.shape[0], feats_hbm.shape[1]
     padded = atoms + 2 * HALO
+    moves = [(counts_hbm, counts_ref), (mask_hbm, mask_ref), (w_qkv_hbm, w_qkv_ref)]
+    for s in range(batch):
+        moves.append((left_hbm.at[first + s], padded_ref.at[s, pl.ds(0, HALO)]))
+        moves.append((feats_hbm.at[first + s], padded_ref.at[s, pl.ds(HALO, atoms)]))
+        moves.append((right_hbm.at[first + s], padded_ref.at[s, pl.ds(HALO + atoms, HALO)]))
+    moves += [(w_out_hbm, w_out_ref), (w_embed_hbm, w_embed_ref), (single_hbm, single_ref)]
+    copies = start_all(moves, sems)
+    for copy in copies[0:2]:
+        copy.wait()
     tok_rows = single_ref.shape[0]
     blocks = atoms // 128
     chunks = atoms // 256
@@ -132,11 +149,6 @@
         hit = jnp.where((at >= start) & (at < start + own), 1.0, 0.0).astype(bf16)
         onehot_ref[g] = jnp.concatenate([hit, hit], axis=1)
     pooled_ref[...] = jnp.zeros_like(pooled_ref)
-    for s in range(batch):
-        padded_ref[s, 0:HALO, :] = left_ref[s]
-        padded_ref[s, HALO : HALO + atoms, :] = feats_ref[s]
-        padded_ref[s, HALO + atoms : padded, :] = right_ref[s]
-
     head_of = iota((32, 128), 1) // ATOM_HD
     head_mask = [(head_of == h).astype(f32).astype(bf16) for h in range(ATOM_HEADS)]
     own_atom = (iota((32, 128), 1) % 32) == iota((32, 128), 0)
@@ -194,7 +206,7 @@
 
     def embed_step(s, g):
         base = pl.multiple_of(g * 256, 256)
-        feats = feats_ref[s, pl.ds(base, 256), :].astype(f32)
+        feats = padded_ref[s, pl.ds(base + HALO, 256), :].astype(f32)
         updated = (feats + nn(mixed_ref[s, pl.ds(base, 256), :], w_out_ref[...])).astype(bf16)
         embedded = jnp.maximum(nn(updated, w_embed_ref[...]), 0.0)
         high = embedded.astype(bf16)
@@ -202,8 +214,12 @@
         split_ref[256:512, :] = (embedded - high.astype(f32)).astype(bf16)
         pooled_ref[s] += nn(onehot_ref[g], split_ref[...])
 
+    for copy in copies[2:6]:
+        copy.wait()
     for i in range(chunks):
         qkv_step(0, i)
+    for copy in copies[6:]:
+        copy.wait()
     for s in range(batch):
         score_step(s, 0, scores_a)
 
@@ -239,22 +255,22 @@
     atoms = feats.shape[1]
     tok_rows = single.shape[0]
     padded = atoms + 2 * HALO
-    of_part = lambda rows, cols: pl.BlockSpec((batch, rows, cols), lambda i: (part, 0, 0))
-    whole = lambda a: pl.BlockSpec(a.shape, lambda i: (0,) * a.ndim)
-    every = pl.BlockSpec((batch, tok_rows, C_TOK), lambda i: (0, 0, 0))
     return pl.pallas_call(
-        atom_kernel,
-        grid=(1,),
-        in_specs=[
-            of_part(atoms, C_ATOM), of_part(HALO, C_ATOM), of_part(HALO, C_ATOM),
-            whole(mask), whole(counts), whole(single), whole(w_qkv), whole(w_out), whole(w_embed),
-        ],
-        out_specs=[every, every],
+        functools.partial(atom_kernel, first=part * batch),
+        in_specs=[pl.BlockSpec(memory_space=pl.ANY)] * 9,
+        out_specs=[pl.BlockSpec(memory_space=pltpu.VMEM)] * 2,
         out_shape=[
             jax.ShapeDtypeStruct((batch, tok_rows, C_TOK), f32),
             jax.ShapeDtypeStruct((batch, tok_rows, C_TOK), bf16),
         ],
         scratch_shapes=[
+            pltpu.VMEM(mask.shape, jnp.int32),
+            pltpu.VMEM(counts.shape, jnp.int32),
+            pltpu.VMEM(single.shape, bf16),
+            pltpu.VMEM(w_qkv.shape, bf16),
+            pltpu.VMEM(w_out.shape, bf16),
+            pltpu.VMEM(w_embed.shape, bf16),
+            pltpu.SemaphoreType.DMA((6 + 3 * batch,)),
             pltpu.VMEM((batch, padded, C_ATOM), bf16),
             pltpu.VMEM((padded, 3 * C_ATOM), bf16),
             pltpu.VMEM((padded, 3 * C_ATOM), bf16),
@@ -293,19 +309,33 @@
     return jnp.concatenate([jnp.where(mask, block, blank) for mask in masks], axis=0)
 
 
-def project(piece_refs, w_qkv_ref, copies, all_ref, queries_ref, keys_ref, values_ref):
-    batch, tok_rows = piece_refs[0].shape[0], piece_refs[0].shape[1]
+def project_moves(piece_hbms, w_qkv_hbm, w_qkv_ref, all_ref):
+    tok_rows = piece_hbms[0].shape[1]
+    weights = [
+        (w_qkv_hbm.at[:, pl.ds(C_TOK * i, C_TOK)], w_qkv_ref.at[i]) for i in range(3)
+    ]
     here = lax.axis_index("tok")
-    for k, piece in enumerate(piece_refs):
+    pieces = []
+    for k, piece in enumerate(piece_hbms):
         at = pl.multiple_of((here ^ k) * tok_rows, tok_rows)
-        for s in range(batch):
-            all_ref[s, pl.ds(at, tok_rows), :] = piece[s]
-    own = piece_refs[0][...].reshape(batch * tok_rows, C_TOK)
-    copies[0].wait()
+        pieces.append((piece, all_ref.at[:, pl.ds(at, tok_rows), :]))
+    return [pieces[0], weights[0]] + pieces[1:] + weights[1:]
+
+
+def project(copies, w_qkv_ref, all_ref, queries_ref, keys_ref, values_ref):
+    batch = all_ref.shape[0]
+    tok_rows = queries_ref.shape[0] // batch
+    at = pl.multiple_of(lax.axis_index("tok") * tok_rows, tok_rows)
+    for copy in copies[0:2]:
+        copy.wait()
+    own = jnp.concatenate([all_ref[s, pl.ds(at, tok_rows), :] for s in range(batch)], axis=0)
     for n in range(0, C_TOK, 256):
         queries_ref[:, n : n + 256] = nn(own, w_qkv_ref[0, :, n : n + 256]).astype(bf16)
+    for copy in copies[2:-1]:
+        copy.wait()
     for which, to_ref in ((1, keys_ref), (2, values_ref)):
-        copies[which].wait()
+        if which == 2:
+            copies[-1].wait()
         for n in range(0, C_TOK, 256):
             for s in range(batch):
                 to_ref[s, :, n : n + 256] = nn(
@@ -318,14 +348,14 @@
     return 384 * (pair // 4) + low, 384 * (pair // 4) + high
 
 
-def attend(bias_ref, queries_ref, keys_ref, values_ref, probs_ref, att_ref):
+def attend(bias_ref, queries_ref, keys_ref, values_ref, probs_ref, att_ref, done=None):
     batch, keys_all = keys_ref.shape[0], keys_ref.shape[1]
     tok_rows = queries_ref.shape[0] // batch
     masks = head_masks(tok_rows)
     factor = HD ** (-0.5)
 
-    def sample_step(s, carry):
-        at = pl.multiple_of(s * tok_rows, 64)
+    for s in range(batch):
+        at = s * tok_rows
         for pair in range(PAIRS):
             low, high = windows(pair)
             queries = two_heads(queries_ref[pl.ds(at, tok_rows), low:high], masks[pair % 4])
@@ -347,33 +377,29 @@
                 lanes[low // 128 + t] = lanes[low // 128 + t] + mix[:, 128 * t : 128 * t + 128]
         for t in range(C_TOK // 128):
             att_ref[pl.ds(at, tok_rows), 128 * t : 128 * t + 128] = lanes[t].astype(bf16)
-        return carry
-
-    lax.fori_loop(0, batch, sample_step, 0)
-
-
-def start_all(moves, sems):
-    copies = [pltpu.make_async_copy(src, dst, sems.at[i]) for i, (src, dst) in enumerate(moves)]
-    for copy in copies:
-        copy.start()
-    return copies
-
-
-def qkv_moves(w_qkv_hbm, w_qkv_ref):
-    return [
-        (w_qkv_hbm.at[:, pl.ds(C_TOK * i, C_TOK)], w_qkv_ref.at[i]) for i in range(3)
-    ]
+        if done is not None:
+            done(s)
 
 
 def attend_kernel(*refs, count):
-    piece_refs = refs[:count]
     (
-        bias_ref, w_qkv_hbm, att_ref, probs_ref, values_ref, w_qkv_ref, sems, all_ref, queries_ref,
-        keys_ref,
+        bias_hbm, w_qkv_hbm, att_ref, probs_hbm, values_hbm, w_qkv_ref, bias_ref, probs_ref,
+        values_ref, sems, all_ref, queries_ref, keys_ref,
     ) = refs[count:]
-    copies = start_all(qkv_moves(w_qkv_hbm, w_qkv_ref), sems)
-    project(piece_refs, w_qkv_ref, copies, all_ref, queries_ref, keys_ref, values_ref)
-    attend(bias_ref, queries_ref, keys_ref, values_ref, probs_ref, att_ref)
+    batch = all_ref.shape[0]
+    moves = project_moves(refs[:count], w_qkv_hbm, w_qkv_ref, all_ref)
+    copies = start_all(moves + [(bias_hbm, bias_ref)], sems)
+    project(copies[:-1], w_qkv_ref, all_ref, queries_ref, keys_ref, values_ref)
+    copies[-1].wait()
+    back = [
+        pltpu.make_async_copy(probs_ref.at[s], probs_hbm.at[s], sems.at[s]) for s in range(batch)
+    ] + [pltpu.make_async_copy(values_ref, values_hbm, sems.at[batch])]
+    back[batch].start()
+    attend(
+        bias_ref, queries_ref, keys_ref, values_ref, probs_ref, att_ref, lambda s: back[s].start()
+    )
+    for copy in back:
+        copy.wait()
 
 
 def attend_scratch(batch, tok_rows, keys_all):
@@ -391,8 +417,8 @@
     hbm = pl.BlockSpec(memory_space=pl.ANY)
     return pl.pallas_call(
         functools.partial(attend_kernel, count=len(pieces)),
-        in_specs=[vmem] * (len(pieces) + 1) + [hbm],
-        out_specs=[vmem] * 3,
+        in_specs=[hbm] * (len(pieces) + 2),
+        out_specs=[vmem, hbm, hbm],
         out_shape=[
             jax.ShapeDtypeStruct((batch * tok_rows, C_TOK), bf16),
             jax.ShapeDtypeStruct((batch, PAIRS, keys_all, 2 * tok_rows), f32),
@@ -400,7 +426,10 @@
         ],
         scratch_shapes=[
             pltpu.VMEM((3, C_TOK, C_TOK), bf16),
-            pltpu.SemaphoreType.DMA((3,)),
+            pltpu.VMEM(bias.shape, bf16),
+            pltpu.VMEM((batch, PAIRS, keys_all, 2 * tok_rows), f32),
+            pltpu.VMEM((batch, keys_all, C_TOK), bf16),
+            pltpu.SemaphoreType.DMA((4 + len(pieces),)),
         ]
         + attend_scratch(batch, tok_rows, keys_all),
         compiler_params=pltpu.CompilerParams(vmem_limit_bytes=GRANT),
@@ -412,11 +441,11 @@
 
 
 def token_kernel(*refs, count):
-    piece_refs = refs[:count]
     (
-        bias_ref, tokens_a_ref, tokens_b_ref, att_a_ref, cot_ref, probs_a_hbm, values_a_hbm,
+        bias_hbm, tokens_a_hbm, tokens_b_hbm, att_a_hbm, cot_hbm, probs_a_hbm, values_a_hbm,
         w_qkv_hbm, w_out_hbm, w_gate_hbm, w_up_hbm, w_down_hbm,
-        resid_ref, hidden_ref, d_bias_ref,
+        resid_hbm, hidden_hbm, d_bias_ref,
+        bias_ref, tokens_ref, att_a_ref, cot_ref, resid_ref, hidden_ref,
         w_qkv_ref, w_out_ref, w_gate_ref, w_up_ref, w_down_ref, probs_ref, values_ref, sems,
         all_ref, queries_ref, keys_ref, grads_ref, d_gate_ref, d_up_ref, hat_ref,
     ) = refs[count:]
@@ -425,31 +454,37 @@
     rows = batch * tok_rows
     ahead = values_a_hbm.shape[0]
     lead = ahead * tok_rows
-    copies = start_all(
-        qkv_moves(w_qkv_hbm, w_qkv_ref)
-        + [
-            (w_out_hbm, w_out_ref), (w_down_hbm, w_down_ref), (w_gate_hbm, w_gate_ref),
-            (w_up_hbm, w_up_ref), (values_a_hbm, values_ref.at[pl.ds(0, ahead)]),
-            (probs_a_hbm, probs_ref.at[pl.ds(0, ahead)]),
-        ],
-        sems,
-    )
+    moves = project_moves(refs[:count], w_qkv_hbm, w_qkv_ref, all_ref)
+    projecting = len(moves)
+    moves += [
+        (bias_hbm, bias_ref), (w_out_hbm, w_out_ref), (att_a_hbm, att_a_ref),
+        (tokens_a_hbm, tokens_ref.at[pl.ds(0, ahead)]),
+        (tokens_b_hbm, tokens_ref.at[pl.ds(ahead, batch - ahead)]), (cot_hbm, cot_ref),
+        (w_down_hbm, w_down_ref), (w_gate_hbm, w_gate_ref), (w_up_hbm, w_up_ref),
+        (values_a_hbm, values_ref.at[pl.ds(0, ahead)]), (probs_a_hbm, probs_ref.at[pl.ds(0, ahead)]),
+    ]
+    copies = start_all(moves, sems)
     own_values = values_ref.at[pl.ds(ahead, batch - ahead)]
     own_probs = probs_ref.at[pl.ds(ahead, batch - ahead)]
-    project(piece_refs, w_qkv_ref, copies, all_ref, queries_ref, keys_ref, own_values)
+    project(copies[:projecting], w_qkv_ref, all_ref, queries_ref, keys_ref, own_values)
+    copies = copies[projecting:]
+    copies[0].wait()
     attend(bias_ref, queries_ref, keys_ref, own_values, own_probs, queries_ref)
 
-    copies[3].wait()
-    resid_ref[0:lead, :] = tokens_a_ref[...].reshape(lead, C_TOK) + nn(
-        att_a_ref[...], w_out_ref[...]
-    )
-    resid_ref[lead:rows, :] = tokens_b_ref[...].reshape(rows - lead, C_TOK) + nn(
-        queries_ref[...], w_out_ref[...]
-    )
+    for copy in copies[1:5]:
+        copy.wait()
+    tokens = tokens_ref[...].reshape(rows, C_TOK)
+    resid_ref[0:lead, :] = tokens[0:lead] + nn(att_a_ref[...], w_out_ref[...])
+    resid_ref[lead:rows, :] = tokens[lead:rows] + nn(queries_ref[...], w_out_ref[...])
+    back = [
+        pltpu.make_async_copy(resid_ref, resid_hbm, sems.at[0]),
+        pltpu.make_async_copy(hidden_ref, hidden_hbm, sems.at[1]),
+    ]
+    back[0].start()
     hat, rstd = norm_rows(resid_ref[...])
     hat_ref[...] = hat
     grads_ref[...] = hat.astype(bf16)
-    for copy in copies[4:7]:
+    for copy in copies[5:9]:
         copy.wait()
 
     for n in range(0, w_gate_ref.shape[1], 256):
@@ -465,6 +500,7 @@
         ).astype(bf16)
         d_up_ref[:, n : n + 256] = (d_hidden * act).astype(bf16)
 
+    back[1].start()
     parts = []
     for n in range(0, C_TOK, 256):
         parts.append(
@@ -479,7 +515,7 @@
         d_normed - first - hat * second
     )
     grads_ref[...] = nt(d_resid.astype(bf16), w_out_ref[...]).astype(bf16)
-    for copy in copies[7:]:
+    for copy in copies[9:]:
         copy.wait()
     masks = head_masks(tok_rows)
     for pair in range(PAIRS):
@@ -496,6 +532,8 @@
         size = d_bias_ref.shape[2]
         for k in range(d_bias_ref.shape[0]):
             d_bias_ref[k, pair] = total[size * k : size * (k + 1)].astype(bf16)
+    for copy in back:
+        copy.wait()
 
 
 def token_stage(
@@ -510,14 +548,20 @@
     hbm = pl.BlockSpec(memory_space=pl.ANY)
     return pl.pallas_call(
         functools.partial(token_kernel, count=len(pieces)),
-        in_specs=[vmem] * (len(pieces) + 5) + [hbm] * 7,
-        out_specs=[vmem] * 3,
+        in_specs=[hbm] * (len(pieces) + 12),
+        out_specs=[hbm, hbm, vmem],
         out_shape=[
             jax.ShapeDtypeStruct((rows, C_TOK), f32),
             jax.ShapeDtypeStruct((rows, hidden), bf16),
             jax.ShapeDtypeStruct(bias.shape, bf16),
         ],
         scratch_shapes=[
+            pltpu.VMEM(bias.shape, bf16),
+            pltpu.VMEM(cot.shape, f32),
+            pltpu.VMEM(att_a.shape, bf16),
+            pltpu.VMEM(cot.shape, bf16),
+            pltpu.VMEM((rows, C_TOK), f32),
+            pltpu.VMEM((rows, hidden), bf16),
             pltpu.VMEM((3, C_TOK, C_TOK), bf16),
             pltpu.VMEM(w_out.shape, bf16),
             pltpu.VMEM(w_gate.shape, bf16),
@@ -525,7 +569,7 @@
             pltpu.VMEM(w_down.shape, bf16),
             pltpu.VMEM((batch, PAIRS, keys_all, 2 * tok_rows), f32),
             pltpu.VMEM((batch, keys_all, C_TOK), bf16),
-            pltpu.SemaphoreType.DMA((9,)),
+            pltpu.SemaphoreType.DMA((14 + len(pieces),)),
         ]
         + attend_scratch(pieces[0].shape[0], tok_rows, keys_all)
         + [

time: 94.5 us -> 92.5 us (0.979)
  Pallas kernels: 59.7 us -> 56.3 us
  waiting for transfers between devices: 9.9 us -> 11.2 us
    pallas_call x1, Pallas kernels: 14.1 us -> 12.4 us  [token_stage(): pl.pallas_call(functools.partial(token_kernel, count=len(pieces)), in_spe...]
    ppermute x6, waiting for transfers between devices: 1.76 us -> 3.05 us  [swap(): lax.ppermute(values, axis, [(i, i ^ k) for i in range(lax.axis_size(axis))])]
    pallas_call x1, Pallas kernels: 7.78 us -> 6.5 us  [attend_stage(): pl.pallas_call(functools.partial(attend_kernel, count=len(pieces)), in_sp...]
  transfers between devices with their start and end apart: 10 -> 10, of which waited for: 2 -> 2; matrix products, arithmetic and copies ran while one was open for 0% -> 0% of each run, Pallas kernels for 44% -> 43%
where the time goes in v6:
time: 92.5 us; the launch traced here: 92 us
  Pallas kernels  56.3 us (61%)
  starting transfers between devices  22.3 us (24%)
  waiting for transfers between devices  11.2 us (12%)
  local copies, waits for them, and re-layouts  1.47 us (2%)
    pallas_call x2, Pallas kernels, atom_stage(): pl.pallas_call(functools.partial(atom_kernel, first=part * batch), in_spe...  23.7 us
    pallas_call x1, Pallas kernels, token_stage(): pl.pallas_call(functools.partial(token_kernel, count=len(pieces)), in_spe...  12.4 us
    all_to_all x1, waiting for transfers between devices, body(): parts = lax.all_to_all(d_bias, 'samp', 0, 0)  8.11 us
    all_to_all x1, starting transfers between devices, body(): lax.all_to_all(local_bias, 'samp', 0, 0)  7.28 us
    pallas_call x1, Pallas kernels, attend_stage(): pl.pallas_call(functools.partial(attend_kernel, count=len(pieces)), in_sp...  6.5 us
    pallas_call x1, Pallas kernels, output_stage(): pl.pallas_call(output_kernel, out_shape=[jax.ShapeDtypeStruct(resid.shape...  6.41 us
    all_to_all x1, starting transfers between devices, body(): parts = lax.all_to_all(d_bias, 'samp', 0, 0)  6 us
    ppermute x6, starting transfers between devices, swap(): lax.ppermute(values, axis, [(i, i ^ k) for i in range(lax.axis_size(axis))])  4.13 us
  transfers between devices with their start and end apart: 10, of which 2 were waited for; matrix products, arithmetic and copies ran while one was open for 0% of the time, Pallas kernels for 43%

profile of v6, /device:TPU:0, one launch (start us, length us, event | category | flops | bytes accessed | tf_op | source)
XLA Modules:
  0.0 92.0 jit_solution(7888771950624724039)
XLA Ops:
  0.6 1.5 %fusion = (bf16[4,48,128]{2,1,0:T(8,128)(2,1)}, bf16[4,48,128]{2,1,0:T(8,128)(2,1)}) fusion(bf16[4,1280,128]{2,1,0:T(8,128)(2,1)} %feats_hbm.3), kind=kLoop, calls=%fused_computation | loop fusion | bytes 196608 | tf_op jit(solution)/shard_map/slice | solution.py:692
  2.1 1.3 %collective-permute-start.1 = (bf16[4,48,128]{2,1,0:T(8,128)(2,1)}, bf16[4,48,128]{2,1,0:T(8,128)(2,1)}, u32[]{:S(2)}, u32[]{:S(2)}) collective-permute-start(bf16[4,48,128]{2,1,0:T(8,128)(2,1)} %get-tuple-element.30), channel_id=1, source_target_pairs={{1,0},{2,1},{3,2},{5,4},{6,5},{7,6},{9,8},{10,9},{11,10},{13,12},{... | collective-permute-start | bytes 147464 | tf_op jit(solution)/shard_map/ppermute | solution.py:692
  3.4 3.6 %collective-permute-start = (bf16[4,48,128]{2,1,0:T(8,128)(2,1)}, bf16[4,48,128]{2,1,0:T(8,128)(2,1)}, u32[]{:S(2)}, u32[]{:S(2)}) collective-permute-start(bf16[4,48,128]{2,1,0:T(8,128)(2,1)} %get-tuple-element.31), channel_id=1, source_target_pairs={{0,1},{1,2},{2,3},{4,5},{5,6},{6,7},{8,9},{9,10},{10,11},{12,13},{... | collective-permute-start | bytes 147464 | tf_op jit(solution)/shard_map/ppermute | solution.py:691
  7.0 3.1 %pair_bias.1 = bf16[8,256,128]{2,1,0:T(8,128)(2,1)} custom-call(bf16[64,32,128]{2,1,0:T(8,128)(2,1)} %pair_ref.3, f32[1,128]{1,0:T(1,128)} %bitcast.9, bf16[16,128]{1,0:T(8,128)(2,1)} %bitcast.7), custom_call_target="tpu_custom_call" | custom-call | flops 10000000 | bytes 10000000 | tf_op jit(solution)/shard_map/pair_bias/pallas_call | solution.py:93
  10.1 7.3 %all-to-all-start = ((bf16[8,256,128]{2,1,0:T(8,128)(2,1)}), bf16[8,256,128]{2,1,0:T(8,128)(2,1)}, u32[]{:S(2)}, u32[]{:S(2)}) async-start(bf16[8,256,128]{2,1,0:T(8,128)(2,1)} %pair_bias.1), calls=%async_computation | async-start | bytes 1048576 | tf_op jit(solution)/shard_map/all_to_all | solution.py:696
  17.4 0.0 collective-permute-done.1.right_hbm
  17.4 0.0 collective-permute-done.left_hbm
  17.4 11.8 %atoms.3 = (f32[2,64,768]{2,1,0:T(8,128)}, bf16[2,64,768]{2,1,0:T(8,128)(2,1)}) custom-call(bf16[4,1280,128]{2,1,0:T(8,128)(2,1)} %feats_hbm.3, bf16[4,48,128]{2,1,0:T(8,128)(2,1)} %collective-permute-done.left_hbm, bf16[4,48,128]{2,1,0:T(8,128)(2,1)} %collective-permute-done.1.right_hbm, s32[40,128]{1,0:T(8,128)} %bitcast.12, s32[1,64]{1,0:T(1,128)} %counts_hbm.3, ...), custom_call_target="tpu_custom_call" | custom-call | flops 10000000000 | bytes 4000000 | tf_op jit(solution)/shard_map/atoms/pallas_call | solution.py:258
  29.2 0.3 collective-permute-start.7
  29.5 1.6 %collective-permute-start.6 = (bf16[2,64,768]{2,1,0:T(8,128)(2,1)}, bf16[2,64,768]{2,1,0:T(8,128)(2,1)}, u32[]{:S(2)}, u32[]{:S(2)}) collective-permute-start(bf16[2,64,768]{2,1,0:T(8,128)(2,1)} %get-tuple-element.20.refs_0_), channel_id=1, source_target_pairs={{0,2},{1,3},{2,0},{3,1},{4,6},{5,7},{6,4},{7,5},{8,10},{9,11},{10,... | collective-permute-start | bytes 589832 | tf_op jit(solution)/shard_map/ppermute | solution.py:673
  31.1 0.0 collective-permute-start.5
  31.1 12.0 %atoms.2 = (f32[2,64,768]{2,1,0:T(8,128)}, bf16[2,64,768]{2,1,0:T(8,128)(2,1)}) custom-call(bf16[4,1280,128]{2,1,0:T(8,128)(2,1)} %feats_hbm.3, bf16[4,48,128]{2,1,0:T(8,128)(2,1)} %collective-permute-done.left_hbm, bf16[4,48,128]{2,1,0:T(8,128)(2,1)} %collective-permute-done.1.right_hbm, s32[40,128]{1,0:T(8,128)} %bitcast.13, s32[1,64]{1,0:T(1,128)} %counts_hbm.3, ...), custom_call_target="tpu_custom_call" | custom-call | flops 10000000000 | bytes 4000000 | tf_op jit(solution)/shard_map/atoms/pallas_call | solution.py:258
  43.1 1.2 %collective-permute-start.4 = (bf16[2,64,768]{2,1,0:T(8,128)(2,1)}, bf16[2,64,768]{2,1,0:T(8,128)(2,1)}, u32[]{:S(2)}, u32[]{:S(2)}) collective-permute-start(bf16[2,64,768]{2,1,0:T(8,128)(2,1)} %get-tuple-element.17.refs_0_), channel_id=1, source_target_pairs={{0,3},{1,2},{2,1},{3,0},{4,7},{5,6},{6,5},{7,4},{8,11},{9,10},{10,... | collective-permute-start | bytes 589832 | tf_op jit(solution)/shard_map/ppermute | solution.py:673
  44.3 1.0 %collective-permute-start.3 = (bf16[2,64,768]{2,1,0:T(8,128)(2,1)}, bf16[2,64,768]{2,1,0:T(8,128)(2,1)}, u32[]{:S(2)}, u32[]{:S(2)}) collective-permute-start(bf16[2,64,768]{2,1,0:T(8,128)(2,1)} %get-tuple-element.17.refs_0_), channel_id=1, source_target_pairs={{0,2},{1,3},{2,0},{3,1},{4,6},{5,7},{6,4},{7,5},{8,10},{9,11},{10,... | collective-permute-start | bytes 589832 | tf_op jit(solution)/shard_map/ppermute | solution.py:673
  45.3 0.0 collective-permute-done.7.refs_3_
  45.3 0.0 collective-permute-start.2
  45.3 0.0 collective-permute-done.6.refs_2_
  45.3 0.0 collective-permute-done.5.refs_1_
  45.3 0.0 all-to-all-done
  45.3 6.5 %attend.1 = (bf16[128,768]{1,0:T(8,128)(2,1)}, f32[2,8,256,128]{3,2,1,0:T(8,128)}, bf16[2,256,768]{2,1,0:T(8,128)(2,1)}) custom-call(bf16[2,64,768]{2,1,0:T(8,128)(2,1)} %get-tuple-element.20.refs_0_, bf16[2,64,768]{2,1,0:T(8,128)(2,1)} %collective-permute-done.5.refs_1_, bf16[2,64,768]{2,1,0:T(8,128)(2,1)} %collective-permute-done.6.refs_2_, ...), custom_call_target="tpu_custom_call" | custom-call | flops 4000000000 | bytes 10000000 | tf_op jit(solution)/shard_map/attend/pallas_call | solution.py:418
  51.8 0.0 collective-permute-done.4.refs_3_
  51.8 3.0 %collective-permute-done.3.refs_2_ = bf16[2,64,768]{2,1,0:T(8,128)(2,1)} collective-permute-done((bf16[2,64,768]{2,1,0:T(8,128)(2,1)}, bf16[2,64,768]{2,1,0:T(8,128)(2,1)}, u32[]{:S(2)}, u32[]{:S(2)}) %collective-permute-start.3) | collective-permute-done | bytes 196640 | tf_op jit(solution)/shard_map/ppermute | solution.py:673
  54.9 0.0 collective-permute-done.2.refs_1_
  54.9 12.4 %tokens.1 = (f32[256,768]{1,0:T(8,128)}, bf16[256,1536]{1,0:T(8,128)(2,1)}, bf16[8,8,32,128]{3,2,1,0:T(8,128)(2,1)}) custom-call(bf16[2,64,768]{2,1,0:T(8,128)(2,1)} %get-tuple-element.17.refs_0_, bf16[2,64,768]{2,1,0:T(8,128)(2,1)} %collective-permute-done.2.refs_1_, bf16[2,64,768]{2,1,0:T(8,128)(2,1)} %collective-permute-done.3.refs_2_, ...), custom_call_target="tpu_custom_call" | custom-call | flops 10000000000 | bytes 20000000 | tf_op jit(solution)/shard_map/tokens/pallas_call | solution.py:549
  67.3 6.0 %all-to-all-start.1 = ((bf16[8,8,32,128]{3,2,1,0:T(8,128)(2,1)}), bf16[8,8,32,128]{3,2,1,0:T(8,128)(2,1)}, u32[]{:S(2)}, u32[]{:S(2)}) async-start(bf16[8,8,32,128]{3,2,1,0:T(8,128)(2,1)} %get-tuple-element.27), calls=%async_computation.1 | async-start | bytes 1048576 | tf_op jit(solution)/shard_map/all_to_all | solution.py:715
  73.3 6.4 %output.1 = (bf16[256,768]{1,0:T(8,128)(2,1)}, f32[2048,128]{1,0:T(8,128)}, f32[2048,128]{1,0:T(8,128)}) custom-call(f32[256,768]{1,0:T(8,128)} %get-tuple-element.24.resid_ref, bf16[256,1536]{1,0:T(8,128)(2,1)} %get-tuple-element.25.hidden_ref, bf16[1536,768]{1,0:T(8,128)(2,1)} %w_down_ref.1, bf16[64,32,128]{2,1,0:T(8,128)(2,1)} %pair_ref.3), custom_call_target="tpu_custom_call" | custom-call | flops 1000000000 | bytes 8000000 | tf_op jit(solution)/shard_map/output/pallas_call | solution.py:614
  79.7 8.1 %all-to-all-done.1.parts_ref = bf16[8,8,32,128]{3,2,1,0:T(8,128)(2,1)} async-done(((bf16[8,8,32,128]{3,2,1,0:T(8,128)(2,1)}), bf16[8,8,32,128]{3,2,1,0:T(8,128)(2,1)}, u32[]{:S(2)}, u32[]{:S(2)}) %all-to-all-start.1) | async-done | bytes 524320 | tf_op jit(solution)/shard_map/all_to_all | solution.py:715
  87.8 4.1 %pair_grad.1 = f32[2048,128]{1,0:T(8,128)} custom-call(bf16[8,8,32,128]{3,2,1,0:T(8,128)(2,1)} %all-to-all-done.1.parts_ref, f32[2048,128]{1,0:T(8,128)} %get-tuple-element.28.hat_ref, f32[2048,128]{1,0:T(8,128)} %get-tuple-element.29.rstd_ref, f32[1,128]{1,0:T(1,128)} %bitcast.10, bf16[16,128]{1,0:T(8,128)(2,1)} %bitcast.8), custom_call_target="tpu_custom_call" | custom-call | flops 100000000 | bytes 4000000 | tf_op jit(solution)/shard_map/pair_grad/pallas_call | solution.py:661
Async XLA Ops:
  2.1 15.3 %collective-permute-start.1 = (bf16[4,48,128]{2,1,0:T(8,128)(2,1)}, bf16[4,48,128]{2,1,0:T(8,128)(2,1)}, u32[]{:S(2)}, u32[]{:S(2)}) collective-permute-start(bf16[4,48,128]{2,1,0:T(8,128)(2,1)} %get-tuple-element.30), channel_id=1, source_target_pairs={{1,0},{2,1},{3,2},{5,4},{6,5},{7,6},{9,8},{10,9},{11,10},{13,12},{... | collective-permute-start | bytes 147464 | tf_op jit(solution)/shard_map/ppermute | solution.py:692
  3.4 14.0 %collective-permute-start = (bf16[4,48,128]{2,1,0:T(8,128)(2,1)}, bf16[4,48,128]{2,1,0:T(8,128)(2,1)}, u32[]{:S(2)}, u32[]{:S(2)}) collective-permute-start(bf16[4,48,128]{2,1,0:T(8,128)(2,1)} %get-tuple-element.31), channel_id=1, source_target_pairs={{0,1},{1,2},{2,3},{4,5},{5,6},{6,7},{8,9},{9,10},{10,11},{12,13},{... | collective-permute-start | bytes 147464 | tf_op jit(solution)/shard_map/ppermute | solution.py:691
  10.1 35.2 %all-to-all-start = ((bf16[8,256,128]{2,1,0:T(8,128)(2,1)}), bf16[8,256,128]{2,1,0:T(8,128)(2,1)}, u32[]{:S(2)}, u32[]{:S(2)}) async-start(bf16[8,256,128]{2,1,0:T(8,128)(2,1)} %pair_bias.1), calls=%async_computation | async-start | bytes 1048576 | tf_op jit(solution)/shard_map/all_to_all | solution.py:696
  29.2 16.1 %collective-permute-start.7 = (bf16[2,64,768]{2,1,0:T(8,128)(2,1)}, bf16[2,64,768]{2,1,0:T(8,128)(2,1)}, u32[]{:S(2)}, u32[]{:S(2)}) collective-permute-start(bf16[2,64,768]{2,1,0:T(8,128)(2,1)} %get-tuple-element.20.refs_0_), channel_id=1, source_target_pairs={{0,3},{1,2},{2,1},{3,0},{4,7},{5,6},{6,5},{7,4},{8,11},{9,10},{10,... | collective-permute-start | bytes 589832 | tf_op jit(solution)/shard_map/ppermute | solution.py:673
  29.5 15.8 %collective-permute-start.6 = (bf16[2,64,768]{2,1,0:T(8,128)(2,1)}, bf16[2,64,768]{2,1,0:T(8,128)(2,1)}, u32[]{:S(2)}, u32[]{:S(2)}) collective-permute-start(bf16[2,64,768]{2,1,0:T(8,128)(2,1)} %get-tuple-element.20.refs_0_), channel_id=1, source_target_pairs={{0,2},{1,3},{2,0},{3,1},{4,6},{5,7},{6,4},{7,5},{8,10},{9,11},{10,... | collective-permute-start | bytes 589832 | tf_op jit(solution)/shard_map/ppermute | solution.py:673
  31.1 14.2 %collective-permute-start.5 = (bf16[2,64,768]{2,1,0:T(8,128)(2,1)}, bf16[2,64,768]{2,1,0:T(8,128)(2,1)}, u32[]{:S(2)}, u32[]{:S(2)}) collective-permute-start(bf16[2,64,768]{2,1,0:T(8,128)(2,1)} %get-tuple-element.20.refs_0_), channel_id=1, source_target_pairs={{0,1},{1,0},{2,3},{3,2},{4,5},{5,4},{6,7},{7,6},{8,9},{9,8},{10,11... | collective-permute-start | bytes 589832 | tf_op jit(solution)/shard_map/ppermute | solution.py:673
  43.1 8.7 %collective-permute-start.4 = (bf16[2,64,768]{2,1,0:T(8,128)(2,1)}, bf16[2,64,768]{2,1,0:T(8,128)(2,1)}, u32[]{:S(2)}, u32[]{:S(2)}) collective-permute-start(bf16[2,64,768]{2,1,0:T(8,128)(2,1)} %get-tuple-element.17.refs_0_), channel_id=1, source_target_pairs={{0,3},{1,2},{2,1},{3,0},{4,7},{5,6},{6,5},{7,4},{8,11},{9,10},{10,... | collective-permute-start | bytes 589832 | tf_op jit(solution)/shard_map/ppermute | solution.py:673
  44.3 10.6 %collective-permute-start.3 = (bf16[2,64,768]{2,1,0:T(8,128)(2,1)}, bf16[2,64,768]{2,1,0:T(8,128)(2,1)}, u32[]{:S(2)}, u32[]{:S(2)}) collective-permute-start(bf16[2,64,768]{2,1,0:T(8,128)(2,1)} %get-tuple-element.17.refs_0_), channel_id=1, source_target_pairs={{0,2},{1,3},{2,0},{3,1},{4,6},{5,7},{6,4},{7,5},{8,10},{9,11},{10,... | collective-permute-start | bytes 589832 | tf_op jit(solution)/shard_map/ppermute | solution.py:673
  45.3 9.6 %collective-permute-start.2 = (bf16[2,64,768]{2,1,0:T(8,128)(2,1)}, bf16[2,64,768]{2,1,0:T(8,128)(2,1)}, u32[]{:S(2)}, u32[]{:S(2)}) collective-permute-start(bf16[2,64,768]{2,1,0:T(8,128)(2,1)} %get-tuple-element.17.refs_0_), channel_id=1, source_target_pairs={{0,1},{1,0},{2,3},{3,2},{4,5},{5,4},{6,7},{7,6},{8,9},{9,8},{10,11... | collective-permute-start | bytes 589832 | tf_op jit(solution)/shard_map/ppermute | solution.py:673
  67.3 20.5 %all-to-all-start.1 = ((bf16[8,8,32,128]{3,2,1,0:T(8,128)(2,1)}), bf16[8,8,32,128]{3,2,1,0:T(8,128)(2,1)}, u32[]{:S(2)}, u32[]{:S(2)}) async-start(bf16[8,8,32,128]{3,2,1,0:T(8,128)(2,1)} %get-tuple-element.27), calls=%async_computation.1 | async-start | bytes 1048576 | tf_op jit(solution)/shard_map/all_to_all | solution.py:715

commit v7 on v6

--- a/solution.py
+++ b/solution.py
@@ -64,18 +64,28 @@
     return [nn(pick_heads(parity), w_bias_t) for parity in range(2)]
 
 
-def bias_kernel(pair_ref, gain_ref, w_bias_ref, out_ref, scaled_ref, stage_ref):
+def bias_kernel(
+    pair_hbm, gain_hbm, w_bias_hbm, feats_hbm, out_hbm, head_hbm, tail_hbm, pair_ref, gain_ref,
+    w_bias_ref, scaled_ref, stage_ref, local_ref, sems,
+):
     rows, keys = pair_ref.shape[0], pair_ref.shape[1]
+    atoms = feats_hbm.shape[1]
+    part = rows // 4
+    moves = [(gain_hbm, gain_ref), (w_bias_hbm, w_bias_ref)]
+    for i in range(4):
+        moves.append((pair_hbm.at[pl.ds(part * i, part)], pair_ref.at[pl.ds(part * i, part)]))
+    moves.append((feats_hbm.at[:, pl.ds(0, HALO), :], head_hbm))
+    moves.append((feats_hbm.at[:, pl.ds(atoms - HALO, HALO), :], tail_hbm))
+    copies = start_all(moves, sems)
+    for copy in copies[0:2]:
+        copy.wait()
     gain = gain_ref[...]
-
-    def norm_step(i, carry):
-        block = pair_ref[pl.ds(i * 8, 8)].astype(f32).reshape(8 * keys, CZ)
-        hat, unused = norm_rows(block)
-        scaled_ref[pl.ds(pl.multiple_of(i * 8 * keys, 8 * keys), 8 * keys), :] = hat * gain
-        return carry
-
-    lax.fori_loop(0, rows // 8, norm_step, 0, unroll=True)
     weights = jnp.concatenate(split_heads(w_bias_ref[...]), axis=1).astype(bf16)
+    for i in range(rows // 8):
+        if 8 * i % part == 0:
+            copies[2 + 8 * i // part].wait()
+        block = pair_ref[8 * i : 8 * i + 8].astype(f32).reshape(8 * keys, CZ)
+        scaled_ref[8 * keys * i : 8 * keys * (i + 1), :] = norm_rows(block)[0] * gain
     blank = jnp.zeros((rows, CZ), bf16)
     for j in range(keys):
         block = scaled_ref[pl.ds(j, rows, stride=keys), :].astype(bf16)
@@ -84,30 +94,45 @@
             axis=0,
         )
         stage_ref[pl.ds(j, PAIRS, stride=keys), :] = nt(weights, both)
-    for k in range(out_ref.shape[0]):
-        out_ref[k] = stage_ref[...].astype(bf16)
-
-
-def pair_bias(pair, pair_gain, w_bias_t, copies):
+    local_ref[...] = stage_ref[...].astype(bf16)
+    for copy in copies[6:]:
+        copy.wait()
+    back = start_all([(local_ref, out_hbm.at[k]) for k in range(out_hbm.shape[0])], sems)
+    for copy in back:
+        copy.wait()
+
+
+def pair_bias(pair, pair_gain, w_bias_t, feats, copies):
     rows, keys = pair.shape[0], pair.shape[1]
+    edge = jax.ShapeDtypeStruct((feats.shape[0], HALO, C_ATOM), bf16)
+    hbm = pl.BlockSpec(memory_space=pl.ANY)
     return pl.pallas_call(
         bias_kernel,
-        out_shape=jax.ShapeDtypeStruct((copies, keys * PAIRS, 2 * rows), bf16),
+        in_specs=[hbm] * 4,
+        out_specs=[hbm] * 3,
+        out_shape=[
+            jax.ShapeDtypeStruct((copies, keys * PAIRS, 2 * rows), bf16), edge, edge,
+        ],
         scratch_shapes=[
+            pltpu.VMEM(pair.shape, bf16),
+            pltpu.VMEM((1, CZ), f32),
+            pltpu.VMEM(w_bias_t.shape, bf16),
             pltpu.VMEM((rows * keys, CZ), f32),
             pltpu.VMEM((keys * PAIRS, 2 * rows), f32),
+            pltpu.VMEM((keys * PAIRS, 2 * rows), bf16),
+            pltpu.SemaphoreType.DMA((max(8, copies),)),
         ],
         compiler_params=pltpu.CompilerParams(vmem_limit_bytes=GRANT),
         cost_estimate=pl.CostEstimate(flops=10**7, bytes_accessed=10**7, transcendentals=0),
         name="pair_bias",
-    )(pair, pair_gain.reshape(1, CZ), w_bias_t)
+    )(pair, pair_gain.reshape(1, CZ), w_bias_t, feats)
 
 
 def atom_kernel(
     feats_hbm, left_hbm, right_hbm, mask_hbm, counts_hbm, single_hbm, w_qkv_hbm, w_out_hbm,
     w_embed_hbm, tokens_ref, normed_ref, mask_ref, counts_ref, single_ref, w_qkv_ref, w_out_ref,
-    w_embed_ref, sems, padded_ref, qkv_a, qkv_b, scores_a, scores_b, probs_a, probs_b, mixed_ref,
-    split_ref, keybias_ref, onehot_ref, pooled_ref, *, first,
+    w_embed_ref, sems, padded_ref, normed_atoms_ref, qkv_a, qkv_b, scores_a, scores_b, probs_a, probs_b, mixed_ref,
+    updated_ref, split_ref, keybias_ref, onehot_ref, *, first,
 ):
     batch, atoms = tokens_ref.shape[0], feats_hbm.shape[1]
     padded = atoms + 2 * HALO
@@ -147,19 +172,20 @@
     for g in range(chunks):
         at = pos + float(g * 256)
         hit = jnp.where((at >= start) & (at < start + own), 1.0, 0.0).astype(bf16)
-        onehot_ref[g] = jnp.concatenate([hit, hit], axis=1)
-    pooled_ref[...] = jnp.zeros_like(pooled_ref)
+        onehot_ref[:, 256 * g : 256 * g + 256] = hit
+        onehot_ref[:, atoms + 256 * g : atoms + 256 * g + 256] = hit
+    probs_a[...] = jnp.zeros_like(probs_a)
+    probs_b[...] = jnp.zeros_like(probs_b)
     head_of = iota((32, 128), 1) // ATOM_HD
     head_mask = [(head_of == h).astype(f32).astype(bf16) for h in range(ATOM_HEADS)]
     own_atom = (iota((32, 128), 1) % 32) == iota((32, 128), 0)
     factor = ATOM_HD ** (-0.5) * LOG2E
-    stride = padded // chunks // 16 * 16
-    span = padded - stride * (chunks - 1)
-
-    def qkv_step(s, i):
-        at = pl.multiple_of(i * stride, 16)
-        normed, unused = norm_rows(padded_ref[s, pl.ds(at, span), :].astype(f32))
-        qkv_refs[s % 2][pl.ds(at, span), :] = nn(normed.astype(bf16), w_qkv_ref[...]).astype(bf16)
+    def qkv_step(s):
+        for low in range(0, padded, padded // 4):
+            part = slice(low, low + padded // 4)
+            normed, unused = norm_rows(padded_ref[s, part, :].astype(f32))
+            normed_atoms_ref[part, :] = normed.astype(bf16)
+        qkv_refs[s % 2][...] = nn(normed_atoms_ref[...], w_qkv_ref[...]).astype(bf16)
 
     def score_step(s, group, to_ref):
         qkv_ref = qkv_refs[s % 2]
@@ -188,47 +214,45 @@
                 scores = from_ref[k, 32 * w : 32 * w + 128, 128 * w : 128 * w + 128] + keybias
                 expo = jnp.exp2((scores - jnp.max(scores, axis=0, keepdims=True)) * factor)
                 weights = expo * (1.0 / jnp.sum(expo, axis=0, keepdims=True))
-                to_ref[2 * k + w] = weights.astype(bf16)
+                to_ref[k, 32 * w : 32 * w + 128, 128 * w : 128 * w + 128] = weights.astype(bf16)
 
     def value_step(s, group, from_ref):
         qkv_ref = qkv_refs[s % 2]
         for k in range(2):
             base = pl.multiple_of(group * 128 + 64 * k, 64)
+            part = tn(from_ref[k], qkv_ref[pl.ds(base, 160), 2 * C_ATOM : 3 * C_ATOM])
             mixes = []
             for w in range(2):
-                values = qkv_ref[pl.ds(base + 32 * w, 128), 2 * C_ATOM : 3 * C_ATOM]
-                part = tn(from_ref[2 * k + w], values)
-                mix = part[0:32]
+                mix = part[128 * w : 128 * w + 32]
                 for h in range(1, ATOM_HEADS):
-                    mix = jnp.where(head_of == h, part[32 * h : 32 * h + 32], mix)
+                    low = 128 * w + 32 * h
+                    mix = jnp.where(head_of == h, part[low : low + 32], mix)
                 mixes.append(mix.astype(bf16))
-            mixed_ref[s, pl.ds(base, 64), :] = jnp.concatenate(mixes, axis=0)
-
-    def embed_step(s, g):
-        base = pl.multiple_of(g * 256, 256)
-        feats = padded_ref[s, pl.ds(base + HALO, 256), :].astype(f32)
-        updated = (feats + nn(mixed_ref[s, pl.ds(base, 256), :], w_out_ref[...])).astype(bf16)
-        embedded = jnp.maximum(nn(updated, w_embed_ref[...]), 0.0)
-        high = embedded.astype(bf16)
-        split_ref[0:256, :] = high
-        split_ref[256:512, :] = (embedded - high.astype(f32)).astype(bf16)
-        pooled_ref[s] += nn(onehot_ref[g], split_ref[...])
+            mixed_ref[pl.ds(base, 64), :] = jnp.concatenate(mixes, axis=0)
+
+    def embed_step(s):
+        feats = padded_ref[s, HALO : HALO + atoms, :].astype(f32)
+        updated_ref[...] = (feats + nn(mixed_ref[...], w_out_ref[...])).astype(bf16)
+        for n in range(0, C_TOK, 256):
+            embedded = jnp.maximum(nn(updated_ref[...], w_embed_ref[:, n : n + 256]), 0.0)
+            high = embedded.astype(bf16)
+            split_ref[0:atoms, n : n + 256] = high
+            split_ref[atoms : 2 * atoms, n : n + 256] = (embedded - high.astype(f32)).astype(bf16)
+        pooled = nn(onehot_ref[...], split_ref[...])
+        tokens = pooled / own + single_ref[...].astype(f32)
+        tokens_ref[s] = tokens
+        normed_ref[s] = norm_rows(tokens)[0].astype(bf16)
 
     for copy in copies[2:6]:
         copy.wait()
-    for i in range(chunks):
-        qkv_step(0, i)
+    qkv_step(0)
     for copy in copies[6:]:
         copy.wait()
     for s in range(batch):
         score_step(s, 0, scores_a)
 
-        def window_step(i, carry, s=s, lagging=True):
+        def window_step(i, carry, s=s):
             even, odd = 2 * i, 2 * i + 1
-            if lagging:
-                embed_step(s, i - 2)
-            if s + 1 < batch:
-                qkv_step(s + 1, i)
             score_step(s, odd, scores_b)
             softmax_step(even, scores_a, probs_a)
             value_step(s, jnp.maximum(even - 1, 0), probs_b)
@@ -237,18 +261,11 @@
             value_step(s, even, probs_a)
             return carry
 
-        for i in range(2):
-            if s > 0:
-                embed_step(s - 1, chunks - 2 + i)
-            window_step(i, 0, lagging=False)
-        lax.fori_loop(2, chunks, window_step, 0)
+        lax.fori_loop(0, chunks, window_step, 0)
         value_step(s, 2 * chunks - 1, probs_b)
-    for i in range(2):
-        embed_step(batch - 1, chunks - 2 + i)
-    for s in range(batch):
-        tokens = pooled_ref[s] / own + single_ref[...].astype(f32)
-        tokens_ref[s] = tokens
-        normed_ref[s] = norm_rows(tokens)[0].astype(bf16)
+        embed_step(s)
+        if s + 1 < batch:
+            qkv_step(s + 1)
 
 
 def atom_stage(part, batch, feats, left, right, mask, counts, single, w_qkv, w_out, w_embed):
@@ -272,17 +289,18 @@
             pltpu.VMEM(w_embed.shape, bf16),
             pltpu.SemaphoreType.DMA((6 + 3 * batch,)),
             pltpu.VMEM((batch, padded, C_ATOM), bf16),
+            pltpu.VMEM((padded, C_ATOM), bf16),
             pltpu.VMEM((padded, 3 * C_ATOM), bf16),
             pltpu.VMEM((padded, 3 * C_ATOM), bf16),
             pltpu.VMEM((2, 160, 256), f32),
             pltpu.VMEM((2, 160, 256), f32),
-            pltpu.VMEM((4, 128, 128), bf16),
-            pltpu.VMEM((4, 128, 128), bf16),
-            pltpu.VMEM((batch, atoms, C_ATOM), bf16),
-            pltpu.VMEM((512, C_TOK), bf16),
+            pltpu.VMEM((2, 160, 256), bf16),
+            pltpu.VMEM((2, 160, 256), bf16),
+            pltpu.VMEM((atoms, C_ATOM), bf16),
+            pltpu.VMEM((atoms, C_ATOM), bf16),
+            pltpu.VMEM((2 * atoms, C_TOK), bf16),
             pltpu.VMEM((padded, 128), f32),
-            pltpu.VMEM((atoms // 256, tok_rows, 512), bf16),
-            pltpu.VMEM((batch, tok_rows, C_TOK), f32),
+            pltpu.VMEM((tok_rows, 2 * atoms), bf16),
         ],
         compiler_params=pltpu.CompilerParams(vmem_limit_bytes=GRANT),
         cost_estimate=pl.CostEstimate(
@@ -383,18 +401,28 @@
 
 def attend_kernel(*refs, count):
     (
-        bias_hbm, w_qkv_hbm, att_ref, probs_hbm, values_hbm, w_qkv_ref, bias_ref, probs_ref,
-        values_ref, sems, all_ref, queries_ref, keys_ref,
+        bias_hbm, w_qkv_hbm, cot_hbm, w_down_hbm, att_ref, probs_hbm, values_hbm, d_hidden_hbm,
+        w_qkv_ref, bias_ref, cot_ref, w_down_ref, probs_ref, values_ref, d_hidden_ref, sems,
+        all_ref, queries_ref, keys_ref,
     ) = refs[count:]
     batch = all_ref.shape[0]
     moves = project_moves(refs[:count], w_qkv_hbm, w_qkv_ref, all_ref)
-    copies = start_all(moves + [(bias_hbm, bias_ref)], sems)
-    project(copies[:-1], w_qkv_ref, all_ref, queries_ref, keys_ref, values_ref)
-    copies[-1].wait()
+    moves += [(bias_hbm, bias_ref), (cot_hbm, cot_ref), (w_down_hbm, w_down_ref)]
+    copies = start_all(moves, sems)
+    project(copies[:-3], w_qkv_ref, all_ref, queries_ref, keys_ref, values_ref)
+    for copy in copies[-3:]:
+        copy.wait()
     back = [
         pltpu.make_async_copy(probs_ref.at[s], probs_hbm.at[s], sems.at[s]) for s in range(batch)
-    ] + [pltpu.make_async_copy(values_ref, values_hbm, sems.at[batch])]
+    ] + [
+        pltpu.make_async_copy(values_ref, values_hbm, sems.at[batch]),
+        pltpu.make_async_copy(d_hidden_ref, d_hidden_hbm, sems.at[batch + 1]),
+    ]
     back[batch].start()
+    cot = cot_ref[...].reshape(-1, C_TOK)
+    for n in range(0, w_down_ref.shape[0], 256):
+        d_hidden_ref[:, n : n + 256] = nt(cot, w_down_ref[n : n + 256, :])
+    back[batch + 1].start()
     attend(
         bias_ref, queries_ref, keys_ref, values_ref, probs_ref, att_ref, lambda s: back[s].start()
     )
@@ -410,26 +438,31 @@
     ]
 
 
-def attend_stage(pieces, bias, w_qkv):
+def attend_stage(pieces, bias, w_qkv, cot, w_down):
     batch, tok_rows, _ = pieces[0].shape
     keys_all = tok_rows * len(pieces)
     vmem = pl.BlockSpec(memory_space=pltpu.VMEM)
     hbm = pl.BlockSpec(memory_space=pl.ANY)
+    d_hidden = jax.ShapeDtypeStruct((cot.shape[0] * tok_rows, w_down.shape[0]), f32)
     return pl.pallas_call(
         functools.partial(attend_kernel, count=len(pieces)),
-        in_specs=[hbm] * (len(pieces) + 2),
-        out_specs=[vmem, hbm, hbm],
+        in_specs=[hbm] * (len(pieces) + 4),
+        out_specs=[vmem, hbm, hbm, hbm],
         out_shape=[
             jax.ShapeDtypeStruct((batch * tok_rows, C_TOK), bf16),
             jax.ShapeDtypeStruct((batch, PAIRS, keys_all, 2 * tok_rows), f32),
             jax.ShapeDtypeStruct((batch, keys_all, C_TOK), bf16),
+            d_hidden,
         ],
         scratch_shapes=[
             pltpu.VMEM((3, C_TOK, C_TOK), bf16),
             pltpu.VMEM(bias.shape, bf16),
+            pltpu.VMEM(cot.shape, bf16),
+            pltpu.VMEM(w_down.shape, bf16),
             pltpu.VMEM((batch, PAIRS, keys_all, 2 * tok_rows), f32),
             pltpu.VMEM((batch, keys_all, C_TOK), bf16),
-            pltpu.SemaphoreType.DMA((4 + len(pieces),)),
+            pltpu.VMEM(d_hidden.shape, f32),
+            pltpu.SemaphoreType.DMA((6 + len(pieces),)),
         ]
         + attend_scratch(batch, tok_rows, keys_all),
         compiler_params=pltpu.CompilerParams(vmem_limit_bytes=GRANT),
@@ -437,16 +470,16 @@
             flops=4 * 10**9, bytes_accessed=10**7, transcendentals=10**6
         ),
         name="attend",
-    )(*pieces, bias, w_qkv)
+    )(*pieces, bias, w_qkv, cot, w_down)
 
 
 def token_kernel(*refs, count):
     (
         bias_hbm, tokens_a_hbm, tokens_b_hbm, att_a_hbm, cot_hbm, probs_a_hbm, values_a_hbm,
-        w_qkv_hbm, w_out_hbm, w_gate_hbm, w_up_hbm, w_down_hbm,
+        w_qkv_hbm, w_out_hbm, w_gate_hbm, w_up_hbm, d_hidden_hbm,
         resid_hbm, hidden_hbm, d_bias_ref,
         bias_ref, tokens_ref, att_a_ref, cot_ref, resid_ref, hidden_ref,
-        w_qkv_ref, w_out_ref, w_gate_ref, w_up_ref, w_down_ref, probs_ref, values_ref, sems,
+        w_qkv_ref, w_out_ref, w_gate_ref, w_up_ref, d_hidden_ref, probs_ref, values_ref, sems,
         all_ref, queries_ref, keys_ref, grads_ref, d_gate_ref, d_up_ref, hat_ref,
     ) = refs[count:]
     batch, tok_rows = cot_ref.shape[0], cot_ref.shape[1]
@@ -460,7 +493,7 @@
         (bias_hbm, bias_ref), (w_out_hbm, w_out_ref), (att_a_hbm, att_a_ref),
         (tokens_a_hbm, tokens_ref.at[pl.ds(0, ahead)]),
         (tokens_b_hbm, tokens_ref.at[pl.ds(ahead, batch - ahead)]), (cot_hbm, cot_ref),
-        (w_down_hbm, w_down_ref), (w_gate_hbm, w_gate_ref), (w_up_hbm, w_up_ref),
+        (d_hidden_hbm, d_hidden_ref), (w_gate_hbm, w_gate_ref), (w_up_hbm, w_up_ref),
         (values_a_hbm, values_ref.at[pl.ds(0, ahead)]), (probs_a_hbm, probs_ref.at[pl.ds(0, ahead)]),
     ]
     copies = start_all(moves, sems)
@@ -491,7 +524,7 @@
         shaped = grads_ref[...]
         gate = nn(shaped, w_gate_ref[:, n : n + 256])
         up = nn(shaped, w_up_ref[:, n : n + 256])
-        d_hidden = nt(cot_ref[...].reshape(rows, C_TOK), w_down_ref[n : n + 256, :])
+        d_hidden = d_hidden_ref[:, n : n + 256]
         sig = 1.0 / (1.0 + jnp.exp(-gate))
         act = gate * sig
         hidden_ref[:, n : n + 256] = (act * up).astype(bf16)
@@ -538,7 +571,7 @@
 
 def token_stage(
     pieces, bias, tokens_a, tokens_b, att_a, cot, probs_a, values_a, w_qkv, w_out, w_gate, w_up,
-    w_down,
+    d_hidden,
 ):
     batch, tok_rows, _ = cot.shape
     keys_all = tok_rows * len(pieces)
@@ -566,7 +599,7 @@
             pltpu.VMEM(w_out.shape, bf16),
             pltpu.VMEM(w_gate.shape, bf16),
             pltpu.VMEM(w_up.shape, bf16),
-            pltpu.VMEM(w_down.shape, bf16),
+            pltpu.VMEM(d_hidden.shape, f32),
             pltpu.VMEM((batch, PAIRS, keys_all, 2 * tok_rows), f32),
             pltpu.VMEM((batch, keys_all, C_TOK), bf16),
             pltpu.SemaphoreType.DMA((14 + len(pieces),)),
@@ -585,7 +618,7 @@
         name="tokens",
     )(
         *pieces, bias, tokens_a, tokens_b, att_a, cot, probs_a, values_a, w_qkv, w_out, w_gate,
-        w_up, w_down,
+        w_up, d_hidden,
     )
 
 
@@ -603,7 +636,8 @@
         hat, rstd = norm_rows(pairf_ref[pl.ds(j, rows, stride=keys), :])
         at = pl.multiple_of(j * rows, rows)
         hat_ref[pl.ds(at, rows), :] = hat
-        rstd_ref[pl.ds(at, rows), :] = jnp.broadcast_to(rstd, (rows, CZ))
+        rstd = jnp.broadcast_to(rstd, (rows, CZ)).T[0:1]
+        rstd_ref[pl.ds(j, 1), :] = jnp.concatenate([rstd, rstd], axis=1)
         return carry
 
     lax.fori_loop(0, keys, norm_step, 0, unroll=4)
@@ -614,7 +648,10 @@
     return pl.pallas_call(
         output_kernel,
         out_shape=[jax.ShapeDtypeStruct(resid.shape, bf16)]
-        + [jax.ShapeDtypeStruct((rows * keys, CZ), f32)] * 2,
+        + [
+            jax.ShapeDtypeStruct((rows * keys, CZ), f32),
+            jax.ShapeDtypeStruct((keys, 2 * rows), f32),
+        ],
         scratch_shapes=[pltpu.VMEM((rows * keys, CZ), f32)],
         compiler_params=pltpu.CompilerParams(vmem_limit_bytes=GRANT),
         cost_estimate=pl.CostEstimate(
@@ -624,14 +661,22 @@
     )(resid, hidden, w_down, pair)
 
 
-def grad_kernel(parts_ref, hat_ref, rstd_ref, gain_ref, w_bias_ref, out_ref, total_ref):
+def grad_kernel(
+    parts_hbm, hat_hbm, rstd_hbm, gain_hbm, w_bias_hbm, out_hbm, parts_ref, hat_ref, rstd_ref,
+    gain_ref, w_bias_ref, total_ref, out_ref, sems,
+):
     keys = parts_ref.shape[2]
     rows = hat_ref.shape[0] // keys
-    for pair in range(PAIRS):
-        total = parts_ref[0, pair].astype(f32)
-        for k in range(1, parts_ref.shape[0]):
-            total = total + parts_ref[k, pair].astype(f32)
-        total_ref[pair * keys : (pair + 1) * keys, :] = total
+    size = 8 * rows
+    moves = [
+        (gain_hbm, gain_ref), (w_bias_hbm, w_bias_ref), (parts_hbm, parts_ref),
+        (rstd_hbm, rstd_ref),
+    ]
+    for c in range(keys // 8):
+        moves.append((hat_hbm.at[pl.ds(size * c, size)], hat_ref.at[pl.ds(size * c, size)]))
+    copies = start_all(moves, sems)
+    for copy in copies[0:2]:
+        copy.wait()
     weights = jnp.concatenate(split_heads(w_bias_ref[...]), axis=0) * gain_ref[...]
     weights = weights - jnp.mean(weights, axis=-1, keepdims=True)
     weights = jnp.concatenate([weights[0:PAIRS], weights[PAIRS:HEADS]], axis=1)
@@ -640,33 +685,62 @@
     w_low = weights - w_high - w_middle
     weights = jnp.concatenate([w_high, w_middle, w_low, w_high, w_middle, w_high], axis=0)
     weights = weights.astype(bf16)
-    for j in range(keys):
-        total = total_ref[pl.ds(j, PAIRS, stride=keys), :]
-        high = total.astype(bf16).astype(f32)
-        middle = (total - high).astype(bf16).astype(f32)
-        low = total - high - middle
-        stack = jnp.concatenate([high, high, high, middle, middle, low], axis=0)
-        both = nn(stack.T.astype(bf16), weights)
-        scaled = both[0:rows, 0:CZ] + both[rows : 2 * rows, CZ : 2 * CZ]
-        hat = hat_ref[rows * j : rows * (j + 1), :]
-        second = jnp.mean(scaled * hat, axis=-1, keepdims=True)
-        out_ref[pl.ds(j, rows, stride=keys), :] = rstd_ref[rows * j : rows * (j + 1), :] * (
-            scaled - hat * second
+    for copy in copies[2:4]:
+        copy.wait()
+    for pair in range(PAIRS):
+        total = parts_ref[0, pair].astype(f32)
+        for k in range(1, parts_ref.shape[0]):
+            total = total + parts_ref[k, pair].astype(f32)
+        total_ref[pair * keys : (pair + 1) * keys, :] = total * rstd_ref[...]
+    back = []
+    for c in range(keys // 8):
+        copies[4 + c].wait()
+        for j in range(8 * c, 8 * c + 8):
+            total = total_ref[pl.ds(j, PAIRS, stride=keys), :]
+            high = total.astype(bf16).astype(f32)
+            middle = (total - high).astype(bf16).astype(f32)
+            low = total - high - middle
+            stack = jnp.concatenate([high, high, high, middle, middle, low], axis=0)
+            both = nn(stack.T.astype(bf16), weights)
+            scaled = both[0:rows, 0:CZ] + both[rows : 2 * rows, CZ : 2 * CZ]
+            hat = hat_ref[rows * j : rows * (j + 1), :]
+            second = jnp.mean(scaled * hat, axis=-1, keepdims=True)
+            out_ref[pl.ds(size * c + j % 8, rows, stride=8), :] = scaled - hat * second
+        back.append(
+            pltpu.make_async_copy(
+                out_ref.at[pl.ds(size * c, size)].reshape(rows, 8, CZ),
+                out_hbm.at[:, pl.ds(8 * c, 8), :],
+                sems.at[c],
+            )
         )
+        back[c].start()
+    for copy in back:
+        copy.wait()
 
 
 def pair_back(parts, hat, rstd, pair_gain, w_bias_t):
     keys = parts.shape[2]
     rows = hat.shape[0] // keys
-    out = pl.pallas_call(
+    hbm = pl.BlockSpec(memory_space=pl.ANY)
+    return pl.pallas_call(
         grad_kernel,
-        out_shape=jax.ShapeDtypeStruct((rows * keys, CZ), f32),
-        scratch_shapes=[pltpu.VMEM((keys * PAIRS, 2 * rows), f32)],
+        in_specs=[hbm] * 5,
+        out_specs=hbm,
+        out_shape=jax.ShapeDtypeStruct((rows, keys, CZ), f32),
+        scratch_shapes=[
+            pltpu.VMEM(parts.shape, bf16),
+            pltpu.VMEM(hat.shape, f32),
+            pltpu.VMEM(rstd.shape, f32),
+            pltpu.VMEM((1, CZ), f32),
+            pltpu.VMEM(w_bias_t.shape, bf16),
+            pltpu.VMEM((keys * PAIRS, 2 * rows), f32),
+            pltpu.VMEM((rows * keys, CZ), f32),
+            pltpu.SemaphoreType.DMA((4 + keys // 8,)),
+        ],
         compiler_params=pltpu.CompilerParams(vmem_limit_bytes=GRANT),
         cost_estimate=pl.CostEstimate(flops=10**8, bytes_accessed=4 * 10**6, transcendentals=0),
         name="pair_grad",
     )(parts, hat, rstd, pair_gain.reshape(1, CZ), w_bias_t)
-    return out.reshape(rows, keys, CZ)
 
 
 def swap(values, axis, k):
@@ -687,12 +761,12 @@
     shards = lax.axis_size("tok")
     groups = lax.axis_size("samp")
 
+    w_bias_t = w_bias.T
+    local_bias, head, tail = pair_bias(pair, pair_gain, w_bias_t, atom_feats, groups)
     steps = [(i, i + 1) for i in range(shards - 1)]
-    left = lax.ppermute(atom_feats[:, atom_rows - HALO :], "tok", steps)
-    right = lax.ppermute(atom_feats[:, :HALO], "tok", [(j, i) for i, j in steps])
-
-    w_bias_t = w_bias.T
-    local_bias = pair_bias(pair, pair_gain, w_bias_t, groups)
+    left = lax.ppermute(tail, "tok", steps)
+    right = lax.ppermute(head, "tok", [(j, i) for i, j in steps])
+
     bias = lax.all_to_all(local_bias, "samp", 0, 0).reshape(groups, PAIRS, -1, 2 * tok_rows)
 
     mask = atom_mask.reshape(-1, 128)
@@ -707,10 +781,12 @@
         )
         tokens.append(tok)
         gathered.append(gather(normed, "tok"))
-    att_a, probs_a, values_a = attend_stage(gathered[0], bias, w_qkv)
+    att_a, probs_a, values_a, d_hidden = attend_stage(
+        gathered[0], bias, w_qkv, cotangent, w_down
+    )
     resid, hidden, d_bias = token_stage(
         gathered[1], bias, *tokens, att_a, cotangent, probs_a, values_a, w_qkv, w_out, w_gate,
-        w_up, w_down,
+        w_up, d_hidden,
     )
     parts = lax.all_to_all(d_bias, "samp", 0, 0)
     token_out, hat, rstd = output_stage(resid, hidden, w_down, pair)

time: 92.5 us -> 90.7 us (0.981)
  waiting for transfers between devices: 11.2 us -> 9.32 us
  local copies, waits for them, and re-layouts: 1.47 us -> 0 us
  Pallas kernels: 56.3 us -> 57.4 us
    pallas_call x2, Pallas kernels: 23.7 us -> 22.1 us  [atom_stage(): pl.pallas_call(functools.partial(atom_kernel, first=part * batch), in_spe...]
    ppermute x6, starting transfers between devices: 4.13 us -> 5.78 us  [swap(): lax.ppermute(values, axis, [(i, i ^ k) for i in range(lax.axis_size(axis))])]
    slice x1 -> x0, local copies, waits for them, and re-layouts: 1.47 us -> none  [body(): atom_feats[:, :HALO]]
    pallas_call x2, Pallas kernels: 7.18 us -> 8.63 us  [the longest x1 4.94 us: pair_bias(): pl.pallas_call(bias_kernel, in_specs=[hbm] * 4, out_specs=[hbm] * 3, out_...]
    all_to_all x1, waiting for transfers between devices: 8.11 us -> 6.9 us  [body(): parts = lax.all_to_all(d_bias, 'samp', 0, 0)]
    pallas_call x1, Pallas kernels: 6.41 us -> 7.41 us  [output_stage(): pl.pallas_call(output_kernel, out_shape=[jax.ShapeDtypeStruct(resid.shape...]
  transfers between devices with their start and end apart: 10 -> 10, of which waited for: 2 -> 2; matrix products, arithmetic and copies ran while one was open for 0% -> 0% of each run, Pallas kernels for 43% -> 41%
where the time goes in v7:
time: 90.7 us; the launch traced here: 90.3 us
  Pallas kernels  57.4 us (63%)
  starting transfers between devices  22.7 us (25%)
  waiting for transfers between devices  9.32 us (10%)
    pallas_call x2, Pallas kernels, atom_stage(): pl.pallas_call(functools.partial(atom_kernel, first=part * batch), in_spe...  22.1 us
    pallas_call x1, Pallas kernels, token_stage(): pl.pallas_call(functools.partial(token_kernel, count=len(pieces)), in_spe...  12.1 us
    pallas_call x1, Pallas kernels, output_stage(): pl.pallas_call(output_kernel, out_shape=[jax.ShapeDtypeStruct(resid.shape...  7.41 us
    pallas_call x1, Pallas kernels, attend_stage(): pl.pallas_call(functools.partial(attend_kernel, count=len(pieces)), in_sp...  7.17 us
    all_to_all x1, waiting for transfers between devices, body(): parts = lax.all_to_all(d_bias, 'samp', 0, 0)  6.9 us
    all_to_all x1, starting transfers between devices, body(): lax.all_to_all(local_bias, 'samp', 0, 0)  6.68 us
    all_to_all x1, starting transfers between devices, body(): parts = lax.all_to_all(d_bias, 'samp', 0, 0)  6.01 us
    ppermute x6, starting transfers between devices, swap(): lax.ppermute(values, axis, [(i, i ^ k) for i in range(lax.axis_size(axis))])  5.78 us
  transfers between devices with their start and end apart: 10, of which 2 were waited for; matrix products, arithmetic and copies ran while one was open for 0% of the time, Pallas kernels for 41%

profile of v7, /device:TPU:0, one launch (start us, length us, event | category | flops | bytes accessed | tf_op | source)
XLA Modules:
  0.0 90.3 jit_solution(5599589502668129723)
XLA Ops:
  0.6 4.9 %pair_bias.1 = (bf16[8,256,128]{2,1,0:T(8,128)(2,1)}, bf16[4,48,128]{2,1,0:T(8,128)(2,1)}, bf16[4,48,128]{2,1,0:T(8,128)(2,1)}) custom-call(bf16[64,32,128]{2,1,0:T(8,128)(2,1)} %pair_ref.1, f32[1,128]{1,0:T(1,128)} %bitcast.7, bf16[16,128]{1,0:T(8,128)(2,1)} %bitcast.5, bf16[4,1280,128]{2,1,0:T(8,128)(2,1)} %feats_hbm.5), custom_call_target="tpu_custom_call" | custom-call | flops 10000000 | bytes 10000000 | tf_op jit(solution)/shard_map/pair_bias/pallas_call | solution.py:109
  5.6 3.0 %collective-permute-start = (bf16[4,48,128]{2,1,0:T(8,128)(2,1)}, bf16[4,48,128]{2,1,0:T(8,128)(2,1)}, u32[]{:S(2)}, u32[]{:S(2)}) collective-permute-start(bf16[4,48,128]{2,1,0:T(8,128)(2,1)} %get-tuple-element.20), channel_id=1, source_target_pairs={{0,1},{1,2},{2,3},{4,5},{5,6},{6,7},{8,9},{9,10},{10,11},{12,13},{... | collective-permute-start | bytes 147464 | tf_op jit(solution)/shard_map/ppermute | solution.py:767
  8.5 1.3 %collective-permute-start.1 = (bf16[4,48,128]{2,1,0:T(8,128)(2,1)}, bf16[4,48,128]{2,1,0:T(8,128)(2,1)}, u32[]{:S(2)}, u32[]{:S(2)}) collective-permute-start(bf16[4,48,128]{2,1,0:T(8,128)(2,1)} %get-tuple-element.21), channel_id=1, source_target_pairs={{1,0},{2,1},{3,2},{5,4},{6,5},{7,6},{9,8},{10,9},{11,10},{13,12},{... | collective-permute-start | bytes 147464 | tf_op jit(solution)/shard_map/ppermute | solution.py:768
  9.8 6.7 %all-to-all-start = ((bf16[8,256,128]{2,1,0:T(8,128)(2,1)}), bf16[8,256,128]{2,1,0:T(8,128)(2,1)}, u32[]{:S(2)}, u32[]{:S(2)}) async-start(bf16[8,256,128]{2,1,0:T(8,128)(2,1)} %get-tuple-element.22), calls=%async_computation | async-start | bytes 1048576 | tf_op jit(solution)/shard_map/all_to_all | solution.py:770
  16.5 0.0 collective-permute-done.left_hbm
  16.5 0.0 collective-permute-done.1.right_hbm
  16.5 11.0 %atoms.3 = (f32[2,64,768]{2,1,0:T(8,128)}, bf16[2,64,768]{2,1,0:T(8,128)(2,1)}) custom-call(bf16[4,1280,128]{2,1,0:T(8,128)(2,1)} %feats_hbm.5, bf16[4,48,128]{2,1,0:T(8,128)(2,1)} %collective-permute-done.left_hbm, bf16[4,48,128]{2,1,0:T(8,128)(2,1)} %collective-permute-done.1.right_hbm, s32[40,128]{1,0:T(8,128)} %bitcast.10, s32[1,64]{1,0:T(1,128)} %counts_hbm.3, ...), custom_call_target="tpu_custom_call" | custom-call | flops 10000000000 | bytes 4000000 | tf_op jit(solution)/shard_map/atoms/pallas_call | solution.py:275
  27.5 2.2 %collective-permute-start.7 = (bf16[2,64,768]{2,1,0:T(8,128)(2,1)}, bf16[2,64,768]{2,1,0:T(8,128)(2,1)}, u32[]{:S(2)}, u32[]{:S(2)}) collective-permute-start(bf16[2,64,768]{2,1,0:T(8,128)(2,1)} %get-tuple-element.27.refs_0_), channel_id=1, source_target_pairs={{0,3},{1,2},{2,1},{3,0},{4,7},{5,6},{6,5},{7,4},{8,11},{9,10},{10,... | collective-permute-start | bytes 589832 | tf_op jit(solution)/shard_map/ppermute | solution.py:747
  29.7 1.4 %collective-permute-start.6 = (bf16[2,64,768]{2,1,0:T(8,128)(2,1)}, bf16[2,64,768]{2,1,0:T(8,128)(2,1)}, u32[]{:S(2)}, u32[]{:S(2)}) collective-permute-start(bf16[2,64,768]{2,1,0:T(8,128)(2,1)} %get-tuple-element.27.refs_0_), channel_id=1, source_target_pairs={{0,2},{1,3},{2,0},{3,1},{4,6},{5,7},{6,4},{7,5},{8,10},{9,11},{10,... | collective-permute-start | bytes 589832 | tf_op jit(solution)/shard_map/ppermute | solution.py:747
  31.1 0.0 collective-permute-start.5
  31.1 11.1 %atoms.2 = (f32[2,64,768]{2,1,0:T(8,128)}, bf16[2,64,768]{2,1,0:T(8,128)(2,1)}) custom-call(bf16[4,1280,128]{2,1,0:T(8,128)(2,1)} %feats_hbm.5, bf16[4,48,128]{2,1,0:T(8,128)(2,1)} %collective-permute-done.left_hbm, bf16[4,48,128]{2,1,0:T(8,128)(2,1)} %collective-permute-done.1.right_hbm, s32[40,128]{1,0:T(8,128)} %bitcast.11, s32[1,64]{1,0:T(1,128)} %counts_hbm.3, ...), custom_call_target="tpu_custom_call" | custom-call | flops 10000000000 | bytes 4000000 | tf_op jit(solution)/shard_map/atoms/pallas_call | solution.py:275
  42.3 1.4 %collective-permute-start.4 = (bf16[2,64,768]{2,1,0:T(8,128)(2,1)}, bf16[2,64,768]{2,1,0:T(8,128)(2,1)}, u32[]{:S(2)}, u32[]{:S(2)}) collective-permute-start(bf16[2,64,768]{2,1,0:T(8,128)(2,1)} %get-tuple-element.24.refs_0_), channel_id=1, source_target_pairs={{0,3},{1,2},{2,1},{3,0},{4,7},{5,6},{6,5},{7,4},{8,11},{9,10},{10,... | collective-permute-start | bytes 589832 | tf_op jit(solution)/shard_map/ppermute | solution.py:747
  43.7 0.7 collective-permute-start.3
  44.4 0.0 collective-permute-done.7.refs_3_
  44.4 0.0 collective-permute-start.2
  44.4 0.0 collective-permute-done.6.refs_2_
  44.4 0.0 collective-permute-done.5.refs_1_
  44.4 0.0 all-to-all-done
  44.5 7.2 %attend.1 = (bf16[128,768]{1,0:T(8,128)(2,1)}, f32[2,8,256,128]{3,2,1,0:T(8,128)}, bf16[2,256,768]{2,1,0:T(8,128)(2,1)}, f32[256,1536]{1,0:T(8,128)}) custom-call(bf16[2,64,768]{2,1,0:T(8,128)(2,1)} %get-tuple-element.27.refs_0_, bf16[2,64,768]{2,1,0:T(8,128)(2,1)} %collective-permute-done.5.refs_1_, bf16[2,64,768]{2,1,0:T(8,128)(2,1)} %collective-permute-done.6.refs_2_, ...), custom_call_target="tpu_custom_call" | custom-call | flops 4000000000 | bytes 10000000 | tf_op jit(solution)/shard_map/attend/pallas_call | solution.py:447
  51.6 0.0 collective-permute-done.4.refs_3_
  51.7 2.4 %collective-permute-done.3.refs_2_ = bf16[2,64,768]{2,1,0:T(8,128)(2,1)} collective-permute-done((bf16[2,64,768]{2,1,0:T(8,128)(2,1)}, bf16[2,64,768]{2,1,0:T(8,128)(2,1)}, u32[]{:S(2)}, u32[]{:S(2)}) %collective-permute-start.3) | collective-permute-done | bytes 196640 | tf_op jit(solution)/shard_map/ppermute | solution.py:747
  54.1 0.0 collective-permute-done.2.refs_1_
  54.1 12.1 %tokens.1 = (f32[256,768]{1,0:T(8,128)}, bf16[256,1536]{1,0:T(8,128)(2,1)}, bf16[8,8,32,128]{3,2,1,0:T(8,128)(2,1)}) custom-call(bf16[2,64,768]{2,1,0:T(8,128)(2,1)} %get-tuple-element.24.refs_0_, bf16[2,64,768]{2,1,0:T(8,128)(2,1)} %collective-permute-done.2.refs_1_, bf16[2,64,768]{2,1,0:T(8,128)(2,1)} %collective-permute-done.3.refs_2_, ...), custom_call_target="tpu_custom_call" | custom-call | flops 10000000000 | bytes 20000000 | tf_op jit(solution)/shard_map/tokens/pallas_call | solution.py:582
  66.1 6.0 %all-to-all-start.1 = ((bf16[8,8,32,128]{3,2,1,0:T(8,128)(2,1)}), bf16[8,8,32,128]{3,2,1,0:T(8,128)(2,1)}, u32[]{:S(2)}, u32[]{:S(2)}) async-start(bf16[8,8,32,128]{3,2,1,0:T(8,128)(2,1)} %get-tuple-element.35), calls=%async_computation.1 | async-start | bytes 1048576 | tf_op jit(solution)/shard_map/all_to_all | solution.py:791
  72.1 7.4 %output.1 = (bf16[256,768]{1,0:T(8,128)(2,1)}, f32[2048,128]{1,0:T(8,128)}, f32[32,128]{1,0:T(8,128)}) custom-call(f32[256,768]{1,0:T(8,128)} %get-tuple-element.32.resid_ref, bf16[256,1536]{1,0:T(8,128)(2,1)} %get-tuple-element.33.hidden_ref, bf16[1536,768]{1,0:T(8,128)(2,1)} %w_down_ref.1, bf16[64,32,128]{2,1,0:T(8,128)(2,1)} %pair_ref.1), custom_call_target="tpu_custom_call" | custom-call | flops 1000000000 | bytes 8000000 | tf_op jit(solution)/shard_map/output/pallas_call | solution.py:648
  79.5 6.9 %all-to-all-done.1.parts_hbm = bf16[8,8,32,128]{3,2,1,0:T(8,128)(2,1)} async-done(((bf16[8,8,32,128]{3,2,1,0:T(8,128)(2,1)}), bf16[8,8,32,128]{3,2,1,0:T(8,128)(2,1)}, u32[]{:S(2)}, u32[]{:S(2)}) %all-to-all-start.1) | async-done | bytes 524320 | tf_op jit(solution)/shard_map/all_to_all | solution.py:791
  86.4 3.7 %pair_grad.1 = f32[64,32,128]{2,1,0:T(8,128)} custom-call(bf16[8,8,32,128]{3,2,1,0:T(8,128)(2,1)} %all-to-all-done.1.parts_hbm, f32[2048,128]{1,0:T(8,128)} %get-tuple-element.36.hat_hbm, f32[32,128]{1,0:T(8,128)} %get-tuple-element.37.rstd_hbm, f32[1,128]{1,0:T(1,128)} %bitcast.8, bf16[16,128]{1,0:T(8,128)(2,1)} %bitcast.6), custom_call_target="tpu_custom_call" | custom-call | flops 100000000 | bytes 4000000 | tf_op jit(solution)/shard_map/pair_grad/pallas_call | solution.py:725
Async XLA Ops:
  5.6 10.9 %collective-permute-start = (bf16[4,48,128]{2,1,0:T(8,128)(2,1)}, bf16[4,48,128]{2,1,0:T(8,128)(2,1)}, u32[]{:S(2)}, u32[]{:S(2)}) collective-permute-start(bf16[4,48,128]{2,1,0:T(8,128)(2,1)} %get-tuple-element.20), channel_id=1, source_target_pairs={{0,1},{1,2},{2,3},{4,5},{5,6},{6,7},{8,9},{9,10},{10,11},{12,13},{... | collective-permute-start | bytes 147464 | tf_op jit(solution)/shard_map/ppermute | solution.py:767
  8.5 8.0 %collective-permute-start.1 = (bf16[4,48,128]{2,1,0:T(8,128)(2,1)}, bf16[4,48,128]{2,1,0:T(8,128)(2,1)}, u32[]{:S(2)}, u32[]{:S(2)}) collective-permute-start(bf16[4,48,128]{2,1,0:T(8,128)(2,1)} %get-tuple-element.21), channel_id=1, source_target_pairs={{1,0},{2,1},{3,2},{5,4},{6,5},{7,6},{9,8},{10,9},{11,10},{13,12},{... | collective-permute-start | bytes 147464 | tf_op jit(solution)/shard_map/ppermute | solution.py:768
  9.8 34.6 %all-to-all-start = ((bf16[8,256,128]{2,1,0:T(8,128)(2,1)}), bf16[8,256,128]{2,1,0:T(8,128)(2,1)}, u32[]{:S(2)}, u32[]{:S(2)}) async-start(bf16[8,256,128]{2,1,0:T(8,128)(2,1)} %get-tuple-element.22), calls=%async_computation | async-start | bytes 1048576 | tf_op jit(solution)/shard_map/all_to_all | solution.py:770
  27.5 16.9 %collective-permute-start.7 = (bf16[2,64,768]{2,1,0:T(8,128)(2,1)}, bf16[2,64,768]{2,1,0:T(8,128)(2,1)}, u32[]{:S(2)}, u32[]{:S(2)}) collective-permute-start(bf16[2,64,768]{2,1,0:T(8,128)(2,1)} %get-tuple-element.27.refs_0_), channel_id=1, source_target_pairs={{0,3},{1,2},{2,1},{3,0},{4,7},{5,6},{6,5},{7,4},{8,11},{9,10},{10,... | collective-permute-start | bytes 589832 | tf_op jit(solution)/shard_map/ppermute | solution.py:747
  29.7 14.7 %collective-permute-start.6 = (bf16[2,64,768]{2,1,0:T(8,128)(2,1)}, bf16[2,64,768]{2,1,0:T(8,128)(2,1)}, u32[]{:S(2)}, u32[]{:S(2)}) collective-permute-start(bf16[2,64,768]{2,1,0:T(8,128)(2,1)} %get-tuple-element.27.refs_0_), channel_id=1, source_target_pairs={{0,2},{1,3},{2,0},{3,1},{4,6},{5,7},{6,4},{7,5},{8,10},{9,11},{10,... | collective-permute-start | bytes 589832 | tf_op jit(solution)/shard_map/ppermute | solution.py:747
  31.1 13.4 %collective-permute-start.5 = (bf16[2,64,768]{2,1,0:T(8,128)(2,1)}, bf16[2,64,768]{2,1,0:T(8,128)(2,1)}, u32[]{:S(2)}, u32[]{:S(2)}) collective-permute-start(bf16[2,64,768]{2,1,0:T(8,128)(2,1)} %get-tuple-element.27.refs_0_), channel_id=1, source_target_pairs={{0,1},{1,0},{2,3},{3,2},{4,5},{5,4},{6,7},{7,6},{8,9},{9,8},{10,11... | collective-permute-start | bytes 589832 | tf_op jit(solution)/shard_map/ppermute | solution.py:747
  42.3 9.4 %collective-permute-start.4 = (bf16[2,64,768]{2,1,0:T(8,128)(2,1)}, bf16[2,64,768]{2,1,0:T(8,128)(2,1)}, u32[]{:S(2)}, u32[]{:S(2)}) collective-permute-start(bf16[2,64,768]{2,1,0:T(8,128)(2,1)} %get-tuple-element.24.refs_0_), channel_id=1, source_target_pairs={{0,3},{1,2},{2,1},{3,0},{4,7},{5,6},{6,5},{7,4},{8,11},{9,10},{10,... | collective-permute-start | bytes 589832 | tf_op jit(solution)/shard_map/ppermute | solution.py:747
  43.7 10.4 %collective-permute-start.3 = (bf16[2,64,768]{2,1,0:T(8,128)(2,1)}, bf16[2,64,768]{2,1,0:T(8,128)(2,1)}, u32[]{:S(2)}, u32[]{:S(2)}) collective-permute-start(bf16[2,64,768]{2,1,0:T(8,128)(2,1)} %get-tuple-element.24.refs_0_), channel_id=1, source_target_pairs={{0,2},{1,3},{2,0},{3,1},{4,6},{5,7},{6,4},{7,5},{8,10},{9,11},{10,... | collective-permute-start | bytes 589832 | tf_op jit(solution)/shard_map/ppermute | solution.py:747
  44.4 9.6 %collective-permute-start.2 = (bf16[2,64,768]{2,1,0:T(8,128)(2,1)}, bf16[2,64,768]{2,1,0:T(8,128)(2,1)}, u32[]{:S(2)}, u32[]{:S(2)}) collective-permute-start(bf16[2,64,768]{2,1,0:T(8,128)(2,1)} %get-tuple-element.24.refs_0_), channel_id=1, source_target_pairs={{0,1},{1,0},{2,3},{3,2},{4,5},{5,4},{6,7},{7,6},{8,9},{9,8},{10,11... | collective-permute-start | bytes 589832 | tf_op jit(solution)/shard_map/ppermute | solution.py:747
  66.1 20.3 %all-to-all-start.1 = ((bf16[8,8,32,128]{3,2,1,0:T(8,128)(2,1)}), bf16[8,8,32,128]{3,2,1,0:T(8,128)(2,1)}, u32[]{:S(2)}, u32[]{:S(2)}) async-start(bf16[8,8,32,128]{3,2,1,0:T(8,128)(2,1)} %get-tuple-element.35), calls=%async_computation.1 | async-start | bytes 1048576 | tf_op jit(solution)/shard_map/all_to_all | solution.py:791

commit v8 on v7

--- a/solution.py
+++ b/solution.py
@@ -23,7 +23,8 @@
 f32 = jnp.float32
 bf16 = jnp.bfloat16
 
-WINDOWS = ((0, 128), (0, 256), (128, 384), (256, 384))
+QUADS = HEADS // 4
+QUAD_WINDOWS = tuple((384 * (q // 2) + 128 * (q % 2), 384 * (q // 2) + 128 * (q % 2) + 256) for q in range(QUADS))
 
 
 def nn(a, b):
@@ -66,16 +67,18 @@
 
 def bias_kernel(
     pair_hbm, gain_hbm, w_bias_hbm, feats_hbm, out_hbm, head_hbm, tail_hbm, pair_ref, gain_ref,
-    w_bias_ref, scaled_ref, stage_ref, local_ref, sems,
+    w_bias_ref, scaled_ref, stage_ref, local_ref, head_ref, tail_ref, sems,
 ):
     rows, keys = pair_ref.shape[0], pair_ref.shape[1]
     atoms = feats_hbm.shape[1]
     part = rows // 4
-    moves = [(gain_hbm, gain_ref), (w_bias_hbm, w_bias_ref)]
+    moves = [
+        (gain_hbm, gain_ref), (w_bias_hbm, w_bias_ref),
+        (feats_hbm.at[:, pl.ds(0, HALO), :], head_ref),
+        (feats_hbm.at[:, pl.ds(atoms - HALO, HALO), :], tail_ref),
+    ]
     for i in range(4):
         moves.append((pair_hbm.at[pl.ds(part * i, part)], pair_ref.at[pl.ds(part * i, part)]))
-    moves.append((feats_hbm.at[:, pl.ds(0, HALO), :], head_hbm))
-    moves.append((feats_hbm.at[:, pl.ds(atoms - HALO, HALO), :], tail_hbm))
     copies = start_all(moves, sems)
     for copy in copies[0:2]:
         copy.wait()
@@ -83,9 +86,12 @@
     weights = jnp.concatenate(split_heads(w_bias_ref[...]), axis=1).astype(bf16)
     for i in range(rows // 8):
         if 8 * i % part == 0:
-            copies[2 + 8 * i // part].wait()
+            copies[4 + 8 * i // part].wait()
         block = pair_ref[8 * i : 8 * i + 8].astype(f32).reshape(8 * keys, CZ)
         scaled_ref[8 * keys * i : 8 * keys * (i + 1), :] = norm_rows(block)[0] * gain
+    for copy in copies[2:4]:
+        copy.wait()
+    edges = start_all([(head_ref, head_hbm), (tail_ref, tail_hbm)], sems)
     blank = jnp.zeros((rows, CZ), bf16)
     for j in range(keys):
         block = scaled_ref[pl.ds(j, rows, stride=keys), :].astype(bf16)
@@ -95,10 +101,13 @@
         )
         stage_ref[pl.ds(j, PAIRS, stride=keys), :] = nt(weights, both)
     local_ref[...] = stage_ref[...].astype(bf16)
-    for copy in copies[6:]:
-        copy.wait()
-    back = start_all([(local_ref, out_hbm.at[k]) for k in range(out_hbm.shape[0])], sems)
+    back = [
+        pltpu.make_async_copy(local_ref, out_hbm.at[k], sems.at[2 + k])
+        for k in range(out_hbm.shape[0])
+    ]
     for copy in back:
+        copy.start()
+    for copy in edges + back:
         copy.wait()
 
 
@@ -120,7 +129,9 @@
             pltpu.VMEM((rows * keys, CZ), f32),
             pltpu.VMEM((keys * PAIRS, 2 * rows), f32),
             pltpu.VMEM((keys * PAIRS, 2 * rows), bf16),
-            pltpu.SemaphoreType.DMA((max(8, copies),)),
+            pltpu.VMEM(edge.shape, bf16),
+            pltpu.VMEM(edge.shape, bf16),
+            pltpu.SemaphoreType.DMA((8 + copies,)),
         ],
         compiler_params=pltpu.CompilerParams(vmem_limit_bytes=GRANT),
         cost_estimate=pl.CostEstimate(flops=10**7, bytes_accessed=10**7, transcendentals=0),
@@ -312,17 +323,16 @@
 
 def head_masks(rows):
     masks = []
-    for pair in range(4):
-        low, high = WINDOWS[pair]
+    for quad, (low, high) in enumerate(QUAD_WINDOWS):
         lane = iota((rows, high - low), 1) + low
-        first = 2 * pair * HD
+        first = 4 * quad * HD
         masks.append(
-            [(lane >= first + HD * k) & (lane < first + HD * (k + 1)) for k in range(2)]
+            [(lane >= first + HD * k) & (lane < first + HD * (k + 1)) for k in range(4)]
         )
     return masks
 
 
-def two_heads(block, masks):
+def spread_heads(block, masks):
     blank = jnp.zeros_like(block)
     return jnp.concatenate([jnp.where(mask, block, blank) for mask in masks], axis=0)
 
@@ -340,7 +350,7 @@
     return [pieces[0], weights[0]] + pieces[1:] + weights[1:]
 
 
-def project(copies, w_qkv_ref, all_ref, queries_ref, keys_ref, values_ref):
+def project(copies, w_qkv_ref, all_ref, queries_ref, keys_ref, values_ref, loaded):
     batch = all_ref.shape[0]
     tok_rows = queries_ref.shape[0] // batch
     at = pl.multiple_of(lax.axis_index("tok") * tok_rows, tok_rows)
@@ -354,6 +364,7 @@
     for which, to_ref in ((1, keys_ref), (2, values_ref)):
         if which == 2:
             copies[-1].wait()
+            loaded()
         for n in range(0, C_TOK, 256):
             for s in range(batch):
                 to_ref[s, :, n : n + 256] = nn(
@@ -361,11 +372,6 @@
                 ).astype(bf16)
 
 
-def windows(pair):
-    low, high = WINDOWS[pair % 4]
-    return 384 * (pair // 4) + low, 384 * (pair // 4) + high
-
-
 def attend(bias_ref, queries_ref, keys_ref, values_ref, probs_ref, att_ref, done=None):
     batch, keys_all = keys_ref.shape[0], keys_ref.shape[1]
     tok_rows = queries_ref.shape[0] // batch
@@ -374,10 +380,13 @@
 
     for s in range(batch):
         at = s * tok_rows
-        for pair in range(PAIRS):
-            low, high = windows(pair)
-            queries = two_heads(queries_ref[pl.ds(at, tok_rows), low:high], masks[pair % 4])
-            probs_ref[s, pair] = nt(keys_ref[s, :, low:high], queries)
+        for quad, (low, high) in enumerate(QUAD_WINDOWS):
+            queries = spread_heads(queries_ref[at : at + tok_rows, low:high], masks[quad])
+            scores = nt(keys_ref[s, :, low:high], queries)
+            for half in range(2):
+                probs_ref[s, 2 * quad + half] = scores[
+                    :, 2 * tok_rows * half : 2 * tok_rows * (half + 1)
+                ]
         for pair in range(PAIRS):
             scores = probs_ref[s, pair] * factor
             bias = [bias_ref[k, pair].astype(f32) for k in range(bias_ref.shape[0])]
@@ -385,16 +394,18 @@
             expo = jnp.exp(scores - jnp.max(scores, axis=0, keepdims=True))
             probs_ref[s, pair] = expo * (1.0 / jnp.sum(expo, axis=0, keepdims=True))
         lanes = [jnp.zeros((tok_rows, 128), f32) for _ in range(C_TOK // 128)]
-        for pair in range(PAIRS):
-            low, high = windows(pair)
-            part = tn(probs_ref[s, pair].astype(bf16), values_ref[s, :, low:high])
-            first, second = masks[pair % 4]
-            mix = jnp.where(first, part[0:tok_rows], 0.0)
-            mix = jnp.where(second, part[tok_rows : 2 * tok_rows], mix)
+        for quad, (low, high) in enumerate(QUAD_WINDOWS):
+            probs = jnp.concatenate(
+                [probs_ref[s, 2 * quad + half].astype(bf16) for half in range(2)], axis=1
+            )
+            part = tn(probs, values_ref[s, :, low:high])
+            mix = jnp.where(masks[quad][0], part[0:tok_rows], 0.0)
+            for k in range(1, 4):
+                mix = jnp.where(masks[quad][k], part[tok_rows * k : tok_rows * (k + 1)], mix)
             for t in range((high - low) // 128):
                 lanes[low // 128 + t] = lanes[low // 128 + t] + mix[:, 128 * t : 128 * t + 128]
         for t in range(C_TOK // 128):
-            att_ref[pl.ds(at, tok_rows), 128 * t : 128 * t + 128] = lanes[t].astype(bf16)
+            att_ref[at : at + tok_rows, 128 * t : 128 * t + 128] = lanes[t].astype(bf16)
         if done is not None:
             done(s)
 
@@ -408,10 +419,16 @@
     batch = all_ref.shape[0]
     moves = project_moves(refs[:count], w_qkv_hbm, w_qkv_ref, all_ref)
     moves += [(bias_hbm, bias_ref), (cot_hbm, cot_ref), (w_down_hbm, w_down_ref)]
-    copies = start_all(moves, sems)
-    project(copies[:-3], w_qkv_ref, all_ref, queries_ref, keys_ref, values_ref)
-    for copy in copies[-3:]:
-        copy.wait()
+    copies = [pltpu.make_async_copy(src, dst, sems.at[i]) for i, (src, dst) in enumerate(moves)]
+    for copy in copies[:-2]:
+        copy.start()
+
+    def start_rest():
+        for copy in copies[-2:]:
+            copy.start()
+
+    project(copies[:-3], w_qkv_ref, all_ref, queries_ref, keys_ref, values_ref, start_rest)
+    copies[-3].wait()
     back = [
         pltpu.make_async_copy(probs_ref.at[s], probs_hbm.at[s], sems.at[s]) for s in range(batch)
     ] + [
@@ -419,13 +436,18 @@
         pltpu.make_async_copy(d_hidden_ref, d_hidden_hbm, sems.at[batch + 1]),
     ]
     back[batch].start()
-    cot = cot_ref[...].reshape(-1, C_TOK)
-    for n in range(0, w_down_ref.shape[0], 256):
-        d_hidden_ref[:, n : n + 256] = nt(cot, w_down_ref[n : n + 256, :])
-    back[batch + 1].start()
-    attend(
-        bias_ref, queries_ref, keys_ref, values_ref, probs_ref, att_ref, lambda s: back[s].start()
-    )
+
+    def done(s):
+        back[s].start()
+        if s == 0:
+            for copy in copies[-2:]:
+                copy.wait()
+            cot = cot_ref[...].reshape(-1, C_TOK)
+            for n in range(0, w_down_ref.shape[0], 256):
+                d_hidden_ref[:, n : n + 256] = nt(cot, w_down_ref[n : n + 256, :])
+            back[batch + 1].start()
+
+    attend(bias_ref, queries_ref, keys_ref, values_ref, probs_ref, att_ref, done)
     for copy in back:
         copy.wait()
 
@@ -496,10 +518,19 @@
         (d_hidden_hbm, d_hidden_ref), (w_gate_hbm, w_gate_ref), (w_up_hbm, w_up_ref),
         (values_a_hbm, values_ref.at[pl.ds(0, ahead)]), (probs_a_hbm, probs_ref.at[pl.ds(0, ahead)]),
     ]
-    copies = start_all(moves, sems)
+    copies = [pltpu.make_async_copy(src, dst, sems.at[i]) for i, (src, dst) in enumerate(moves)]
+    for copy in copies[: projecting + 1]:
+        copy.start()
+
+    def start_rest():
+        for copy in copies[projecting + 1 :]:
+            copy.start()
+
     own_values = values_ref.at[pl.ds(ahead, batch - ahead)]
     own_probs = probs_ref.at[pl.ds(ahead, batch - ahead)]
-    project(copies[:projecting], w_qkv_ref, all_ref, queries_ref, keys_ref, own_values)
+    project(
+        copies[:projecting], w_qkv_ref, all_ref, queries_ref, keys_ref, own_values, start_rest
+    )
     copies = copies[projecting:]
     copies[0].wait()
     attend(bias_ref, queries_ref, keys_ref, own_values, own_probs, queries_ref)
@@ -534,13 +565,9 @@
         d_up_ref[:, n : n + 256] = (d_hidden * act).astype(bf16)
 
     back[1].start()
-    parts = []
-    for n in range(0, C_TOK, 256):
-        parts.append(
-            nt(d_gate_ref[...], w_gate_ref[n : n + 256, :])
-            + nt(d_up_ref[...], w_up_ref[n : n + 256, :])
-        )
-    d_normed = jnp.concatenate(parts, axis=1)
+    d_normed = (
+        nt(w_gate_ref[...], d_gate_ref[...]) + nt(w_up_ref[...], d_up_ref[...])
+    ).T
     hat = hat_ref[...]
     first = jnp.mean(d_normed, axis=-1, keepdims=True)
     second = jnp.mean(d_normed * hat, axis=-1, keepdims=True)
@@ -551,20 +578,24 @@
     for copy in copies[9:]:
         copy.wait()
     masks = head_masks(tok_rows)
-    for pair in range(PAIRS):
-        low, high = windows(pair)
-        total = jnp.zeros((keys_all, 2 * tok_rows), f32)
+    size = d_bias_ref.shape[2]
+    for quad, (low, high) in enumerate(QUAD_WINDOWS):
+        totals = [jnp.zeros((keys_all, 2 * tok_rows), f32) for _ in range(2)]
         for s in range(batch):
-            grads = two_heads(
-                grads_ref[s * tok_rows : (s + 1) * tok_rows, low:high], masks[pair % 4]
+            grads = spread_heads(
+                grads_ref[s * tok_rows : (s + 1) * tok_rows, low:high], masks[quad]
             )
-            d_probs = nt(values_ref[s, :, low:high], grads)
-            probs = probs_ref[s, pair]
-            delta = jnp.sum(probs * d_probs, axis=0, keepdims=True)
-            total = total + probs * (d_probs - delta)
-        size = d_bias_ref.shape[2]
-        for k in range(d_bias_ref.shape[0]):
-            d_bias_ref[k, pair] = total[size * k : size * (k + 1)].astype(bf16)
+            d_both = nt(values_ref[s, :, low:high], grads)
+            for half in range(2):
+                d_probs = d_both[:, 2 * tok_rows * half : 2 * tok_rows * (half + 1)]
+                probs = probs_ref[s, 2 * quad + half]
+                delta = jnp.sum(probs * d_probs, axis=0, keepdims=True)
+                totals[half] = totals[half] + probs * (d_probs - delta)
+        for half in range(2):
+            for k in range(d_bias_ref.shape[0]):
+                d_bias_ref[k, 2 * quad + half] = totals[half][size * k : size * (k + 1)].astype(
+                    bf16
+                )
     for copy in back:
         copy.wait()
 

time: 90.7 us -> 90.8 us (level)
    pallas_call x1, Pallas kernels: 12.1 us -> 13.5 us  [token_stage(): pl.pallas_call(functools.partial(token_kernel, count=len(pieces)), in_spe...]
    pallas_call x1, Pallas kernels: 4.94 us -> 3.61 us  [pair_bias(): pl.pallas_call(bias_kernel, in_specs=[hbm] * 4, out_specs=[hbm] * 3, out_...]
where the time goes in v8:
time: 90.8 us; the launch traced here: 90.4 us
  Pallas kernels  58 us (64%)
  starting transfers between devices  22.7 us (25%)
  waiting for transfers between devices  8.81 us (10%)
    pallas_call x2, Pallas kernels, atom_stage(): pl.pallas_call(functools.partial(atom_kernel, first=part * batch), in_spe...  22.1 us
    pallas_call x1, Pallas kernels, token_stage(): pl.pallas_call(functools.partial(token_kernel, count=len(pieces)), in_spe...  13.5 us
    pallas_call x1, Pallas kernels, attend_stage(): pl.pallas_call(functools.partial(attend_kernel, count=len(pieces)), in_sp...  7.68 us
    pallas_call x1, Pallas kernels, output_stage(): pl.pallas_call(output_kernel, out_shape=[jax.ShapeDtypeStruct(resid.shape...  7.41 us
    all_to_all x1, waiting for transfers between devices, body(): parts = lax.all_to_all(d_bias, 'samp', 0, 0)  6.89 us
    all_to_all x1, starting transfers between devices, body(): lax.all_to_all(local_bias, 'samp', 0, 0)  6.68 us
    all_to_all x1, starting transfers between devices, body(): parts = lax.all_to_all(d_bias, 'samp', 0, 0)  6.01 us
    ppermute x6, starting transfers between devices, swap(): lax.ppermute(values, axis, [(i, i ^ k) for i in range(lax.axis_size(axis))])  5.78 us
  transfers between devices with their start and end apart: 10, of which 2 were waited for; matrix products, arithmetic and copies ran while one was open for 0% of the time, Pallas kernels for 41%

profile of v8, /device:TPU:0, one launch (start us, length us, event | category | flops | bytes accessed | tf_op | source)
XLA Modules:
  0.0 90.4 jit_solution(12681865399337802587)
XLA Ops:
  0.6 3.6 %pair_bias.1 = (bf16[8,256,128]{2,1,0:T(8,128)(2,1)}, bf16[4,48,128]{2,1,0:T(8,128)(2,1)}, bf16[4,48,128]{2,1,0:T(8,128)(2,1)}) custom-call(bf16[64,32,128]{2,1,0:T(8,128)(2,1)} %pair_ref.1, f32[1,128]{1,0:T(1,128)} %bitcast.7, bf16[16,128]{1,0:T(8,128)(2,1)} %bitcast.5, bf16[4,1280,128]{2,1,0:T(8,128)(2,1)} %feats_hbm.5), custom_call_target="tpu_custom_call" | custom-call | flops 10000000 | bytes 10000000 | tf_op jit(solution)/shard_map/pair_bias/pallas_call | solution.py:118
  4.2 3.0 %collective-permute-start = (bf16[4,48,128]{2,1,0:T(8,128)(2,1)}, bf16[4,48,128]{2,1,0:T(8,128)(2,1)}, u32[]{:S(2)}, u32[]{:S(2)}) collective-permute-start(bf16[4,48,128]{2,1,0:T(8,128)(2,1)} %get-tuple-element.20), channel_id=1, source_target_pairs={{0,1},{1,2},{2,3},{4,5},{5,6},{6,7},{8,9},{9,10},{10,11},{12,13},{... | collective-permute-start | bytes 147464 | tf_op jit(solution)/shard_map/ppermute | solution.py:798
  7.2 1.3 %collective-permute-start.1 = (bf16[4,48,128]{2,1,0:T(8,128)(2,1)}, bf16[4,48,128]{2,1,0:T(8,128)(2,1)}, u32[]{:S(2)}, u32[]{:S(2)}) collective-permute-start(bf16[4,48,128]{2,1,0:T(8,128)(2,1)} %get-tuple-element.21), channel_id=1, source_target_pairs={{1,0},{2,1},{3,2},{5,4},{6,5},{7,6},{9,8},{10,9},{11,10},{13,12},{... | collective-permute-start | bytes 147464 | tf_op jit(solution)/shard_map/ppermute | solution.py:799
  8.5 6.7 %all-to-all-start = ((bf16[8,256,128]{2,1,0:T(8,128)(2,1)}), bf16[8,256,128]{2,1,0:T(8,128)(2,1)}, u32[]{:S(2)}, u32[]{:S(2)}) async-start(bf16[8,256,128]{2,1,0:T(8,128)(2,1)} %get-tuple-element.22), calls=%async_computation | async-start | bytes 1048576 | tf_op jit(solution)/shard_map/all_to_all | solution.py:801
  15.2 0.0 collective-permute-done.left_hbm
  15.2 0.0 collective-permute-done.1.right_hbm
  15.2 11.0 %atoms.3 = (f32[2,64,768]{2,1,0:T(8,128)}, bf16[2,64,768]{2,1,0:T(8,128)(2,1)}) custom-call(bf16[4,1280,128]{2,1,0:T(8,128)(2,1)} %feats_hbm.5, bf16[4,48,128]{2,1,0:T(8,128)(2,1)} %collective-permute-done.left_hbm, bf16[4,48,128]{2,1,0:T(8,128)(2,1)} %collective-permute-done.1.right_hbm, s32[40,128]{1,0:T(8,128)} %bitcast.10, s32[1,64]{1,0:T(1,128)} %counts_hbm.3, ...), custom_call_target="tpu_custom_call" | custom-call | flops 10000000000 | bytes 4000000 | tf_op jit(solution)/shard_map/atoms/pallas_call | solution.py:286
  26.2 2.2 %collective-permute-start.7 = (bf16[2,64,768]{2,1,0:T(8,128)(2,1)}, bf16[2,64,768]{2,1,0:T(8,128)(2,1)}, u32[]{:S(2)}, u32[]{:S(2)}) collective-permute-start(bf16[2,64,768]{2,1,0:T(8,128)(2,1)} %get-tuple-element.27.refs_0_), channel_id=1, source_target_pairs={{0,3},{1,2},{2,1},{3,0},{4,7},{5,6},{6,5},{7,4},{8,11},{9,10},{10,... | collective-permute-start | bytes 589832 | tf_op jit(solution)/shard_map/ppermute | solution.py:778
  28.4 1.4 %collective-permute-start.6 = (bf16[2,64,768]{2,1,0:T(8,128)(2,1)}, bf16[2,64,768]{2,1,0:T(8,128)(2,1)}, u32[]{:S(2)}, u32[]{:S(2)}) collective-permute-start(bf16[2,64,768]{2,1,0:T(8,128)(2,1)} %get-tuple-element.27.refs_0_), channel_id=1, source_target_pairs={{0,2},{1,3},{2,0},{3,1},{4,6},{5,7},{6,4},{7,5},{8,10},{9,11},{10,... | collective-permute-start | bytes 589832 | tf_op jit(solution)/shard_map/ppermute | solution.py:778
  29.8 0.0 collective-permute-start.5
  29.8 11.1 %atoms.2 = (f32[2,64,768]{2,1,0:T(8,128)}, bf16[2,64,768]{2,1,0:T(8,128)(2,1)}) custom-call(bf16[4,1280,128]{2,1,0:T(8,128)(2,1)} %feats_hbm.5, bf16[4,48,128]{2,1,0:T(8,128)(2,1)} %collective-permute-done.left_hbm, bf16[4,48,128]{2,1,0:T(8,128)(2,1)} %collective-permute-done.1.right_hbm, s32[40,128]{1,0:T(8,128)} %bitcast.11, s32[1,64]{1,0:T(1,128)} %counts_hbm.3, ...), custom_call_target="tpu_custom_call" | custom-call | flops 10000000000 | bytes 4000000 | tf_op jit(solution)/shard_map/atoms/pallas_call | solution.py:286
  40.9 1.4 %collective-permute-start.4 = (bf16[2,64,768]{2,1,0:T(8,128)(2,1)}, bf16[2,64,768]{2,1,0:T(8,128)(2,1)}, u32[]{:S(2)}, u32[]{:S(2)}) collective-permute-start(bf16[2,64,768]{2,1,0:T(8,128)(2,1)} %get-tuple-element.24.refs_0_), channel_id=1, source_target_pairs={{0,3},{1,2},{2,1},{3,0},{4,7},{5,6},{6,5},{7,4},{8,11},{9,10},{10,... | collective-permute-start | bytes 589832 | tf_op jit(solution)/shard_map/ppermute | solution.py:778
  42.3 0.7 collective-permute-start.3
  43.1 0.0 collective-permute-done.7.refs_3_
  43.1 0.0 collective-permute-start.2
  43.1 0.0 collective-permute-done.6.refs_2_
  43.1 0.0 collective-permute-done.5.refs_1_
  43.1 0.0 all-to-all-done
  43.1 7.7 %attend.1 = (bf16[128,768]{1,0:T(8,128)(2,1)}, f32[2,8,256,128]{3,2,1,0:T(8,128)}, bf16[2,256,768]{2,1,0:T(8,128)(2,1)}, f32[256,1536]{1,0:T(8,128)}) custom-call(bf16[2,64,768]{2,1,0:T(8,128)(2,1)} %get-tuple-element.27.refs_0_, bf16[2,64,768]{2,1,0:T(8,128)(2,1)} %collective-permute-done.5.refs_1_, bf16[2,64,768]{2,1,0:T(8,128)(2,1)} %collective-permute-done.6.refs_2_, ...), custom_call_target="tpu_custom_call" | custom-call | flops 4000000000 | bytes 10000000 | tf_op jit(solution)/shard_map/attend/pallas_call | solution.py:469
  50.8 0.0 collective-permute-done.4.refs_3_
  50.8 1.9 %collective-permute-done.3.refs_2_ = bf16[2,64,768]{2,1,0:T(8,128)(2,1)} collective-permute-done((bf16[2,64,768]{2,1,0:T(8,128)(2,1)}, bf16[2,64,768]{2,1,0:T(8,128)(2,1)}, u32[]{:S(2)}, u32[]{:S(2)}) %collective-permute-start.3) | collective-permute-done | bytes 196640 | tf_op jit(solution)/shard_map/ppermute | solution.py:778
  52.7 0.0 collective-permute-done.2.refs_1_
  52.7 13.5 %tokens.1 = (f32[256,768]{1,0:T(8,128)}, bf16[256,1536]{1,0:T(8,128)(2,1)}, bf16[8,8,32,128]{3,2,1,0:T(8,128)(2,1)}) custom-call(bf16[2,64,768]{2,1,0:T(8,128)(2,1)} %get-tuple-element.24.refs_0_, bf16[2,64,768]{2,1,0:T(8,128)(2,1)} %collective-permute-done.2.refs_1_, bf16[2,64,768]{2,1,0:T(8,128)(2,1)} %collective-permute-done.3.refs_2_, ...), custom_call_target="tpu_custom_call" | custom-call | flops 10000000000 | bytes 20000000 | tf_op jit(solution)/shard_map/tokens/pallas_call | solution.py:613
  66.2 6.0 %all-to-all-start.1 = ((bf16[8,8,32,128]{3,2,1,0:T(8,128)(2,1)}), bf16[8,8,32,128]{3,2,1,0:T(8,128)(2,1)}, u32[]{:S(2)}, u32[]{:S(2)}) async-start(bf16[8,8,32,128]{3,2,1,0:T(8,128)(2,1)} %get-tuple-element.35), calls=%async_computation.1 | async-start | bytes 1048576 | tf_op jit(solution)/shard_map/all_to_all | solution.py:822
  72.2 7.4 %output.1 = (bf16[256,768]{1,0:T(8,128)(2,1)}, f32[2048,128]{1,0:T(8,128)}, f32[32,128]{1,0:T(8,128)}) custom-call(f32[256,768]{1,0:T(8,128)} %get-tuple-element.32.resid_ref, bf16[256,1536]{1,0:T(8,128)(2,1)} %get-tuple-element.33.hidden_ref, bf16[1536,768]{1,0:T(8,128)(2,1)} %w_down_ref.1, bf16[64,32,128]{2,1,0:T(8,128)(2,1)} %pair_ref.1), custom_call_target="tpu_custom_call" | custom-call | flops 1000000000 | bytes 8000000 | tf_op jit(solution)/shard_map/output/pallas_call | solution.py:679
  79.6 6.9 %all-to-all-done.1.parts_hbm = bf16[8,8,32,128]{3,2,1,0:T(8,128)(2,1)} async-done(((bf16[8,8,32,128]{3,2,1,0:T(8,128)(2,1)}), bf16[8,8,32,128]{3,2,1,0:T(8,128)(2,1)}, u32[]{:S(2)}, u32[]{:S(2)}) %all-to-all-start.1) | async-done | bytes 524320 | tf_op jit(solution)/shard_map/all_to_all | solution.py:822
  86.5 3.7 %pair_grad.1 = f32[64,32,128]{2,1,0:T(8,128)} custom-call(bf16[8,8,32,128]{3,2,1,0:T(8,128)(2,1)} %all-to-all-done.1.parts_hbm, f32[2048,128]{1,0:T(8,128)} %get-tuple-element.36.hat_hbm, f32[32,128]{1,0:T(8,128)} %get-tuple-element.37.rstd_hbm, f32[1,128]{1,0:T(1,128)} %bitcast.8, bf16[16,128]{1,0:T(8,128)(2,1)} %bitcast.6), custom_call_target="tpu_custom_call" | custom-call | flops 100000000 | bytes 4000000 | tf_op jit(solution)/shard_map/pair_grad/pallas_call | solution.py:756
Async XLA Ops:
  4.2 10.9 %collective-permute-start = (bf16[4,48,128]{2,1,0:T(8,128)(2,1)}, bf16[4,48,128]{2,1,0:T(8,128)(2,1)}, u32[]{:S(2)}, u32[]{:S(2)}) collective-permute-start(bf16[4,48,128]{2,1,0:T(8,128)(2,1)} %get-tuple-element.20), channel_id=1, source_target_pairs={{0,1},{1,2},{2,3},{4,5},{5,6},{6,7},{8,9},{9,10},{10,11},{12,13},{... | collective-permute-start | bytes 147464 | tf_op jit(solution)/shard_map/ppermute | solution.py:798
  7.2 8.0 %collective-permute-start.1 = (bf16[4,48,128]{2,1,0:T(8,128)(2,1)}, bf16[4,48,128]{2,1,0:T(8,128)(2,1)}, u32[]{:S(2)}, u32[]{:S(2)}) collective-permute-start(bf16[4,48,128]{2,1,0:T(8,128)(2,1)} %get-tuple-element.21), channel_id=1, source_target_pairs={{1,0},{2,1},{3,2},{5,4},{6,5},{7,6},{9,8},{10,9},{11,10},{13,12},{... | collective-permute-start | bytes 147464 | tf_op jit(solution)/shard_map/ppermute | solution.py:799
  8.5 34.6 %all-to-all-start = ((bf16[8,256,128]{2,1,0:T(8,128)(2,1)}), bf16[8,256,128]{2,1,0:T(8,128)(2,1)}, u32[]{:S(2)}, u32[]{:S(2)}) async-start(bf16[8,256,128]{2,1,0:T(8,128)(2,1)} %get-tuple-element.22), calls=%async_computation | async-start | bytes 1048576 | tf_op jit(solution)/shard_map/all_to_all | solution.py:801
  26.2 16.9 %collective-permute-start.7 = (bf16[2,64,768]{2,1,0:T(8,128)(2,1)}, bf16[2,64,768]{2,1,0:T(8,128)(2,1)}, u32[]{:S(2)}, u32[]{:S(2)}) collective-permute-start(bf16[2,64,768]{2,1,0:T(8,128)(2,1)} %get-tuple-element.27.refs_0_), channel_id=1, source_target_pairs={{0,3},{1,2},{2,1},{3,0},{4,7},{5,6},{6,5},{7,4},{8,11},{9,10},{10,... | collective-permute-start | bytes 589832 | tf_op jit(solution)/shard_map/ppermute | solution.py:778
  28.4 14.7 %collective-permute-start.6 = (bf16[2,64,768]{2,1,0:T(8,128)(2,1)}, bf16[2,64,768]{2,1,0:T(8,128)(2,1)}, u32[]{:S(2)}, u32[]{:S(2)}) collective-permute-start(bf16[2,64,768]{2,1,0:T(8,128)(2,1)} %get-tuple-element.27.refs_0_), channel_id=1, source_target_pairs={{0,2},{1,3},{2,0},{3,1},{4,6},{5,7},{6,4},{7,5},{8,10},{9,11},{10,... | collective-permute-start | bytes 589832 | tf_op jit(solution)/shard_map/ppermute | solution.py:778
  29.8 13.4 %collective-permute-start.5 = (bf16[2,64,768]{2,1,0:T(8,128)(2,1)}, bf16[2,64,768]{2,1,0:T(8,128)(2,1)}, u32[]{:S(2)}, u32[]{:S(2)}) collective-permute-start(bf16[2,64,768]{2,1,0:T(8,128)(2,1)} %get-tuple-element.27.refs_0_), channel_id=1, source_target_pairs={{0,1},{1,0},{2,3},{3,2},{4,5},{5,4},{6,7},{7,6},{8,9},{9,8},{10,11... | collective-permute-start | bytes 589832 | tf_op jit(solution)/shard_map/ppermute | solution.py:778
  40.9 9.9 %collective-permute-start.4 = (bf16[2,64,768]{2,1,0:T(8,128)(2,1)}, bf16[2,64,768]{2,1,0:T(8,128)(2,1)}, u32[]{:S(2)}, u32[]{:S(2)}) collective-permute-start(bf16[2,64,768]{2,1,0:T(8,128)(2,1)} %get-tuple-element.24.refs_0_), channel_id=1, source_target_pairs={{0,3},{1,2},{2,1},{3,0},{4,7},{5,6},{6,5},{7,4},{8,11},{9,10},{10,... | collective-permute-start | bytes 589832 | tf_op jit(solution)/shard_map/ppermute | solution.py:778
  42.3 10.4 %collective-permute-start.3 = (bf16[2,64,768]{2,1,0:T(8,128)(2,1)}, bf16[2,64,768]{2,1,0:T(8,128)(2,1)}, u32[]{:S(2)}, u32[]{:S(2)}) collective-permute-start(bf16[2,64,768]{2,1,0:T(8,128)(2,1)} %get-tuple-element.24.refs_0_), channel_id=1, source_target_pairs={{0,2},{1,3},{2,0},{3,1},{4,6},{5,7},{6,4},{7,5},{8,10},{9,11},{10,... | collective-permute-start | bytes 589832 | tf_op jit(solution)/shard_map/ppermute | solution.py:778
  43.1 9.6 %collective-permute-start.2 = (bf16[2,64,768]{2,1,0:T(8,128)(2,1)}, bf16[2,64,768]{2,1,0:T(8,128)(2,1)}, u32[]{:S(2)}, u32[]{:S(2)}) collective-permute-start(bf16[2,64,768]{2,1,0:T(8,128)(2,1)} %get-tuple-element.24.refs_0_), channel_id=1, source_target_pairs={{0,1},{1,0},{2,3},{3,2},{4,5},{5,4},{6,7},{7,6},{8,9},{9,8},{10,11... | collective-permute-start | bytes 589832 | tf_op jit(solution)/shard_map/ppermute | solution.py:778
  66.2 20.3 %all-to-all-start.1 = ((bf16[8,8,32,128]{3,2,1,0:T(8,128)(2,1)}), bf16[8,8,32,128]{3,2,1,0:T(8,128)(2,1)}, u32[]{:S(2)}, u32[]{:S(2)}) async-start(bf16[8,8,32,128]{3,2,1,0:T(8,128)(2,1)} %get-tuple-element.35), calls=%async_computation.1 | async-start | bytes 1048576 | tf_op jit(solution)/shard_map/all_to_all | solution.py:822

commit v9 on v7

--- a/solution.py
+++ b/solution.py
@@ -65,17 +65,19 @@
 
 
 def bias_kernel(
-    pair_hbm, gain_hbm, w_bias_hbm, feats_hbm, out_hbm, head_hbm, tail_hbm, pair_ref, gain_ref,
-    w_bias_ref, scaled_ref, stage_ref, local_ref, sems,
+    pair_hbm, gain_hbm, w_bias_hbm, feats_hbm, out_hbm, edges_hbm, pair_ref, gain_ref, w_bias_ref,
+    scaled_ref, stage_ref, local_ref, head_ref, tail_ref, edges_ref, sems,
 ):
     rows, keys = pair_ref.shape[0], pair_ref.shape[1]
     atoms = feats_hbm.shape[1]
     part = rows // 4
-    moves = [(gain_hbm, gain_ref), (w_bias_hbm, w_bias_ref)]
+    moves = [
+        (gain_hbm, gain_ref), (w_bias_hbm, w_bias_ref),
+        (feats_hbm.at[:, pl.ds(0, HALO), :], head_ref),
+        (feats_hbm.at[:, pl.ds(atoms - HALO, HALO), :], tail_ref),
+    ]
     for i in range(4):
         moves.append((pair_hbm.at[pl.ds(part * i, part)], pair_ref.at[pl.ds(part * i, part)]))
-    moves.append((feats_hbm.at[:, pl.ds(0, HALO), :], head_hbm))
-    moves.append((feats_hbm.at[:, pl.ds(atoms - HALO, HALO), :], tail_hbm))
     copies = start_all(moves, sems)
     for copy in copies[0:2]:
         copy.wait()
@@ -83,9 +85,18 @@
     weights = jnp.concatenate(split_heads(w_bias_ref[...]), axis=1).astype(bf16)
     for i in range(rows // 8):
         if 8 * i % part == 0:
-            copies[2 + 8 * i // part].wait()
+            copies[4 + 8 * i // part].wait()
         block = pair_ref[8 * i : 8 * i + 8].astype(f32).reshape(8 * keys, CZ)
         scaled_ref[8 * keys * i : 8 * keys * (i + 1), :] = norm_rows(block)[0] * gain
+    for copy in copies[2:4]:
+        copy.wait()
+    here = lax.axis_index("tok")
+    head, tail = head_ref[...].astype(f32), tail_ref[...].astype(f32)
+    for k in range(edges_ref.shape[0]):
+        before = jnp.where(here == k + 1, 1.0, 0.0)
+        after = jnp.where(here == k - 1, 1.0, 0.0)
+        edges_ref[k] = (head * before + tail * after).astype(bf16)
+    edges = start_all([(edges_ref, edges_hbm)], sems)
     blank = jnp.zeros((rows, CZ), bf16)
     for j in range(keys):
         block = scaled_ref[pl.ds(j, rows, stride=keys), :].astype(bf16)
@@ -95,23 +106,27 @@
         )
         stage_ref[pl.ds(j, PAIRS, stride=keys), :] = nt(weights, both)
     local_ref[...] = stage_ref[...].astype(bf16)
-    for copy in copies[6:]:
-        copy.wait()
-    back = start_all([(local_ref, out_hbm.at[k]) for k in range(out_hbm.shape[0])], sems)
+    back = [
+        pltpu.make_async_copy(local_ref, out_hbm.at[k], sems.at[2 + k])
+        for k in range(out_hbm.shape[0])
+    ]
     for copy in back:
-        copy.wait()
-
-
-def pair_bias(pair, pair_gain, w_bias_t, feats, copies):
+        copy.start()
+    for copy in edges + back:
+        copy.wait()
+
+
+def pair_bias(pair, pair_gain, w_bias_t, feats, copies, shards):
     rows, keys = pair.shape[0], pair.shape[1]
-    edge = jax.ShapeDtypeStruct((feats.shape[0], HALO, C_ATOM), bf16)
+    edge = (feats.shape[0], HALO, C_ATOM)
     hbm = pl.BlockSpec(memory_space=pl.ANY)
     return pl.pallas_call(
         bias_kernel,
         in_specs=[hbm] * 4,
-        out_specs=[hbm] * 3,
+        out_specs=[hbm] * 2,
         out_shape=[
-            jax.ShapeDtypeStruct((copies, keys * PAIRS, 2 * rows), bf16), edge, edge,
+            jax.ShapeDtypeStruct((copies, keys * PAIRS, 2 * rows), bf16),
+            jax.ShapeDtypeStruct((shards,) + edge, bf16),
         ],
         scratch_shapes=[
             pltpu.VMEM(pair.shape, bf16),
@@ -120,7 +135,10 @@
             pltpu.VMEM((rows * keys, CZ), f32),
             pltpu.VMEM((keys * PAIRS, 2 * rows), f32),
             pltpu.VMEM((keys * PAIRS, 2 * rows), bf16),
-            pltpu.SemaphoreType.DMA((max(8, copies),)),
+            pltpu.VMEM(edge, bf16),
+            pltpu.VMEM(edge, bf16),
+            pltpu.VMEM((shards,) + edge, bf16),
+            pltpu.SemaphoreType.DMA((8 + copies,)),
         ],
         compiler_params=pltpu.CompilerParams(vmem_limit_bytes=GRANT),
         cost_estimate=pl.CostEstimate(flops=10**7, bytes_accessed=10**7, transcendentals=0),
@@ -129,7 +147,7 @@
 
 
 def atom_kernel(
-    feats_hbm, left_hbm, right_hbm, mask_hbm, counts_hbm, single_hbm, w_qkv_hbm, w_out_hbm,
+    feats_hbm, halos_hbm, mask_hbm, counts_hbm, single_hbm, w_qkv_hbm, w_out_hbm,
     w_embed_hbm, tokens_ref, normed_ref, mask_ref, counts_ref, single_ref, w_qkv_ref, w_out_ref,
     w_embed_ref, sems, padded_ref, normed_atoms_ref, qkv_a, qkv_b, scores_a, scores_b, probs_a, probs_b, mixed_ref,
     updated_ref, split_ref, keybias_ref, onehot_ref, *, first,
@@ -137,13 +155,16 @@
     batch, atoms = tokens_ref.shape[0], feats_hbm.shape[1]
     padded = atoms + 2 * HALO
     moves = [(counts_hbm, counts_ref), (mask_hbm, mask_ref), (w_qkv_hbm, w_qkv_ref)]
+    here = lax.axis_index("tok")
+    left = halos_hbm.at[jnp.maximum(here - 1, 0)]
+    right = halos_hbm.at[jnp.minimum(here + 1, halos_hbm.shape[0] - 1)]
     for s in range(batch):
-        moves.append((left_hbm.at[first + s], padded_ref.at[s, pl.ds(0, HALO)]))
+        moves.append((left.at[first + s], padded_ref.at[s, pl.ds(0, HALO)]))
         moves.append((feats_hbm.at[first + s], padded_ref.at[s, pl.ds(HALO, atoms)]))
-        moves.append((right_hbm.at[first + s], padded_ref.at[s, pl.ds(HALO + atoms, HALO)]))
+        moves.append((right.at[first + s], padded_ref.at[s, pl.ds(HALO + atoms, HALO)]))
     moves += [(w_out_hbm, w_out_ref), (w_embed_hbm, w_embed_ref), (single_hbm, single_ref)]
     copies = start_all(moves, sems)
-    for copy in copies[0:2]:
+    for copy in copies:
         copy.wait()
     tok_rows = single_ref.shape[0]
     blocks = atoms // 128
@@ -243,11 +264,7 @@
         tokens_ref[s] = tokens
         normed_ref[s] = norm_rows(tokens)[0].astype(bf16)
 
-    for copy in copies[2:6]:
-        copy.wait()
     qkv_step(0)
-    for copy in copies[6:]:
-        copy.wait()
     for s in range(batch):
         score_step(s, 0, scores_a)
 
@@ -268,13 +285,13 @@
             qkv_step(s + 1)
 
 
-def atom_stage(part, batch, feats, left, right, mask, counts, single, w_qkv, w_out, w_embed):
+def atom_stage(part, batch, feats, halos, mask, counts, single, w_qkv, w_out, w_embed):
     atoms = feats.shape[1]
     tok_rows = single.shape[0]
     padded = atoms + 2 * HALO
     return pl.pallas_call(
         functools.partial(atom_kernel, first=part * batch),
-        in_specs=[pl.BlockSpec(memory_space=pl.ANY)] * 9,
+        in_specs=[pl.BlockSpec(memory_space=pl.ANY)] * 8,
         out_specs=[pl.BlockSpec(memory_space=pltpu.VMEM)] * 2,
         out_shape=[
             jax.ShapeDtypeStruct((batch, tok_rows, C_TOK), f32),
@@ -307,7 +324,7 @@
             flops=10**10, bytes_accessed=4 * 10**6, transcendentals=3 * 10**6
         ),
         name="atoms",
-    )(feats, left, right, mask, counts, single, w_qkv, w_out, w_embed)
+    )(feats, halos, mask, counts, single, w_qkv, w_out, w_embed)
 
 
 def head_masks(rows):
@@ -340,7 +357,7 @@
     return [pieces[0], weights[0]] + pieces[1:] + weights[1:]
 
 
-def project(copies, w_qkv_ref, all_ref, queries_ref, keys_ref, values_ref):
+def project(copies, w_qkv_ref, all_ref, queries_ref, keys_ref, values_ref, loaded):
     batch = all_ref.shape[0]
     tok_rows = queries_ref.shape[0] // batch
     at = pl.multiple_of(lax.axis_index("tok") * tok_rows, tok_rows)
@@ -354,6 +371,7 @@
     for which, to_ref in ((1, keys_ref), (2, values_ref)):
         if which == 2:
             copies[-1].wait()
+            loaded()
         for n in range(0, C_TOK, 256):
             for s in range(batch):
                 to_ref[s, :, n : n + 256] = nn(
@@ -409,7 +427,7 @@
     moves = project_moves(refs[:count], w_qkv_hbm, w_qkv_ref, all_ref)
     moves += [(bias_hbm, bias_ref), (cot_hbm, cot_ref), (w_down_hbm, w_down_ref)]
     copies = start_all(moves, sems)
-    project(copies[:-3], w_qkv_ref, all_ref, queries_ref, keys_ref, values_ref)
+    project(copies[:-3], w_qkv_ref, all_ref, queries_ref, keys_ref, values_ref, lambda: None)
     for copy in copies[-3:]:
         copy.wait()
     back = [
@@ -496,10 +514,19 @@
         (d_hidden_hbm, d_hidden_ref), (w_gate_hbm, w_gate_ref), (w_up_hbm, w_up_ref),
         (values_a_hbm, values_ref.at[pl.ds(0, ahead)]), (probs_a_hbm, probs_ref.at[pl.ds(0, ahead)]),
     ]
-    copies = start_all(moves, sems)
+    copies = [pltpu.make_async_copy(src, dst, sems.at[i]) for i, (src, dst) in enumerate(moves)]
+    for copy in copies[: projecting + 1]:
+        copy.start()
+
+    def start_rest():
+        for copy in copies[projecting + 1 :]:
+            copy.start()
+
     own_values = values_ref.at[pl.ds(ahead, batch - ahead)]
     own_probs = probs_ref.at[pl.ds(ahead, batch - ahead)]
-    project(copies[:projecting], w_qkv_ref, all_ref, queries_ref, keys_ref, own_values)
+    project(
+        copies[:projecting], w_qkv_ref, all_ref, queries_ref, keys_ref, own_values, start_rest
+    )
     copies = copies[projecting:]
     copies[0].wait()
     attend(bias_ref, queries_ref, keys_ref, own_values, own_probs, queries_ref)
@@ -762,11 +789,8 @@
     groups = lax.axis_size("samp")
 
     w_bias_t = w_bias.T
-    local_bias, head, tail = pair_bias(pair, pair_gain, w_bias_t, atom_feats, groups)
-    steps = [(i, i + 1) for i in range(shards - 1)]
-    left = lax.ppermute(tail, "tok", steps)
-    right = lax.ppermute(head, "tok", [(j, i) for i, j in steps])
-
+    local_bias, edges = pair_bias(pair, pair_gain, w_bias_t, atom_feats, groups, shards)
+    halos = lax.all_to_all(edges, "tok", 0, 0)
     bias = lax.all_to_all(local_bias, "samp", 0, 0).reshape(groups, PAIRS, -1, 2 * tok_rows)
 
     mask = atom_mask.reshape(-1, 128)
@@ -776,7 +800,7 @@
     tokens, gathered = [], []
     for part in range(2):
         tok, normed = atom_stage(
-            part, each, atom_feats, left, right, mask, atom_counts, token_single, w_atom_qkv,
+            part, each, atom_feats, halos, mask, atom_counts, token_single, w_atom_qkv,
             w_atom_out, w_embed,
         )
         tokens.append(tok)

time: 90.7 us -> 94.7 us (1.044)
  waiting for transfers between devices: 9.32 us -> 15.7 us
  starting transfers between devices: 22.7 us -> 20.7 us
    all_to_all x0 -> x1, waiting for transfers between devices: none -> 5.8 us  [body(): halos = lax.all_to_all(edges, 'tok', 0, 0)]
    ppermute x2 -> x0, starting transfers between devices: 4.25 us -> none  [the longest x1 2.97 us: body(): left = lax.ppermute(tail, 'tok', steps)]
    all_to_all x0 -> x1, starting transfers between devices: none -> 4.22 us  [body(): halos = lax.all_to_all(edges, 'tok', 0, 0)]
    ppermute x6, starting transfers between devices: 5.78 us -> 3.85 us  [swap(): lax.ppermute(values, axis, [(i, i ^ k) for i in range(lax.axis_size(axis))])]
    pallas_call x1, Pallas kernels: 4.94 us -> 3.65 us  [pair_bias(): pl.pallas_call(bias_kernel, in_specs=[hbm] * 4, out_specs=[hbm] * 2, out_...]
  transfers between devices with their start and end apart: 10 -> 9, of which waited for: 2 -> 3; matrix products, arithmetic and copies ran while one was open for 0% -> 0% of each run, Pallas kernels for 41% -> 39%
where the time goes in v9:
time: 94.7 us; the launch traced here: 94.2 us
  Pallas kernels  56.9 us (60%)
  starting transfers between devices  20.7 us (22%)
  waiting for transfers between devices  15.7 us (17%)
    pallas_call x2, Pallas kernels, atom_stage(): pl.pallas_call(functools.partial(atom_kernel, first=part * batch), in_spe...  22.2 us
    pallas_call x1, Pallas kernels, token_stage(): pl.pallas_call(functools.partial(token_kernel, count=len(pieces)), in_spe...  12.7 us
    pallas_call x1, Pallas kernels, output_stage(): pl.pallas_call(output_kernel, out_shape=[jax.ShapeDtypeStruct(resid.shape...  7.41 us
    all_to_all x1, waiting for transfers between devices, body(): parts = lax.all_to_all(d_bias, 'samp', 0, 0)  7.28 us
    pallas_call x1, Pallas kernels, attend_stage(): pl.pallas_call(functools.partial(attend_kernel, count=len(pieces)), in_sp...  7.17 us
    all_to_all x1, starting transfers between devices, body(): lax.all_to_all(local_bias, 'samp', 0, 0)  6.67 us
    all_to_all x1, starting transfers between devices, body(): parts = lax.all_to_all(d_bias, 'samp', 0, 0)  6.01 us
    all_to_all x1, waiting for transfers between devices, body(): halos = lax.all_to_all(edges, 'tok', 0, 0)  5.8 us
  transfers between devices with their start and end apart: 9, of which 3 were waited for; matrix products, arithmetic and copies ran while one was open for 0% of the time, Pallas kernels for 39%

profile of v9, /device:TPU:0, one launch (start us, length us, event | category | flops | bytes accessed | tf_op | source)
XLA Modules:
  0.0 94.2 jit_solution(12312312863468356900)
XLA Ops:
  0.6 3.6 %pair_bias.1 = (bf16[8,256,128]{2,1,0:T(8,128)(2,1)}, bf16[4,4,48,128]{3,2,1,0:T(8,128)(2,1)}) custom-call(bf16[64,32,128]{2,1,0:T(8,128)(2,1)} %pair_ref.1, f32[1,128]{1,0:T(1,128)} %bitcast.7, bf16[16,128]{1,0:T(8,128)(2,1)} %bitcast.5, bf16[4,1280,128]{2,1,0:T(8,128)(2,1)} %feats_hbm.5), custom_call_target="tpu_custom_call" | custom-call | flops 10000000 | bytes 10000000 | tf_op jit(solution)/shard_map/pair_bias/pallas_call | solution.py:123
  4.3 4.2 %all-to-all-start = ((bf16[4,4,48,128]{3,2,1,0:T(8,128)(2,1)}), bf16[4,4,48,128]{3,2,1,0:T(8,128)(2,1)}, u32[]{:S(2)}, u32[]{:S(2)}) async-start(bf16[4,4,48,128]{3,2,1,0:T(8,128)(2,1)} %get-tuple-element.19), calls=%async_computation | async-start | bytes 393216 | tf_op jit(solution)/shard_map/all_to_all | solution.py:793
  8.5 5.8 %all-to-all-done.halos_hbm = bf16[4,4,48,128]{3,2,1,0:T(8,128)(2,1)} async-done(((bf16[4,4,48,128]{3,2,1,0:T(8,128)(2,1)}), bf16[4,4,48,128]{3,2,1,0:T(8,128)(2,1)}, u32[]{:S(2)}, u32[]{:S(2)}) %all-to-all-start) | async-done | bytes 196640 | tf_op jit(solution)/shard_map/all_to_all | solution.py:793
  14.3 6.7 %all-to-all-start.1 = ((bf16[8,256,128]{2,1,0:T(8,128)(2,1)}), bf16[8,256,128]{2,1,0:T(8,128)(2,1)}, u32[]{:S(2)}, u32[]{:S(2)}) async-start(bf16[8,256,128]{2,1,0:T(8,128)(2,1)} %get-tuple-element.20), calls=%async_computation.1 | async-start | bytes 1048576 | tf_op jit(solution)/shard_map/all_to_all | solution.py:794
  21.0 11.0 %atoms.3 = (f32[2,64,768]{2,1,0:T(8,128)}, bf16[2,64,768]{2,1,0:T(8,128)(2,1)}) custom-call(bf16[4,1280,128]{2,1,0:T(8,128)(2,1)} %feats_hbm.5, bf16[4,4,48,128]{3,2,1,0:T(8,128)(2,1)} %all-to-all-done.halos_hbm, s32[40,128]{1,0:T(8,128)} %bitcast.10, s32[1,64]{1,0:T(1,128)} %counts_hbm.3, bf16[64,768]{1,0:T(8,128)(2,1)} %single_hbm.3, ...), custom_call_target="tpu_custom_call" | custom-call | flops 10000000000 | bytes 4000000 | tf_op jit(solution)/shard_map/atoms/pallas_call | solution.py:292
  32.0 0.1 collective-permute-start.5
  32.1 1.0 %collective-permute-start.4 = (bf16[2,64,768]{2,1,0:T(8,128)(2,1)}, bf16[2,64,768]{2,1,0:T(8,128)(2,1)}, u32[]{:S(2)}, u32[]{:S(2)}) collective-permute-start(bf16[2,64,768]{2,1,0:T(8,128)(2,1)} %get-tuple-element.25.refs_0_), channel_id=1, source_target_pairs={{0,2},{1,3},{2,0},{3,1},{4,6},{5,7},{6,4},{7,5},{8,10},{9,11},{10,... | collective-permute-start | bytes 589832 | tf_op jit(solution)/shard_map/ppermute | solution.py:774
  33.1 0.9 collective-permute-start.3
  33.9 11.2 %atoms.2 = (f32[2,64,768]{2,1,0:T(8,128)}, bf16[2,64,768]{2,1,0:T(8,128)(2,1)}) custom-call(bf16[4,1280,128]{2,1,0:T(8,128)(2,1)} %feats_hbm.5, bf16[4,4,48,128]{3,2,1,0:T(8,128)(2,1)} %all-to-all-done.halos_hbm, s32[40,128]{1,0:T(8,128)} %bitcast.11, s32[1,64]{1,0:T(1,128)} %counts_hbm.3, bf16[64,768]{1,0:T(8,128)(2,1)} %single_hbm.3, ...), custom_call_target="tpu_custom_call" | custom-call | flops 10000000000 | bytes 4000000 | tf_op jit(solution)/shard_map/atoms/pallas_call | solution.py:292
  45.1 0.5 collective-permute-start.2
  45.6 1.2 %collective-permute-start.1 = (bf16[2,64,768]{2,1,0:T(8,128)(2,1)}, bf16[2,64,768]{2,1,0:T(8,128)(2,1)}, u32[]{:S(2)}, u32[]{:S(2)}) collective-permute-start(bf16[2,64,768]{2,1,0:T(8,128)(2,1)} %get-tuple-element.22.refs_0_), channel_id=1, source_target_pairs={{0,2},{1,3},{2,0},{3,1},{4,6},{5,7},{6,4},{7,5},{8,10},{9,11},{10,... | collective-permute-start | bytes 589832 | tf_op jit(solution)/shard_map/ppermute | solution.py:774
  46.8 0.0 collective-permute-done.5.refs_3_
  46.8 0.2 collective-permute-start
  47.1 0.0 collective-permute-done.4.refs_2_
  47.1 0.0 collective-permute-done.3.refs_1_
  47.1 0.0 all-to-all-done.1
  47.1 7.2 %attend.1 = (bf16[128,768]{1,0:T(8,128)(2,1)}, f32[2,8,256,128]{3,2,1,0:T(8,128)}, bf16[2,256,768]{2,1,0:T(8,128)(2,1)}, f32[256,1536]{1,0:T(8,128)}) custom-call(bf16[2,64,768]{2,1,0:T(8,128)(2,1)} %get-tuple-element.25.refs_0_, bf16[2,64,768]{2,1,0:T(8,128)(2,1)} %collective-permute-done.3.refs_1_, bf16[2,64,768]{2,1,0:T(8,128)(2,1)} %collective-permute-done.4.refs_2_, ...), custom_call_target="tpu_custom_call" | custom-call | flops 4000000000 | bytes 10000000 | tf_op jit(solution)/shard_map/attend/pallas_call | solution.py:465
  54.2 0.0 collective-permute-done.2.refs_3_
  54.3 2.7 %collective-permute-done.1.refs_2_ = bf16[2,64,768]{2,1,0:T(8,128)(2,1)} collective-permute-done((bf16[2,64,768]{2,1,0:T(8,128)(2,1)}, bf16[2,64,768]{2,1,0:T(8,128)(2,1)}, u32[]{:S(2)}, u32[]{:S(2)}) %collective-permute-start.1) | collective-permute-done | bytes 196640 | tf_op jit(solution)/shard_map/ppermute | solution.py:774
  56.9 0.0 collective-permute-done.refs_1_
  56.9 12.7 %tokens.1 = (f32[256,768]{1,0:T(8,128)}, bf16[256,1536]{1,0:T(8,128)(2,1)}, bf16[8,8,32,128]{3,2,1,0:T(8,128)(2,1)}) custom-call(bf16[2,64,768]{2,1,0:T(8,128)(2,1)} %get-tuple-element.22.refs_0_, bf16[2,64,768]{2,1,0:T(8,128)(2,1)} %collective-permute-done.refs_1_, bf16[2,64,768]{2,1,0:T(8,128)(2,1)} %collective-permute-done.1.refs_2_, ...), custom_call_target="tpu_custom_call" | custom-call | flops 10000000000 | bytes 20000000 | tf_op jit(solution)/shard_map/tokens/pallas_call | solution.py:609
  69.7 6.0 %all-to-all-start.2 = ((bf16[8,8,32,128]{3,2,1,0:T(8,128)(2,1)}), bf16[8,8,32,128]{3,2,1,0:T(8,128)(2,1)}, u32[]{:S(2)}, u32[]{:S(2)}) async-start(bf16[8,8,32,128]{3,2,1,0:T(8,128)(2,1)} %get-tuple-element.33), calls=%async_computation.2 | async-start | bytes 1048576 | tf_op jit(solution)/shard_map/all_to_all | solution.py:815
  75.7 7.4 %output.1 = (bf16[256,768]{1,0:T(8,128)(2,1)}, f32[2048,128]{1,0:T(8,128)}, f32[32,128]{1,0:T(8,128)}) custom-call(f32[256,768]{1,0:T(8,128)} %get-tuple-element.30.resid_ref, bf16[256,1536]{1,0:T(8,128)(2,1)} %get-tuple-element.31.hidden_ref, bf16[1536,768]{1,0:T(8,128)(2,1)} %w_down_ref.1, bf16[64,32,128]{2,1,0:T(8,128)(2,1)} %pair_ref.1), custom_call_target="tpu_custom_call" | custom-call | flops 1000000000 | bytes 8000000 | tf_op jit(solution)/shard_map/output/pallas_call | solution.py:675
  83.1 7.3 %all-to-all-done.2.parts_hbm = bf16[8,8,32,128]{3,2,1,0:T(8,128)(2,1)} async-done(((bf16[8,8,32,128]{3,2,1,0:T(8,128)(2,1)}), bf16[8,8,32,128]{3,2,1,0:T(8,128)(2,1)}, u32[]{:S(2)}, u32[]{:S(2)}) %all-to-all-start.2) | async-done | bytes 524320 | tf_op jit(solution)/shard_map/all_to_all | solution.py:815
  90.4 3.7 %pair_grad.1 = f32[64,32,128]{2,1,0:T(8,128)} custom-call(bf16[8,8,32,128]{3,2,1,0:T(8,128)(2,1)} %all-to-all-done.2.parts_hbm, f32[2048,128]{1,0:T(8,128)} %get-tuple-element.34.hat_hbm, f32[32,128]{1,0:T(8,128)} %get-tuple-element.35.rstd_hbm, f32[1,128]{1,0:T(1,128)} %bitcast.8, bf16[16,128]{1,0:T(8,128)(2,1)} %bitcast.6), custom_call_target="tpu_custom_call" | custom-call | flops 100000000 | bytes 4000000 | tf_op jit(solution)/shard_map/pair_grad/pallas_call | solution.py:752
Async XLA Ops:
  4.3 10.0 %all-to-all-start = ((bf16[4,4,48,128]{3,2,1,0:T(8,128)(2,1)}), bf16[4,4,48,128]{3,2,1,0:T(8,128)(2,1)}, u32[]{:S(2)}, u32[]{:S(2)}) async-start(bf16[4,4,48,128]{3,2,1,0:T(8,128)(2,1)} %get-tuple-element.19), calls=%async_computation | async-start | bytes 393216 | tf_op jit(solution)/shard_map/all_to_all | solution.py:793
  14.3 32.8 %all-to-all-start.1 = ((bf16[8,256,128]{2,1,0:T(8,128)(2,1)}), bf16[8,256,128]{2,1,0:T(8,128)(2,1)}, u32[]{:S(2)}, u32[]{:S(2)}) async-start(bf16[8,256,128]{2,1,0:T(8,128)(2,1)} %get-tuple-element.20), calls=%async_computation.1 | async-start | bytes 1048576 | tf_op jit(solution)/shard_map/all_to_all | solution.py:794
  32.0 14.8 %collective-permute-start.5 = (bf16[2,64,768]{2,1,0:T(8,128)(2,1)}, bf16[2,64,768]{2,1,0:T(8,128)(2,1)}, u32[]{:S(2)}, u32[]{:S(2)}) collective-permute-start(bf16[2,64,768]{2,1,0:T(8,128)(2,1)} %get-tuple-element.25.refs_0_), channel_id=1, source_target_pairs={{0,3},{1,2},{2,1},{3,0},{4,7},{5,6},{6,5},{7,4},{8,11},{9,10},{10,... | collective-permute-start | bytes 589832 | tf_op jit(solution)/shard_map/ppermute | solution.py:774
  32.1 15.0 %collective-permute-start.4 = (bf16[2,64,768]{2,1,0:T(8,128)(2,1)}, bf16[2,64,768]{2,1,0:T(8,128)(2,1)}, u32[]{:S(2)}, u32[]{:S(2)}) collective-permute-start(bf16[2,64,768]{2,1,0:T(8,128)(2,1)} %get-tuple-element.25.refs_0_), channel_id=1, source_target_pairs={{0,2},{1,3},{2,0},{3,1},{4,6},{5,7},{6,4},{7,5},{8,10},{9,11},{10,... | collective-permute-start | bytes 589832 | tf_op jit(solution)/shard_map/ppermute | solution.py:774
  33.1 14.0 %collective-permute-start.3 = (bf16[2,64,768]{2,1,0:T(8,128)(2,1)}, bf16[2,64,768]{2,1,0:T(8,128)(2,1)}, u32[]{:S(2)}, u32[]{:S(2)}) collective-permute-start(bf16[2,64,768]{2,1,0:T(8,128)(2,1)} %get-tuple-element.25.refs_0_), channel_id=1, source_target_pairs={{0,1},{1,0},{2,3},{3,2},{4,5},{5,4},{6,7},{7,6},{8,9},{9,8},{10,11... | collective-permute-start | bytes 589832 | tf_op jit(solution)/shard_map/ppermute | solution.py:774
  45.1 9.1 %collective-permute-start.2 = (bf16[2,64,768]{2,1,0:T(8,128)(2,1)}, bf16[2,64,768]{2,1,0:T(8,128)(2,1)}, u32[]{:S(2)}, u32[]{:S(2)}) collective-permute-start(bf16[2,64,768]{2,1,0:T(8,128)(2,1)} %get-tuple-element.22.refs_0_), channel_id=1, source_target_pairs={{0,3},{1,2},{2,1},{3,0},{4,7},{5,6},{6,5},{7,4},{8,11},{9,10},{10,... | collective-permute-start | bytes 589832 | tf_op jit(solution)/shard_map/ppermute | solution.py:774
  45.6 11.3 %collective-permute-start.1 = (bf16[2,64,768]{2,1,0:T(8,128)(2,1)}, bf16[2,64,768]{2,1,0:T(8,128)(2,1)}, u32[]{:S(2)}, u32[]{:S(2)}) collective-permute-start(bf16[2,64,768]{2,1,0:T(8,128)(2,1)} %get-tuple-element.22.refs_0_), channel_id=1, source_target_pairs={{0,2},{1,3},{2,0},{3,1},{4,6},{5,7},{6,4},{7,5},{8,10},{9,11},{10,... | collective-permute-start | bytes 589832 | tf_op jit(solution)/shard_map/ppermute | solution.py:774
  46.8 10.1 %collective-permute-start = (bf16[2,64,768]{2,1,0:T(8,128)(2,1)}, bf16[2,64,768]{2,1,0:T(8,128)(2,1)}, u32[]{:S(2)}, u32[]{:S(2)}) collective-permute-start(bf16[2,64,768]{2,1,0:T(8,128)(2,1)} %get-tuple-element.22.refs_0_), channel_id=1, source_target_pairs={{0,1},{1,0},{2,3},{3,2},{4,5},{5,4},{6,7},{7,6},{8,9},{9,8},{10,11... | collective-permute-start | bytes 589832 | tf_op jit(solution)/shard_map/ppermute | solution.py:774
  69.7 20.7 %all-to-all-start.2 = ((bf16[8,8,32,128]{3,2,1,0:T(8,128)(2,1)}), bf16[8,8,32,128]{3,2,1,0:T(8,128)(2,1)}, u32[]{:S(2)}, u32[]{:S(2)}) async-start(bf16[8,8,32,128]{3,2,1,0:T(8,128)(2,1)} %get-tuple-element.33), calls=%async_computation.2 | async-start | bytes 1048576 | tf_op jit(solution)/shard_map/all_to_all | solution.py:815

commit v10 on v7

--- a/solution.py
+++ b/solution.py
@@ -66,16 +66,18 @@
 
 def bias_kernel(
     pair_hbm, gain_hbm, w_bias_hbm, feats_hbm, out_hbm, head_hbm, tail_hbm, pair_ref, gain_ref,
-    w_bias_ref, scaled_ref, stage_ref, local_ref, sems,
+    w_bias_ref, scaled_ref, stage_ref, local_ref, head_ref, tail_ref, sems,
 ):
     rows, keys = pair_ref.shape[0], pair_ref.shape[1]
     atoms = feats_hbm.shape[1]
     part = rows // 4
-    moves = [(gain_hbm, gain_ref), (w_bias_hbm, w_bias_ref)]
+    moves = [
+        (gain_hbm, gain_ref), (w_bias_hbm, w_bias_ref),
+        (feats_hbm.at[:, pl.ds(0, HALO), :], head_ref),
+        (feats_hbm.at[:, pl.ds(atoms - HALO, HALO), :], tail_ref),
+    ]
     for i in range(4):
         moves.append((pair_hbm.at[pl.ds(part * i, part)], pair_ref.at[pl.ds(part * i, part)]))
-    moves.append((feats_hbm.at[:, pl.ds(0, HALO), :], head_hbm))
-    moves.append((feats_hbm.at[:, pl.ds(atoms - HALO, HALO), :], tail_hbm))
     copies = start_all(moves, sems)
     for copy in copies[0:2]:
         copy.wait()
@@ -83,9 +85,12 @@
     weights = jnp.concatenate(split_heads(w_bias_ref[...]), axis=1).astype(bf16)
     for i in range(rows // 8):
         if 8 * i % part == 0:
-            copies[2 + 8 * i // part].wait()
+            copies[4 + 8 * i // part].wait()
         block = pair_ref[8 * i : 8 * i + 8].astype(f32).reshape(8 * keys, CZ)
         scaled_ref[8 * keys * i : 8 * keys * (i + 1), :] = norm_rows(block)[0] * gain
+    for copy in copies[2:4]:
+        copy.wait()
+    edges = start_all([(head_ref, head_hbm), (tail_ref, tail_hbm)], sems)
     blank = jnp.zeros((rows, CZ), bf16)
     for j in range(keys):
         block = scaled_ref[pl.ds(j, rows, stride=keys), :].astype(bf16)
@@ -95,10 +100,13 @@
         )
         stage_ref[pl.ds(j, PAIRS, stride=keys), :] = nt(weights, both)
     local_ref[...] = stage_ref[...].astype(bf16)
-    for copy in copies[6:]:
-        copy.wait()
-    back = start_all([(local_ref, out_hbm.at[k]) for k in range(out_hbm.shape[0])], sems)
+    back = [
+        pltpu.make_async_copy(local_ref, out_hbm.at[k], sems.at[2 + k])
+        for k in range(out_hbm.shape[0])
+    ]
     for copy in back:
+        copy.start()
+    for copy in edges + back:
         copy.wait()
 
 
@@ -120,7 +128,9 @@
             pltpu.VMEM((rows * keys, CZ), f32),
             pltpu.VMEM((keys * PAIRS, 2 * rows), f32),
             pltpu.VMEM((keys * PAIRS, 2 * rows), bf16),
-            pltpu.SemaphoreType.DMA((max(8, copies),)),
+            pltpu.VMEM(edge.shape, bf16),
+            pltpu.VMEM(edge.shape, bf16),
+            pltpu.SemaphoreType.DMA((8 + copies,)),
         ],
         compiler_params=pltpu.CompilerParams(vmem_limit_bytes=GRANT),
         cost_estimate=pl.CostEstimate(flops=10**7, bytes_accessed=10**7, transcendentals=0),
@@ -327,37 +337,29 @@
     return jnp.concatenate([jnp.where(mask, block, blank) for mask in masks], axis=0)
 
 
-def project_moves(piece_hbms, w_qkv_hbm, w_qkv_ref, all_ref):
+def project_moves(piece_hbms, w_qkv_hbm, w_kv_ref, all_ref):
     tok_rows = piece_hbms[0].shape[1]
-    weights = [
-        (w_qkv_hbm.at[:, pl.ds(C_TOK * i, C_TOK)], w_qkv_ref.at[i]) for i in range(3)
-    ]
     here = lax.axis_index("tok")
-    pieces = []
+    moves = []
     for k, piece in enumerate(piece_hbms):
         at = pl.multiple_of((here ^ k) * tok_rows, tok_rows)
-        pieces.append((piece, all_ref.at[:, pl.ds(at, tok_rows), :]))
-    return [pieces[0], weights[0]] + pieces[1:] + weights[1:]
-
-
-def project(copies, w_qkv_ref, all_ref, queries_ref, keys_ref, values_ref):
+        moves.append((piece, all_ref.at[:, pl.ds(at, tok_rows), :]))
+    for i in range(2):
+        moves.append((w_qkv_hbm.at[:, pl.ds(C_TOK * (i + 1), C_TOK)], w_kv_ref.at[i]))
+    return moves
+
+
+def project(copies, w_kv_ref, all_ref, keys_ref, values_ref):
     batch = all_ref.shape[0]
-    tok_rows = queries_ref.shape[0] // batch
-    at = pl.multiple_of(lax.axis_index("tok") * tok_rows, tok_rows)
-    for copy in copies[0:2]:
-        copy.wait()
-    own = jnp.concatenate([all_ref[s, pl.ds(at, tok_rows), :] for s in range(batch)], axis=0)
-    for n in range(0, C_TOK, 256):
-        queries_ref[:, n : n + 256] = nn(own, w_qkv_ref[0, :, n : n + 256]).astype(bf16)
-    for copy in copies[2:-1]:
-        copy.wait()
-    for which, to_ref in ((1, keys_ref), (2, values_ref)):
-        if which == 2:
+    for copy in copies[:-1]:
+        copy.wait()
+    for which, to_ref in enumerate((keys_ref, values_ref)):
+        if which == 1:
             copies[-1].wait()
         for n in range(0, C_TOK, 256):
             for s in range(batch):
                 to_ref[s, :, n : n + 256] = nn(
-                    all_ref[s], w_qkv_ref[which, :, n : n + 256]
+                    all_ref[s], w_kv_ref[which, :, n : n + 256]
                 ).astype(bf16)
 
 
@@ -401,15 +403,28 @@
 
 def attend_kernel(*refs, count):
     (
-        bias_hbm, w_qkv_hbm, cot_hbm, w_down_hbm, att_ref, probs_hbm, values_hbm, d_hidden_hbm,
-        w_qkv_ref, bias_ref, cot_ref, w_down_ref, probs_ref, values_ref, d_hidden_ref, sems,
-        all_ref, queries_ref, keys_ref,
+        later_hbm, bias_hbm, w_qkv_hbm, cot_hbm, w_down_hbm, att_ref, probs_hbm, values_hbm,
+        d_hidden_hbm, later_queries_ref, w_q_ref, w_kv_ref, own_ref, bias_ref, cot_ref, w_down_ref,
+        probs_ref, values_ref, d_hidden_ref, sems, all_ref, queries_ref, keys_ref,
     ) = refs[count:]
-    batch = all_ref.shape[0]
-    moves = project_moves(refs[:count], w_qkv_hbm, w_qkv_ref, all_ref)
+    batch, tok_rows = all_ref.shape[0], refs[0].shape[1]
+    moves = [
+        (refs[0], own_ref.at[pl.ds(0, batch)]),
+        (later_hbm, own_ref.at[pl.ds(batch, own_ref.shape[0] - batch)]),
+        (w_qkv_hbm.at[:, pl.ds(0, C_TOK)], w_q_ref),
+    ]
+    moves += project_moves(refs[:count], w_qkv_hbm, w_kv_ref, all_ref)
     moves += [(bias_hbm, bias_ref), (cot_hbm, cot_ref), (w_down_hbm, w_down_ref)]
     copies = start_all(moves, sems)
-    project(copies[:-3], w_qkv_ref, all_ref, queries_ref, keys_ref, values_ref)
+    for copy in copies[0:3]:
+        copy.wait()
+    own = own_ref[...].reshape(-1, C_TOK)
+    split = batch * tok_rows
+    for n in range(0, C_TOK, 256):
+        queries = nn(own, w_q_ref[:, n : n + 256]).astype(bf16)
+        queries_ref[:, n : n + 256] = queries[0:split]
+        later_queries_ref[:, n : n + 256] = queries[split:]
+    project(copies[3:-3], w_kv_ref, all_ref, keys_ref, values_ref)
     for copy in copies[-3:]:
         copy.wait()
     back = [
@@ -438,7 +453,7 @@
     ]
 
 
-def attend_stage(pieces, bias, w_qkv, cot, w_down):
+def attend_stage(pieces, later, bias, w_qkv, cot, w_down):
     batch, tok_rows, _ = pieces[0].shape
     keys_all = tok_rows * len(pieces)
     vmem = pl.BlockSpec(memory_space=pltpu.VMEM)
@@ -446,23 +461,26 @@
     d_hidden = jax.ShapeDtypeStruct((cot.shape[0] * tok_rows, w_down.shape[0]), f32)
     return pl.pallas_call(
         functools.partial(attend_kernel, count=len(pieces)),
-        in_specs=[hbm] * (len(pieces) + 4),
-        out_specs=[vmem, hbm, hbm, hbm],
+        in_specs=[hbm] * (len(pieces) + 5),
+        out_specs=[vmem, hbm, hbm, hbm, vmem],
         out_shape=[
             jax.ShapeDtypeStruct((batch * tok_rows, C_TOK), bf16),
             jax.ShapeDtypeStruct((batch, PAIRS, keys_all, 2 * tok_rows), f32),
             jax.ShapeDtypeStruct((batch, keys_all, C_TOK), bf16),
             d_hidden,
+            jax.ShapeDtypeStruct((later.shape[0] * tok_rows, C_TOK), bf16),
         ],
         scratch_shapes=[
-            pltpu.VMEM((3, C_TOK, C_TOK), bf16),
+            pltpu.VMEM((C_TOK, C_TOK), bf16),
+            pltpu.VMEM((2, C_TOK, C_TOK), bf16),
+            pltpu.VMEM(cot.shape, bf16),
             pltpu.VMEM(bias.shape, bf16),
             pltpu.VMEM(cot.shape, bf16),
             pltpu.VMEM(w_down.shape, bf16),
             pltpu.VMEM((batch, PAIRS, keys_all, 2 * tok_rows), f32),
             pltpu.VMEM((batch, keys_all, C_TOK), bf16),
             pltpu.VMEM(d_hidden.shape, f32),
-            pltpu.SemaphoreType.DMA((6 + len(pieces),)),
+            pltpu.SemaphoreType.DMA((8 + len(pieces),)),
         ]
         + attend_scratch(batch, tok_rows, keys_all),
         compiler_params=pltpu.CompilerParams(vmem_limit_bytes=GRANT),
@@ -470,16 +488,16 @@
             flops=4 * 10**9, bytes_accessed=10**7, transcendentals=10**6
         ),
         name="attend",
-    )(*pieces, bias, w_qkv, cot, w_down)
+    )(*pieces, later, bias, w_qkv, cot, w_down)
 
 
 def token_kernel(*refs, count):
     (
-        bias_hbm, tokens_a_hbm, tokens_b_hbm, att_a_hbm, cot_hbm, probs_a_hbm, values_a_hbm,
+        queries_hbm, bias_hbm, tokens_a_hbm, tokens_b_hbm, att_a_hbm, cot_hbm, probs_a_hbm, values_a_hbm,
         w_qkv_hbm, w_out_hbm, w_gate_hbm, w_up_hbm, d_hidden_hbm,
         resid_hbm, hidden_hbm, d_bias_ref,
         bias_ref, tokens_ref, att_a_ref, cot_ref, resid_ref, hidden_ref,
-        w_qkv_ref, w_out_ref, w_gate_ref, w_up_ref, d_hidden_ref, probs_ref, values_ref, sems,
+        w_kv_ref, w_out_ref, w_gate_ref, w_up_ref, d_hidden_ref, probs_ref, values_ref, sems,
         all_ref, queries_ref, keys_ref, grads_ref, d_gate_ref, d_up_ref, hat_ref,
     ) = refs[count:]
     batch, tok_rows = cot_ref.shape[0], cot_ref.shape[1]
@@ -487,10 +505,10 @@
     rows = batch * tok_rows
     ahead = values_a_hbm.shape[0]
     lead = ahead * tok_rows
-    moves = project_moves(refs[:count], w_qkv_hbm, w_qkv_ref, all_ref)
+    moves = project_moves(refs[:count], w_qkv_hbm, w_kv_ref, all_ref)
     projecting = len(moves)
     moves += [
-        (bias_hbm, bias_ref), (w_out_hbm, w_out_ref), (att_a_hbm, att_a_ref),
+        (queries_hbm, queries_ref), (bias_hbm, bias_ref), (w_out_hbm, w_out_ref), (att_a_hbm, att_a_ref),
         (tokens_a_hbm, tokens_ref.at[pl.ds(0, ahead)]),
         (tokens_b_hbm, tokens_ref.at[pl.ds(ahead, batch - ahead)]), (cot_hbm, cot_ref),
         (d_hidden_hbm, d_hidden_ref), (w_gate_hbm, w_gate_ref), (w_up_hbm, w_up_ref),
@@ -499,8 +517,9 @@
     copies = start_all(moves, sems)
     own_values = values_ref.at[pl.ds(ahead, batch - ahead)]
     own_probs = probs_ref.at[pl.ds(ahead, batch - ahead)]
-    project(copies[:projecting], w_qkv_ref, all_ref, queries_ref, keys_ref, own_values)
-    copies = copies[projecting:]
+    project(copies[:projecting], w_kv_ref, all_ref, keys_ref, own_values)
+    copies[projecting].wait()
+    copies = copies[projecting + 1 :]
     copies[0].wait()
     attend(bias_ref, queries_ref, keys_ref, own_values, own_probs, queries_ref)
 
@@ -570,7 +589,7 @@
 
 
 def token_stage(
-    pieces, bias, tokens_a, tokens_b, att_a, cot, probs_a, values_a, w_qkv, w_out, w_gate, w_up,
+    pieces, queries, bias, tokens_a, tokens_b, att_a, cot, probs_a, values_a, w_qkv, w_out, w_gate, w_up,
     d_hidden,
 ):
     batch, tok_rows, _ = cot.shape
@@ -581,7 +600,7 @@
     hbm = pl.BlockSpec(memory_space=pl.ANY)
     return pl.pallas_call(
         functools.partial(token_kernel, count=len(pieces)),
-        in_specs=[hbm] * (len(pieces) + 12),
+        in_specs=[hbm] * (len(pieces) + 13),
         out_specs=[hbm, hbm, vmem],
         out_shape=[
             jax.ShapeDtypeStruct((rows, C_TOK), f32),
@@ -595,14 +614,14 @@
             pltpu.VMEM(cot.shape, bf16),
             pltpu.VMEM((rows, C_TOK), f32),
             pltpu.VMEM((rows, hidden), bf16),
-            pltpu.VMEM((3, C_TOK, C_TOK), bf16),
+            pltpu.VMEM((2, C_TOK, C_TOK), bf16),
             pltpu.VMEM(w_out.shape, bf16),
             pltpu.VMEM(w_gate.shape, bf16),
             pltpu.VMEM(w_up.shape, bf16),
             pltpu.VMEM(d_hidden.shape, f32),
             pltpu.VMEM((batch, PAIRS, keys_all, 2 * tok_rows), f32),
             pltpu.VMEM((batch, keys_all, C_TOK), bf16),
-            pltpu.SemaphoreType.DMA((14 + len(pieces),)),
+            pltpu.SemaphoreType.DMA((16 + len(pieces),)),
         ]
         + attend_scratch(pieces[0].shape[0], tok_rows, keys_all)
         + [
@@ -617,7 +636,7 @@
         ),
         name="tokens",
     )(
-        *pieces, bias, tokens_a, tokens_b, att_a, cot, probs_a, values_a, w_qkv, w_out, w_gate,
+        *pieces, queries, bias, tokens_a, tokens_b, att_a, cot, probs_a, values_a, w_qkv, w_out, w_gate,
         w_up, d_hidden,
     )
 
@@ -781,11 +800,11 @@
         )
         tokens.append(tok)
         gathered.append(gather(normed, "tok"))
-    att_a, probs_a, values_a, d_hidden = attend_stage(
-        gathered[0], bias, w_qkv, cotangent, w_down
+    att_a, probs_a, values_a, d_hidden, queries_b = attend_stage(
+        gathered[0], gathered[1][0], bias, w_qkv, cotangent, w_down
     )
     resid, hidden, d_bias = token_stage(
-        gathered[1], bias, *tokens, att_a, cotangent, probs_a, values_a, w_qkv, w_out, w_gate,
+        gathered[1], queries_b, bias, *tokens, att_a, cotangent, probs_a, values_a, w_qkv, w_out, w_gate,
         w_up, d_hidden,
     )
     parts = lax.all_to_all(d_bias, "samp", 0, 0)

time: 90.7 us -> 89.2 us (0.983)
  Pallas kernels: 57.4 us -> 56.1 us
    pallas_call x1, Pallas kernels: 4.94 us -> 3.61 us  [pair_bias(): pl.pallas_call(bias_kernel, in_specs=[hbm] * 4, out_specs=[hbm] * 3, out_...]
  transfers between devices with their start and end apart: 10 -> 10, of which waited for: 2 -> 2; matrix products, arithmetic and copies ran while one was open for 0% -> 0% of each run, Pallas kernels for 41% -> 42%
where the time goes in v10:
time: 89.2 us; the launch traced here: 88.7 us
  Pallas kernels  56.1 us (63%)
  starting transfers between devices  22.7 us (25%)
  waiting for transfers between devices  9.05 us (10%)
  between operations  0.9 us (1%)
    pallas_call x2, Pallas kernels, atom_stage(): pl.pallas_call(functools.partial(atom_kernel, first=part * batch), in_spe...  22.1 us
    pallas_call x1, Pallas kernels, token_stage(): pl.pallas_call(functools.partial(token_kernel, count=len(pieces)), in_spe...  11.8 us
    pallas_call x1, Pallas kernels, attend_stage(): pl.pallas_call(functools.partial(attend_kernel, count=len(pieces)), in_sp...  7.44 us
    pallas_call x1, Pallas kernels, output_stage(): pl.pallas_call(output_kernel, out_shape=[jax.ShapeDtypeStruct(resid.shape...  7.41 us
    all_to_all x1, waiting for transfers between devices, body(): parts = lax.all_to_all(d_bias, 'samp', 0, 0)  6.9 us
    all_to_all x1, starting transfers between devices, body(): lax.all_to_all(local_bias, 'samp', 0, 0)  6.68 us
    all_to_all x1, starting transfers between devices, body(): parts = lax.all_to_all(d_bias, 'samp', 0, 0)  6.01 us
    ppermute x6, starting transfers between devices, swap(): lax.ppermute(values, axis, [(i, i ^ k) for i in range(lax.axis_size(axis))])  5.78 us
  transfers between devices with their start and end apart: 10, of which 2 were waited for; matrix products, arithmetic and copies ran while one was open for 0% of the time, Pallas kernels for 42%

profile of v10, /device:TPU:0, one launch (start us, length us, event | category | flops | bytes accessed | tf_op | source)
XLA Modules:
  0.0 88.7 jit_solution(902878375165772518)
XLA Ops:
  0.6 3.6 %pair_bias.1 = (bf16[8,256,128]{2,1,0:T(8,128)(2,1)}, bf16[4,48,128]{2,1,0:T(8,128)(2,1)}, bf16[4,48,128]{2,1,0:T(8,128)(2,1)}) custom-call(bf16[64,32,128]{2,1,0:T(8,128)(2,1)} %pair_ref.1, f32[1,128]{1,0:T(1,128)} %bitcast.7, bf16[16,128]{1,0:T(8,128)(2,1)} %bitcast.5, bf16[4,1280,128]{2,1,0:T(8,128)(2,1)} %feats_hbm.5), custom_call_target="tpu_custom_call" | custom-call | flops 10000000 | bytes 10000000 | tf_op jit(solution)/shard_map/pair_bias/pallas_call | solution.py:117
  4.2 3.0 %collective-permute-start = (bf16[4,48,128]{2,1,0:T(8,128)(2,1)}, bf16[4,48,128]{2,1,0:T(8,128)(2,1)}, u32[]{:S(2)}, u32[]{:S(2)}) collective-permute-start(bf16[4,48,128]{2,1,0:T(8,128)(2,1)} %get-tuple-element.21), channel_id=1, source_target_pairs={{0,1},{1,2},{2,3},{4,5},{5,6},{6,7},{8,9},{9,10},{10,11},{12,13},{... | collective-permute-start | bytes 147464 | tf_op jit(solution)/shard_map/ppermute | solution.py:786
  7.2 1.3 %collective-permute-start.1 = (bf16[4,48,128]{2,1,0:T(8,128)(2,1)}, bf16[4,48,128]{2,1,0:T(8,128)(2,1)}, u32[]{:S(2)}, u32[]{:S(2)}) collective-permute-start(bf16[4,48,128]{2,1,0:T(8,128)(2,1)} %get-tuple-element.22), channel_id=1, source_target_pairs={{1,0},{2,1},{3,2},{5,4},{6,5},{7,6},{9,8},{10,9},{11,10},{13,12},{... | collective-permute-start | bytes 147464 | tf_op jit(solution)/shard_map/ppermute | solution.py:787
  8.5 6.7 %all-to-all-start = ((bf16[8,256,128]{2,1,0:T(8,128)(2,1)}), bf16[8,256,128]{2,1,0:T(8,128)(2,1)}, u32[]{:S(2)}, u32[]{:S(2)}) async-start(bf16[8,256,128]{2,1,0:T(8,128)(2,1)} %get-tuple-element.23), calls=%async_computation | async-start | bytes 1048576 | tf_op jit(solution)/shard_map/all_to_all | solution.py:789
  15.2 0.0 collective-permute-done.left_hbm
  15.2 0.0 collective-permute-done.1.right_hbm
  15.2 11.0 %atoms.3 = (f32[2,64,768]{2,1,0:T(8,128)}, bf16[2,64,768]{2,1,0:T(8,128)(2,1)}) custom-call(bf16[4,1280,128]{2,1,0:T(8,128)(2,1)} %feats_hbm.5, bf16[4,48,128]{2,1,0:T(8,128)(2,1)} %collective-permute-done.left_hbm, bf16[4,48,128]{2,1,0:T(8,128)(2,1)} %collective-permute-done.1.right_hbm, s32[40,128]{1,0:T(8,128)} %bitcast.10, s32[1,64]{1,0:T(1,128)} %counts_hbm.3, ...), custom_call_target="tpu_custom_call" | custom-call | flops 10000000000 | bytes 4000000 | tf_op jit(solution)/shard_map/atoms/pallas_call | solution.py:285
  26.2 2.2 %collective-permute-start.7 = (bf16[2,64,768]{2,1,0:T(8,128)(2,1)}, bf16[2,64,768]{2,1,0:T(8,128)(2,1)}, u32[]{:S(2)}, u32[]{:S(2)}) collective-permute-start(bf16[2,64,768]{2,1,0:T(8,128)(2,1)} %get-tuple-element.26.refs_0_), channel_id=1, source_target_pairs={{0,3},{1,2},{2,1},{3,0},{4,7},{5,6},{6,5},{7,4},{8,11},{9,10},{10,... | collective-permute-start | bytes 589832 | tf_op jit(solution)/shard_map/ppermute | solution.py:766
  28.4 1.4 %collective-permute-start.6 = (bf16[2,64,768]{2,1,0:T(8,128)(2,1)}, bf16[2,64,768]{2,1,0:T(8,128)(2,1)}, u32[]{:S(2)}, u32[]{:S(2)}) collective-permute-start(bf16[2,64,768]{2,1,0:T(8,128)(2,1)} %get-tuple-element.26.refs_0_), channel_id=1, source_target_pairs={{0,2},{1,3},{2,0},{3,1},{4,6},{5,7},{6,4},{7,5},{8,10},{9,11},{10,... | collective-permute-start | bytes 589832 | tf_op jit(solution)/shard_map/ppermute | solution.py:766
  29.8 0.0 collective-permute-start.5
  29.8 11.1 %atoms.2 = (f32[2,64,768]{2,1,0:T(8,128)}, bf16[2,64,768]{2,1,0:T(8,128)(2,1)}) custom-call(bf16[4,1280,128]{2,1,0:T(8,128)(2,1)} %feats_hbm.5, bf16[4,48,128]{2,1,0:T(8,128)(2,1)} %collective-permute-done.left_hbm, bf16[4,48,128]{2,1,0:T(8,128)(2,1)} %collective-permute-done.1.right_hbm, s32[40,128]{1,0:T(8,128)} %bitcast.11, s32[1,64]{1,0:T(1,128)} %counts_hbm.3, ...), custom_call_target="tpu_custom_call" | custom-call | flops 10000000000 | bytes 4000000 | tf_op jit(solution)/shard_map/atoms/pallas_call | solution.py:285
  40.9 1.4 %collective-permute-start.4 = (bf16[2,64,768]{2,1,0:T(8,128)(2,1)}, bf16[2,64,768]{2,1,0:T(8,128)(2,1)}, u32[]{:S(2)}, u32[]{:S(2)}) collective-permute-start(bf16[2,64,768]{2,1,0:T(8,128)(2,1)} %get-tuple-element.25.refs_4_.refs_0_), channel_id=1, source_target_pairs={{0,3},{1,2},{2,1},{3,0},{4,7},{5,6},{6,5},{7,4},{8,11},{9,10},{10,... | collective-permute-start | bytes 589832 | tf_op jit(solution)/shard_map/ppermute | solution.py:766
  42.3 0.7 collective-permute-start.3
  43.1 0.0 collective-permute-done.7.refs_3_
  43.1 0.0 collective-permute-start.2
  43.1 0.0 collective-permute-done.6.refs_2_
  43.1 0.0 collective-permute-done.5.refs_1_
  43.1 0.0 all-to-all-done
  43.1 7.4 %attend.1 = (bf16[128,768]{1,0:T(8,128)(2,1)}, f32[2,8,256,128]{3,2,1,0:T(8,128)}, bf16[2,256,768]{2,1,0:T(8,128)(2,1)}, f32[256,1536]{1,0:T(8,128)}, bf16[128,768]{1,0:T(8,128)(2,1)}) custom-call(bf16[2,64,768]{2,1,0:T(8,128)(2,1)} %get-tuple-element.26.refs_0_, bf16[2,64,768]{2,1,0:T(8,128)(2,1)} %collective-permute-done.5.refs_1_, ...), custom_call_target="tpu_custom_call" | custom-call | flops 4000000000 | bytes 10000000 | tf_op jit(solution)/shard_map/attend/pallas_call | solution.py:462
  50.6 0.0 collective-permute-done.4.refs_3_
  50.6 2.1 %collective-permute-done.3.refs_2_ = bf16[2,64,768]{2,1,0:T(8,128)(2,1)} collective-permute-done((bf16[2,64,768]{2,1,0:T(8,128)(2,1)}, bf16[2,64,768]{2,1,0:T(8,128)(2,1)}, u32[]{:S(2)}, u32[]{:S(2)}) %collective-permute-start.3) | collective-permute-done | bytes 196640 | tf_op jit(solution)/shard_map/ppermute | solution.py:766
  52.7 0.0 collective-permute-done.2.refs_1_
  52.7 11.8 %tokens.1 = (f32[256,768]{1,0:T(8,128)}, bf16[256,1536]{1,0:T(8,128)(2,1)}, bf16[8,8,32,128]{3,2,1,0:T(8,128)(2,1)}) custom-call(bf16[2,64,768]{2,1,0:T(8,128)(2,1)} %get-tuple-element.25.refs_4_.refs_0_, bf16[2,64,768]{2,1,0:T(8,128)(2,1)} %collective-permute-done.2.refs_1_, bf16[2,64,768]{2,1,0:T(8,128)(2,1)} %collective-permute-done.3.refs_2_, ...), custom_call_target="tpu_custom_call" | custom-call | flops 10000000000 | bytes 20000000 | tf_op jit(solution)/shard_map/tokens/pallas_call | solution.py:601
  64.5 6.0 %all-to-all-start.1 = ((bf16[8,8,32,128]{3,2,1,0:T(8,128)(2,1)}), bf16[8,8,32,128]{3,2,1,0:T(8,128)(2,1)}, u32[]{:S(2)}, u32[]{:S(2)}) async-start(bf16[8,8,32,128]{3,2,1,0:T(8,128)(2,1)} %get-tuple-element.37), calls=%async_computation.1 | async-start | bytes 1048576 | tf_op jit(solution)/shard_map/all_to_all | solution.py:810
  70.6 7.4 %output.1 = (bf16[256,768]{1,0:T(8,128)(2,1)}, f32[2048,128]{1,0:T(8,128)}, f32[32,128]{1,0:T(8,128)}) custom-call(f32[256,768]{1,0:T(8,128)} %get-tuple-element.34.resid_ref, bf16[256,1536]{1,0:T(8,128)(2,1)} %get-tuple-element.35.hidden_ref, bf16[1536,768]{1,0:T(8,128)(2,1)} %w_down_ref.1, bf16[64,32,128]{2,1,0:T(8,128)(2,1)} %pair_ref.1), custom_call_target="tpu_custom_call" | custom-call | flops 1000000000 | bytes 8000000 | tf_op jit(solution)/shard_map/output/pallas_call | solution.py:667
  78.0 6.9 %all-to-all-done.1.parts_hbm = bf16[8,8,32,128]{3,2,1,0:T(8,128)(2,1)} async-done(((bf16[8,8,32,128]{3,2,1,0:T(8,128)(2,1)}), bf16[8,8,32,128]{3,2,1,0:T(8,128)(2,1)}, u32[]{:S(2)}, u32[]{:S(2)}) %all-to-all-start.1) | async-done | bytes 524320 | tf_op jit(solution)/shard_map/all_to_all | solution.py:810
  84.9 3.7 %pair_grad.1 = f32[64,32,128]{2,1,0:T(8,128)} custom-call(bf16[8,8,32,128]{3,2,1,0:T(8,128)(2,1)} %all-to-all-done.1.parts_hbm, f32[2048,128]{1,0:T(8,128)} %get-tuple-element.38.hat_hbm, f32[32,128]{1,0:T(8,128)} %get-tuple-element.39.rstd_hbm, f32[1,128]{1,0:T(1,128)} %bitcast.8, bf16[16,128]{1,0:T(8,128)(2,1)} %bitcast.6), custom_call_target="tpu_custom_call" | custom-call | flops 100000000 | bytes 4000000 | tf_op jit(solution)/shard_map/pair_grad/pallas_call | solution.py:744
Async XLA Ops:
  4.2 10.9 %collective-permute-start = (bf16[4,48,128]{2,1,0:T(8,128)(2,1)}, bf16[4,48,128]{2,1,0:T(8,128)(2,1)}, u32[]{:S(2)}, u32[]{:S(2)}) collective-permute-start(bf16[4,48,128]{2,1,0:T(8,128)(2,1)} %get-tuple-element.21), channel_id=1, source_target_pairs={{0,1},{1,2},{2,3},{4,5},{5,6},{6,7},{8,9},{9,10},{10,11},{12,13},{... | collective-permute-start | bytes 147464 | tf_op jit(solution)/shard_map/ppermute | solution.py:786
  7.2 8.0 %collective-permute-start.1 = (bf16[4,48,128]{2,1,0:T(8,128)(2,1)}, bf16[4,48,128]{2,1,0:T(8,128)(2,1)}, u32[]{:S(2)}, u32[]{:S(2)}) collective-permute-start(bf16[4,48,128]{2,1,0:T(8,128)(2,1)} %get-tuple-element.22), channel_id=1, source_target_pairs={{1,0},{2,1},{3,2},{5,4},{6,5},{7,6},{9,8},{10,9},{11,10},{13,12},{... | collective-permute-start | bytes 147464 | tf_op jit(solution)/shard_map/ppermute | solution.py:787
  8.5 34.6 %all-to-all-start = ((bf16[8,256,128]{2,1,0:T(8,128)(2,1)}), bf16[8,256,128]{2,1,0:T(8,128)(2,1)}, u32[]{:S(2)}, u32[]{:S(2)}) async-start(bf16[8,256,128]{2,1,0:T(8,128)(2,1)} %get-tuple-element.23), calls=%async_computation | async-start | bytes 1048576 | tf_op jit(solution)/shard_map/all_to_all | solution.py:789
  26.2 16.9 %collective-permute-start.7 = (bf16[2,64,768]{2,1,0:T(8,128)(2,1)}, bf16[2,64,768]{2,1,0:T(8,128)(2,1)}, u32[]{:S(2)}, u32[]{:S(2)}) collective-permute-start(bf16[2,64,768]{2,1,0:T(8,128)(2,1)} %get-tuple-element.26.refs_0_), channel_id=1, source_target_pairs={{0,3},{1,2},{2,1},{3,0},{4,7},{5,6},{6,5},{7,4},{8,11},{9,10},{10,... | collective-permute-start | bytes 589832 | tf_op jit(solution)/shard_map/ppermute | solution.py:766
  28.4 14.7 %collective-permute-start.6 = (bf16[2,64,768]{2,1,0:T(8,128)(2,1)}, bf16[2,64,768]{2,1,0:T(8,128)(2,1)}, u32[]{:S(2)}, u32[]{:S(2)}) collective-permute-start(bf16[2,64,768]{2,1,0:T(8,128)(2,1)} %get-tuple-element.26.refs_0_), channel_id=1, source_target_pairs={{0,2},{1,3},{2,0},{3,1},{4,6},{5,7},{6,4},{7,5},{8,10},{9,11},{10,... | collective-permute-start | bytes 589832 | tf_op jit(solution)/shard_map/ppermute | solution.py:766
  29.8 13.4 %collective-permute-start.5 = (bf16[2,64,768]{2,1,0:T(8,128)(2,1)}, bf16[2,64,768]{2,1,0:T(8,128)(2,1)}, u32[]{:S(2)}, u32[]{:S(2)}) collective-permute-start(bf16[2,64,768]{2,1,0:T(8,128)(2,1)} %get-tuple-element.26.refs_0_), channel_id=1, source_target_pairs={{0,1},{1,0},{2,3},{3,2},{4,5},{5,4},{6,7},{7,6},{8,9},{9,8},{10,11... | collective-permute-start | bytes 589832 | tf_op jit(solution)/shard_map/ppermute | solution.py:766
  40.9 9.7 %collective-permute-start.4 = (bf16[2,64,768]{2,1,0:T(8,128)(2,1)}, bf16[2,64,768]{2,1,0:T(8,128)(2,1)}, u32[]{:S(2)}, u32[]{:S(2)}) collective-permute-start(bf16[2,64,768]{2,1,0:T(8,128)(2,1)} %get-tuple-element.25.refs_4_.refs_0_), channel_id=1, source_target_pairs={{0,3},{1,2},{2,1},{3,0},{4,7},{5,6},{6,5},{7,4},{8,11},{9,10},{10,... | collective-permute-start | bytes 589832 | tf_op jit(solution)/shard_map/ppermute | solution.py:766
  42.3 10.4 %collective-permute-start.3 = (bf16[2,64,768]{2,1,0:T(8,128)(2,1)}, bf16[2,64,768]{2,1,0:T(8,128)(2,1)}, u32[]{:S(2)}, u32[]{:S(2)}) collective-permute-start(bf16[2,64,768]{2,1,0:T(8,128)(2,1)} %get-tuple-element.25.refs_4_.refs_0_), channel_id=1, source_target_pairs={{0,2},{1,3},{2,0},{3,1},{4,6},{5,7},{6,4},{7,5},{8,10},{9,11},{10,... | collective-permute-start | bytes 589832 | tf_op jit(solution)/shard_map/ppermute | solution.py:766
  43.1 9.6 %collective-permute-start.2 = (bf16[2,64,768]{2,1,0:T(8,128)(2,1)}, bf16[2,64,768]{2,1,0:T(8,128)(2,1)}, u32[]{:S(2)}, u32[]{:S(2)}) collective-permute-start(bf16[2,64,768]{2,1,0:T(8,128)(2,1)} %get-tuple-element.25.refs_4_.refs_0_), channel_id=1, source_target_pairs={{0,1},{1,0},{2,3},{3,2},{4,5},{5,4},{6,7},{7,6},{8,9},{9,8},{10,11... | collective-permute-start | bytes 589832 | tf_op jit(solution)/shard_map/ppermute | solution.py:766
  64.5 20.3 %all-to-all-start.1 = ((bf16[8,8,32,128]{3,2,1,0:T(8,128)(2,1)}), bf16[8,8,32,128]{3,2,1,0:T(8,128)(2,1)}, u32[]{:S(2)}, u32[]{:S(2)}) async-start(bf16[8,8,32,128]{3,2,1,0:T(8,128)(2,1)} %get-tuple-element.37), calls=%async_computation.1 | async-start | bytes 1048576 | tf_op jit(solution)/shard_map/all_to_all | solution.py:810

commit v11 on v10

--- a/solution.py
+++ b/solution.py
@@ -65,12 +65,13 @@
 
 
 def bias_kernel(
-    pair_hbm, gain_hbm, w_bias_hbm, feats_hbm, out_hbm, head_hbm, tail_hbm, pair_ref, gain_ref,
+    pair_hbm, gain_hbm, w_bias_hbm, feats_hbm, out_hbm, near_hbm, next_hbm, pair_ref, gain_ref,
     w_bias_ref, scaled_ref, stage_ref, local_ref, head_ref, tail_ref, sems,
 ):
     rows, keys = pair_ref.shape[0], pair_ref.shape[1]
     atoms = feats_hbm.shape[1]
     part = rows // 4
+    stride = scaled_ref.shape[0] // rows
     moves = [
         (gain_hbm, gain_ref), (w_bias_hbm, w_bias_ref),
         (feats_hbm.at[:, pl.ds(0, HALO), :], head_ref),
@@ -87,13 +88,20 @@
         if 8 * i % part == 0:
             copies[4 + 8 * i // part].wait()
         block = pair_ref[8 * i : 8 * i + 8].astype(f32).reshape(8 * keys, CZ)
-        scaled_ref[8 * keys * i : 8 * keys * (i + 1), :] = norm_rows(block)[0] * gain
+        scaled = norm_rows(block)[0] * gain
+        for k in range(8):
+            at = (8 * i + k) * stride
+            scaled_ref[at : at + keys, :] = scaled[keys * k : keys * (k + 1)]
     for copy in copies[2:4]:
         copy.wait()
-    edges = start_all([(head_ref, head_hbm), (tail_ref, tail_hbm)], sems)
+    even = jnp.where(lax.axis_index("tok") % 2 == 0, 1.0, 0.0)
+    head, tail = head_ref[...].astype(f32), tail_ref[...].astype(f32)
+    head_ref[...] = (tail * even + head * (1.0 - even)).astype(bf16)
+    tail_ref[...] = (head * even + tail * (1.0 - even)).astype(bf16)
+    edges = start_all([(head_ref, near_hbm), (tail_ref, next_hbm)], sems)
     blank = jnp.zeros((rows, CZ), bf16)
     for j in range(keys):
-        block = scaled_ref[pl.ds(j, rows, stride=keys), :].astype(bf16)
+        block = scaled_ref[pl.ds(j, rows, stride=stride), :].astype(bf16)
         both = jnp.concatenate(
             [jnp.concatenate([block, blank], axis=1), jnp.concatenate([blank, block], axis=1)],
             axis=0,
@@ -125,7 +133,7 @@
             pltpu.VMEM(pair.shape, bf16),
             pltpu.VMEM((1, CZ), f32),
             pltpu.VMEM(w_bias_t.shape, bf16),
-            pltpu.VMEM((rows * keys, CZ), f32),
+            pltpu.VMEM((rows * (keys + 8), CZ), f32),
             pltpu.VMEM((keys * PAIRS, 2 * rows), f32),
             pltpu.VMEM((keys * PAIRS, 2 * rows), bf16),
             pltpu.VMEM(edge.shape, bf16),
@@ -139,18 +147,19 @@
 
 
 def atom_kernel(
-    feats_hbm, left_hbm, right_hbm, mask_hbm, counts_hbm, single_hbm, w_qkv_hbm, w_out_hbm,
+    feats_hbm, near_hbm, next_hbm, mask_hbm, counts_hbm, single_hbm, w_qkv_hbm, w_out_hbm,
     w_embed_hbm, tokens_ref, normed_ref, mask_ref, counts_ref, single_ref, w_qkv_ref, w_out_ref,
-    w_embed_ref, sems, padded_ref, normed_atoms_ref, qkv_a, qkv_b, scores_a, scores_b, probs_a, probs_b, mixed_ref,
+    w_embed_ref, sems, halos_ref, padded_ref, normed_atoms_ref, qkv_a, qkv_b, scores_a, scores_b,
+    probs_a, probs_b, mixed_ref,
     updated_ref, split_ref, keybias_ref, onehot_ref, *, first,
 ):
     batch, atoms = tokens_ref.shape[0], feats_hbm.shape[1]
     padded = atoms + 2 * HALO
     moves = [(counts_hbm, counts_ref), (mask_hbm, mask_ref), (w_qkv_hbm, w_qkv_ref)]
     for s in range(batch):
-        moves.append((left_hbm.at[first + s], padded_ref.at[s, pl.ds(0, HALO)]))
+        moves.append((near_hbm.at[first + s], halos_ref.at[0, s]))
         moves.append((feats_hbm.at[first + s], padded_ref.at[s, pl.ds(HALO, atoms)]))
-        moves.append((right_hbm.at[first + s], padded_ref.at[s, pl.ds(HALO + atoms, HALO)]))
+        moves.append((next_hbm.at[first + s], halos_ref.at[1, s]))
     moves += [(w_out_hbm, w_out_ref), (w_embed_hbm, w_embed_ref), (single_hbm, single_ref)]
     copies = start_all(moves, sems)
     for copy in copies[0:2]:
@@ -184,8 +193,6 @@
         hit = jnp.where((at >= start) & (at < start + own), 1.0, 0.0).astype(bf16)
         onehot_ref[:, 256 * g : 256 * g + 256] = hit
         onehot_ref[:, atoms + 256 * g : atoms + 256 * g + 256] = hit
-    probs_a[...] = jnp.zeros_like(probs_a)
-    probs_b[...] = jnp.zeros_like(probs_b)
     head_of = iota((32, 128), 1) // ATOM_HD
     head_mask = [(head_of == h).astype(f32).astype(bf16) for h in range(ATOM_HEADS)]
     own_atom = (iota((32, 128), 1) % 32) == iota((32, 128), 0)
@@ -224,19 +231,19 @@
                 scores = from_ref[k, 32 * w : 32 * w + 128, 128 * w : 128 * w + 128] + keybias
                 expo = jnp.exp2((scores - jnp.max(scores, axis=0, keepdims=True)) * factor)
                 weights = expo * (1.0 / jnp.sum(expo, axis=0, keepdims=True))
-                to_ref[k, 32 * w : 32 * w + 128, 128 * w : 128 * w + 128] = weights.astype(bf16)
+                to_ref[2 * k + w] = weights.astype(bf16)
 
     def value_step(s, group, from_ref):
         qkv_ref = qkv_refs[s % 2]
         for k in range(2):
             base = pl.multiple_of(group * 128 + 64 * k, 64)
-            part = tn(from_ref[k], qkv_ref[pl.ds(base, 160), 2 * C_ATOM : 3 * C_ATOM])
             mixes = []
             for w in range(2):
-                mix = part[128 * w : 128 * w + 32]
+                values = qkv_ref[pl.ds(base + 32 * w, 128), 2 * C_ATOM : 3 * C_ATOM]
+                part = tn(from_ref[2 * k + w], values)
+                mix = part[0:32]
                 for h in range(1, ATOM_HEADS):
-                    low = 128 * w + 32 * h
-                    mix = jnp.where(head_of == h, part[low : low + 32], mix)
+                    mix = jnp.where(head_of == h, part[32 * h : 32 * h + 32], mix)
                 mixes.append(mix.astype(bf16))
             mixed_ref[pl.ds(base, 64), :] = jnp.concatenate(mixes, axis=0)
 
@@ -253,11 +260,13 @@
         tokens_ref[s] = tokens
         normed_ref[s] = norm_rows(tokens)[0].astype(bf16)
 
-    for copy in copies[2:6]:
-        copy.wait()
+    for copy in copies[2:]:
+        copy.wait()
+    even = jnp.where(lax.axis_index("tok") % 2 == 0, 1.0, 0.0)
+    near, after = halos_ref[0].astype(f32), halos_ref[1].astype(f32)
+    padded_ref[:, 0:HALO, :] = (after * even + near * (1.0 - even)).astype(bf16)
+    padded_ref[:, HALO + atoms : padded, :] = (near * even + after * (1.0 - even)).astype(bf16)
     qkv_step(0)
-    for copy in copies[6:]:
-        copy.wait()
     for s in range(batch):
         score_step(s, 0, scores_a)
 
@@ -278,7 +287,7 @@
             qkv_step(s + 1)
 
 
-def atom_stage(part, batch, feats, left, right, mask, counts, single, w_qkv, w_out, w_embed):
+def atom_stage(part, batch, feats, near, next_, mask, counts, single, w_qkv, w_out, w_embed):
     atoms = feats.shape[1]
     tok_rows = single.shape[0]
     padded = atoms + 2 * HALO
@@ -298,14 +307,15 @@
             pltpu.VMEM(w_out.shape, bf16),
             pltpu.VMEM(w_embed.shape, bf16),
             pltpu.SemaphoreType.DMA((6 + 3 * batch,)),
+            pltpu.VMEM((2, batch, HALO, C_ATOM), bf16),
             pltpu.VMEM((batch, padded, C_ATOM), bf16),
             pltpu.VMEM((padded, C_ATOM), bf16),
             pltpu.VMEM((padded, 3 * C_ATOM), bf16),
             pltpu.VMEM((padded, 3 * C_ATOM), bf16),
             pltpu.VMEM((2, 160, 256), f32),
             pltpu.VMEM((2, 160, 256), f32),
-            pltpu.VMEM((2, 160, 256), bf16),
-            pltpu.VMEM((2, 160, 256), bf16),
+            pltpu.VMEM((4, 128, 128), bf16),
+            pltpu.VMEM((4, 128, 128), bf16),
             pltpu.VMEM((atoms, C_ATOM), bf16),
             pltpu.VMEM((atoms, C_ATOM), bf16),
             pltpu.VMEM((2 * atoms, C_TOK), bf16),
@@ -317,7 +327,7 @@
             flops=10**10, bytes_accessed=4 * 10**6, transcendentals=3 * 10**6
         ),
         name="atoms",
-    )(feats, left, right, mask, counts, single, w_qkv, w_out, w_embed)
+    )(feats, near, next_, mask, counts, single, w_qkv, w_out, w_embed)
 
 
 def head_masks(rows):
@@ -781,10 +791,10 @@
     groups = lax.axis_size("samp")
 
     w_bias_t = w_bias.T
-    local_bias, head, tail = pair_bias(pair, pair_gain, w_bias_t, atom_feats, groups)
-    steps = [(i, i + 1) for i in range(shards - 1)]
-    left = lax.ppermute(tail, "tok", steps)
-    right = lax.ppermute(head, "tok", [(j, i) for i, j in steps])
+    local_bias, near, next_ = pair_bias(pair, pair_gain, w_bias_t, atom_feats, groups)
+    near = swap(near, "tok", 1)
+    steps = [(i, i + 1) for i in range(1, shards - 1, 2)]
+    next_ = lax.ppermute(next_, "tok", steps + [(j, i) for i, j in steps])
 
     bias = lax.all_to_all(local_bias, "samp", 0, 0).reshape(groups, PAIRS, -1, 2 * tok_rows)
 
@@ -795,7 +805,7 @@
     tokens, gathered = [], []
     for part in range(2):
         tok, normed = atom_stage(
-            part, each, atom_feats, left, right, mask, atom_counts, token_single, w_atom_qkv,
+            part, each, atom_feats, near, next_, mask, atom_counts, token_single, w_atom_qkv,
             w_atom_out, w_embed,
         )
         tokens.append(tok)

time: 89.2 us -> 85.4 us (0.957)
  starting transfers between devices: 22.7 us -> 20.2 us
  Pallas kernels: 56.1 us -> 54.9 us
    ppermute x2 -> x1, starting transfers between devices: 4.25 us -> 1.26 us  [body(): next_ = lax.ppermute(next_, 'tok', steps + [(j, i) for i, j in steps])]
    pallas_call x2, Pallas kernels: 22.1 us -> 21 us  [atom_stage(): pl.pallas_call(functools.partial(atom_kernel, first=part * batch), in_spe...]
    ppermute x6 -> x7, starting transfers between devices: 5.78 us -> 6.4 us  [swap(): lax.ppermute(values, axis, [(i, i ^ k) for i in range(lax.axis_size(axis))])]
    ppermute x6 -> x7, waiting for transfers between devices: 2.15 us -> 2.11 us  [swap(): lax.ppermute(values, axis, [(i, i ^ k) for i in range(lax.axis_size(axis))])]
where the time goes in v11:
time: 85.4 us; the launch traced here: 85 us
  Pallas kernels  54.9 us (64%)
  starting transfers between devices  20.2 us (24%)
  waiting for transfers between devices  8.97 us (11%)
  between operations  0.89 us (1%)
    pallas_call x2, Pallas kernels, atom_stage(): pl.pallas_call(functools.partial(atom_kernel, first=part * batch), in_spe...  21 us
    pallas_call x1, Pallas kernels, token_stage(): pl.pallas_call(functools.partial(token_kernel, count=len(pieces)), in_spe...  11.8 us
    pallas_call x1, Pallas kernels, attend_stage(): pl.pallas_call(functools.partial(attend_kernel, count=len(pieces)), in_sp...  7.45 us
    pallas_call x1, Pallas kernels, output_stage(): pl.pallas_call(output_kernel, out_shape=[jax.ShapeDtypeStruct(resid.shape...  7.41 us
    all_to_all x1, waiting for transfers between devices, body(): parts = lax.all_to_all(d_bias, 'samp', 0, 0)  6.86 us
    all_to_all x1, starting transfers between devices, body(): lax.all_to_all(local_bias, 'samp', 0, 0)  6.86 us
    ppermute x7, starting transfers between devices, swap(): lax.ppermute(values, axis, [(i, i ^ k) for i in range(lax.axis_size(axis))])  6.4 us
    all_to_all x1, starting transfers between devices, body(): parts = lax.all_to_all(d_bias, 'samp', 0, 0)  5.72 us
  transfers between devices with their start and end apart: 10, of which 2 were waited for; matrix products, arithmetic and copies ran while one was open for 0% of the time, Pallas kernels for 42%

profile of v11, /device:TPU:0, one launch (start us, length us, event | category | flops | bytes accessed | tf_op | source)
XLA Modules:
  0.0 85.0 jit_solution(5062805697547760354)
XLA Ops:
  0.6 3.5 %pair_bias.1 = (bf16[8,256,128]{2,1,0:T(8,128)(2,1)}, bf16[4,48,128]{2,1,0:T(8,128)(2,1)}, bf16[4,48,128]{2,1,0:T(8,128)(2,1)}) custom-call(bf16[64,32,128]{2,1,0:T(8,128)(2,1)} %pair_ref.1, f32[1,128]{1,0:T(1,128)} %bitcast.7, bf16[16,128]{1,0:T(8,128)(2,1)} %bitcast.5, bf16[4,1280,128]{2,1,0:T(8,128)(2,1)} %feats_hbm.5), custom_call_target="tpu_custom_call" | custom-call | flops 10000000 | bytes 10000000 | tf_op jit(solution)/shard_map/pair_bias/pallas_call | solution.py:125
  4.2 0.5 collective-permute-start
  4.7 1.3 %collective-permute-start.1 = (bf16[4,48,128]{2,1,0:T(8,128)(2,1)}, bf16[4,48,128]{2,1,0:T(8,128)(2,1)}, u32[]{:S(2)}, u32[]{:S(2)}) collective-permute-start(bf16[4,48,128]{2,1,0:T(8,128)(2,1)} %get-tuple-element.22), channel_id=1, source_target_pairs={{1,2},{2,1},{5,6},{6,5},{9,10},{10,9},{13,14},{14,13},{17,18},{18,... | collective-permute-start | bytes 147464 | tf_op jit(solution)/shard_map/ppermute | solution.py:797
  5.9 6.9 %all-to-all-start = ((bf16[8,256,128]{2,1,0:T(8,128)(2,1)}), bf16[8,256,128]{2,1,0:T(8,128)(2,1)}, u32[]{:S(2)}, u32[]{:S(2)}) async-start(bf16[8,256,128]{2,1,0:T(8,128)(2,1)} %get-tuple-element.23), calls=%async_computation | async-start | bytes 1048576 | tf_op jit(solution)/shard_map/all_to_all | solution.py:799
  12.8 0.0 collective-permute-done.near_hbm
  12.8 0.0 collective-permute-done.1.next_hbm
  12.8 10.4 %atoms.3 = (f32[2,64,768]{2,1,0:T(8,128)}, bf16[2,64,768]{2,1,0:T(8,128)(2,1)}) custom-call(bf16[4,1280,128]{2,1,0:T(8,128)(2,1)} %feats_hbm.5, bf16[4,48,128]{2,1,0:T(8,128)(2,1)} %collective-permute-done.near_hbm, bf16[4,48,128]{2,1,0:T(8,128)(2,1)} %collective-permute-done.1.next_hbm, s32[40,128]{1,0:T(8,128)} %bitcast.10, s32[1,64]{1,0:T(1,128)} %counts_hbm.3, ...), custom_call_target="tpu_custom_call" | custom-call | flops 10000000000 | bytes 4000000 | tf_op jit(solution)/shard_map/atoms/pallas_call | solution.py:294
  23.2 1.4 %collective-permute-start.7 = (bf16[2,64,768]{2,1,0:T(8,128)(2,1)}, bf16[2,64,768]{2,1,0:T(8,128)(2,1)}, u32[]{:S(2)}, u32[]{:S(2)}) collective-permute-start(bf16[2,64,768]{2,1,0:T(8,128)(2,1)} %get-tuple-element.26.refs_0_), channel_id=1, source_target_pairs={{0,3},{1,2},{2,1},{3,0},{4,7},{5,6},{6,5},{7,4},{8,11},{9,10},{10,... | collective-permute-start | bytes 589832 | tf_op jit(solution)/shard_map/ppermute | solution.py:776
  24.6 2.3 %collective-permute-start.6 = (bf16[2,64,768]{2,1,0:T(8,128)(2,1)}, bf16[2,64,768]{2,1,0:T(8,128)(2,1)}, u32[]{:S(2)}, u32[]{:S(2)}) collective-permute-start(bf16[2,64,768]{2,1,0:T(8,128)(2,1)} %get-tuple-element.26.refs_0_), channel_id=1, source_target_pairs={{0,2},{1,3},{2,0},{3,1},{4,6},{5,7},{6,4},{7,5},{8,10},{9,11},{10,... | collective-permute-start | bytes 589832 | tf_op jit(solution)/shard_map/ppermute | solution.py:776
  26.9 0.0 collective-permute-start.5
  26.9 10.6 %atoms.2 = (f32[2,64,768]{2,1,0:T(8,128)}, bf16[2,64,768]{2,1,0:T(8,128)(2,1)}) custom-call(bf16[4,1280,128]{2,1,0:T(8,128)(2,1)} %feats_hbm.5, bf16[4,48,128]{2,1,0:T(8,128)(2,1)} %collective-permute-done.near_hbm, bf16[4,48,128]{2,1,0:T(8,128)(2,1)} %collective-permute-done.1.next_hbm, s32[40,128]{1,0:T(8,128)} %bitcast.11, s32[1,64]{1,0:T(1,128)} %counts_hbm.3, ...), custom_call_target="tpu_custom_call" | custom-call | flops 10000000000 | bytes 4000000 | tf_op jit(solution)/shard_map/atoms/pallas_call | solution.py:294
  37.5 0.7 collective-permute-start.4
  38.2 1.5 %collective-permute-start.3 = (bf16[2,64,768]{2,1,0:T(8,128)(2,1)}, bf16[2,64,768]{2,1,0:T(8,128)(2,1)}, u32[]{:S(2)}, u32[]{:S(2)}) collective-permute-start(bf16[2,64,768]{2,1,0:T(8,128)(2,1)} %get-tuple-element.25.refs_4_.refs_0_), channel_id=1, source_target_pairs={{0,2},{1,3},{2,0},{3,1},{4,6},{5,7},{6,4},{7,5},{8,10},{9,11},{10,... | collective-permute-start | bytes 589832 | tf_op jit(solution)/shard_map/ppermute | solution.py:776
  39.7 0.0 collective-permute-done.7.refs_3_
  39.7 0.0 collective-permute-start.2
  39.7 0.0 collective-permute-done.6.refs_2_
  39.7 0.0 collective-permute-done.5.refs_1_
  39.7 0.0 all-to-all-done
  39.7 7.4 %attend.1 = (bf16[128,768]{1,0:T(8,128)(2,1)}, f32[2,8,256,128]{3,2,1,0:T(8,128)}, bf16[2,256,768]{2,1,0:T(8,128)(2,1)}, f32[256,1536]{1,0:T(8,128)}, bf16[128,768]{1,0:T(8,128)(2,1)}) custom-call(bf16[2,64,768]{2,1,0:T(8,128)(2,1)} %get-tuple-element.26.refs_0_, bf16[2,64,768]{2,1,0:T(8,128)(2,1)} %collective-permute-done.5.refs_1_, ...), custom_call_target="tpu_custom_call" | custom-call | flops 4000000000 | bytes 10000000 | tf_op jit(solution)/shard_map/attend/pallas_call | solution.py:472
  47.2 0.0 collective-permute-done.4.refs_3_
  47.2 2.1 %collective-permute-done.3.refs_2_ = bf16[2,64,768]{2,1,0:T(8,128)(2,1)} collective-permute-done((bf16[2,64,768]{2,1,0:T(8,128)(2,1)}, bf16[2,64,768]{2,1,0:T(8,128)(2,1)}, u32[]{:S(2)}, u32[]{:S(2)}) %collective-permute-start.3) | collective-permute-done | bytes 196640 | tf_op jit(solution)/shard_map/ppermute | solution.py:776
  49.3 0.0 collective-permute-done.2.refs_1_
  49.3 11.8 %tokens.1 = (f32[256,768]{1,0:T(8,128)}, bf16[256,1536]{1,0:T(8,128)(2,1)}, bf16[8,8,32,128]{3,2,1,0:T(8,128)(2,1)}) custom-call(bf16[2,64,768]{2,1,0:T(8,128)(2,1)} %get-tuple-element.25.refs_4_.refs_0_, bf16[2,64,768]{2,1,0:T(8,128)(2,1)} %collective-permute-done.2.refs_1_, bf16[2,64,768]{2,1,0:T(8,128)(2,1)} %collective-permute-done.3.refs_2_, ...), custom_call_target="tpu_custom_call" | custom-call | flops 10000000000 | bytes 20000000 | tf_op jit(solution)/shard_map/tokens/pallas_call | solution.py:611
  61.1 5.7 %all-to-all-start.1 = ((bf16[8,8,32,128]{3,2,1,0:T(8,128)(2,1)}), bf16[8,8,32,128]{3,2,1,0:T(8,128)(2,1)}, u32[]{:S(2)}, u32[]{:S(2)}) async-start(bf16[8,8,32,128]{3,2,1,0:T(8,128)(2,1)} %get-tuple-element.37), calls=%async_computation.1 | async-start | bytes 1048576 | tf_op jit(solution)/shard_map/all_to_all | solution.py:820
  66.8 7.4 %output.1 = (bf16[256,768]{1,0:T(8,128)(2,1)}, f32[2048,128]{1,0:T(8,128)}, f32[32,128]{1,0:T(8,128)}) custom-call(f32[256,768]{1,0:T(8,128)} %get-tuple-element.34.resid_ref, bf16[256,1536]{1,0:T(8,128)(2,1)} %get-tuple-element.35.hidden_ref, bf16[1536,768]{1,0:T(8,128)(2,1)} %w_down_ref.1, bf16[64,32,128]{2,1,0:T(8,128)(2,1)} %pair_ref.1), custom_call_target="tpu_custom_call" | custom-call | flops 1000000000 | bytes 8000000 | tf_op jit(solution)/shard_map/output/pallas_call | solution.py:677
  74.2 6.9 %all-to-all-done.1.parts_hbm = bf16[8,8,32,128]{3,2,1,0:T(8,128)(2,1)} async-done(((bf16[8,8,32,128]{3,2,1,0:T(8,128)(2,1)}), bf16[8,8,32,128]{3,2,1,0:T(8,128)(2,1)}, u32[]{:S(2)}, u32[]{:S(2)}) %all-to-all-start.1) | async-done | bytes 524320 | tf_op jit(solution)/shard_map/all_to_all | solution.py:820
  81.1 3.7 %pair_grad.1 = f32[64,32,128]{2,1,0:T(8,128)} custom-call(bf16[8,8,32,128]{3,2,1,0:T(8,128)(2,1)} %all-to-all-done.1.parts_hbm, f32[2048,128]{1,0:T(8,128)} %get-tuple-element.38.hat_hbm, f32[32,128]{1,0:T(8,128)} %get-tuple-element.39.rstd_hbm, f32[1,128]{1,0:T(1,128)} %bitcast.8, bf16[16,128]{1,0:T(8,128)(2,1)} %bitcast.6), custom_call_target="tpu_custom_call" | custom-call | flops 100000000 | bytes 4000000 | tf_op jit(solution)/shard_map/pair_grad/pallas_call | solution.py:754
Async XLA Ops:
  4.2 8.6 %collective-permute-start = (bf16[4,48,128]{2,1,0:T(8,128)(2,1)}, bf16[4,48,128]{2,1,0:T(8,128)(2,1)}, u32[]{:S(2)}, u32[]{:S(2)}) collective-permute-start(bf16[4,48,128]{2,1,0:T(8,128)(2,1)} %get-tuple-element.21), channel_id=1, source_target_pairs={{0,1},{1,0},{2,3},{3,2},{4,5},{5,4},{6,7},{7,6},{8,9},{9,8},{10,11... | collective-permute-start | bytes 147464 | tf_op jit(solution)/shard_map/ppermute | solution.py:776
  4.7 8.1 %collective-permute-start.1 = (bf16[4,48,128]{2,1,0:T(8,128)(2,1)}, bf16[4,48,128]{2,1,0:T(8,128)(2,1)}, u32[]{:S(2)}, u32[]{:S(2)}) collective-permute-start(bf16[4,48,128]{2,1,0:T(8,128)(2,1)} %get-tuple-element.22), channel_id=1, source_target_pairs={{1,2},{2,1},{5,6},{6,5},{9,10},{10,9},{13,14},{14,13},{17,18},{18,... | collective-permute-start | bytes 147464 | tf_op jit(solution)/shard_map/ppermute | solution.py:797
  5.9 33.8 %all-to-all-start = ((bf16[8,256,128]{2,1,0:T(8,128)(2,1)}), bf16[8,256,128]{2,1,0:T(8,128)(2,1)}, u32[]{:S(2)}, u32[]{:S(2)}) async-start(bf16[8,256,128]{2,1,0:T(8,128)(2,1)} %get-tuple-element.23), calls=%async_computation | async-start | bytes 1048576 | tf_op jit(solution)/shard_map/all_to_all | solution.py:799
  23.2 16.5 %collective-permute-start.7 = (bf16[2,64,768]{2,1,0:T(8,128)(2,1)}, bf16[2,64,768]{2,1,0:T(8,128)(2,1)}, u32[]{:S(2)}, u32[]{:S(2)}) collective-permute-start(bf16[2,64,768]{2,1,0:T(8,128)(2,1)} %get-tuple-element.26.refs_0_), channel_id=1, source_target_pairs={{0,3},{1,2},{2,1},{3,0},{4,7},{5,6},{6,5},{7,4},{8,11},{9,10},{10,... | collective-permute-start | bytes 589832 | tf_op jit(solution)/shard_map/ppermute | solution.py:776
  24.6 15.1 %collective-permute-start.6 = (bf16[2,64,768]{2,1,0:T(8,128)(2,1)}, bf16[2,64,768]{2,1,0:T(8,128)(2,1)}, u32[]{:S(2)}, u32[]{:S(2)}) collective-permute-start(bf16[2,64,768]{2,1,0:T(8,128)(2,1)} %get-tuple-element.26.refs_0_), channel_id=1, source_target_pairs={{0,2},{1,3},{2,0},{3,1},{4,6},{5,7},{6,4},{7,5},{8,10},{9,11},{10,... | collective-permute-start | bytes 589832 | tf_op jit(solution)/shard_map/ppermute | solution.py:776
  26.9 12.8 %collective-permute-start.5 = (bf16[2,64,768]{2,1,0:T(8,128)(2,1)}, bf16[2,64,768]{2,1,0:T(8,128)(2,1)}, u32[]{:S(2)}, u32[]{:S(2)}) collective-permute-start(bf16[2,64,768]{2,1,0:T(8,128)(2,1)} %get-tuple-element.26.refs_0_), channel_id=1, source_target_pairs={{0,1},{1,0},{2,3},{3,2},{4,5},{5,4},{6,7},{7,6},{8,9},{9,8},{10,11... | collective-permute-start | bytes 589832 | tf_op jit(solution)/shard_map/ppermute | solution.py:776
  37.5 9.7 %collective-permute-start.4 = (bf16[2,64,768]{2,1,0:T(8,128)(2,1)}, bf16[2,64,768]{2,1,0:T(8,128)(2,1)}, u32[]{:S(2)}, u32[]{:S(2)}) collective-permute-start(bf16[2,64,768]{2,1,0:T(8,128)(2,1)} %get-tuple-element.25.refs_4_.refs_0_), channel_id=1, source_target_pairs={{0,3},{1,2},{2,1},{3,0},{4,7},{5,6},{6,5},{7,4},{8,11},{9,10},{10,... | collective-permute-start | bytes 589832 | tf_op jit(solution)/shard_map/ppermute | solution.py:776
  38.2 11.1 %collective-permute-start.3 = (bf16[2,64,768]{2,1,0:T(8,128)(2,1)}, bf16[2,64,768]{2,1,0:T(8,128)(2,1)}, u32[]{:S(2)}, u32[]{:S(2)}) collective-permute-start(bf16[2,64,768]{2,1,0:T(8,128)(2,1)} %get-tuple-element.25.refs_4_.refs_0_), channel_id=1, source_target_pairs={{0,2},{1,3},{2,0},{3,1},{4,6},{5,7},{6,4},{7,5},{8,10},{9,11},{10,... | collective-permute-start | bytes 589832 | tf_op jit(solution)/shard_map/ppermute | solution.py:776
  39.7 9.6 %collective-permute-start.2 = (bf16[2,64,768]{2,1,0:T(8,128)(2,1)}, bf16[2,64,768]{2,1,0:T(8,128)(2,1)}, u32[]{:S(2)}, u32[]{:S(2)}) collective-permute-start(bf16[2,64,768]{2,1,0:T(8,128)(2,1)} %get-tuple-element.25.refs_4_.refs_0_), channel_id=1, source_target_pairs={{0,1},{1,0},{2,3},{3,2},{4,5},{5,4},{6,7},{7,6},{8,9},{9,8},{10,11... | collective-permute-start | bytes 589832 | tf_op jit(solution)/shard_map/ppermute | solution.py:776
  61.1 20.0 %all-to-all-start.1 = ((bf16[8,8,32,128]{3,2,1,0:T(8,128)(2,1)}), bf16[8,8,32,128]{3,2,1,0:T(8,128)(2,1)}, u32[]{:S(2)}, u32[]{:S(2)}) async-start(bf16[8,8,32,128]{3,2,1,0:T(8,128)(2,1)} %get-tuple-element.37), calls=%async_computation.1 | async-start | bytes 1048576 | tf_op jit(solution)/shard_map/all_to_all | solution.py:820

commit v12 on v11

--- a/solution.py
+++ b/solution.py
@@ -207,7 +207,7 @@
     def score_step(s, group, to_ref):
         qkv_ref = qkv_refs[s % 2]
         for k in range(2):
-            base = pl.multiple_of(group * 128 + 64 * k, 64)
+            base = group * 128 + 64 * k
             queries = qkv_ref[pl.ds(base + HALO, 64), 0:C_ATOM]
             spread = jnp.concatenate(
                 [
@@ -221,7 +221,7 @@
 
     def softmax_step(group, from_ref, to_ref):
         for k in range(2):
-            base = pl.multiple_of(group * 128 + 64 * k, 64)
+            base = group * 128 + 64 * k
             for w in range(2):
                 keybias = keybias_ref[pl.ds(base + 32 * w, 128), :]
                 keybias = jnp.concatenate(
@@ -236,7 +236,7 @@
     def value_step(s, group, from_ref):
         qkv_ref = qkv_refs[s % 2]
         for k in range(2):
-            base = pl.multiple_of(group * 128 + 64 * k, 64)
+            base = group * 128 + 64 * k
             mixes = []
             for w in range(2):
                 values = qkv_ref[pl.ds(base + 32 * w, 128), 2 * C_ATOM : 3 * C_ATOM]
@@ -270,17 +270,16 @@
     for s in range(batch):
         score_step(s, 0, scores_a)
 
-        def window_step(i, carry, s=s):
+        for i in range(chunks):
             even, odd = 2 * i, 2 * i + 1
             score_step(s, odd, scores_b)
             softmax_step(even, scores_a, probs_a)
-            value_step(s, jnp.maximum(even - 1, 0), probs_b)
-            score_step(s, jnp.minimum(odd + 1, 2 * chunks - 1), scores_a)
+            if even > 0:
+                value_step(s, even - 1, probs_b)
+            if odd + 1 < 2 * chunks:
+                score_step(s, odd + 1, scores_a)
             softmax_step(odd, scores_b, probs_b)
             value_step(s, even, probs_a)
-            return carry
-
-        lax.fori_loop(0, chunks, window_step, 0)
         value_step(s, 2 * chunks - 1, probs_b)
         embed_step(s)
         if s + 1 < batch:
@@ -505,8 +504,8 @@
     (
         queries_hbm, bias_hbm, tokens_a_hbm, tokens_b_hbm, att_a_hbm, cot_hbm, probs_a_hbm, values_a_hbm,
         w_qkv_hbm, w_out_hbm, w_gate_hbm, w_up_hbm, d_hidden_hbm,
-        resid_hbm, hidden_hbm, d_bias_ref,
-        bias_ref, tokens_ref, att_a_ref, cot_ref, resid_ref, hidden_ref,
+        resid_hbm, hidden_hbm, d_bias_hbm,
+        d_bias_ref, bias_ref, tokens_ref, att_a_ref, cot_ref, resid_ref, hidden_ref,
         w_kv_ref, w_out_ref, w_gate_ref, w_up_ref, d_hidden_ref, probs_ref, values_ref, sems,
         all_ref, queries_ref, keys_ref, grads_ref, d_gate_ref, d_up_ref, hat_ref,
     ) = refs[count:]
@@ -594,6 +593,12 @@
         size = d_bias_ref.shape[2]
         for k in range(d_bias_ref.shape[0]):
             d_bias_ref[k, pair] = total[size * k : size * (k + 1)].astype(bf16)
+        back.append(
+            pltpu.make_async_copy(
+                d_bias_ref.at[:, pair], d_bias_hbm.at[:, pair], sems.at[2 + pair]
+            )
+        )
+        back[-1].start()
     for copy in back:
         copy.wait()
 
@@ -611,13 +616,14 @@
     return pl.pallas_call(
         functools.partial(token_kernel, count=len(pieces)),
         in_specs=[hbm] * (len(pieces) + 13),
-        out_specs=[hbm, hbm, vmem],
+        out_specs=[hbm, hbm, hbm],
         out_shape=[
             jax.ShapeDtypeStruct((rows, C_TOK), f32),
             jax.ShapeDtypeStruct((rows, hidden), bf16),
             jax.ShapeDtypeStruct(bias.shape, bf16),
         ],
         scratch_shapes=[
+            pltpu.VMEM(bias.shape, bf16),
             pltpu.VMEM(bias.shape, bf16),
             pltpu.VMEM(cot.shape, f32),
             pltpu.VMEM(att_a.shape, bf16),

time: 85.4 us -> 81.8 us (0.958)
  Pallas kernels: 54.9 us -> 51.3 us
    pallas_call x2, Pallas kernels: 21 us -> 17.9 us  [atom_stage(): pl.pallas_call(functools.partial(atom_kernel, first=part * batch), in_spe...]
  transfers between devices with their start and end apart: 10 -> 10, of which waited for: 2 -> 2; matrix products, arithmetic and copies ran while one was open for 0% -> 0% of each run, Pallas kernels for 42% -> 40%
where the time goes in v12:
time: 81.8 us; the launch traced here: 81.4 us
  Pallas kernels  51.3 us (63%)
  starting transfers between devices  20.2 us (25%)
  waiting for transfers between devices  8.99 us (11%)
  between operations  0.87 us (1%)
    pallas_call x2, Pallas kernels, atom_stage(): pl.pallas_call(functools.partial(atom_kernel, first=part * batch), in_spe...  17.9 us
    pallas_call x1, Pallas kernels, token_stage(): pl.pallas_call(functools.partial(token_kernel, count=len(pieces)), in_spe...  11.4 us
    pallas_call x1, Pallas kernels, attend_stage(): pl.pallas_call(functools.partial(attend_kernel, count=len(pieces)), in_sp...  7.44 us
    pallas_call x1, Pallas kernels, output_stage(): pl.pallas_call(output_kernel, out_shape=[jax.ShapeDtypeStruct(resid.shape...  7.41 us
    all_to_all x1, waiting for transfers between devices, body(): parts = lax.all_to_all(d_bias, 'samp', 0, 0)  6.86 us
    all_to_all x1, starting transfers between devices, body(): lax.all_to_all(local_bias, 'samp', 0, 0)  6.86 us
    ppermute x7, starting transfers between devices, swap(): lax.ppermute(values, axis, [(i, i ^ k) for i in range(lax.axis_size(axis))])  6.39 us
    all_to_all x1, starting transfers between devices, body(): parts = lax.all_to_all(d_bias, 'samp', 0, 0)  5.72 us
  transfers between devices with their start and end apart: 10, of which 2 were waited for; matrix products, arithmetic and copies ran while one was open for 0% of the time, Pallas kernels for 40%

profile of v12, /device:TPU:0, one launch (start us, length us, event | category | flops | bytes accessed | tf_op | source)
XLA Modules:
  0.0 81.4 jit_solution(1797140477217016181)
XLA Ops:
  0.6 3.5 %pair_bias.1 = (bf16[8,256,128]{2,1,0:T(8,128)(2,1)}, bf16[4,48,128]{2,1,0:T(8,128)(2,1)}, bf16[4,48,128]{2,1,0:T(8,128)(2,1)}) custom-call(bf16[64,32,128]{2,1,0:T(8,128)(2,1)} %pair_ref.1, f32[1,128]{1,0:T(1,128)} %bitcast.7, bf16[16,128]{1,0:T(8,128)(2,1)} %bitcast.5, bf16[4,1280,128]{2,1,0:T(8,128)(2,1)} %feats_hbm.5), custom_call_target="tpu_custom_call" | custom-call | flops 10000000 | bytes 10000000 | tf_op jit(solution)/shard_map/pair_bias/pallas_call | solution.py:125
  4.2 0.5 collective-permute-start
  4.7 1.3 %collective-permute-start.1 = (bf16[4,48,128]{2,1,0:T(8,128)(2,1)}, bf16[4,48,128]{2,1,0:T(8,128)(2,1)}, u32[]{:S(2)}, u32[]{:S(2)}) collective-permute-start(bf16[4,48,128]{2,1,0:T(8,128)(2,1)} %get-tuple-element.22), channel_id=1, source_target_pairs={{1,2},{2,1},{5,6},{6,5},{9,10},{10,9},{13,14},{14,13},{17,18},{18,... | collective-permute-start | bytes 147464 | tf_op jit(solution)/shard_map/ppermute | solution.py:803
  5.9 6.9 %all-to-all-start = ((bf16[8,256,128]{2,1,0:T(8,128)(2,1)}), bf16[8,256,128]{2,1,0:T(8,128)(2,1)}, u32[]{:S(2)}, u32[]{:S(2)}) async-start(bf16[8,256,128]{2,1,0:T(8,128)(2,1)} %get-tuple-element.23), calls=%async_computation | async-start | bytes 1048576 | tf_op jit(solution)/shard_map/all_to_all | solution.py:805
  12.8 0.0 collective-permute-done.near_hbm
  12.8 0.0 collective-permute-done.1.next_hbm
  12.8 8.8 %atoms.3 = (f32[2,64,768]{2,1,0:T(8,128)}, bf16[2,64,768]{2,1,0:T(8,128)(2,1)}) custom-call(bf16[4,1280,128]{2,1,0:T(8,128)(2,1)} %feats_hbm.5, bf16[4,48,128]{2,1,0:T(8,128)(2,1)} %collective-permute-done.near_hbm, bf16[4,48,128]{2,1,0:T(8,128)(2,1)} %collective-permute-done.1.next_hbm, s32[40,128]{1,0:T(8,128)} %bitcast.10, s32[1,64]{1,0:T(1,128)} %counts_hbm.3, ...), custom_call_target="tpu_custom_call" | custom-call | flops 10000000000 | bytes 4000000 | tf_op jit(solution)/shard_map/atoms/pallas_call | solution.py:293
  21.7 1.4 %collective-permute-start.7 = (bf16[2,64,768]{2,1,0:T(8,128)(2,1)}, bf16[2,64,768]{2,1,0:T(8,128)(2,1)}, u32[]{:S(2)}, u32[]{:S(2)}) collective-permute-start(bf16[2,64,768]{2,1,0:T(8,128)(2,1)} %get-tuple-element.26.refs_0_), channel_id=1, source_target_pairs={{0,3},{1,2},{2,1},{3,0},{4,7},{5,6},{6,5},{7,4},{8,11},{9,10},{10,... | collective-permute-start | bytes 589832 | tf_op jit(solution)/shard_map/ppermute | solution.py:782
  23.0 2.3 %collective-permute-start.6 = (bf16[2,64,768]{2,1,0:T(8,128)(2,1)}, bf16[2,64,768]{2,1,0:T(8,128)(2,1)}, u32[]{:S(2)}, u32[]{:S(2)}) collective-permute-start(bf16[2,64,768]{2,1,0:T(8,128)(2,1)} %get-tuple-element.26.refs_0_), channel_id=1, source_target_pairs={{0,2},{1,3},{2,0},{3,1},{4,6},{5,7},{6,4},{7,5},{8,10},{9,11},{10,... | collective-permute-start | bytes 589832 | tf_op jit(solution)/shard_map/ppermute | solution.py:782
  25.3 0.0 collective-permute-start.5
  25.3 9.0 %atoms.2 = (f32[2,64,768]{2,1,0:T(8,128)}, bf16[2,64,768]{2,1,0:T(8,128)(2,1)}) custom-call(bf16[4,1280,128]{2,1,0:T(8,128)(2,1)} %feats_hbm.5, bf16[4,48,128]{2,1,0:T(8,128)(2,1)} %collective-permute-done.near_hbm, bf16[4,48,128]{2,1,0:T(8,128)(2,1)} %collective-permute-done.1.next_hbm, s32[40,128]{1,0:T(8,128)} %bitcast.11, s32[1,64]{1,0:T(1,128)} %counts_hbm.3, ...), custom_call_target="tpu_custom_call" | custom-call | flops 10000000000 | bytes 4000000 | tf_op jit(solution)/shard_map/atoms/pallas_call | solution.py:293
  34.4 0.7 collective-permute-start.4
  35.1 1.5 %collective-permute-start.3 = (bf16[2,64,768]{2,1,0:T(8,128)(2,1)}, bf16[2,64,768]{2,1,0:T(8,128)(2,1)}, u32[]{:S(2)}, u32[]{:S(2)}) collective-permute-start(bf16[2,64,768]{2,1,0:T(8,128)(2,1)} %get-tuple-element.25.refs_4_.refs_0_), channel_id=1, source_target_pairs={{0,2},{1,3},{2,0},{3,1},{4,6},{5,7},{6,4},{7,5},{8,10},{9,11},{10,... | collective-permute-start | bytes 589832 | tf_op jit(solution)/shard_map/ppermute | solution.py:782
  36.6 0.0 collective-permute-done.7.refs_3_
  36.6 0.0 collective-permute-start.2
  36.6 0.0 collective-permute-done.6.refs_2_
  36.6 0.0 collective-permute-done.5.refs_1_
  36.6 0.0 all-to-all-done
  36.6 7.4 %attend.1 = (bf16[128,768]{1,0:T(8,128)(2,1)}, f32[2,8,256,128]{3,2,1,0:T(8,128)}, bf16[2,256,768]{2,1,0:T(8,128)(2,1)}, f32[256,1536]{1,0:T(8,128)}, bf16[128,768]{1,0:T(8,128)(2,1)}) custom-call(bf16[2,64,768]{2,1,0:T(8,128)(2,1)} %get-tuple-element.26.refs_0_, bf16[2,64,768]{2,1,0:T(8,128)(2,1)} %collective-permute-done.5.refs_1_, ...), custom_call_target="tpu_custom_call" | custom-call | flops 4000000000 | bytes 10000000 | tf_op jit(solution)/shard_map/attend/pallas_call | solution.py:471
  44.0 0.0 collective-permute-done.4.refs_3_
  44.1 2.1 %collective-permute-done.3.refs_2_ = bf16[2,64,768]{2,1,0:T(8,128)(2,1)} collective-permute-done((bf16[2,64,768]{2,1,0:T(8,128)(2,1)}, bf16[2,64,768]{2,1,0:T(8,128)(2,1)}, u32[]{:S(2)}, u32[]{:S(2)}) %collective-permute-start.3) | collective-permute-done | bytes 196640 | tf_op jit(solution)/shard_map/ppermute | solution.py:782
  46.2 0.0 collective-permute-done.2.refs_1_
  46.2 11.4 %tokens.1 = (f32[256,768]{1,0:T(8,128)}, bf16[256,1536]{1,0:T(8,128)(2,1)}, bf16[8,8,32,128]{3,2,1,0:T(8,128)(2,1)}) custom-call(bf16[2,64,768]{2,1,0:T(8,128)(2,1)} %get-tuple-element.25.refs_4_.refs_0_, bf16[2,64,768]{2,1,0:T(8,128)(2,1)} %collective-permute-done.2.refs_1_, bf16[2,64,768]{2,1,0:T(8,128)(2,1)} %collective-permute-done.3.refs_2_, ...), custom_call_target="tpu_custom_call" | custom-call | flops 10000000000 | bytes 20000000 | tf_op jit(solution)/shard_map/tokens/pallas_call | solution.py:616
  57.6 5.7 %all-to-all-start.1 = ((bf16[8,8,32,128]{3,2,1,0:T(8,128)(2,1)}), bf16[8,8,32,128]{3,2,1,0:T(8,128)(2,1)}, u32[]{:S(2)}, u32[]{:S(2)}) async-start(bf16[8,8,32,128]{3,2,1,0:T(8,128)(2,1)} %get-tuple-element.37), calls=%async_computation.1 | async-start | bytes 1048576 | tf_op jit(solution)/shard_map/all_to_all | solution.py:826
  63.3 7.4 %output.1 = (bf16[256,768]{1,0:T(8,128)(2,1)}, f32[2048,128]{1,0:T(8,128)}, f32[32,128]{1,0:T(8,128)}) custom-call(f32[256,768]{1,0:T(8,128)} %get-tuple-element.34.resid_ref, bf16[256,1536]{1,0:T(8,128)(2,1)} %get-tuple-element.35.hidden_ref, bf16[1536,768]{1,0:T(8,128)(2,1)} %w_down_ref.1, bf16[64,32,128]{2,1,0:T(8,128)(2,1)} %pair_ref.1), custom_call_target="tpu_custom_call" | custom-call | flops 1000000000 | bytes 8000000 | tf_op jit(solution)/shard_map/output/pallas_call | solution.py:683
  70.7 6.9 %all-to-all-done.1.parts_hbm = bf16[8,8,32,128]{3,2,1,0:T(8,128)(2,1)} async-done(((bf16[8,8,32,128]{3,2,1,0:T(8,128)(2,1)}), bf16[8,8,32,128]{3,2,1,0:T(8,128)(2,1)}, u32[]{:S(2)}, u32[]{:S(2)}) %all-to-all-start.1) | async-done | bytes 524320 | tf_op jit(solution)/shard_map/all_to_all | solution.py:826
  77.6 3.7 %pair_grad.1 = f32[64,32,128]{2,1,0:T(8,128)} custom-call(bf16[8,8,32,128]{3,2,1,0:T(8,128)(2,1)} %all-to-all-done.1.parts_hbm, f32[2048,128]{1,0:T(8,128)} %get-tuple-element.38.hat_hbm, f32[32,128]{1,0:T(8,128)} %get-tuple-element.39.rstd_hbm, f32[1,128]{1,0:T(1,128)} %bitcast.8, bf16[16,128]{1,0:T(8,128)(2,1)} %bitcast.6), custom_call_target="tpu_custom_call" | custom-call | flops 100000000 | bytes 4000000 | tf_op jit(solution)/shard_map/pair_grad/pallas_call | solution.py:760
Async XLA Ops:
  4.2 8.6 %collective-permute-start = (bf16[4,48,128]{2,1,0:T(8,128)(2,1)}, bf16[4,48,128]{2,1,0:T(8,128)(2,1)}, u32[]{:S(2)}, u32[]{:S(2)}) collective-permute-start(bf16[4,48,128]{2,1,0:T(8,128)(2,1)} %get-tuple-element.21), channel_id=1, source_target_pairs={{0,1},{1,0},{2,3},{3,2},{4,5},{5,4},{6,7},{7,6},{8,9},{9,8},{10,11... | collective-permute-start | bytes 147464 | tf_op jit(solution)/shard_map/ppermute | solution.py:782
  4.7 8.1 %collective-permute-start.1 = (bf16[4,48,128]{2,1,0:T(8,128)(2,1)}, bf16[4,48,128]{2,1,0:T(8,128)(2,1)}, u32[]{:S(2)}, u32[]{:S(2)}) collective-permute-start(bf16[4,48,128]{2,1,0:T(8,128)(2,1)} %get-tuple-element.22), channel_id=1, source_target_pairs={{1,2},{2,1},{5,6},{6,5},{9,10},{10,9},{13,14},{14,13},{17,18},{18,... | collective-permute-start | bytes 147464 | tf_op jit(solution)/shard_map/ppermute | solution.py:803
  5.9 30.6 %all-to-all-start = ((bf16[8,256,128]{2,1,0:T(8,128)(2,1)}), bf16[8,256,128]{2,1,0:T(8,128)(2,1)}, u32[]{:S(2)}, u32[]{:S(2)}) async-start(bf16[8,256,128]{2,1,0:T(8,128)(2,1)} %get-tuple-element.23), calls=%async_computation | async-start | bytes 1048576 | tf_op jit(solution)/shard_map/all_to_all | solution.py:805
  21.7 14.9 %collective-permute-start.7 = (bf16[2,64,768]{2,1,0:T(8,128)(2,1)}, bf16[2,64,768]{2,1,0:T(8,128)(2,1)}, u32[]{:S(2)}, u32[]{:S(2)}) collective-permute-start(bf16[2,64,768]{2,1,0:T(8,128)(2,1)} %get-tuple-element.26.refs_0_), channel_id=1, source_target_pairs={{0,3},{1,2},{2,1},{3,0},{4,7},{5,6},{6,5},{7,4},{8,11},{9,10},{10,... | collective-permute-start | bytes 589832 | tf_op jit(solution)/shard_map/ppermute | solution.py:782
  23.0 13.5 %collective-permute-start.6 = (bf16[2,64,768]{2,1,0:T(8,128)(2,1)}, bf16[2,64,768]{2,1,0:T(8,128)(2,1)}, u32[]{:S(2)}, u32[]{:S(2)}) collective-permute-start(bf16[2,64,768]{2,1,0:T(8,128)(2,1)} %get-tuple-element.26.refs_0_), channel_id=1, source_target_pairs={{0,2},{1,3},{2,0},{3,1},{4,6},{5,7},{6,4},{7,5},{8,10},{9,11},{10,... | collective-permute-start | bytes 589832 | tf_op jit(solution)/shard_map/ppermute | solution.py:782
  25.3 11.2 %collective-permute-start.5 = (bf16[2,64,768]{2,1,0:T(8,128)(2,1)}, bf16[2,64,768]{2,1,0:T(8,128)(2,1)}, u32[]{:S(2)}, u32[]{:S(2)}) collective-permute-start(bf16[2,64,768]{2,1,0:T(8,128)(2,1)} %get-tuple-element.26.refs_0_), channel_id=1, source_target_pairs={{0,1},{1,0},{2,3},{3,2},{4,5},{5,4},{6,7},{7,6},{8,9},{9,8},{10,11... | collective-permute-start | bytes 589832 | tf_op jit(solution)/shard_map/ppermute | solution.py:782
  34.4 9.7 %collective-permute-start.4 = (bf16[2,64,768]{2,1,0:T(8,128)(2,1)}, bf16[2,64,768]{2,1,0:T(8,128)(2,1)}, u32[]{:S(2)}, u32[]{:S(2)}) collective-permute-start(bf16[2,64,768]{2,1,0:T(8,128)(2,1)} %get-tuple-element.25.refs_4_.refs_0_), channel_id=1, source_target_pairs={{0,3},{1,2},{2,1},{3,0},{4,7},{5,6},{6,5},{7,4},{8,11},{9,10},{10,... | collective-permute-start | bytes 589832 | tf_op jit(solution)/shard_map/ppermute | solution.py:782
  35.1 11.1 %collective-permute-start.3 = (bf16[2,64,768]{2,1,0:T(8,128)(2,1)}, bf16[2,64,768]{2,1,0:T(8,128)(2,1)}, u32[]{:S(2)}, u32[]{:S(2)}) collective-permute-start(bf16[2,64,768]{2,1,0:T(8,128)(2,1)} %get-tuple-element.25.refs_4_.refs_0_), channel_id=1, source_target_pairs={{0,2},{1,3},{2,0},{3,1},{4,6},{5,7},{6,4},{7,5},{8,10},{9,11},{10,... | collective-permute-start | bytes 589832 | tf_op jit(solution)/shard_map/ppermute | solution.py:782
  36.6 9.6 %collective-permute-start.2 = (bf16[2,64,768]{2,1,0:T(8,128)(2,1)}, bf16[2,64,768]{2,1,0:T(8,128)(2,1)}, u32[]{:S(2)}, u32[]{:S(2)}) collective-permute-start(bf16[2,64,768]{2,1,0:T(8,128)(2,1)} %get-tuple-element.25.refs_4_.refs_0_), channel_id=1, source_target_pairs={{0,1},{1,0},{2,3},{3,2},{4,5},{5,4},{6,7},{7,6},{8,9},{9,8},{10,11... | collective-permute-start | bytes 589832 | tf_op jit(solution)/shard_map/ppermute | solution.py:782
  57.6 20.0 %all-to-all-start.1 = ((bf16[8,8,32,128]{3,2,1,0:T(8,128)(2,1)}), bf16[8,8,32,128]{3,2,1,0:T(8,128)(2,1)}, u32[]{:S(2)}, u32[]{:S(2)}) async-start(bf16[8,8,32,128]{3,2,1,0:T(8,128)(2,1)} %get-tuple-element.37), calls=%async_computation.1 | async-start | bytes 1048576 | tf_op jit(solution)/shard_map/all_to_all | solution.py:826

commit v13 on v12

--- a/solution.py
+++ b/solution.py
@@ -150,7 +150,7 @@
     feats_hbm, near_hbm, next_hbm, mask_hbm, counts_hbm, single_hbm, w_qkv_hbm, w_out_hbm,
     w_embed_hbm, tokens_ref, normed_ref, mask_ref, counts_ref, single_ref, w_qkv_ref, w_out_ref,
     w_embed_ref, sems, halos_ref, padded_ref, normed_atoms_ref, qkv_a, qkv_b, scores_a, scores_b,
-    probs_a, probs_b, mixed_ref,
+    probs_a, probs_b, mixed_a, mixed_b,
     updated_ref, split_ref, keybias_ref, onehot_ref, *, first,
 ):
     batch, atoms = tokens_ref.shape[0], feats_hbm.shape[1]
@@ -167,7 +167,7 @@
     tok_rows = single_ref.shape[0]
     blocks = atoms // 128
     chunks = atoms // 256
-    qkv_refs = (qkv_a, qkv_b)
+    qkv_refs, mixed_refs = (qkv_a, qkv_b), (mixed_a, mixed_b)
 
     eye = iota((128, 128), 0) == iota((128, 128), 1)
     for b in range(-1, blocks + 1):
@@ -245,20 +245,24 @@
                 for h in range(1, ATOM_HEADS):
                     mix = jnp.where(head_of == h, part[32 * h : 32 * h + 32], mix)
                 mixes.append(mix.astype(bf16))
-            mixed_ref[pl.ds(base, 64), :] = jnp.concatenate(mixes, axis=0)
-
-    def embed_step(s):
-        feats = padded_ref[s, HALO : HALO + atoms, :].astype(f32)
-        updated_ref[...] = (feats + nn(mixed_ref[...], w_out_ref[...])).astype(bf16)
-        for n in range(0, C_TOK, 256):
-            embedded = jnp.maximum(nn(updated_ref[...], w_embed_ref[:, n : n + 256]), 0.0)
+            mixed_refs[s % 2][pl.ds(base, 64), :] = jnp.concatenate(mixes, axis=0)
+
+    def embed_step(s, part):
+        if part == 0:
+            feats = padded_ref[s, HALO : HALO + atoms, :].astype(f32)
+            mixed = mixed_refs[s % 2][...]
+            updated_ref[...] = (feats + nn(mixed, w_out_ref[...])).astype(bf16)
+        elif part < 4:
+            cols = slice(256 * (part - 1), 256 * part)
+            embedded = jnp.maximum(nn(updated_ref[...], w_embed_ref[:, cols]), 0.0)
             high = embedded.astype(bf16)
-            split_ref[0:atoms, n : n + 256] = high
-            split_ref[atoms : 2 * atoms, n : n + 256] = (embedded - high.astype(f32)).astype(bf16)
-        pooled = nn(onehot_ref[...], split_ref[...])
-        tokens = pooled / own + single_ref[...].astype(f32)
-        tokens_ref[s] = tokens
-        normed_ref[s] = norm_rows(tokens)[0].astype(bf16)
+            split_ref[0:atoms, cols] = high
+            split_ref[atoms : 2 * atoms, cols] = (embedded - high.astype(f32)).astype(bf16)
+        else:
+            pooled = nn(onehot_ref[...], split_ref[...])
+            tokens = pooled / own + single_ref[...].astype(f32)
+            tokens_ref[s] = tokens
+            normed_ref[s] = norm_rows(tokens)[0].astype(bf16)
 
     for copy in copies[2:]:
         copy.wait()
@@ -280,10 +284,13 @@
                 score_step(s, odd + 1, scores_a)
             softmax_step(odd, scores_b, probs_b)
             value_step(s, even, probs_a)
+            if s > 0:
+                embed_step(s - 1, i)
+            if s + 1 < batch and i == chunks // 2:
+                qkv_step(s + 1)
         value_step(s, 2 * chunks - 1, probs_b)
-        embed_step(s)
-        if s + 1 < batch:
-            qkv_step(s + 1)
+    for part in range(5):
+        embed_step(batch - 1, part)
 
 
 def atom_stage(part, batch, feats, near, next_, mask, counts, single, w_qkv, w_out, w_embed):
@@ -315,6 +322,7 @@
             pltpu.VMEM((2, 160, 256), f32),
             pltpu.VMEM((4, 128, 128), bf16),
             pltpu.VMEM((4, 128, 128), bf16),
+            pltpu.VMEM((atoms, C_ATOM), bf16),
             pltpu.VMEM((atoms, C_ATOM), bf16),
             pltpu.VMEM((atoms, C_ATOM), bf16),
             pltpu.VMEM((2 * atoms, C_TOK), bf16),

time: 81.8 us -> 81.3 us (level)
  no operation moved by 1% of the time
where the time goes in v13:
time: 81.3 us; the launch traced here: 80.9 us
  Pallas kernels  50.8 us (62%)
  starting transfers between devices  20.2 us (25%)
  waiting for transfers between devices  8.97 us (11%)
  between operations  0.87 us (1%)
    pallas_call x2, Pallas kernels, atom_stage(): pl.pallas_call(functools.partial(atom_kernel, first=part * batch), in_spe...  17.3 us
    pallas_call x1, Pallas kernels, token_stage(): pl.pallas_call(functools.partial(token_kernel, count=len(pieces)), in_spe...  11.4 us
    pallas_call x1, Pallas kernels, attend_stage(): pl.pallas_call(functools.partial(attend_kernel, count=len(pieces)), in_sp...  7.45 us
    pallas_call x1, Pallas kernels, output_stage(): pl.pallas_call(output_kernel, out_shape=[jax.ShapeDtypeStruct(resid.shape...  7.41 us
    all_to_all x1, waiting for transfers between devices, body(): parts = lax.all_to_all(d_bias, 'samp', 0, 0)  6.86 us
    all_to_all x1, starting transfers between devices, body(): lax.all_to_all(local_bias, 'samp', 0, 0)  6.86 us
    ppermute x7, starting transfers between devices, swap(): lax.ppermute(values, axis, [(i, i ^ k) for i in range(lax.axis_size(axis))])  6.41 us
    all_to_all x1, starting transfers between devices, body(): parts = lax.all_to_all(d_bias, 'samp', 0, 0)  5.72 us
  transfers between devices with their start and end apart: 10, of which 2 were waited for; matrix products, arithmetic and copies ran while one was open for 0% of the time, Pallas kernels for 40%

profile of v13, /device:TPU:0, one launch (start us, length us, event | category | flops | bytes accessed | tf_op | source)
XLA Modules:
  0.0 80.9 jit_solution(15587379411904167071)
XLA Ops:
  0.6 3.5 %pair_bias.1 = (bf16[8,256,128]{2,1,0:T(8,128)(2,1)}, bf16[4,48,128]{2,1,0:T(8,128)(2,1)}, bf16[4,48,128]{2,1,0:T(8,128)(2,1)}) custom-call(bf16[64,32,128]{2,1,0:T(8,128)(2,1)} %pair_ref.1, f32[1,128]{1,0:T(1,128)} %bitcast.7, bf16[16,128]{1,0:T(8,128)(2,1)} %bitcast.5, bf16[4,1280,128]{2,1,0:T(8,128)(2,1)} %feats_hbm.5), custom_call_target="tpu_custom_call" | custom-call | flops 10000000 | bytes 10000000 | tf_op jit(solution)/shard_map/pair_bias/pallas_call | solution.py:125
  4.2 0.5 collective-permute-start
  4.7 1.3 %collective-permute-start.1 = (bf16[4,48,128]{2,1,0:T(8,128)(2,1)}, bf16[4,48,128]{2,1,0:T(8,128)(2,1)}, u32[]{:S(2)}, u32[]{:S(2)}) collective-permute-start(bf16[4,48,128]{2,1,0:T(8,128)(2,1)} %get-tuple-element.22), channel_id=1, source_target_pairs={{1,2},{2,1},{5,6},{6,5},{9,10},{10,9},{13,14},{14,13},{17,18},{18,... | collective-permute-start | bytes 147464 | tf_op jit(solution)/shard_map/ppermute | solution.py:811
  5.9 6.9 %all-to-all-start = ((bf16[8,256,128]{2,1,0:T(8,128)(2,1)}), bf16[8,256,128]{2,1,0:T(8,128)(2,1)}, u32[]{:S(2)}, u32[]{:S(2)}) async-start(bf16[8,256,128]{2,1,0:T(8,128)(2,1)} %get-tuple-element.23), calls=%async_computation | async-start | bytes 1048576 | tf_op jit(solution)/shard_map/all_to_all | solution.py:813
  12.8 0.0 collective-permute-done.near_hbm
  12.8 0.0 collective-permute-done.1.next_hbm
  12.8 8.6 %atoms.3 = (f32[2,64,768]{2,1,0:T(8,128)}, bf16[2,64,768]{2,1,0:T(8,128)(2,1)}) custom-call(bf16[4,1280,128]{2,1,0:T(8,128)(2,1)} %feats_hbm.5, bf16[4,48,128]{2,1,0:T(8,128)(2,1)} %collective-permute-done.near_hbm, bf16[4,48,128]{2,1,0:T(8,128)(2,1)} %collective-permute-done.1.next_hbm, s32[40,128]{1,0:T(8,128)} %bitcast.10, s32[1,64]{1,0:T(1,128)} %counts_hbm.3, ...), custom_call_target="tpu_custom_call" | custom-call | flops 10000000000 | bytes 4000000 | tf_op jit(solution)/shard_map/atoms/pallas_call | solution.py:300
  21.4 1.4 %collective-permute-start.7 = (bf16[2,64,768]{2,1,0:T(8,128)(2,1)}, bf16[2,64,768]{2,1,0:T(8,128)(2,1)}, u32[]{:S(2)}, u32[]{:S(2)}) collective-permute-start(bf16[2,64,768]{2,1,0:T(8,128)(2,1)} %get-tuple-element.26.refs_0_), channel_id=1, source_target_pairs={{0,3},{1,2},{2,1},{3,0},{4,7},{5,6},{6,5},{7,4},{8,11},{9,10},{10,... | collective-permute-start | bytes 589832 | tf_op jit(solution)/shard_map/ppermute | solution.py:790
  22.8 2.3 %collective-permute-start.6 = (bf16[2,64,768]{2,1,0:T(8,128)(2,1)}, bf16[2,64,768]{2,1,0:T(8,128)(2,1)}, u32[]{:S(2)}, u32[]{:S(2)}) collective-permute-start(bf16[2,64,768]{2,1,0:T(8,128)(2,1)} %get-tuple-element.26.refs_0_), channel_id=1, source_target_pairs={{0,2},{1,3},{2,0},{3,1},{4,6},{5,7},{6,4},{7,5},{8,10},{9,11},{10,... | collective-permute-start | bytes 589832 | tf_op jit(solution)/shard_map/ppermute | solution.py:790
  25.1 0.0 collective-permute-start.5
  25.1 8.7 %atoms.2 = (f32[2,64,768]{2,1,0:T(8,128)}, bf16[2,64,768]{2,1,0:T(8,128)(2,1)}) custom-call(bf16[4,1280,128]{2,1,0:T(8,128)(2,1)} %feats_hbm.5, bf16[4,48,128]{2,1,0:T(8,128)(2,1)} %collective-permute-done.near_hbm, bf16[4,48,128]{2,1,0:T(8,128)(2,1)} %collective-permute-done.1.next_hbm, s32[40,128]{1,0:T(8,128)} %bitcast.11, s32[1,64]{1,0:T(1,128)} %counts_hbm.3, ...), custom_call_target="tpu_custom_call" | custom-call | flops 10000000000 | bytes 4000000 | tf_op jit(solution)/shard_map/atoms/pallas_call | solution.py:300
  33.8 0.7 collective-permute-start.4
  34.5 1.5 %collective-permute-start.3 = (bf16[2,64,768]{2,1,0:T(8,128)(2,1)}, bf16[2,64,768]{2,1,0:T(8,128)(2,1)}, u32[]{:S(2)}, u32[]{:S(2)}) collective-permute-start(bf16[2,64,768]{2,1,0:T(8,128)(2,1)} %get-tuple-element.25.refs_4_.refs_0_), channel_id=1, source_target_pairs={{0,2},{1,3},{2,0},{3,1},{4,6},{5,7},{6,4},{7,5},{8,10},{9,11},{10,... | collective-permute-start | bytes 589832 | tf_op jit(solution)/shard_map/ppermute | solution.py:790
  36.0 0.0 collective-permute-done.7.refs_3_
  36.0 0.0 collective-permute-start.2
  36.0 0.0 collective-permute-done.6.refs_2_
  36.0 0.0 collective-permute-done.5.refs_1_
  36.0 0.0 all-to-all-done
  36.0 7.4 %attend.1 = (bf16[128,768]{1,0:T(8,128)(2,1)}, f32[2,8,256,128]{3,2,1,0:T(8,128)}, bf16[2,256,768]{2,1,0:T(8,128)(2,1)}, f32[256,1536]{1,0:T(8,128)}, bf16[128,768]{1,0:T(8,128)(2,1)}) custom-call(bf16[2,64,768]{2,1,0:T(8,128)(2,1)} %get-tuple-element.26.refs_0_, bf16[2,64,768]{2,1,0:T(8,128)(2,1)} %collective-permute-done.5.refs_1_, ...), custom_call_target="tpu_custom_call" | custom-call | flops 4000000000 | bytes 10000000 | tf_op jit(solution)/shard_map/attend/pallas_call | solution.py:479
  43.5 0.0 collective-permute-done.4.refs_3_
  43.5 2.1 %collective-permute-done.3.refs_2_ = bf16[2,64,768]{2,1,0:T(8,128)(2,1)} collective-permute-done((bf16[2,64,768]{2,1,0:T(8,128)(2,1)}, bf16[2,64,768]{2,1,0:T(8,128)(2,1)}, u32[]{:S(2)}, u32[]{:S(2)}) %collective-permute-start.3) | collective-permute-done | bytes 196640 | tf_op jit(solution)/shard_map/ppermute | solution.py:790
  45.6 0.0 collective-permute-done.2.refs_1_
  45.6 11.4 %tokens.1 = (f32[256,768]{1,0:T(8,128)}, bf16[256,1536]{1,0:T(8,128)(2,1)}, bf16[8,8,32,128]{3,2,1,0:T(8,128)(2,1)}) custom-call(bf16[2,64,768]{2,1,0:T(8,128)(2,1)} %get-tuple-element.25.refs_4_.refs_0_, bf16[2,64,768]{2,1,0:T(8,128)(2,1)} %collective-permute-done.2.refs_1_, bf16[2,64,768]{2,1,0:T(8,128)(2,1)} %collective-permute-done.3.refs_2_, ...), custom_call_target="tpu_custom_call" | custom-call | flops 10000000000 | bytes 20000000 | tf_op jit(solution)/shard_map/tokens/pallas_call | solution.py:624
  57.0 5.7 %all-to-all-start.1 = ((bf16[8,8,32,128]{3,2,1,0:T(8,128)(2,1)}), bf16[8,8,32,128]{3,2,1,0:T(8,128)(2,1)}, u32[]{:S(2)}, u32[]{:S(2)}) async-start(bf16[8,8,32,128]{3,2,1,0:T(8,128)(2,1)} %get-tuple-element.37), calls=%async_computation.1 | async-start | bytes 1048576 | tf_op jit(solution)/shard_map/all_to_all | solution.py:834
  62.7 7.4 %output.1 = (bf16[256,768]{1,0:T(8,128)(2,1)}, f32[2048,128]{1,0:T(8,128)}, f32[32,128]{1,0:T(8,128)}) custom-call(f32[256,768]{1,0:T(8,128)} %get-tuple-element.34.resid_ref, bf16[256,1536]{1,0:T(8,128)(2,1)} %get-tuple-element.35.hidden_ref, bf16[1536,768]{1,0:T(8,128)(2,1)} %w_down_ref.1, bf16[64,32,128]{2,1,0:T(8,128)(2,1)} %pair_ref.1), custom_call_target="tpu_custom_call" | custom-call | flops 1000000000 | bytes 8000000 | tf_op jit(solution)/shard_map/output/pallas_call | solution.py:691
  70.1 6.9 %all-to-all-done.1.parts_hbm = bf16[8,8,32,128]{3,2,1,0:T(8,128)(2,1)} async-done(((bf16[8,8,32,128]{3,2,1,0:T(8,128)(2,1)}), bf16[8,8,32,128]{3,2,1,0:T(8,128)(2,1)}, u32[]{:S(2)}, u32[]{:S(2)}) %all-to-all-start.1) | async-done | bytes 524320 | tf_op jit(solution)/shard_map/all_to_all | solution.py:834
  77.0 3.7 %pair_grad.1 = f32[64,32,128]{2,1,0:T(8,128)} custom-call(bf16[8,8,32,128]{3,2,1,0:T(8,128)(2,1)} %all-to-all-done.1.parts_hbm, f32[2048,128]{1,0:T(8,128)} %get-tuple-element.38.hat_hbm, f32[32,128]{1,0:T(8,128)} %get-tuple-element.39.rstd_hbm, f32[1,128]{1,0:T(1,128)} %bitcast.8, bf16[16,128]{1,0:T(8,128)(2,1)} %bitcast.6), custom_call_target="tpu_custom_call" | custom-call | flops 100000000 | bytes 4000000 | tf_op jit(solution)/shard_map/pair_grad/pallas_call | solution.py:768
Async XLA Ops:
  4.2 8.6 %collective-permute-start = (bf16[4,48,128]{2,1,0:T(8,128)(2,1)}, bf16[4,48,128]{2,1,0:T(8,128)(2,1)}, u32[]{:S(2)}, u32[]{:S(2)}) collective-permute-start(bf16[4,48,128]{2,1,0:T(8,128)(2,1)} %get-tuple-element.21), channel_id=1, source_target_pairs={{0,1},{1,0},{2,3},{3,2},{4,5},{5,4},{6,7},{7,6},{8,9},{9,8},{10,11... | collective-permute-start | bytes 147464 | tf_op jit(solution)/shard_map/ppermute | solution.py:790
  4.7 8.1 %collective-permute-start.1 = (bf16[4,48,128]{2,1,0:T(8,128)(2,1)}, bf16[4,48,128]{2,1,0:T(8,128)(2,1)}, u32[]{:S(2)}, u32[]{:S(2)}) collective-permute-start(bf16[4,48,128]{2,1,0:T(8,128)(2,1)} %get-tuple-element.22), channel_id=1, source_target_pairs={{1,2},{2,1},{5,6},{6,5},{9,10},{10,9},{13,14},{14,13},{17,18},{18,... | collective-permute-start | bytes 147464 | tf_op jit(solution)/shard_map/ppermute | solution.py:811
  5.9 30.1 %all-to-all-start = ((bf16[8,256,128]{2,1,0:T(8,128)(2,1)}), bf16[8,256,128]{2,1,0:T(8,128)(2,1)}, u32[]{:S(2)}, u32[]{:S(2)}) async-start(bf16[8,256,128]{2,1,0:T(8,128)(2,1)} %get-tuple-element.23), calls=%async_computation | async-start | bytes 1048576 | tf_op jit(solution)/shard_map/all_to_all | solution.py:813
  21.4 14.6 %collective-permute-start.7 = (bf16[2,64,768]{2,1,0:T(8,128)(2,1)}, bf16[2,64,768]{2,1,0:T(8,128)(2,1)}, u32[]{:S(2)}, u32[]{:S(2)}) collective-permute-start(bf16[2,64,768]{2,1,0:T(8,128)(2,1)} %get-tuple-element.26.refs_0_), channel_id=1, source_target_pairs={{0,3},{1,2},{2,1},{3,0},{4,7},{5,6},{6,5},{7,4},{8,11},{9,10},{10,... | collective-permute-start | bytes 589832 | tf_op jit(solution)/shard_map/ppermute | solution.py:790
  22.8 13.3 %collective-permute-start.6 = (bf16[2,64,768]{2,1,0:T(8,128)(2,1)}, bf16[2,64,768]{2,1,0:T(8,128)(2,1)}, u32[]{:S(2)}, u32[]{:S(2)}) collective-permute-start(bf16[2,64,768]{2,1,0:T(8,128)(2,1)} %get-tuple-element.26.refs_0_), channel_id=1, source_target_pairs={{0,2},{1,3},{2,0},{3,1},{4,6},{5,7},{6,4},{7,5},{8,10},{9,11},{10,... | collective-permute-start | bytes 589832 | tf_op jit(solution)/shard_map/ppermute | solution.py:790
  25.1 10.9 %collective-permute-start.5 = (bf16[2,64,768]{2,1,0:T(8,128)(2,1)}, bf16[2,64,768]{2,1,0:T(8,128)(2,1)}, u32[]{:S(2)}, u32[]{:S(2)}) collective-permute-start(bf16[2,64,768]{2,1,0:T(8,128)(2,1)} %get-tuple-element.26.refs_0_), channel_id=1, source_target_pairs={{0,1},{1,0},{2,3},{3,2},{4,5},{5,4},{6,7},{7,6},{8,9},{9,8},{10,11... | collective-permute-start | bytes 589832 | tf_op jit(solution)/shard_map/ppermute | solution.py:790
  33.8 9.7 %collective-permute-start.4 = (bf16[2,64,768]{2,1,0:T(8,128)(2,1)}, bf16[2,64,768]{2,1,0:T(8,128)(2,1)}, u32[]{:S(2)}, u32[]{:S(2)}) collective-permute-start(bf16[2,64,768]{2,1,0:T(8,128)(2,1)} %get-tuple-element.25.refs_4_.refs_0_), channel_id=1, source_target_pairs={{0,3},{1,2},{2,1},{3,0},{4,7},{5,6},{6,5},{7,4},{8,11},{9,10},{10,... | collective-permute-start | bytes 589832 | tf_op jit(solution)/shard_map/ppermute | solution.py:790
  34.5 11.1 %collective-permute-start.3 = (bf16[2,64,768]{2,1,0:T(8,128)(2,1)}, bf16[2,64,768]{2,1,0:T(8,128)(2,1)}, u32[]{:S(2)}, u32[]{:S(2)}) collective-permute-start(bf16[2,64,768]{2,1,0:T(8,128)(2,1)} %get-tuple-element.25.refs_4_.refs_0_), channel_id=1, source_target_pairs={{0,2},{1,3},{2,0},{3,1},{4,6},{5,7},{6,4},{7,5},{8,10},{9,11},{10,... | collective-permute-start | bytes 589832 | tf_op jit(solution)/shard_map/ppermute | solution.py:790
  36.0 9.6 %collective-permute-start.2 = (bf16[2,64,768]{2,1,0:T(8,128)(2,1)}, bf16[2,64,768]{2,1,0:T(8,128)(2,1)}, u32[]{:S(2)}, u32[]{:S(2)}) collective-permute-start(bf16[2,64,768]{2,1,0:T(8,128)(2,1)} %get-tuple-element.25.refs_4_.refs_0_), channel_id=1, source_target_pairs={{0,1},{1,0},{2,3},{3,2},{4,5},{5,4},{6,7},{7,6},{8,9},{9,8},{10,11... | collective-permute-start | bytes 589832 | tf_op jit(solution)/shard_map/ppermute | solution.py:790
  57.0 20.0 %all-to-all-start.1 = ((bf16[8,8,32,128]{3,2,1,0:T(8,128)(2,1)}), bf16[8,8,32,128]{3,2,1,0:T(8,128)(2,1)}, u32[]{:S(2)}, u32[]{:S(2)}) async-start(bf16[8,8,32,128]{3,2,1,0:T(8,128)(2,1)} %get-tuple-element.37), calls=%async_computation.1 | async-start | bytes 1048576 | tf_op jit(solution)/shard_map/all_to_all | solution.py:834

commit v14 on v13

--- a/solution.py
+++ b/solution.py
@@ -151,7 +151,7 @@
     w_embed_hbm, tokens_ref, normed_ref, mask_ref, counts_ref, single_ref, w_qkv_ref, w_out_ref,
     w_embed_ref, sems, halos_ref, padded_ref, normed_atoms_ref, qkv_a, qkv_b, scores_a, scores_b,
     probs_a, probs_b, mixed_a, mixed_b,
-    updated_ref, split_ref, keybias_ref, onehot_ref, *, first,
+    updated_ref, split_ref, last_ref, keybias_ref, onehot_ref, *, first,
 ):
     batch, atoms = tokens_ref.shape[0], feats_hbm.shape[1]
     padded = atoms + 2 * HALO
@@ -259,10 +259,21 @@
             split_ref[0:atoms, cols] = high
             split_ref[atoms : 2 * atoms, cols] = (embedded - high.astype(f32)).astype(bf16)
         else:
-            pooled = nn(onehot_ref[...], split_ref[...])
+            pooled = nn(onehot_ref[...], (last_ref if s + 1 == batch else split_ref)[...])
             tokens = pooled / own + single_ref[...].astype(f32)
             tokens_ref[s] = tokens
             normed_ref[s] = norm_rows(tokens)[0].astype(bf16)
+
+    def embed_rows(s, g):
+        rows = slice(256 * g, 256 * g + 256)
+        feats = padded_ref[s, HALO + 256 * g : HALO + 256 * g + 256, :].astype(f32)
+        updated = (feats + nn(mixed_refs[s % 2][rows, :], w_out_ref[...])).astype(bf16)
+        embedded = jnp.maximum(nn(updated, w_embed_ref[...]), 0.0)
+        high = embedded.astype(bf16)
+        last_ref[rows, :] = high
+        last_ref[atoms + 256 * g : atoms + 256 * g + 256, :] = (
+            embedded - high.astype(f32)
+        ).astype(bf16)
 
     for copy in copies[2:]:
         copy.wait()
@@ -288,9 +299,11 @@
                 embed_step(s - 1, i)
             if s + 1 < batch and i == chunks // 2:
                 qkv_step(s + 1)
+            if s + 1 == batch and i > 0:
+                embed_rows(s, i - 1)
         value_step(s, 2 * chunks - 1, probs_b)
-    for part in range(5):
-        embed_step(batch - 1, part)
+    embed_rows(batch - 1, chunks - 1)
+    embed_step(batch - 1, 4)
 
 
 def atom_stage(part, batch, feats, near, next_, mask, counts, single, w_qkv, w_out, w_embed):
@@ -325,6 +338,7 @@
             pltpu.VMEM((atoms, C_ATOM), bf16),
             pltpu.VMEM((atoms, C_ATOM), bf16),
             pltpu.VMEM((atoms, C_ATOM), bf16),
+            pltpu.VMEM((2 * atoms, C_TOK), bf16),
             pltpu.VMEM((2 * atoms, C_TOK), bf16),
             pltpu.VMEM((padded, 128), f32),
             pltpu.VMEM((tok_rows, 2 * atoms), bf16),

time: 81.3 us -> 83 us (1.021)
  Pallas kernels: 50.8 us -> 52.4 us
    pallas_call x2, Pallas kernels: 17.3 us -> 18.8 us  [atom_stage(): pl.pallas_call(functools.partial(atom_kernel, first=part * batch), in_spe...]
  transfers between devices with their start and end apart: 10 -> 10, of which waited for: 2 -> 2; matrix products, arithmetic and copies ran while one was open for 0% -> 0% of each run, Pallas kernels for 40% -> 41%
where the time goes in v14:
time: 83 us; the launch traced here: 82.6 us
  Pallas kernels  52.4 us (63%)
  starting transfers between devices  20.2 us (24%)
  waiting for transfers between devices  8.99 us (11%)
  between operations  0.89 us (1%)
    pallas_call x2, Pallas kernels, atom_stage(): pl.pallas_call(functools.partial(atom_kernel, first=part * batch), in_spe...  18.8 us
    pallas_call x1, Pallas kernels, token_stage(): pl.pallas_call(functools.partial(token_kernel, count=len(pieces)), in_spe...  11.6 us
    pallas_call x1, Pallas kernels, attend_stage(): pl.pallas_call(functools.partial(attend_kernel, count=len(pieces)), in_sp...  7.44 us
    pallas_call x1, Pallas kernels, output_stage(): pl.pallas_call(output_kernel, out_shape=[jax.ShapeDtypeStruct(resid.shape...  7.41 us
    all_to_all x1, waiting for transfers between devices, body(): parts = lax.all_to_all(d_bias, 'samp', 0, 0)  6.87 us
    all_to_all x1, starting transfers between devices, body(): lax.all_to_all(local_bias, 'samp', 0, 0)  6.86 us
    ppermute x7, starting transfers between devices, swap(): lax.ppermute(values, axis, [(i, i ^ k) for i in range(lax.axis_size(axis))])  6.4 us
    all_to_all x1, starting transfers between devices, body(): parts = lax.all_to_all(d_bias, 'samp', 0, 0)  5.72 us
  transfers between devices with their start and end apart: 10, of which 2 were waited for; matrix products, arithmetic and copies ran while one was open for 0% of the time, Pallas kernels for 41%

profile of v14, /device:TPU:0, one launch (start us, length us, event | category | flops | bytes accessed | tf_op | source)
XLA Modules:
  0.0 82.6 jit_solution(8361922742804663801)
XLA Ops:
  0.6 3.5 %pair_bias.1 = (bf16[8,256,128]{2,1,0:T(8,128)(2,1)}, bf16[4,48,128]{2,1,0:T(8,128)(2,1)}, bf16[4,48,128]{2,1,0:T(8,128)(2,1)}) custom-call(bf16[64,32,128]{2,1,0:T(8,128)(2,1)} %pair_ref.1, f32[1,128]{1,0:T(1,128)} %bitcast.7, bf16[16,128]{1,0:T(8,128)(2,1)} %bitcast.5, bf16[4,1280,128]{2,1,0:T(8,128)(2,1)} %feats_hbm.5), custom_call_target="tpu_custom_call" | custom-call | flops 10000000 | bytes 10000000 | tf_op jit(solution)/shard_map/pair_bias/pallas_call | solution.py:125
  4.2 0.5 collective-permute-start
  4.7 1.3 %collective-permute-start.1 = (bf16[4,48,128]{2,1,0:T(8,128)(2,1)}, bf16[4,48,128]{2,1,0:T(8,128)(2,1)}, u32[]{:S(2)}, u32[]{:S(2)}) collective-permute-start(bf16[4,48,128]{2,1,0:T(8,128)(2,1)} %get-tuple-element.22), channel_id=1, source_target_pairs={{1,2},{2,1},{5,6},{6,5},{9,10},{10,9},{13,14},{14,13},{17,18},{18,... | collective-permute-start | bytes 147464 | tf_op jit(solution)/shard_map/ppermute | solution.py:825
  5.9 6.9 %all-to-all-start = ((bf16[8,256,128]{2,1,0:T(8,128)(2,1)}), bf16[8,256,128]{2,1,0:T(8,128)(2,1)}, u32[]{:S(2)}, u32[]{:S(2)}) async-start(bf16[8,256,128]{2,1,0:T(8,128)(2,1)} %get-tuple-element.23), calls=%async_computation | async-start | bytes 1048576 | tf_op jit(solution)/shard_map/all_to_all | solution.py:827
  12.8 0.0 collective-permute-done.near_hbm
  12.8 0.0 collective-permute-done.1.next_hbm
  12.8 9.3 %atoms.3 = (f32[2,64,768]{2,1,0:T(8,128)}, bf16[2,64,768]{2,1,0:T(8,128)(2,1)}) custom-call(bf16[4,1280,128]{2,1,0:T(8,128)(2,1)} %feats_hbm.5, bf16[4,48,128]{2,1,0:T(8,128)(2,1)} %collective-permute-done.near_hbm, bf16[4,48,128]{2,1,0:T(8,128)(2,1)} %collective-permute-done.1.next_hbm, s32[40,128]{1,0:T(8,128)} %bitcast.10, s32[1,64]{1,0:T(1,128)} %counts_hbm.3, ...), custom_call_target="tpu_custom_call" | custom-call | flops 10000000000 | bytes 4000000 | tf_op jit(solution)/shard_map/atoms/pallas_call | solution.py:313
  22.1 1.4 %collective-permute-start.7 = (bf16[2,64,768]{2,1,0:T(8,128)(2,1)}, bf16[2,64,768]{2,1,0:T(8,128)(2,1)}, u32[]{:S(2)}, u32[]{:S(2)}) collective-permute-start(bf16[2,64,768]{2,1,0:T(8,128)(2,1)} %get-tuple-element.26.refs_0_), channel_id=1, source_target_pairs={{0,3},{1,2},{2,1},{3,0},{4,7},{5,6},{6,5},{7,4},{8,11},{9,10},{10,... | collective-permute-start | bytes 589832 | tf_op jit(solution)/shard_map/ppermute | solution.py:804
  23.5 2.3 %collective-permute-start.6 = (bf16[2,64,768]{2,1,0:T(8,128)(2,1)}, bf16[2,64,768]{2,1,0:T(8,128)(2,1)}, u32[]{:S(2)}, u32[]{:S(2)}) collective-permute-start(bf16[2,64,768]{2,1,0:T(8,128)(2,1)} %get-tuple-element.26.refs_0_), channel_id=1, source_target_pairs={{0,2},{1,3},{2,0},{3,1},{4,6},{5,7},{6,4},{7,5},{8,10},{9,11},{10,... | collective-permute-start | bytes 589832 | tf_op jit(solution)/shard_map/ppermute | solution.py:804
  25.8 0.0 collective-permute-start.5
  25.8 9.4 %atoms.2 = (f32[2,64,768]{2,1,0:T(8,128)}, bf16[2,64,768]{2,1,0:T(8,128)(2,1)}) custom-call(bf16[4,1280,128]{2,1,0:T(8,128)(2,1)} %feats_hbm.5, bf16[4,48,128]{2,1,0:T(8,128)(2,1)} %collective-permute-done.near_hbm, bf16[4,48,128]{2,1,0:T(8,128)(2,1)} %collective-permute-done.1.next_hbm, s32[40,128]{1,0:T(8,128)} %bitcast.11, s32[1,64]{1,0:T(1,128)} %counts_hbm.3, ...), custom_call_target="tpu_custom_call" | custom-call | flops 10000000000 | bytes 4000000 | tf_op jit(solution)/shard_map/atoms/pallas_call | solution.py:313
  35.3 0.7 collective-permute-start.4
  35.9 1.5 %collective-permute-start.3 = (bf16[2,64,768]{2,1,0:T(8,128)(2,1)}, bf16[2,64,768]{2,1,0:T(8,128)(2,1)}, u32[]{:S(2)}, u32[]{:S(2)}) collective-permute-start(bf16[2,64,768]{2,1,0:T(8,128)(2,1)} %get-tuple-element.25.refs_4_.refs_0_), channel_id=1, source_target_pairs={{0,2},{1,3},{2,0},{3,1},{4,6},{5,7},{6,4},{7,5},{8,10},{9,11},{10,... | collective-permute-start | bytes 589832 | tf_op jit(solution)/shard_map/ppermute | solution.py:804
  37.5 0.0 collective-permute-done.7.refs_3_
  37.5 0.0 collective-permute-start.2
  37.5 0.0 collective-permute-done.6.refs_2_
  37.5 0.0 collective-permute-done.5.refs_1_
  37.5 0.0 all-to-all-done
  37.5 7.4 %attend.1 = (bf16[128,768]{1,0:T(8,128)(2,1)}, f32[2,8,256,128]{3,2,1,0:T(8,128)}, bf16[2,256,768]{2,1,0:T(8,128)(2,1)}, f32[256,1536]{1,0:T(8,128)}, bf16[128,768]{1,0:T(8,128)(2,1)}) custom-call(bf16[2,64,768]{2,1,0:T(8,128)(2,1)} %get-tuple-element.26.refs_0_, bf16[2,64,768]{2,1,0:T(8,128)(2,1)} %collective-permute-done.5.refs_1_, ...), custom_call_target="tpu_custom_call" | custom-call | flops 4000000000 | bytes 10000000 | tf_op jit(solution)/shard_map/attend/pallas_call | solution.py:493
  44.9 0.0 collective-permute-done.4.refs_3_
  45.0 2.1 %collective-permute-done.3.refs_2_ = bf16[2,64,768]{2,1,0:T(8,128)(2,1)} collective-permute-done((bf16[2,64,768]{2,1,0:T(8,128)(2,1)}, bf16[2,64,768]{2,1,0:T(8,128)(2,1)}, u32[]{:S(2)}, u32[]{:S(2)}) %collective-permute-start.3) | collective-permute-done | bytes 196640 | tf_op jit(solution)/shard_map/ppermute | solution.py:804
  47.1 0.0 collective-permute-done.2.refs_1_
  47.1 11.6 %tokens.1 = (f32[256,768]{1,0:T(8,128)}, bf16[256,1536]{1,0:T(8,128)(2,1)}, bf16[8,8,32,128]{3,2,1,0:T(8,128)(2,1)}) custom-call(bf16[2,64,768]{2,1,0:T(8,128)(2,1)} %get-tuple-element.25.refs_4_.refs_0_, bf16[2,64,768]{2,1,0:T(8,128)(2,1)} %collective-permute-done.2.refs_1_, bf16[2,64,768]{2,1,0:T(8,128)(2,1)} %collective-permute-done.3.refs_2_, ...), custom_call_target="tpu_custom_call" | custom-call | flops 10000000000 | bytes 20000000 | tf_op jit(solution)/shard_map/tokens/pallas_call | solution.py:638
  58.7 5.7 %all-to-all-start.1 = ((bf16[8,8,32,128]{3,2,1,0:T(8,128)(2,1)}), bf16[8,8,32,128]{3,2,1,0:T(8,128)(2,1)}, u32[]{:S(2)}, u32[]{:S(2)}) async-start(bf16[8,8,32,128]{3,2,1,0:T(8,128)(2,1)} %get-tuple-element.37), calls=%async_computation.1 | async-start | bytes 1048576 | tf_op jit(solution)/shard_map/all_to_all | solution.py:848
  64.4 7.4 %output.1 = (bf16[256,768]{1,0:T(8,128)(2,1)}, f32[2048,128]{1,0:T(8,128)}, f32[32,128]{1,0:T(8,128)}) custom-call(f32[256,768]{1,0:T(8,128)} %get-tuple-element.34.resid_ref, bf16[256,1536]{1,0:T(8,128)(2,1)} %get-tuple-element.35.hidden_ref, bf16[1536,768]{1,0:T(8,128)(2,1)} %w_down_ref.1, bf16[64,32,128]{2,1,0:T(8,128)(2,1)} %pair_ref.1), custom_call_target="tpu_custom_call" | custom-call | flops 1000000000 | bytes 8000000 | tf_op jit(solution)/shard_map/output/pallas_call | solution.py:705
  71.8 6.9 %all-to-all-done.1.parts_hbm = bf16[8,8,32,128]{3,2,1,0:T(8,128)(2,1)} async-done(((bf16[8,8,32,128]{3,2,1,0:T(8,128)(2,1)}), bf16[8,8,32,128]{3,2,1,0:T(8,128)(2,1)}, u32[]{:S(2)}, u32[]{:S(2)}) %all-to-all-start.1) | async-done | bytes 524320 | tf_op jit(solution)/shard_map/all_to_all | solution.py:848
  78.7 3.7 %pair_grad.1 = f32[64,32,128]{2,1,0:T(8,128)} custom-call(bf16[8,8,32,128]{3,2,1,0:T(8,128)(2,1)} %all-to-all-done.1.parts_hbm, f32[2048,128]{1,0:T(8,128)} %get-tuple-element.38.hat_hbm, f32[32,128]{1,0:T(8,128)} %get-tuple-element.39.rstd_hbm, f32[1,128]{1,0:T(1,128)} %bitcast.8, bf16[16,128]{1,0:T(8,128)(2,1)} %bitcast.6), custom_call_target="tpu_custom_call" | custom-call | flops 100000000 | bytes 4000000 | tf_op jit(solution)/shard_map/pair_grad/pallas_call | solution.py:782
Async XLA Ops:
  4.2 8.6 %collective-permute-start = (bf16[4,48,128]{2,1,0:T(8,128)(2,1)}, bf16[4,48,128]{2,1,0:T(8,128)(2,1)}, u32[]{:S(2)}, u32[]{:S(2)}) collective-permute-start(bf16[4,48,128]{2,1,0:T(8,128)(2,1)} %get-tuple-element.21), channel_id=1, source_target_pairs={{0,1},{1,0},{2,3},{3,2},{4,5},{5,4},{6,7},{7,6},{8,9},{9,8},{10,11... | collective-permute-start | bytes 147464 | tf_op jit(solution)/shard_map/ppermute | solution.py:804
  4.7 8.1 %collective-permute-start.1 = (bf16[4,48,128]{2,1,0:T(8,128)(2,1)}, bf16[4,48,128]{2,1,0:T(8,128)(2,1)}, u32[]{:S(2)}, u32[]{:S(2)}) collective-permute-start(bf16[4,48,128]{2,1,0:T(8,128)(2,1)} %get-tuple-element.22), channel_id=1, source_target_pairs={{1,2},{2,1},{5,6},{6,5},{9,10},{10,9},{13,14},{14,13},{17,18},{18,... | collective-permute-start | bytes 147464 | tf_op jit(solution)/shard_map/ppermute | solution.py:825
  5.9 31.5 %all-to-all-start = ((bf16[8,256,128]{2,1,0:T(8,128)(2,1)}), bf16[8,256,128]{2,1,0:T(8,128)(2,1)}, u32[]{:S(2)}, u32[]{:S(2)}) async-start(bf16[8,256,128]{2,1,0:T(8,128)(2,1)} %get-tuple-element.23), calls=%async_computation | async-start | bytes 1048576 | tf_op jit(solution)/shard_map/all_to_all | solution.py:827
  22.1 15.3 %collective-permute-start.7 = (bf16[2,64,768]{2,1,0:T(8,128)(2,1)}, bf16[2,64,768]{2,1,0:T(8,128)(2,1)}, u32[]{:S(2)}, u32[]{:S(2)}) collective-permute-start(bf16[2,64,768]{2,1,0:T(8,128)(2,1)} %get-tuple-element.26.refs_0_), channel_id=1, source_target_pairs={{0,3},{1,2},{2,1},{3,0},{4,7},{5,6},{6,5},{7,4},{8,11},{9,10},{10,... | collective-permute-start | bytes 589832 | tf_op jit(solution)/shard_map/ppermute | solution.py:804
  23.5 14.0 %collective-permute-start.6 = (bf16[2,64,768]{2,1,0:T(8,128)(2,1)}, bf16[2,64,768]{2,1,0:T(8,128)(2,1)}, u32[]{:S(2)}, u32[]{:S(2)}) collective-permute-start(bf16[2,64,768]{2,1,0:T(8,128)(2,1)} %get-tuple-element.26.refs_0_), channel_id=1, source_target_pairs={{0,2},{1,3},{2,0},{3,1},{4,6},{5,7},{6,4},{7,5},{8,10},{9,11},{10,... | collective-permute-start | bytes 589832 | tf_op jit(solution)/shard_map/ppermute | solution.py:804
  25.8 11.7 %collective-permute-start.5 = (bf16[2,64,768]{2,1,0:T(8,128)(2,1)}, bf16[2,64,768]{2,1,0:T(8,128)(2,1)}, u32[]{:S(2)}, u32[]{:S(2)}) collective-permute-start(bf16[2,64,768]{2,1,0:T(8,128)(2,1)} %get-tuple-element.26.refs_0_), channel_id=1, source_target_pairs={{0,1},{1,0},{2,3},{3,2},{4,5},{5,4},{6,7},{7,6},{8,9},{9,8},{10,11... | collective-permute-start | bytes 589832 | tf_op jit(solution)/shard_map/ppermute | solution.py:804
  35.3 9.7 %collective-permute-start.4 = (bf16[2,64,768]{2,1,0:T(8,128)(2,1)}, bf16[2,64,768]{2,1,0:T(8,128)(2,1)}, u32[]{:S(2)}, u32[]{:S(2)}) collective-permute-start(bf16[2,64,768]{2,1,0:T(8,128)(2,1)} %get-tuple-element.25.refs_4_.refs_0_), channel_id=1, source_target_pairs={{0,3},{1,2},{2,1},{3,0},{4,7},{5,6},{6,5},{7,4},{8,11},{9,10},{10,... | collective-permute-start | bytes 589832 | tf_op jit(solution)/shard_map/ppermute | solution.py:804
  35.9 11.1 %collective-permute-start.3 = (bf16[2,64,768]{2,1,0:T(8,128)(2,1)}, bf16[2,64,768]{2,1,0:T(8,128)(2,1)}, u32[]{:S(2)}, u32[]{:S(2)}) collective-permute-start(bf16[2,64,768]{2,1,0:T(8,128)(2,1)} %get-tuple-element.25.refs_4_.refs_0_), channel_id=1, source_target_pairs={{0,2},{1,3},{2,0},{3,1},{4,6},{5,7},{6,4},{7,5},{8,10},{9,11},{10,... | collective-permute-start | bytes 589832 | tf_op jit(solution)/shard_map/ppermute | solution.py:804
  37.5 9.6 %collective-permute-start.2 = (bf16[2,64,768]{2,1,0:T(8,128)(2,1)}, bf16[2,64,768]{2,1,0:T(8,128)(2,1)}, u32[]{:S(2)}, u32[]{:S(2)}) collective-permute-start(bf16[2,64,768]{2,1,0:T(8,128)(2,1)} %get-tuple-element.25.refs_4_.refs_0_), channel_id=1, source_target_pairs={{0,1},{1,0},{2,3},{3,2},{4,5},{5,4},{6,7},{7,6},{8,9},{9,8},{10,11... | collective-permute-start | bytes 589832 | tf_op jit(solution)/shard_map/ppermute | solution.py:804
  58.7 20.0 %all-to-all-start.1 = ((bf16[8,8,32,128]{3,2,1,0:T(8,128)(2,1)}), bf16[8,8,32,128]{3,2,1,0:T(8,128)(2,1)}, u32[]{:S(2)}, u32[]{:S(2)}) async-start(bf16[8,8,32,128]{3,2,1,0:T(8,128)(2,1)} %get-tuple-element.37), calls=%async_computation.1 | async-start | bytes 1048576 | tf_op jit(solution)/shard_map/all_to_all | solution.py:848
